TPU v7x, 32 devices: a whole 2x2x4 slice. The times are simulated.
32 devices in a mesh: dp: 8 (over y, x, core), tm: 4 (over z).
Axes of the slice: x: 2, y: 2, z: 4, core: 2. Of those that a mesh axis runs over, the one named last changes fastest.
Arguments:
- query_rows: bfloat16 [8, 896, 1024], P('dp', 'tm'), may hold values from -6 to 6
- key_rows: bfloat16 [8, 896, 1024], P('dp', 'tm'), may hold values from -6 to 6
- value_rows: bfloat16 [8, 896, 1024], P('dp', 'tm'), may hold values from -6 to 6
- head_scale: float32 [16], replicated, may hold values from 2 to 16
- out_proj: bfloat16 [1024, 1536], replicated, may hold values from -0.1875 to 0.1875
- conv_taps: float32 [31, 1536], replicated, may hold values from -1 to 1
- router: bfloat16 [1536, 8], replicated, may hold values from -0.15625 to 0.15625
- expert_in: bfloat16 [8, 2048, 1536], P('dp', 'tm'), may hold values from -0.15625 to 0.15625
- expert_out: bfloat16 [8, 2048, 1536], P('dp', 'tm'), may hold values from -0.125 to 0.125
- lengths: int32 [8, 4], P('dp'), may hold values from 1 to 672, 896 in all within a row
- routes: int32 [8, 896, 2], P('dp', 'tm'), may hold values from 0 to 7, all different within a row; in each aligned block of 224 rows (0 to 223, 224 to 447, ..., all dimensions but the last counted through in order) at most 84 rows name the same one
Outputs:
- block_out: bfloat16 [8, 896, 1536], P('dp', 'tm')
Inputs may be any that keep to these rules, and one draw needn't show every extreme that they name: Every length is at least 1, the 4 lengths of a pack sum to 896, and the largest of each pack is exactly 672. `routes`: the 2 experts of a frame differ. Among the 224 frames of one block (frames j * 224 to (j + 1) * 224 - 1 of a pack), no expert is named by more than 84 frames, and in some block some expert is named by exactly 84. Every expert is named somewhere.
All inputs are finite; a program needn't handle non-finite values.
Results may differ from a plain program's by a relative error of at most 0.0099.
Values may be sent and summed in bfloat16 or wider, within the bound.
No kernel may reach another device: no remote copies, remote signals or barrier semaphores. Data moves between devices by JAX's collectives and lax.ppermute only.
A program may use at most 128 MiB of HBM per device.

v0:
```python
import jax
import jax.numpy as jnp
from jax import lax
from jax.sharding import PartitionSpec as P

D = 1536
HEADS = 16
HEAD_DIM = 64
KERNEL = 31
TOPK = 2
RECS = 4


def with_halo(cells, sides, width):
    for axis, dim in sides:
        count = lax.axis_size(axis)
        ends = count - 1
        head = lax.slice_in_dim(cells, 0, width, axis=dim)
        tail = lax.slice_in_dim(cells, cells.shape[dim] - width, cells.shape[dim], axis=dim)
        cells = jnp.concatenate(
            [
                lax.ppermute(tail, axis, [(i, (i + 1) % count) for i in range(ends)]),
                cells,
                lax.ppermute(head, axis, [((i + 1) % count, i) for i in range(ends)]),
            ],
            axis=dim,
        )
    return cells


def layer_norm(values):
    average = jnp.mean(values, axis=-1, keepdims=True)
    centered = values - average
    spread = jnp.mean(centered * centered, axis=-1, keepdims=True)
    return centered * lax.rsqrt(spread + 1e-05)


def unit_heads(rows):
    lifted = rows.astype(jnp.float32).reshape(rows.shape[0], HEADS, HEAD_DIM)
    factor = lax.rsqrt(jnp.sum(lifted * lifted, axis=-1, keepdims=True) + 1e-06)
    return (lifted * factor).astype(jnp.bfloat16)


def recording_of(positions, pack_lengths):
    bounds = jnp.cumsum(pack_lengths)[: RECS - 1]
    return jnp.sum((positions[:, None] >= bounds[None, :]).astype(jnp.int32), axis=1)


def add_scores(query_heads, own_labels, piece_keys, piece_values, piece_labels, head_scale):
    count = piece_keys.shape[0]
    key_heads = jnp.transpose(piece_keys.reshape(count, HEADS, HEAD_DIM), (1, 0, 2))
    value_heads = jnp.transpose(piece_values.reshape(count, HEADS, HEAD_DIM), (1, 0, 2))
    inside = own_labels[:, None] == piece_labels[None, :]

    def per_head(items):
        query_one, key_one, value_one, scale = items
        scores = lax.dot_general(
            query_one, key_one, (((1,), (1,)), ((), ())), preferred_element_type=jnp.float32
        )
        weights = jnp.where(inside, jnp.exp(scale * (scores - 1.0)), 0.0)
        weight_sum = jnp.sum(weights, axis=1)
        product = jnp.dot(
            weights.astype(jnp.bfloat16), value_one, preferred_element_type=jnp.float32
        )
        return (product, weight_sum)

    products, weight_sums = lax.map(per_head, (query_heads, key_heads, value_heads, head_scale))
    return (products, weight_sums)


def body(
    query_rows,
    key_rows,
    value_rows,
    head_scale,
    out_proj,
    conv_taps,
    router,
    expert_in,
    expert_out,
    lengths,
    routes,
):
    row_count = query_rows.shape[1]
    experts = lax.axis_size("dp")
    capacity = 3 * row_count // experts
    offset = lax.axis_index("tm") * row_count
    pack_lengths = lengths[0]
    own_labels = recording_of(offset + jnp.arange(row_count, dtype=jnp.int32), pack_lengths)
    query_heads = jnp.transpose(unit_heads(query_rows[0]), (1, 0, 2))
    key_unit = unit_heads(key_rows[0]).reshape(row_count, HEADS * HEAD_DIM)
    piece_keys = lax.all_gather(key_unit, "tm", axis=0, tiled=True)
    piece_values = lax.all_gather(value_rows[0], "tm", axis=0, tiled=True)
    count = piece_keys.shape[0]
    piece_labels = recording_of(jnp.arange(count, dtype=jnp.int32), pack_lengths)
    sums, masses = add_scores(
        query_heads, own_labels, piece_keys, piece_values, piece_labels, head_scale
    )
    attended = (
        jnp.transpose(sums / masses[:, :, None], (1, 0, 2))
        .reshape(row_count, HEADS * HEAD_DIM)
        .astype(jnp.bfloat16)
    )
    first = jnp.dot(attended, out_proj, preferred_element_type=jnp.float32)
    normed = layer_norm(first).astype(jnp.bfloat16)
    half = (KERNEL - 1) // 2
    padded = with_halo(normed, (("tm", 0),), half)
    padded_labels = recording_of(
        offset - half + jnp.arange(row_count + 2 * half, dtype=jnp.int32), pack_lengths
    )
    total = jnp.zeros((row_count, D), jnp.float32)
    for tap in range(KERNEL):
        same = (padded_labels[tap : tap + row_count] == own_labels)[:, None]
        term = conv_taps[tap][None, :] * padded[tap : tap + row_count].astype(jnp.float32)
        total = total + jnp.where(same, term, 0.0)
    second = first + jax.nn.silu(total)
    mixed_in = layer_norm(second).astype(jnp.bfloat16)
    logits = jnp.dot(mixed_in, router, preferred_element_type=jnp.float32)
    own_routes = routes[0]
    chosen = jnp.exp(jnp.take_along_axis(logits, own_routes, axis=1))
    gates = chosen / jnp.sum(chosen, axis=1, keepdims=True)
    picks = jnp.sum(
        (own_routes[:, :, None] == jnp.arange(experts, dtype=jnp.int32)).astype(jnp.int32), axis=1
    )
    ranks = jnp.cumsum(picks, axis=0) - picks
    slots = own_routes * capacity + jnp.take_along_axis(ranks, own_routes, axis=1)
    placing = jnp.sum(
        (slots[:, :, None] == jnp.arange(experts * capacity, dtype=jnp.int32)).astype(jnp.bfloat16),
        axis=1,
    )
    outgoing = lax.dot_general(
        placing, mixed_in, (((0,), (0,)), ((), ())), preferred_element_type=jnp.float32
    )
    outgoing = outgoing.astype(jnp.bfloat16).reshape(experts, capacity, D)
    arrived = lax.all_to_all(outgoing, "dp", split_axis=0, concat_axis=0, tiled=True).reshape(
        experts * capacity, D
    )
    piece_in = lax.all_gather(expert_in[0], "tm", axis=0, tiled=True)
    piece_out = lax.all_gather(expert_out[0], "tm", axis=0, tiled=True)
    hidden_part = jax.nn.silu(
        lax.dot_general(
            arrived, piece_in, (((1,), (1,)), ((), ())), preferred_element_type=jnp.float32
        )
    ).astype(jnp.bfloat16)
    produced = jnp.dot(hidden_part, piece_out, preferred_element_type=jnp.float32)
    returned = lax.all_to_all(
        produced.astype(jnp.bfloat16).reshape(experts, capacity, D),
        "dp",
        split_axis=0,
        concat_axis=0,
        tiled=True,
    )
    returned = returned.reshape(experts * capacity, D)
    mixture = jnp.zeros((row_count, D), jnp.float32)
    for pick in range(TOPK):
        mixture = mixture + gates[:, pick : pick + 1] * returned[slots[:, pick]].astype(jnp.float32)
    return (second + 0.5 * mixture).astype(jnp.bfloat16)[None]


def solution(mesh):
    return jax.shard_map(
        body,
        mesh=mesh,
        in_specs=(
            P("dp", "tm", None),
            P("dp", "tm", None),
            P("dp", "tm", None),
            P(),
            P(),
            P(),
            P(),
            P("dp", "tm", None),
            P("dp", "tm", None),
            P("dp", None),
            P("dp", "tm", None),
        ),
        out_specs=P("dp", "tm", None),
        check_vma=False,
    )
```

profile of v0, /device:TPU:0, one launch (start us, length us, event | category | flops | bytes accessed | tf_op | source)
XLA Modules:
  0.0 407.9 jit_solution(12586347686912792872)
XLA Ops:
  6.5 2.2 copy.63
  8.7 2.1 convert_multiply_fusion.2
  14.1 2.0 copy.64
  22.6 2.0 copy.62
  29.2 3.0 gather_fusion.3
  33.0 27.4 %all-gather.8.cloned.1.call-done = bf16[896,1024]{1,0:T(8,128)(2,1)} async-done(((bf16[224,1024]{1,0:T(8,128)(2,1)}), bf16[896,1024]{1,0:T(8,128)(2,1)}) %all-gather.8.cloned.1.call-update) | async-done | bytes 1835024 | tf_op jit(solution)/shard_map/all_gather | solution.py:92
  60.4 3.8 copy.65
  64.2 38.0 %all-gather.10.cloned.1.call-done = bf16[1,896,1024]{2,1,0:T(8,128)(2,1)} async-done(((bf16[1,224,1024]{2,1,0:T(8,128)(2,1)}), bf16[1,896,1024]{2,1,0:T(8,128)(2,1)}) %all-gather.10.cloned.1.call-update) | async-done | bytes 1835024 | tf_op jit(solution)/shard_map/all_gather | solution.py:93
  102.2 3.8 copy.66
  106.1 71.1 %while.15 = (s32[]{:T(128)}, f32[16,224,64]{1,2,0:T(8,128)}, f32[16,224]{1,0:T(8,128)S(1)}, f32[16]{0:T(128)S(1)}, bf16[16,224,64]{1,2,0:T(8,128)(2,1)}, /*index...) while((s32[]{:T(128)}, f32[16,224,64]{1,2,0:T(8,128)}, ...), condition=%wide.region_7.8_spmd.clone, body=%wide.region_5.7_spmd.clone.sunk | while | flops 52584224 | bytes 1140349 | solution.py:67
  111.1 2.0 fusion.90
  120.0 2.0 fusion.90
  133.4 2.0 fusion.90
  142.2 2.0 fusion.90
  160.0 2.0 fusion.90
  180.5 2.2 collective-permute-start
  185.3 8.6 %collective-permute-done.1 = bf16[15,1536]{1,0:T(8,128)(2,1)S(1)} collective-permute-done((bf16[15,1536]{1,0:T(8,128)(2,1)S(1)}, bf16[15,1536]{1,0:T(8,128)(2,1)S(1)}, u32[]{:S(2)}, u32[]{:S(2)}) %collective-permute-start.1) | collective-permute-done | bytes 46112 | tf_op jit(solution)/shard_map/ppermute | solution.py:24
  194.3 17.5 %fusion.71 = (f32[224]{0:T(256)S(1)}, f32[224,1536]{1,0:T(8,128)S(1)}) fusion(f32[224,1536]{1,0:T(8,128)S(1)} %get-tuple-element.267, bf16[15,1536]{1,0:T(8,128)(2,1)S(1)} %collective-permute-done.1, bf16[224,1536]{1,0:T(8,128)(2,1)S(1)} %multiply_convert_fusion.3, f32[1536]{0:T(1024)S(1)} %copy-done.27, pred[224]{0:T(512)(128)(4,1)S(1)} %copy-done.37, ...), kind=kLoop, calls=%fused_computation.224 | loop fusion | flops 75349792 | bytes 3731104 | tf_op jit(solution)/shard_map/reduce_sum | solution.py:32
  213.7 2.0 convolution_convert_fusion
  215.7 3.9 reshape.193
  219.7 31.7 %all_to_all.10 = bf16[8,84,1536]{2,1,0:T(8,128)(2,1)} all-to-all(bf16[8,84,1536]{2,1,0:T(8,128)(2,1)} %reshape.193), channel_id=1, replica_groups=mesh['dp'=8,'tm'=4] {'dp'}, dimensions={0} | all-to-all | bytes 4128768 | tf_op jit(solution)/shard_map/all_to_all | solution.py:135
  251.3 4.0 reshape.194
  255.3 78.9 %all-gather.14.cloned.1.call-done = bf16[1,2048,1536]{2,1,0:T(8,128)(2,1)} async-done(((bf16[1,512,1536]{2,1,0:T(8,128)(2,1)}), bf16[1,2048,1536]{2,1,0:T(8,128)(2,1)}) %all-gather.14.cloned.1.call-update) | async-done | bytes 6291472 | tf_op jit(solution)/shard_map/all_gather | solution.py:139
  334.2 15.5 %fusion.19 = bf16[672,1536]{1,0:T(8,128)(2,1)} fusion(bf16[1,2048,1536]{2,1,0:T(8,128)(2,1)} %all-gather.14.cloned.1.call-done, bf16[672,1536]{1,0:T(8,128)(2,1)} %reshape.194, bf16[1,2048,1536]{2,1,0:T(8,128)(2,1)} %all-gather.12.cloned.1.call-done), kind=kOutput, calls=%fused_computation.53 | convolution fusion | flops 8463630336 | bytes 16711680 | tf_op jit(solution)/shard_map/dot_general | solution.py:145
  349.7 3.9 reshape.195
  353.6 4.5 %all-to-all-start.1 = ((bf16[8,84,1536]{2,1,0:T(8,128)(2,1)}), bf16[8,84,1536]{2,1,0:T(8,128)(2,1)}, u32[]{:S(2)}, u32[]{:S(2)}) async-start(bf16[8,84,1536]{2,1,0:T(8,128)(2,1)} %reshape.195), calls=%async_computation.1 | async-start | bytes 4325376 | tf_op jit(solution)/shard_map/all_to_all | solution.py:146
  359.7 3.0 gather_fusion.2
  363.3 22.2 %all-to-all-done.1 = bf16[8,84,1536]{2,1,0:T(8,128)(2,1)} async-done(((bf16[8,84,1536]{2,1,0:T(8,128)(2,1)}), bf16[8,84,1536]{2,1,0:T(8,128)(2,1)}, u32[]{:S(2)}, u32[]{:S(2)}) %all-to-all-start.1) | async-done | bytes 2064416 | tf_op jit(solution)/shard_map/all_to_all | solution.py:146
  385.4 3.9 reshape.196
  389.4 4.5 %gather_fusion = bf16[224,1536]{1,0:T(8,128)(2,1)} fusion(bf16[672,1536]{1,0:T(8,128)(2,1)} %reshape.196, s32[1024]{0:T(1024)S(1)} %get-tuple-element.269), kind=kCustom, calls=%fused_computation | custom fusion | bytes 1377152 | tf_op jit(solution)/shard_map/gather | solution.py:156
  393.9 4.5 %gather_fusion.1 = bf16[224,1536]{1,0:T(8,128)(2,1)} fusion(bf16[672,1536]{1,0:T(8,128)(2,1)} %reshape.196, s32[1024]{0:T(1024)S(1)} %get-tuple-element.268), kind=kCustom, calls=%fused_computation.1 | custom fusion | bytes 1377152 | tf_op jit(solution)/shard_map/gather | solution.py:156
  398.4 3.0 fusion.33
  (228 shorter events, 85.5 us)
Async XLA Ops:
  6.5 172.0 %copy-start = (bf16[1024,1536]{1,0:T(8,128)(2,1)S(1)}, bf16[1024,1536]{1,0:T(8,128)(2,1)}, u32[]{:S(2)}) copy-start(bf16[1024,1536]{1,0:T(8,128)(2,1)} %param.17) | copy-start | bytes 9437188
  6.5 53.8 %all-gather.8.cloned.1.call-start = ((), (), s32[]{:S(2)}) async-start(), calls=%async_computation.2 | async-start | bytes 2293760 | tf_op jit(solution)/shard_map/all_gather | solution.py:92
  16.1 86.1 %all-gather.10.cloned.1.call-start = ((), (), s32[]{:S(2)}) async-start(), calls=%async_computation.3 | async-start | bytes 2293760 | tf_op jit(solution)/shard_map/all_gather | solution.py:93
  16.9 238.4 %all-gather.12.cloned.1.call-start = ((), (), s32[]{:S(2)}) async-start(), calls=%async_computation.4 | async-start | bytes 7864320 | tf_op jit(solution)/shard_map/all_gather | solution.py:138
  17.7 316.5 %all-gather.14.cloned.1.call-start = ((), (), s32[]{:S(2)}) async-start(), calls=%async_computation.5 | async-start | bytes 7864320 | tf_op jit(solution)/shard_map/all_gather | solution.py:139
  64.2 41.9 %copy-start.30 = (f32[16,224]{1,0:T(8,128)S(1)}, f32[16,224]{1,0:T(8,128)}, u32[]{:S(2)}) copy-start(f32[16,224]{1,0:T(8,128)} %custom-call.9) | copy-start | bytes 43012
  64.2 41.9 %copy-start.32 = (s32[224]{0:T(256)S(1)}, s32[224]{0:T(256)}, u32[]{:S(2)}) copy-start(s32[224]{0:T(256)} %copy-done.31) | copy-start | bytes 2692
  64.2 41.9 %copy-start.35 = (s32[896]{0:T(1024)S(1)}, s32[896]{0:T(1024)}, u32[]{:S(2)}) copy-start(s32[896]{0:T(1024)} %convert_reduce_fusion.1) | copy-start | bytes 10756
  64.2 41.9 %copy-start.51 = (f32[16]{0:T(128)S(1)}, f32[16]{0:T(128)}, u32[]{:S(2)}) copy-start(f32[16]{0:T(128)} %param.16) | copy-start | bytes 196
  179.8 14.1 %copy-start.4 = (f32[1536]{0:T(1024)S(1)}, f32[1536]{0:T(1024)}, u32[]{:S(2)}) copy-start(f32[1536]{0:T(1024)} %get-tuple-element.182) | copy-start | bytes 18436
  179.8 14.1 %copy-start.5 = (f32[1536]{0:T(1024)S(1)}, f32[1536]{0:T(1024)}, u32[]{:S(2)}) copy-start(f32[1536]{0:T(1024)} %get-tuple-element.183) | copy-start | bytes 18436
  179.8 14.1 %copy-start.6 = (f32[1536]{0:T(1024)S(1)}, f32[1536]{0:T(1024)}, u32[]{:S(2)}) copy-start(f32[1536]{0:T(1024)} %get-tuple-element.184) | copy-start | bytes 18436
  179.8 14.1 %copy-start.7 = (f32[1536]{0:T(1024)S(1)}, f32[1536]{0:T(1024)}, u32[]{:S(2)}) copy-start(f32[1536]{0:T(1024)} %get-tuple-element.185) | copy-start | bytes 18436
  179.9 14.1 %copy-start.8 = (f32[1536]{0:T(1024)S(1)}, f32[1536]{0:T(1024)}, u32[]{:S(2)}) copy-start(f32[1536]{0:T(1024)} %get-tuple-element.186) | copy-start | bytes 18436
  179.9 14.1 %copy-start.9 = (f32[1536]{0:T(1024)S(1)}, f32[1536]{0:T(1024)}, u32[]{:S(2)}) copy-start(f32[1536]{0:T(1024)} %get-tuple-element.187) | copy-start | bytes 18436
  179.9 14.1 %copy-start.10 = (f32[1536]{0:T(1024)S(1)}, f32[1536]{0:T(1024)}, u32[]{:S(2)}) copy-start(f32[1536]{0:T(1024)} %get-tuple-element.188) | copy-start | bytes 18436
  179.9 14.1 %copy-start.11 = (f32[1536]{0:T(1024)S(1)}, f32[1536]{0:T(1024)}, u32[]{:S(2)}) copy-start(f32[1536]{0:T(1024)} %get-tuple-element.189) | copy-start | bytes 18436
  179.9 14.1 %copy-start.12 = (f32[1536]{0:T(1024)S(1)}, f32[1536]{0:T(1024)}, u32[]{:S(2)}) copy-start(f32[1536]{0:T(1024)} %get-tuple-element.190) | copy-start | bytes 18436
  179.9 14.1 %copy-start.13 = (f32[1536]{0:T(1024)S(1)}, f32[1536]{0:T(1024)}, u32[]{:S(2)}) copy-start(f32[1536]{0:T(1024)} %get-tuple-element.191) | copy-start | bytes 18436
  179.9 14.1 %copy-start.14 = (f32[1536]{0:T(1024)S(1)}, f32[1536]{0:T(1024)}, u32[]{:S(2)}) copy-start(f32[1536]{0:T(1024)} %get-tuple-element.192) | copy-start | bytes 18436
  179.9 14.1 %copy-start.15 = (f32[1536]{0:T(1024)S(1)}, f32[1536]{0:T(1024)}, u32[]{:S(2)}) copy-start(f32[1536]{0:T(1024)} %get-tuple-element.193) | copy-start | bytes 18436
  179.9 14.1 %copy-start.16 = (f32[1536]{0:T(1024)S(1)}, f32[1536]{0:T(1024)}, u32[]{:S(2)}) copy-start(f32[1536]{0:T(1024)} %get-tuple-element.194) | copy-start | bytes 18436
  179.9 14.1 %copy-start.17 = (f32[1536]{0:T(1024)S(1)}, f32[1536]{0:T(1024)}, u32[]{:S(2)}) copy-start(f32[1536]{0:T(1024)} %get-tuple-element.195) | copy-start | bytes 18436
  180.0 14.1 %copy-start.18 = (f32[1536]{0:T(1024)S(1)}, f32[1536]{0:T(1024)}, u32[]{:S(2)}) copy-start(f32[1536]{0:T(1024)} %get-tuple-element.196) | copy-start | bytes 18436
  180.0 14.1 %copy-start.19 = (f32[1536]{0:T(1024)S(1)}, f32[1536]{0:T(1024)}, u32[]{:S(2)}) copy-start(f32[1536]{0:T(1024)} %get-tuple-element.197) | copy-start | bytes 18436
  180.0 14.1 %copy-start.20 = (f32[1536]{0:T(1024)S(1)}, f32[1536]{0:T(1024)}, u32[]{:S(2)}) copy-start(f32[1536]{0:T(1024)} %get-tuple-element.198) | copy-start | bytes 18436
  180.0 14.1 %copy-start.21 = (f32[1536]{0:T(1024)S(1)}, f32[1536]{0:T(1024)}, u32[]{:S(2)}) copy-start(f32[1536]{0:T(1024)} %get-tuple-element.199) | copy-start | bytes 18436
  180.0 14.1 %copy-start.22 = (f32[1536]{0:T(1024)S(1)}, f32[1536]{0:T(1024)}, u32[]{:S(2)}) copy-start(f32[1536]{0:T(1024)} %get-tuple-element.200) | copy-start | bytes 18436
  180.0 14.1 %copy-start.23 = (f32[1536]{0:T(1024)S(1)}, f32[1536]{0:T(1024)}, u32[]{:S(2)}) copy-start(f32[1536]{0:T(1024)} %get-tuple-element.201) | copy-start | bytes 18436
  180.5 4.9 %collective-permute-start = (bf16[15,1536]{1,0:T(8,128)(2,1)S(1)}, bf16[15,1536]{1,0:T(8,128)(2,1)S(1)}, u32[]{:S(2)}, u32[]{:S(2)}) collective-permute-start(bf16[15,1536]{1,0:T(8,128)(2,1)S(1)} %get-tuple-element.233), channel_id=1, source_target_pairs={{0,1},{1,2},{2,3},{4,5},{5,6},{6,7},{8,9},{9,10},{10,11},{12,13},{... | collective-permute-start | bytes 138248 | tf_op jit(solution)/shard_map/ppermute | solution.py:22
  182.7 11.3 %collective-permute-start.1 = (bf16[15,1536]{1,0:T(8,128)(2,1)S(1)}, bf16[15,1536]{1,0:T(8,128)(2,1)S(1)}, u32[]{:S(2)}, u32[]{:S(2)}) collective-permute-start(bf16[15,1536]{1,0:T(8,128)(2,1)S(1)} %get-tuple-element.234), channel_id=1, source_target_pairs={{1,0},{2,1},{3,2},{5,4},{6,5},{7,6},{9,8},{10,9},{11,10},{13,12},{... | collective-permute-start | bytes 138248 | tf_op jit(solution)/shard_map/ppermute | solution.py:24
  353.6 31.8 %all-to-all-start.1 = ((bf16[8,84,1536]{2,1,0:T(8,128)(2,1)}), bf16[8,84,1536]{2,1,0:T(8,128)(2,1)}, u32[]{:S(2)}, u32[]{:S(2)}) async-start(bf16[8,84,1536]{2,1,0:T(8,128)(2,1)} %reshape.195), calls=%async_computation.1 | async-start | bytes 4325376 | tf_op jit(solution)/shard_map/all_to_all | solution.py:146
  (27 other events, 295.2 us)
Sparse Core Ops, SparseCore 0:
  16.2 44.0 all-gather.7
  61.9 40.2 all-gather.9
  103.8 115.2 all-gather.11
  220.5 113.6 all-gather.13
where the time goes:
time: 410 us; the launch traced here: 408 us
  waiting for transfers between devices  178 us (43%)
  matrix products  80.7 us (20%)
  local copies, waits for them, and re-layouts  59.8 us (15%)
  other arithmetic  35.2 us (9%)
  blocking collectives  31.7 us (8%)
  between operations  14.1 us (3%)
  starting transfers between devices  8.26 us (2%)
    all_gather x1, waiting for transfers between devices, body(): piece_out = lax.all_gather(expert_out[0], 'tm', axis=0, tiled=True)  78.9 us
    all_gather x1, waiting for transfers between devices, body(): piece_values = lax.all_gather(value_rows[0], 'tm', axis=0, tiled=True)  38 us
    dot_general x16, matrix products, per_head(): lax.dot_general(query_one, key_one, (((1,), (1,)), ((), ())), preferred_e...  32.2 us
    all_to_all x1, blocking collectives, body(): lax.all_to_all(outgoing, 'dp', split_axis=0, concat_axis=0, tiled=True)  31.7 us
    dot_general x16, matrix products, per_head(): jnp.dot(weights.astype(jnp.bfloat16), value_one, preferred_element_type=j...  28.7 us
    all_gather x1, waiting for transfers between devices, body(): piece_keys = lax.all_gather(key_unit, 'tm', axis=0, tiled=True)  27.4 us
    all_to_all x1, waiting for transfers between devices, body(): lax.all_to_all(produced.astype(jnp.bfloat16).reshape(experts, capacity, D...  22.2 us
    reduce_sum x1, other arithmetic, layer_norm(): average = jnp.mean(values, axis=-1, keepdims=True)  17.5 us
  transfers between devices with their start and end apart: 7, of which 6 were waited for; matrix products, arithmetic and copies ran while one was open for 32% of the time, Pallas kernels for 0%

commit v1 on v0

v1 whole, which is shorter than its diff:
```python
import functools

import jax
import jax.numpy as jnp
from jax import lax
from jax.experimental import pallas as pl
from jax.experimental.pallas import tpu as pltpu
from jax.sharding import PartitionSpec as P

D = 1536
HEADS = 16
HEAD_DIM = 64
KERNEL = 31
TOPK = 2
RECS = 4
HALO = 16
LANES = 128
APART = 64.0
LOG2E = 1.4426950408889634
F32 = jnp.float32
BF16 = jnp.bfloat16
VMEM = pl.BlockSpec(memory_space=pltpu.VMEM)
SMEM = pl.BlockSpec(memory_space=pltpu.SMEM)


def params(mib):
    return pltpu.CompilerParams(vmem_limit_bytes=mib << 20)


def labels_of(frames, len_ref):
    first = len_ref[0, 0]
    second = first + len_ref[0, 1]
    third = second + len_ref[0, 2]
    return (
        (frames >= first).astype(F32)
        + (frames >= second).astype(F32)
        + (frames >= third).astype(F32)
    )


def unit_tile(tile, low):
    lifted = tile.astype(F32)
    square = lifted * lifted
    left = jnp.sum(jnp.where(low, square, 0.0), axis=1, keepdims=True)
    right = jnp.sum(jnp.where(low, 0.0, square), axis=1, keepdims=True)
    factor = jnp.where(low, lax.rsqrt(left + 1e-06), lax.rsqrt(right + 1e-06))
    return lifted * factor


def attend_kernel(count, rows, heads, scale_ref, len_ref, x_ref, o_ref, k_ref, v_ref, a_ref):
    block = pl.program_id(0)
    width = heads * HEAD_DIM
    tiles = max(1, width // LANES)
    half = count // 2
    window = rows + 2 * HALO

    def tile_of(source, which, place):
        if width >= LANES:
            return x_ref[source, which, :, place * LANES : (place + 1) * LANES]
        piece = x_ref[source, which]
        return jnp.concatenate([piece, jnp.zeros((rows, LANES - width), BF16)], axis=1)

    low = lax.broadcasted_iota(jnp.int32, (rows, LANES), 1) < HEAD_DIM
    lane = lax.broadcasted_iota(jnp.int32, (rows, LANES), 1).astype(F32)
    row = lax.broadcasted_iota(jnp.int32, (rows, LANES), 0)

    @pl.when(block == 0)
    def _():
        edge = jnp.zeros((HALO, width), BF16)
        a_ref[0:HALO, :] = edge
        a_ref[HALO + count * rows :, :] = edge
        for source in range(count):
            at = slice(source * rows, (source + 1) * rows)
            label = labels_of(row + source * rows, len_ref)
            other = jnp.where((lane >= 1.0) & (lane <= 4.0) & (lane != label + 1.0), -APART, 0.0)
            extra = jnp.where(lane == 0.0, -1.0, other).astype(BF16)
            for place in range(tiles):
                k_ref[place, at, 0:LANES] = unit_tile(tile_of(source, 1, place), low).astype(BF16)
                k_ref[place, at, LANES:] = extra
                v_ref[place, at, 0:LANES] = tile_of(source, 2, place)
                v_ref[place, at, LANES:] = jnp.ones((rows, LANES), BF16)

    label = labels_of(row + block * rows, len_ref)
    extra = jnp.where((lane == 0.0) | (lane == label + 1.0), 1.0, 0.0).astype(BF16)
    for place in range(tiles):
        unit = unit_tile(tile_of(block, 0, place), low)
        parts = []
        for side in range(min(2, heads)):
            head = place * 2 + side
            kept = jnp.where(low if side == 0 else ~low, unit, 0.0).astype(BF16)
            query = jnp.concatenate([kept, extra], axis=1)
            scores = lax.dot_general(
                query, k_ref[place], (((1,), (1,)), ((), ())), preferred_element_type=F32
            )
            weights = jnp.exp2(scores * (scale_ref[head] * LOG2E)).astype(BF16)
            summed = jnp.dot(weights, v_ref[place], preferred_element_type=F32)
            parts.append(summed[:, 0:LANES] / summed[:, LANES:])
        done = parts[0] if len(parts) == 1 else jnp.where(low, parts[0], parts[1])
        start = pl.multiple_of(HALO + block * rows, HALO)
        wide = min(LANES, width)
        a_ref[pl.ds(start, rows), place * LANES : place * LANES + wide] = done[:, 0:wide].astype(BF16)

    @pl.when(block == count - 1)
    def _():
        for target in range(count):
            for which in range(2):
                begin = (target % half + which * half) * rows
                o_ref[target, which] = a_ref[begin : begin + window, :]


def normalize(values):
    average = jnp.mean(values, axis=-1, keepdims=True)
    centered = values - average
    spread = jnp.mean(centered * centered, axis=-1, keepdims=True)
    return centered * lax.rsqrt(spread + 1e-05)


def frame_kernel(
    count,
    rows,
    experts,
    capacity,
    block_ref,
    len_ref,
    att_ref,
    proj_ref,
    taps_ref,
    router_ref,
    routes_ref,
    turned_ref,
    out_ref,
    second_ref,
    info_ref,
    x_ref,
    first_ref,
    lab_ref,
    mixed_ref,
):
    window = rows + 2 * HALO
    half = (KERNEL - 1) // 2
    tiles = D // LANES
    step = 56
    for which in range(2):
        attended = jnp.concatenate([att_ref[i, which] for i in range(count)], axis=1)
        first = jnp.dot(attended, proj_ref[...], preferred_element_type=F32)
        normed = normalize(first).astype(BF16).astype(F32)
        origin = block_ref[which] * rows - HALO
        frames = lax.broadcasted_iota(jnp.int32, (window, LANES), 0) + origin
        lab_ref[which] = labels_of(frames, len_ref)
        for tile in range(tiles):
            at = slice(tile * LANES, (tile + 1) * LANES)
            x_ref[which, tile] = normed[:, at]
            first_ref[which, tile] = first[HALO : HALO + rows, at]

    starts = [len_ref[0, 0], len_ref[0, 0] + len_ref[0, 1]]
    starts.append(starts[1] + len_ref[0, 2])
    for which in range(2):
        for begin in range(0, rows, step):
            low = block_ref[which] * rows + begin - half
            high = low + step + 2 * half
            mixed = functools.reduce(
                jnp.logical_or, [(low < start) & (start < high) for start in starts]
            )

            def columns(tile, masked):
                total = jnp.zeros((step, LANES), F32)
                own = lab_ref[which, HALO + begin : HALO + begin + step, :] if masked else None
                for tap in range(KERNEL):
                    source = HALO - half + begin + tap
                    term = taps_ref[tile, tap : tap + 1, :] * x_ref[which, tile, source : source + step, :]
                    if masked:
                        term = jnp.where(lab_ref[which, source : source + step, :] == own, term, 0.0)
                    total = total + term
                gated = total / (1.0 + jnp.exp(-total))
                second_ref[which, tile, begin : begin + step, :] = (
                    first_ref[which, tile, begin : begin + step, :] + gated
                )

            @pl.when(mixed)
            def _():
                lax.fori_loop(0, tiles, lambda tile, c: (columns(tile, True), c)[1], 0)

            @pl.when(jnp.logical_not(mixed))
            def _():
                lax.fori_loop(0, tiles, lambda tile, c: (columns(tile, False), c)[1], 0)

    for which in range(2):
        second = jnp.concatenate([second_ref[which, tile] for tile in range(tiles)], axis=1)
        mixed_ref[which * rows : (which + 1) * rows, :] = normalize(second).astype(BF16)

    frames = 2 * rows
    logits = jnp.dot(mixed_ref[...], router_ref[...], preferred_element_type=F32)
    lane = lax.broadcasted_iota(jnp.int32, (frames, experts), 1)
    named = [lane == routes_ref[:, pick : pick + 1] for pick in range(TOPK)]
    picked = [jnp.sum(jnp.where(one, logits, 0.0), axis=1, keepdims=True) for one in named]
    top = jnp.maximum(picked[0], picked[1])
    raised = [jnp.exp(one - top) for one in picked]
    mass = raised[0] + raised[1]
    down = lax.broadcasted_iota(jnp.int32, (frames, frames), 0)
    across = lax.broadcasted_iota(jnp.int32, (frames, frames), 1)
    picks = jnp.where(named[0] | named[1], 1.0, 0.0).astype(BF16)
    earlier = jnp.where(across < down, 1.0, 0.0).astype(BF16)
    ranks = jnp.dot(earlier, picks, preferred_element_type=F32)
    columns = lax.broadcasted_iota(jnp.int32, (frames, LANES), 1)
    info = jnp.zeros((frames, LANES), F32)
    for pick in range(TOPK):
        rank = jnp.sum(jnp.where(named[pick], ranks, 0.0), axis=1, keepdims=True)
        slot = rank + (routes_ref[:, pick : pick + 1] * capacity).astype(F32)
        info = jnp.where(columns == pick, slot, info)
        info = jnp.where(columns == TOPK + pick, raised[pick] / mass, info)
    for which in range(2):
        info_ref[which] = info[which * rows : (which + 1) * rows, :]

    expert = lax.broadcasted_iota(jnp.int32, (experts, frames), 0)
    chosen = (expert == turned_ref[0:1, :]) | (expert == turned_ref[1:2, :])
    later = jnp.where(down < across, 1.0, 0.0).astype(BF16)
    order = jnp.dot(jnp.where(chosen, 1.0, 0.0).astype(BF16), later, preferred_element_type=F32)
    order = jnp.where(chosen, order, -1.0)
    place = lax.broadcasted_iota(jnp.int32, (capacity, frames), 0).astype(F32)
    for e in range(experts):
        select = jnp.where(place == order[e : e + 1, :], 1.0, 0.0).astype(BF16)
        out_ref[e] = jnp.dot(select, mixed_ref[...], preferred_element_type=F32).astype(BF16)


def expert_kernel(pieces, x_ref, *refs):
    ins, outs, o_ref = refs[:pieces], refs[pieces : 2 * pieces], refs[2 * pieces]
    total = None
    for piece_in, piece_out in zip(ins, outs):
        raw = lax.dot_general(
            x_ref[...], piece_in[...], (((1,), (1,)), ((), ())), preferred_element_type=F32
        )
        hidden = (raw / (1.0 + jnp.exp(-raw))).astype(BF16)
        product = jnp.dot(hidden, piece_out[...], preferred_element_type=F32)
        total = product if total is None else total + product
    o_ref[...] = total.astype(BF16)


def mixture_of(info, back):
    column = lax.broadcasted_iota(jnp.int32, (info.shape[0], back.shape[0]), 1).astype(F32)
    spread = jnp.where(column == info[:, 0:1], info[:, 2:3], 0.0)
    spread = jnp.where(column == info[:, 1:2], info[:, 3:4], spread).astype(BF16)
    return jnp.dot(spread, back, preferred_element_type=F32)


def theirs_kernel(own_ref, info_ref, back_ref, o_ref):
    o_ref[...] = mixture_of(info_ref[1 - own_ref[0]], back_ref[...]).astype(BF16)


def mine_kernel(own_ref, info_ref, back_ref, second_ref, o_ref):
    mixture = mixture_of(info_ref[own_ref[0]], back_ref[...])
    for tile in range(D // LANES):
        at = slice(tile * LANES, (tile + 1) * LANES)
        o_ref[:, at] = second_ref[own_ref[0], tile] + 0.5 * mixture[:, at]


def body(
    query_rows,
    key_rows,
    value_rows,
    head_scale,
    out_proj,
    conv_taps,
    router,
    expert_in,
    expert_out,
    lengths,
    routes,
):
    rows = query_rows.shape[1]
    experts = lax.axis_size("dp")
    count = lax.axis_size("tm")
    half = count // 2
    heads = HEADS // count
    width = heads * HEAD_DIM
    window = rows + 2 * HALO
    capacity = -(-2 * (3 * rows // experts) // 16) * 16
    me = lax.axis_index("tm").astype(jnp.int32)
    side = (me // half).reshape(1)
    blocks = jnp.stack([me % half, me % half + half])
    partner = [(i, (i + half) % count) for i in range(count)]

    packed = jnp.stack([query_rows[0], key_rows[0], value_rows[0]])
    packed = jnp.transpose(packed.reshape(3, rows, count, width), (2, 0, 1, 3))
    arrived = lax.all_to_all(packed, "tm", split_axis=0, concat_axis=0, tiled=True)
    scales = lax.dynamic_slice_in_dim(head_scale, me * heads, heads)

    other_routes = lax.ppermute(routes[0], "tm", partner)
    is_low = me < half
    both = jnp.concatenate(
        [
            jnp.where(is_low, routes[0], other_routes),
            jnp.where(is_low, other_routes, routes[0]),
        ]
    )

    if half == 2:
        swap = [(i, i ^ 1) for i in range(count)]
        ins = [expert_in[0], lax.ppermute(expert_in[0], "tm", swap)]
        outs = [expert_out[0], lax.ppermute(expert_out[0], "tm", swap)]
    else:
        groups = [list(range(half)), list(range(half, count))]
        ins = [lax.all_gather(expert_in[0], "tm", axis=0, tiled=True, axis_index_groups=groups)]
        outs = [lax.all_gather(expert_out[0], "tm", axis=0, tiled=True, axis_index_groups=groups)]

    tiles = max(1, width // LANES)
    total = count * rows
    attended = pl.pallas_call(
        functools.partial(attend_kernel, count, rows, heads),
        grid=(count,),
        out_shape=jax.ShapeDtypeStruct((count, 2, window, width), BF16),
        in_specs=[SMEM, SMEM, pl.BlockSpec((count, 3, rows, width), lambda i: (0, 0, 0, 0))],
        out_specs=pl.BlockSpec((count, 2, window, width), lambda i: (0, 0, 0, 0)),
        scratch_shapes=[
            pltpu.VMEM((tiles, total, 2 * LANES), BF16),
            pltpu.VMEM((tiles, total, 2 * LANES), BF16),
            pltpu.VMEM((total + 2 * HALO, width), BF16),
        ],
        compiler_params=params(40),
        name="attend",
    )(scales, lengths, arrived)
    gathered = lax.all_to_all(attended, "tm", split_axis=0, concat_axis=0, tiled=True)

    taps = jnp.transpose(conv_taps.reshape(KERNEL, D // LANES, LANES), (1, 0, 2))
    outgoing, second, info = pl.pallas_call(
        functools.partial(frame_kernel, count, rows, experts, capacity),
        out_shape=(
            jax.ShapeDtypeStruct((experts, capacity, D), BF16),
            jax.ShapeDtypeStruct((2, D // LANES, rows, LANES), F32),
            jax.ShapeDtypeStruct((2, rows, LANES), F32),
        ),
        in_specs=[SMEM, SMEM, VMEM, VMEM, VMEM, VMEM, VMEM, VMEM],
        out_specs=(VMEM, VMEM, VMEM),
        scratch_shapes=[
            pltpu.VMEM((2, D // LANES, window, LANES), F32),
            pltpu.VMEM((2, D // LANES, rows, LANES), F32),
            pltpu.VMEM((2, window, LANES), F32),
            pltpu.VMEM((2 * rows, D), BF16),
        ],
        compiler_params=params(50),
        name="frames",
    )(blocks, lengths, gathered, out_proj, taps, router, both, both.T)

    tokens = lax.all_to_all(outgoing, "dp", split_axis=0, concat_axis=0, tiled=True)
    tokens = tokens.reshape(experts * capacity, D)

    pieces = len(ins)
    units = ins[0].shape[0]
    parts = 4
    tall = experts * capacity // parts
    produced = pl.pallas_call(
        functools.partial(expert_kernel, pieces),
        grid=(parts,),
        out_shape=jax.ShapeDtypeStruct((experts * capacity, D), BF16),
        in_specs=[pl.BlockSpec((tall, D), lambda i: (i, 0))]
        + [pl.BlockSpec((units, D), lambda i: (0, 0))] * (2 * pieces),
        out_specs=pl.BlockSpec((tall, D), lambda i: (i, 0)),
        compiler_params=params(50),
        name="experts",
    )(tokens, *ins, *outs)

    back = lax.all_to_all(
        produced.reshape(experts, capacity, D), "dp", split_axis=0, concat_axis=0, tiled=True
    )
    back = back.reshape(experts * capacity, D)

    theirs = pl.pallas_call(
        theirs_kernel,
        out_shape=jax.ShapeDtypeStruct((rows, D), BF16),
        in_specs=[SMEM, VMEM, VMEM],
        out_specs=VMEM,
        compiler_params=params(40),
        name="theirs",
    )(side, info, back)
    received = lax.ppermute(theirs, "tm", partner)
    mine = pl.pallas_call(
        mine_kernel,
        out_shape=jax.ShapeDtypeStruct((rows, D), F32),
        in_specs=[SMEM, VMEM, VMEM, VMEM],
        out_specs=VMEM,
        compiler_params=params(40),
        name="mine",
    )(side, info, back, second)
    return (mine + 0.5 * received.astype(F32)).astype(BF16)[None]


def solution(mesh):
    return jax.shard_map(
        body,
        mesh=mesh,
        in_specs=(
            P("dp", "tm", None),
            P("dp", "tm", None),
            P("dp", "tm", None),
            P(),
            P(),
            P(),
            P(),
            P("dp", "tm", None),
            P("dp", "tm", None),
            P("dp", None),
            P("dp", "tm", None),
        ),
        out_specs=P("dp", "tm", None),
        check_vma=False,
    )
```

time: 410 us -> 280 us (0.68)
  matrix products: 80.7 us -> 0 us
  local copies, waits for them, and re-layouts: 59.8 us -> 1.77 us
  Pallas kernels: 0 us -> 50.1 us
  other arithmetic: 35.2 us -> 2.63 us
  blocking collectives: 31.7 us -> 0 us
  waiting for transfers between devices: 178 us -> 199 us
  starting transfers between devices: 8.26 us -> 24.6 us
  between operations: 14.1 us -> 0.15 us
    all_gather x4 -> x0, waiting for transfers between devices: 144 us -> none  [the longest x1 78.9 us: body(): piece_out = lax.all_gather(expert_out[0], 'tm', axis=0, tiled=True)]
    ppermute x2 -> x4, waiting for transfers between devices: 9.56 us -> 116 us  [the longest x1 35.2 us: body(): ins = [expert_in[0], lax.ppermute(expert_in[0], 'tm', swap)]]
    dot_general x36 -> x0, matrix products: 80.7 us -> none  [the longest x16 32.2 us: per_head(): lax.dot_general(query_one, key_one, (((1,), (1,)), ((), ())), preferred_e...]
    all_to_all x1 -> x4, waiting for transfers between devices: 22.2 us -> 83.2 us  [the longest x1 50.5 us: body(): lax.all_to_all(produced.reshape(experts, capacity, D), 'dp', split_axis=0...]
    pallas_call x0 -> x5, Pallas kernels: none -> 50.1 us  [the longest x1 20.8 us: body(): pl.pallas_call(functools.partial(frame_kernel, count, rows, experts, capa...]
    all_to_all x1 -> x0, blocking collectives: 31.7 us -> none  [body(): lax.all_to_all(outgoing, 'dp', split_axis=0, concat_axis=0, tiled=True)]
    reduce_sum x11 -> x0, other arithmetic: 21.7 us -> none  [the longest x1 17.5 us: layer_norm(): average = jnp.mean(values, axis=-1, keepdims=True)]
    gather x8 -> x0, local copies, waits for them, and re-layouts: 15.6 us -> none  [the longest x2 9.01 us: body(): returned[slots[:, pick]].astype(jnp.float32)]
  transfers between devices with their start and end apart: 7 -> 8, of which waited for: 6 -> 6; matrix products, arithmetic and copies ran while one was open for 32% -> 0% of each run, Pallas kernels for 0% -> 1%
where the time goes in v1:
time: 280 us; the launch traced here: 278 us
  waiting for transfers between devices  199 us (71%)
  Pallas kernels  50.1 us (18%)
  starting transfers between devices  24.6 us (9%)
    all_to_all x1, waiting for transfers between devices, body(): lax.all_to_all(produced.reshape(experts, capacity, D), 'dp', split_axis=0...  50.5 us
    ppermute x1, waiting for transfers between devices, body(): ins = [expert_in[0], lax.ppermute(expert_in[0], 'tm', swap)]  35.2 us
    ppermute x1, waiting for transfers between devices, body(): outs = [expert_out[0], lax.ppermute(expert_out[0], 'tm', swap)]  33 us
    all_to_all x1, waiting for transfers between devices, body(): lax.all_to_all(packed, 'tm', split_axis=0, concat_axis=0, tiled=True)  32.7 us
    ppermute x1, waiting for transfers between devices, body(): received = lax.ppermute(theirs, 'tm', partner)  25.9 us
    ppermute x1, waiting for transfers between devices, body(): other_routes = lax.ppermute(routes[0], 'tm', partner)  22 us
    pallas_call x1, Pallas kernels, body(): pl.pallas_call(functools.partial(frame_kernel, count, rows, experts, capa...  20.8 us
    pallas_call x1, Pallas kernels, body(): pl.pallas_call(functools.partial(expert_kernel, pieces), grid=(parts,), o...  13.9 us
  transfers between devices with their start and end apart: 8, of which 6 were waited for; matrix products, arithmetic and copies ran while one was open for 0% of the time, Pallas kernels for 1%

profile of v1, /device:TPU:0, one launch (start us, length us, event | category | flops | bytes accessed | tf_op | source)
XLA Modules:
  0.0 278.5 jit_solution(5984168769818636364)
XLA Ops:
  0.0 1.4 pad_maximum_fusion
  1.4 1.2 copy.21
  2.7 6.4 %all-to-all-start = ((bf16[4,3,224,256]{3,2,1,0:T(8,128)(2,1)}), bf16[4,3,224,256]{3,2,1,0:T(8,128)(2,1)S(1)}, u32[]{:S(2)}, u32[]{:S(2)}) async-start(bf16[4,3,224,256]{3,2,1,0:T(8,128)(2,1)} %bitcast.23), calls=%async_computation | async-start | bytes 2752512 | tf_op jit(solution)/shard_map/all_to_all | solution.py:284
  9.1 0.0 copy-done.6
  9.1 0.1 dynamic_slice.3.scale_ref
  9.2 32.7 %all-to-all-done.x_ref = bf16[4,3,224,256]{3,2,1,0:T(8,128)(2,1)S(1)} async-done(((bf16[4,3,224,256]{3,2,1,0:T(8,128)(2,1)}), bf16[4,3,224,256]{3,2,1,0:T(8,128)(2,1)S(1)}, u32[]{:S(2)}, u32[]{:S(2)}) %all-to-all-start) | async-done | bytes 1376288 | tf_op jit(solution)/shard_map/all_to_all | solution.py:284
  41.9 0.0 copy-done.2
  41.9 8.0 %attend.1 = bf16[4,2,256,256]{3,2,1,0:T(8,128)(2,1)} custom-call(f32[4]{0:T(128)S(1)} %dynamic_slice.3.scale_ref, s32[1,4]{1,0:T(1,128)S(1)} %copy-done.2, bf16[4,3,224,256]{3,2,1,0:T(8,128)(2,1)S(1)} %all-to-all-done.x_ref), custom_call_target="tpu_custom_call" | custom-call | tf_op jit(solution)/shard_map/attend/pallas_call | solution.py:307
  49.9 3.6 %all-to-all-start.1 = ((bf16[4,2,256,256]{3,2,1,0:T(8,128)(2,1)}), bf16[4,2,256,256]{3,2,1,0:T(8,128)(2,1)S(1)}, u32[]{:S(2)}, u32[]{:S(2)}) async-start(bf16[4,2,256,256]{3,2,1,0:T(8,128)(2,1)} %attend.1), calls=%async_computation.1 | async-start | bytes 2097152 | tf_op jit(solution)/shard_map/all_to_all | solution.py:321
  53.5 2.9 %collective-permute-start = (s32[224,2]{0,1:T(2,128)S(1)}, s32[224,2]{0,1:T(2,128)S(1)}, u32[]{:S(2)}, u32[]{:S(2)}) collective-permute-start(s32[224,2]{0,1:T(2,128)S(1)} %bitcast.32), channel_id=1, source_target_pairs={{0,2},{1,3},{2,0},{3,1},{4,6},{5,7},{6,4},{7,5},{8,10},{9,11},{10,... | collective-permute-start | bytes 5384 | tf_op jit(solution)/shard_map/ppermute | solution.py:287
  56.4 0.1 pad_add_fusion.1.block_ref
  56.5 0.1 copy.22
  56.6 0.2 copy.16.router_ref
  56.8 22.0 %collective-permute-done = s32[224,2]{0,1:T(2,128)S(1)} collective-permute-done((s32[224,2]{0,1:T(2,128)S(1)}, s32[224,2]{0,1:T(2,128)S(1)}, u32[]{:S(2)}, u32[]{:S(2)}) %collective-permute-start) | collective-permute-done | bytes 1824 | tf_op jit(solution)/shard_map/ppermute | solution.py:287
  78.8 0.1 fusion.1
  78.9 0.1 copy.17.routes_ref
  79.0 0.0 all-to-all-done.1.att_ref
  79.0 20.8 %frames.1 = (bf16[8,176,1536]{2,1,0:T(8,128)(2,1)}, f32[2,12,224,128]{3,2,1,0:T(8,128)}, f32[2,224,128]{2,1,0:T(8,128)S(1)}) custom-call(s32[2]{0:T(128)S(1)} %pad_add_fusion.1.block_ref, s32[1,4]{1,0:T(1,128)S(1)} %copy-done.2, bf16[4,2,256,256]{3,2,1,0:T(8,128)(2,1)S(1)} %all-to-all-done.1.att_ref, bf16[1024,1536]{1,0:T(8,128)(2,1)} %proj_ref.1, ...), custom_call_target="tpu_custom_call" | custom-call | tf_op jit(solution)/shard_map/frames/pallas_call | solution.py:324
  99.8 4.9 %all-to-all-start.2 = ((bf16[8,176,1536]{2,1,0:T(8,128)(2,1)}), bf16[8,176,1536]{2,1,0:T(8,128)(2,1)}, u32[]{:S(2)}, u32[]{:S(2)}) async-start(bf16[8,176,1536]{2,1,0:T(8,128)(2,1)} %get-tuple-element.9), calls=%async_computation.2 | async-start | bytes 8650752 | tf_op jit(solution)/shard_map/all_to_all | solution.py:343
  104.7 0.1 collective-permute-start.1
  104.8 2.0 collective-permute-start.2
  106.8 35.2 %collective-permute-done.1.refs_1_ = bf16[512,1536]{1,0:T(8,128)(2,1)S(1)} collective-permute-done((bf16[512,1536]{1,0:T(8,128)(2,1)S(1)}, bf16[512,1536]{1,0:T(8,128)(2,1)S(1)}, u32[]{:S(2)}, u32[]{:S(2)}) %collective-permute-start.1) | collective-permute-done | bytes 1572896 | tf_op jit(solution)/shard_map/ppermute | solution.py:298
  142.1 33.0 %collective-permute-done.2.refs_3_ = bf16[512,1536]{1,0:T(8,128)(2,1)} collective-permute-done((bf16[512,1536]{1,0:T(8,128)(2,1)}, bf16[512,1536]{1,0:T(8,128)(2,1)}, u32[]{:S(2)}, u32[]{:S(2)}) %collective-permute-start.2) | collective-permute-done | bytes 1572896 | tf_op jit(solution)/shard_map/ppermute | solution.py:299
  175.1 0.0 all-to-all-done.2
  175.1 13.9 %experts.1 = bf16[1408,1536]{1,0:T(8,128)(2,1)} custom-call(bf16[1408,1536]{1,0:T(8,128)(2,1)} %bitcast.7.x_ref, bf16[512,1536]{1,0:T(8,128)(2,1)S(1)} %bitcast.26, bf16[512,1536]{1,0:T(8,128)(2,1)S(1)} %collective-permute-done.1.refs_1_, bf16[512,1536]{1,0:T(8,128)(2,1)} %bitcast.31, bf16[512,1536]{1,0:T(8,128)(2,1)} %collective-permute-done.2.refs_3_), custom_call_target="tpu_custom_call" | custom-call | tf_op jit(solution)/shard_map/experts/pallas_call | solution.py:350
  189.0 4.6 %all-to-all-start.3 = ((bf16[8,176,1536]{2,1,0:T(8,128)(2,1)}), bf16[8,176,1536]{2,1,0:T(8,128)(2,1)}, u32[]{:S(2)}, u32[]{:S(2)}) async-start(bf16[8,176,1536]{2,1,0:T(8,128)(2,1)} %bitcast.28), calls=%async_computation.3 | async-start | bytes 8650752 | tf_op jit(solution)/shard_map/all_to_all | solution.py:361
  193.6 50.5 %all-to-all-done.3 = bf16[8,176,1536]{2,1,0:T(8,128)(2,1)} async-done(((bf16[8,176,1536]{2,1,0:T(8,128)(2,1)}), bf16[8,176,1536]{2,1,0:T(8,128)(2,1)}, u32[]{:S(2)}, u32[]{:S(2)}) %all-to-all-start.3) | async-done | bytes 4325408 | tf_op jit(solution)/shard_map/all_to_all | solution.py:361
  244.1 3.7 %theirs.1 = bf16[224,1536]{1,0:T(8,128)(2,1)S(1)} custom-call(s32[1]{0:T(128)} %bitcast.own_ref, f32[2,224,128]{2,1,0:T(8,128)S(1)} %get-tuple-element.8.info_ref, bf16[1408,1536]{1,0:T(8,128)(2,1)} %bitcast.11.back_ref), custom_call_target="tpu_custom_call" | custom-call | tf_op jit(solution)/shard_map/theirs/pallas_call | solution.py:366
  247.8 0.1 collective-permute-start.3
  247.9 3.6 %mine.1 = f32[224,1536]{1,0:T(8,128)S(1)} custom-call(s32[1]{0:T(128)} %bitcast.own_ref, f32[2,224,128]{2,1,0:T(8,128)S(1)} %get-tuple-element.8.info_ref, bf16[1408,1536]{1,0:T(8,128)(2,1)} %bitcast.11.back_ref, f32[2,12,224,128]{3,2,1,0:T(8,128)S(1)} %copy-done), custom_call_target="tpu_custom_call" | custom-call | tf_op jit(solution)/shard_map/mine/pallas_call | solution.py:375
  251.5 25.9 %collective-permute-done.3 = bf16[224,1536]{1,0:T(8,128)(2,1)S(1)} collective-permute-done((bf16[224,1536]{1,0:T(8,128)(2,1)S(1)}, bf16[224,1536]{1,0:T(8,128)(2,1)S(1)}, u32[]{:S(2)}, u32[]{:S(2)}) %collective-permute-start.3) | collective-permute-done | bytes 688160 | tf_op jit(solution)/shard_map/ppermute | solution.py:374
  277.4 1.0 fusion
  (14 shorter events, 0.1 us)
Async XLA Ops:
  2.7 6.5 %copy-start.6 = (f32[16]{0:T(128)S(1)}, f32[16]{0:T(128)}, u32[]{:S(2)}) copy-start(f32[16]{0:T(128)} %param.14) | copy-start | bytes 196
  2.7 39.2 %copy-start.2 = (s32[1,4]{1,0:T(1,128)S(1)}, s32[1,4]{1,0:T(1,128)}, u32[]{:S(2)}) copy-start(s32[1,4]{1,0:T(1,128)} %len_ref.3) | copy-start | bytes 52
  2.7 39.2 %all-to-all-start = ((bf16[4,3,224,256]{3,2,1,0:T(8,128)(2,1)}), bf16[4,3,224,256]{3,2,1,0:T(8,128)(2,1)S(1)}, u32[]{:S(2)}, u32[]{:S(2)}) async-start(bf16[4,3,224,256]{3,2,1,0:T(8,128)(2,1)} %bitcast.23), calls=%async_computation | async-start | bytes 2752512 | tf_op jit(solution)/shard_map/all_to_all | solution.py:284
  49.8 3.7 %copy-start.5 = (s32[1,224,2]{1,2,0:T(2,128)S(1)}, s32[1,224,2]{1,2,0:T(2,128)}, u32[]{:S(2)}) copy-start(s32[1,224,2]{1,2,0:T(2,128)} %param.21) | copy-start | bytes 5380
  49.9 6.6 %copy-start.3 = (f32[31,1536]{1,0:T(8,128)S(1)}, f32[31,1536]{1,0:T(8,128)}, u32[]{:S(2)}) copy-start(f32[31,1536]{1,0:T(8,128)} %param.16) | copy-start | bytes 571396
  49.9 6.7 %copy-start.4 = (bf16[1536,8]{0,1:T(8,128)(2,1)S(1)}, bf16[1536,8]{0,1:T(8,128)(2,1)}, u32[]{:S(2)}) copy-start(bf16[1536,8]{0,1:T(8,128)(2,1)} %param.17) | copy-start | bytes 73732
  49.9 29.2 %all-to-all-start.1 = ((bf16[4,2,256,256]{3,2,1,0:T(8,128)(2,1)}), bf16[4,2,256,256]{3,2,1,0:T(8,128)(2,1)S(1)}, u32[]{:S(2)}, u32[]{:S(2)}) async-start(bf16[4,2,256,256]{3,2,1,0:T(8,128)(2,1)} %attend.1), calls=%async_computation.1 | async-start | bytes 2097152 | tf_op jit(solution)/shard_map/all_to_all | solution.py:321
  53.5 25.3 %collective-permute-start = (s32[224,2]{0,1:T(2,128)S(1)}, s32[224,2]{0,1:T(2,128)S(1)}, u32[]{:S(2)}, u32[]{:S(2)}) collective-permute-start(s32[224,2]{0,1:T(2,128)S(1)} %bitcast.32), channel_id=1, source_target_pairs={{0,2},{1,3},{2,0},{3,1},{4,6},{5,7},{6,4},{7,5},{8,10},{9,11},{10,... | collective-permute-start | bytes 5384 | tf_op jit(solution)/shard_map/ppermute | solution.py:287
  99.8 4.9 %copy-start.1 = (bf16[1,512,1536]{2,1,0:T(8,128)(2,1)S(1)}, bf16[1,512,1536]{2,1,0:T(8,128)(2,1)}, u32[]{:S(2)}) copy-start(bf16[1,512,1536]{2,1,0:T(8,128)(2,1)} %param.18) | copy-start | bytes 4718596
  99.8 75.2 %all-to-all-start.2 = ((bf16[8,176,1536]{2,1,0:T(8,128)(2,1)}), bf16[8,176,1536]{2,1,0:T(8,128)(2,1)}, u32[]{:S(2)}, u32[]{:S(2)}) async-start(bf16[8,176,1536]{2,1,0:T(8,128)(2,1)} %get-tuple-element.9), calls=%async_computation.2 | async-start | bytes 8650752 | tf_op jit(solution)/shard_map/all_to_all | solution.py:343
  104.7 37.3 %collective-permute-start.1 = (bf16[512,1536]{1,0:T(8,128)(2,1)S(1)}, bf16[512,1536]{1,0:T(8,128)(2,1)S(1)}, u32[]{:S(2)}, u32[]{:S(2)}) collective-permute-start(bf16[512,1536]{1,0:T(8,128)(2,1)S(1)} %bitcast.25), channel_id=1, source_target_pairs={{0,1},{1,0},{2,3},{3,2},{4,5},{5,4},{6,7},{7,6},{8,9},{9,8},{10,11... | collective-permute-start | bytes 4718600 | tf_op jit(solution)/shard_map/ppermute | solution.py:298
  104.8 70.2 %collective-permute-start.2 = (bf16[512,1536]{1,0:T(8,128)(2,1)}, bf16[512,1536]{1,0:T(8,128)(2,1)}, u32[]{:S(2)}, u32[]{:S(2)}) collective-permute-start(bf16[512,1536]{1,0:T(8,128)(2,1)} %bitcast.30), channel_id=1, source_target_pairs={{0,1},{1,0},{2,3},{3,2},{4,5},{5,4},{6,7},{7,6},{8,9},{9,8},{10,11... | collective-permute-start | bytes 4718600 | tf_op jit(solution)/shard_map/ppermute | solution.py:299
  189.0 55.1 %all-to-all-start.3 = ((bf16[8,176,1536]{2,1,0:T(8,128)(2,1)}), bf16[8,176,1536]{2,1,0:T(8,128)(2,1)}, u32[]{:S(2)}, u32[]{:S(2)}) async-start(bf16[8,176,1536]{2,1,0:T(8,128)(2,1)} %bitcast.28), calls=%async_computation.3 | async-start | bytes 8650752 | tf_op jit(solution)/shard_map/all_to_all | solution.py:361
  244.1 3.8 %copy-start = (f32[2,12,224,128]{3,2,1,0:T(8,128)S(1)}, f32[2,12,224,128]{3,2,1,0:T(8,128)}, u32[]{:S(2)}) copy-start(f32[2,12,224,128]{3,2,1,0:T(8,128)} %get-tuple-element.10.second_ref) | copy-start | bytes 8257540
  247.8 29.6 %collective-permute-start.3 = (bf16[224,1536]{1,0:T(8,128)(2,1)S(1)}, bf16[224,1536]{1,0:T(8,128)(2,1)S(1)}, u32[]{:S(2)}, u32[]{:S(2)}) collective-permute-start(bf16[224,1536]{1,0:T(8,128)(2,1)S(1)} %theirs.1), channel_id=1, source_target_pairs={{0,2},{1,3},{2,0},{3,1},{4,6},{5,7},{6,4},{7,5},{8,10},{9,11},{10,... | collective-permute-start | bytes 2064392 | tf_op jit(solution)/shard_map/ppermute | solution.py:374

commit v2 on v1

v2 whole, which is shorter than its diff:
```python
import functools

import jax
import jax.numpy as jnp
from jax import lax
from jax.experimental import pallas as pl
from jax.experimental.pallas import tpu as pltpu
from jax.sharding import PartitionSpec as P

D = 1536
HEADS = 16
HEAD_DIM = 64
KERNEL = 31
TOPK = 2
RECS = 4
HALO = 16
LANES = 128
APART = 64.0
LOG2E = 1.4426950408889634
F32 = jnp.float32
BF16 = jnp.bfloat16
VMEM = pl.BlockSpec(memory_space=pltpu.VMEM)
SMEM = pl.BlockSpec(memory_space=pltpu.SMEM)


def params(mib):
    return pltpu.CompilerParams(vmem_limit_bytes=mib << 20)


def cost(micros):
    return pl.CostEstimate(flops=micros * 1_100_000_000, bytes_accessed=0, transcendentals=0)


def labels_of(frames, len_ref):
    first = len_ref[0, 0]
    second = first + len_ref[0, 1]
    third = second + len_ref[0, 2]
    return (
        (frames >= first).astype(F32)
        + (frames >= second).astype(F32)
        + (frames >= third).astype(F32)
    )


def unit_tile(tile, low):
    lifted = tile.astype(F32)
    square = lifted * lifted
    left = jnp.sum(jnp.where(low, square, 0.0), axis=1, keepdims=True)
    right = jnp.sum(jnp.where(low, 0.0, square), axis=1, keepdims=True)
    factor = jnp.where(low, lax.rsqrt(left + 1e-06), lax.rsqrt(right + 1e-06))
    return lifted * factor


def attend_kernel(count, rows, heads, scale_ref, len_ref, x_ref, oa_ref, ob_ref, k_ref, v_ref, a_ref
):
    block = pl.program_id(0)
    width = heads * HEAD_DIM
    tiles = max(1, width // LANES)
    half = count // 2
    window = rows + 2 * HALO

    def tile_of(source, which, place):
        if width >= LANES:
            return x_ref[source, which, :, place * LANES : (place + 1) * LANES]
        piece = x_ref[source, which]
        return jnp.concatenate([piece, jnp.zeros((rows, LANES - width), BF16)], axis=1)

    low = lax.broadcasted_iota(jnp.int32, (rows, LANES), 1) < HEAD_DIM
    lane = lax.broadcasted_iota(jnp.int32, (rows, LANES), 1).astype(F32)
    row = lax.broadcasted_iota(jnp.int32, (rows, LANES), 0)

    @pl.when(block == 0)
    def _():
        edge = jnp.zeros((HALO, width), BF16)
        a_ref[0:HALO, :] = edge
        a_ref[HALO + count * rows :, :] = edge
        for source in range(count):
            at = slice(source * rows, (source + 1) * rows)
            label = labels_of(row + source * rows, len_ref)
            other = jnp.where((lane >= 1.0) & (lane <= 4.0) & (lane != label + 1.0), -APART, 0.0)
            extra = jnp.where(lane == 0.0, -1.0, other).astype(BF16)
            for place in range(tiles):
                k_ref[place, at, 0:LANES] = unit_tile(tile_of(source, 1, place), low).astype(BF16)
                k_ref[place, at, LANES:] = extra
                v_ref[place, at, 0:LANES] = tile_of(source, 2, place)
                v_ref[place, at, LANES:] = jnp.ones((rows, LANES), BF16)

    label = labels_of(row + block * rows, len_ref)
    extra = jnp.where((lane == 0.0) | (lane == label + 1.0), 1.0, 0.0).astype(BF16)
    for place in range(tiles):
        unit = unit_tile(tile_of(block, 0, place), low)
        parts = []
        for side in range(min(2, heads)):
            head = place * 2 + side
            kept = jnp.where(low if side == 0 else ~low, unit, 0.0).astype(BF16)
            query = jnp.concatenate([kept, extra], axis=1)
            scores = lax.dot_general(
                query, k_ref[place], (((1,), (1,)), ((), ())), preferred_element_type=F32
            )
            weights = jnp.exp2(scores * (scale_ref[head] * LOG2E)).astype(BF16)
            summed = jnp.dot(weights, v_ref[place], preferred_element_type=F32)
            parts.append(summed[:, 0:LANES] / summed[:, LANES:])
        done = parts[0] if len(parts) == 1 else jnp.where(low, parts[0], parts[1])
        start = pl.multiple_of(HALO + block * rows, HALO)
        wide = min(LANES, width)
        a_ref[pl.ds(start, rows), place * LANES : place * LANES + wide] = done[:, 0:wide].astype(BF16)

    @pl.when(block == count - 1)
    def _():
        for target in range(count):
            for o_ref, block_of in ((oa_ref, (target + half) % count), (ob_ref, target)):
                begin = block_of * rows
                o_ref[target] = a_ref[begin : begin + window, :]


def normalize(values):
    average = jnp.mean(values, axis=-1, keepdims=True)
    centered = values - average
    spread = jnp.mean(centered * centered, axis=-1, keepdims=True)
    return centered * lax.rsqrt(spread + 1e-05)


def frame_kernel(
    count,
    rows,
    experts,
    capacity,
    block_ref,
    len_ref,
    att_ref,
    proj_ref,
    taps_ref,
    router_ref,
    routes_ref,
    turned_ref,
    out_ref,
    info_ref,
    second_ref,
    x_ref,
    first_ref,
    lab_ref,
):
    window = rows + 2 * HALO
    half = (KERNEL - 1) // 2
    tiles = D // LANES
    step = 56
    attended = jnp.concatenate([att_ref[i] for i in range(count)], axis=1)
    first = jnp.dot(attended, proj_ref[...], preferred_element_type=F32)
    normed = normalize(first).astype(BF16).astype(F32)
    origin = block_ref[0] * rows
    frames = lax.broadcasted_iota(jnp.int32, (window, LANES), 0) + (origin - HALO)
    lab_ref[...] = labels_of(frames, len_ref)
    for tile in range(tiles):
        at = slice(tile * LANES, (tile + 1) * LANES)
        x_ref[tile] = normed[:, at]
        first_ref[tile] = first[HALO : HALO + rows, at]

    starts = [len_ref[0, 0], len_ref[0, 0] + len_ref[0, 1]]
    starts.append(starts[1] + len_ref[0, 2])
    for begin in range(0, rows, step):
        low = origin + begin - half
        high = low + step + 2 * half
        crossed = functools.reduce(
            jnp.logical_or, [(low < start) & (start < high) for start in starts]
        )

        def columns(tile, masked):
            total = jnp.zeros((step, LANES), F32)
            own = lab_ref[HALO + begin : HALO + begin + step, :] if masked else None
            for tap in range(KERNEL):
                source = HALO - half + begin + tap
                term = taps_ref[tile, tap : tap + 1, :] * x_ref[tile, source : source + step, :]
                if masked:
                    term = jnp.where(lab_ref[source : source + step, :] == own, term, 0.0)
                total = total + term
            gated = total / (1.0 + jnp.exp(-total))
            second_ref[tile, begin : begin + step, :] = (
                first_ref[tile, begin : begin + step, :] + gated
            )

        @pl.when(crossed)
        def _():
            lax.fori_loop(0, tiles, lambda tile, c: (columns(tile, True), c)[1], 0)

        @pl.when(jnp.logical_not(crossed))
        def _():
            lax.fori_loop(0, tiles, lambda tile, c: (columns(tile, False), c)[1], 0)

    second = jnp.concatenate([second_ref[tile] for tile in range(tiles)], axis=1)
    mixed = normalize(second).astype(BF16)

    logits = jnp.dot(mixed, router_ref[...], preferred_element_type=F32)
    lane = lax.broadcasted_iota(jnp.int32, (rows, experts), 1)
    named = [lane == routes_ref[:, pick : pick + 1] for pick in range(TOPK)]
    picked = [jnp.sum(jnp.where(one, logits, 0.0), axis=1, keepdims=True) for one in named]
    top = jnp.maximum(picked[0], picked[1])
    raised = [jnp.exp(one - top) for one in picked]
    mass = raised[0] + raised[1]
    down = lax.broadcasted_iota(jnp.int32, (rows, rows), 0)
    across = lax.broadcasted_iota(jnp.int32, (rows, rows), 1)
    picks = jnp.where(named[0] | named[1], 1.0, 0.0).astype(BF16)
    earlier = jnp.where(across < down, 1.0, 0.0).astype(BF16)
    ranks = jnp.dot(earlier, picks, preferred_element_type=F32)
    column = lax.broadcasted_iota(jnp.int32, (rows, LANES), 1)
    info = jnp.zeros((rows, LANES), F32)
    for pick in range(TOPK):
        rank = jnp.sum(jnp.where(named[pick], ranks, 0.0), axis=1, keepdims=True)
        slot = rank + (routes_ref[:, pick : pick + 1] * capacity).astype(F32)
        info = jnp.where(column == pick, slot, info)
        info = jnp.where(column == TOPK + pick, raised[pick] / mass, info)
    info_ref[...] = info

    expert = lax.broadcasted_iota(jnp.int32, (experts, rows), 0)
    chosen = (expert == turned_ref[0:1, :]) | (expert == turned_ref[1:2, :])
    later = jnp.where(down < across, 1.0, 0.0).astype(BF16)
    order = jnp.dot(jnp.where(chosen, 1.0, 0.0).astype(BF16), later, preferred_element_type=F32)
    order = jnp.where(chosen, order, -1.0)
    place = lax.broadcasted_iota(jnp.int32, (capacity, rows), 0).astype(F32)
    select = jnp.concatenate(
        [jnp.where(place == order[e : e + 1, :], 1.0, 0.0) for e in range(experts)], axis=0
    ).astype(BF16)
    out_ref[...] = jnp.dot(select, mixed, preferred_element_type=F32).astype(BF16)


def expert_kernel(pieces, x_ref, *refs):
    ins, outs, o_ref = refs[:pieces], refs[pieces : 2 * pieces], refs[2 * pieces]
    total = None
    for piece_in, piece_out in zip(ins, outs):
        raw = lax.dot_general(
            x_ref[...], piece_in[...], (((1,), (1,)), ((), ())), preferred_element_type=F32
        )
        hidden = (raw / (1.0 + jnp.exp(-raw))).astype(BF16)
        product = jnp.dot(hidden, piece_out[...], preferred_element_type=F32)
        total = product if total is None else total + product
    o_ref[...] = total.astype(BF16)


def mixture_of(info, back):
    column = lax.broadcasted_iota(jnp.int32, (info.shape[0], back.shape[0]), 1).astype(F32)
    spread = jnp.where(column == info[:, 0:1], info[:, 2:3], 0.0)
    spread = jnp.where(column == info[:, 1:2], info[:, 3:4], spread).astype(BF16)
    return jnp.dot(spread, back, preferred_element_type=F32)


def theirs_kernel(info_ref, back_ref, o_ref):
    o_ref[...] = mixture_of(info_ref[...], back_ref[...]).astype(BF16)


def mine_kernel(info_ref, back_ref, second_ref, part_ref, o_ref):
    mixture = mixture_of(info_ref[...], back_ref[...])
    for tile in range(D // LANES):
        at = slice(tile * LANES, (tile + 1) * LANES)
        both = mixture[:, at] + part_ref[:, at].astype(F32)
        o_ref[:, at] = (second_ref[tile] + 0.5 * both).astype(BF16)


def body(
    query_rows,
    key_rows,
    value_rows,
    head_scale,
    out_proj,
    conv_taps,
    router,
    expert_in,
    expert_out,
    lengths,
    routes,
):
    rows = query_rows.shape[1]
    experts = lax.axis_size("dp")
    count = lax.axis_size("tm")
    half = count // 2
    heads = HEADS // count
    width = heads * HEAD_DIM
    window = rows + 2 * HALO
    capacity = -(-(3 * rows // experts) // 8) * 8
    slots = experts * capacity
    me = lax.axis_index("tm").astype(jnp.int32)
    partner = [(i, (i + half) % count) for i in range(count)]

    packed = jnp.stack([query_rows[0], key_rows[0], value_rows[0]])
    packed = jnp.transpose(packed.reshape(3, rows, count, width), (2, 0, 1, 3))
    arrived = lax.all_to_all(packed, "tm", split_axis=0, concat_axis=0, tiled=True)
    scales = lax.dynamic_slice_in_dim(head_scale, me * heads, heads)
    partner_routes = lax.ppermute(routes[0], "tm", partner)

    own_in, own_out, _ = lax.optimization_barrier((expert_in[0], expert_out[0], arrived))
    if half == 2:
        swap = [(i, i ^ 1) for i in range(count)]
        ins = [own_in, lax.ppermute(own_in, "tm", swap)]
        outs = [own_out, lax.ppermute(own_out, "tm", swap)]
    else:
        groups = [list(range(half)), list(range(half, count))]
        ins = [lax.all_gather(own_in, "tm", axis=0, tiled=True, axis_index_groups=groups)]
        outs = [lax.all_gather(own_out, "tm", axis=0, tiled=True, axis_index_groups=groups)]

    tiles = max(1, width // LANES)
    total = count * rows
    sent = jax.ShapeDtypeStruct((count, window, width), BF16)
    attended = pl.pallas_call(
        functools.partial(attend_kernel, count, rows, heads),
        grid=(count,),
        out_shape=(sent, sent),
        in_specs=[SMEM, SMEM, pl.BlockSpec((count, 3, rows, width), lambda i: (0, 0, 0, 0))],
        out_specs=(pl.BlockSpec((count, window, width), lambda i: (0, 0, 0)),) * 2,
        scratch_shapes=[
            pltpu.VMEM((tiles, total, 2 * LANES), BF16),
            pltpu.VMEM((tiles, total, 2 * LANES), BF16),
            pltpu.VMEM((total + 2 * HALO, width), BF16),
        ],
        compiler_params=params(40),
        cost_estimate=cost(8),
        name="attend",
    )(scales, lengths, arrived)
    gathered = [
        lax.all_to_all(one, "tm", split_axis=0, concat_axis=0, tiled=True) for one in attended
    ]

    taps = jnp.transpose(conv_taps.reshape(KERNEL, D // LANES, LANES), (1, 0, 2))
    pieces = len(ins)
    units = ins[0].shape[0]
    tall = slots // 2

    def send_frames(windows, block, block_routes):
        outgoing, info, second = pl.pallas_call(
            functools.partial(frame_kernel, count, rows, experts, capacity),
            out_shape=(
                jax.ShapeDtypeStruct((slots, D), BF16),
                jax.ShapeDtypeStruct((rows, LANES), F32),
                jax.ShapeDtypeStruct((D // LANES, rows, LANES), F32),
            ),
            in_specs=[SMEM, SMEM, VMEM, VMEM, VMEM, VMEM, VMEM, VMEM],
            out_specs=(VMEM, VMEM, VMEM),
            scratch_shapes=[
                pltpu.VMEM((D // LANES, window, LANES), F32),
                pltpu.VMEM((D // LANES, rows, LANES), F32),
                pltpu.VMEM((window, LANES), F32),
            ],
            compiler_params=params(50),
            cost_estimate=cost(10),
            name="frames",
        )(block.reshape(1), lengths, windows, out_proj, taps, router, block_routes, block_routes.T)
        tokens = lax.all_to_all(
            outgoing.reshape(experts, capacity, D), "dp", split_axis=0, concat_axis=0, tiled=True
        )
        return tokens.reshape(slots, D), info, second

    def run_expert(tokens):
        produced = pl.pallas_call(
            functools.partial(expert_kernel, pieces),
            grid=(2,),
            out_shape=jax.ShapeDtypeStruct((slots, D), BF16),
            in_specs=[pl.BlockSpec((tall, D), lambda i: (i, 0))]
            + [pl.BlockSpec((units, D), lambda i: (0, 0))] * (2 * pieces),
            out_specs=pl.BlockSpec((tall, D), lambda i: (i, 0)),
            compiler_params=params(50),
            cost_estimate=cost(7),
            name="experts",
        )(tokens, *ins, *outs)
        back = lax.all_to_all(
            produced.reshape(experts, capacity, D), "dp", split_axis=0, concat_axis=0, tiled=True
        )
        return back.reshape(slots, D)

    tokens_a, info_a, _ = send_frames(gathered[0], (me + half) % count, partner_routes)
    tokens_b, info_b, second = send_frames(gathered[1], me, routes[0])
    back_a = run_expert(tokens_a)
    back_b = run_expert(tokens_b)

    theirs = pl.pallas_call(
        theirs_kernel,
        out_shape=jax.ShapeDtypeStruct((rows, D), BF16),
        in_specs=[VMEM, VMEM],
        out_specs=VMEM,
        compiler_params=params(40),
        cost_estimate=cost(3),
        name="theirs",
    )(info_a, back_a)
    received = lax.ppermute(theirs, "tm", partner)
    out = pl.pallas_call(
        mine_kernel,
        out_shape=jax.ShapeDtypeStruct((rows, D), BF16),
        in_specs=[VMEM, VMEM, VMEM, VMEM],
        out_specs=VMEM,
        compiler_params=params(40),
        cost_estimate=cost(3),
        name="mine",
    )(info_b, back_b, second, received)
    return out[None]


def solution(mesh):
    return jax.shard_map(
        body,
        mesh=mesh,
        in_specs=(
            P("dp", "tm", None),
            P("dp", "tm", None),
            P("dp", "tm", None),
            P(),
            P(),
            P(),
            P(),
            P("dp", "tm", None),
            P("dp", "tm", None),
            P("dp", None),
            P("dp", "tm", None),
        ),
        out_specs=P("dp", "tm", None),
        check_vma=False,
    )
```

time: 280 us -> 246 us (0.88)
  waiting for transfers between devices: 199 us -> 143 us
  starting transfers between devices: 24.6 us -> 38.4 us
  local copies, waits for them, and re-layouts: 1.77 us -> 10.2 us
    ppermute x3, waiting for transfers between devices: 90.2 us -> 49.6 us  [the longest x1 33.2 us: body(): outs = [own_out, lax.ppermute(own_out, 'tm', swap)]]
    ppermute x1, waiting for transfers between devices: 25.9 us -> 8.82 us  [body(): received = lax.ppermute(theirs, 'tm', partner)]
    all_to_all x3 -> x6, starting transfers between devices: 13.1 us -> 23.7 us  [the longest x2 9.04 us: send_frames(): lax.all_to_all(outgoing.reshape(experts, capacity, D), 'dp', split_axis=0...]
    unnamed x15 -> x31, local copies, waits for them, and re-layouts: 0.24 us -> 8.56 us
    pallas_call x3 -> x5, Pallas kernels: 38.3 us -> 43.5 us  [the longest x2 23.8 us: send_frames(): pl.pallas_call(functools.partial(frame_kernel, count, rows, experts, capa...]
    ppermute x1, starting transfers between devices: 0.07 us -> 3.19 us  [body(): received = lax.ppermute(theirs, 'tm', partner)]
    pallas_call x1, Pallas kernels: 3.73 us -> 0.82 us  [body(): pl.pallas_call(theirs_kernel, out_shape=jax.ShapeDtypeStruct((rows, D), B...]
    all_to_all x3 -> x6, waiting for transfers between devices: 50.5 us -> 52.2 us  [the longest x2 38.6 us: run_expert(): lax.all_to_all(produced.reshape(experts, capacity, D), 'dp', split_axis=0...]
  transfers between devices with their start and end apart: 8 -> 11, of which waited for: 6 -> 9; matrix products, arithmetic and copies ran while one was open for 0% -> 0% of each run, Pallas kernels for 1% -> 17%
where the time goes in v2:
time: 246 us
  waiting for transfers between devices  143 us (58%)
  Pallas kernels  52.3 us (21%)
  starting transfers between devices  38.4 us (16%)
  local copies, waits for them, and re-layouts  10.2 us (4%)
    all_to_all x2, waiting for transfers between devices, run_expert(): lax.all_to_all(produced.reshape(experts, capacity, D), 'dp', split_axis=0...  38.6 us
    ppermute x1, waiting for transfers between devices, body(): outs = [own_out, lax.ppermute(own_out, 'tm', swap)]  33.2 us
    all_to_all x1, waiting for transfers between devices, body(): lax.all_to_all(packed, 'tm', split_axis=0, concat_axis=0, tiled=True)  32.7 us
    pallas_call x2, Pallas kernels, send_frames(): pl.pallas_call(functools.partial(frame_kernel, count, rows, experts, capa...  23.8 us
    pallas_call x2, Pallas kernels, run_expert(): pl.pallas_call(functools.partial(expert_kernel, pieces), grid=(2,), out_s...  17.9 us
    ppermute x1, waiting for transfers between devices, body(): partner_routes = lax.ppermute(routes[0], 'tm', partner)  10.8 us
    all_to_all x2, waiting for transfers between devices, send_frames(): lax.all_to_all(outgoing.reshape(experts, capacity, D), 'dp', split_axis=0...  10.7 us
    all_to_all x2, starting transfers between devices, send_frames(): lax.all_to_all(outgoing.reshape(experts, capacity, D), 'dp', split_axis=0...  9.04 us
  transfers between devices with their start and end apart: 11, of which 9 were waited for; matrix products, arithmetic and copies ran while one was open for 0% of the time, Pallas kernels for 17%

profile of v2, /device:TPU:0, one launch (start us, length us, event | category | flops | bytes accessed | tf_op | source)
XLA Modules:
  0.0 245.7 jit_solution(14553152426268133242)
XLA Ops:
  0.0 1.4 pad_maximum_fusion
  1.4 1.2 copy.25
  2.7 6.4 %all-to-all-start = ((bf16[4,3,224,256]{3,2,1,0:T(8,128)(2,1)}), bf16[4,3,224,256]{3,2,1,0:T(8,128)(2,1)S(1)}, u32[]{:S(2)}, u32[]{:S(2)}) async-start(bf16[4,3,224,256]{3,2,1,0:T(8,128)(2,1)} %bitcast.25), calls=%async_computation | async-start | bytes 2752512 | tf_op jit(solution)/shard_map/all_to_all | solution.py:284
  9.2 32.7 %all-to-all-done.x_ref = bf16[4,3,224,256]{3,2,1,0:T(8,128)(2,1)S(1)} async-done(((bf16[4,3,224,256]{3,2,1,0:T(8,128)(2,1)}), bf16[4,3,224,256]{3,2,1,0:T(8,128)(2,1)S(1)}, u32[]{:S(2)}, u32[]{:S(2)}) %all-to-all-start) | async-done | bytes 1376288 | tf_op jit(solution)/shard_map/all_to_all | solution.py:284
  41.9 8.0 %attend.1 = (bf16[4,256,256]{2,1,0:T(8,128)(2,1)}, bf16[4,256,256]{2,1,0:T(8,128)(2,1)}) custom-call(f32[4]{0:T(128)S(1)} %dynamic_slice.3.scale_ref, s32[1,4]{1,0:T(1,128)S(1)} %copy-done.5, bf16[4,3,224,256]{3,2,1,0:T(8,128)(2,1)S(1)} %all-to-all-done.x_ref), custom_call_target="tpu_custom_call" | custom-call | flops 8800000000 | tf_op jit(solution)/shard_map/attend/pallas_call | solution.py:301
  49.9 3.6 %all-to-all-start.4 = ((bf16[4,256,256]{2,1,0:T(8,128)(2,1)}), bf16[4,256,256]{2,1,0:T(8,128)(2,1)S(1)}, u32[]{:S(2)}, u32[]{:S(2)}) async-start(bf16[4,256,256]{2,1,0:T(8,128)(2,1)} %get-tuple-element.20), calls=%async_computation.4 | async-start | bytes 1048576 | tf_op jit(solution)/shard_map/all_to_all | solution.py:317
  53.5 2.9 %collective-permute-start.2 = (s32[224,2]{0,1:T(2,128)S(1)}, s32[224,2]{0,1:T(2,128)S(1)}, u32[]{:S(2)}, u32[]{:S(2)}) collective-permute-start(s32[224,2]{0,1:T(2,128)S(1)} %bitcast.31), channel_id=1, source_target_pairs={{0,2},{1,3},{2,0},{3,1},{4,6},{5,7},{6,4},{7,5},{8,10},{9,11},{10,... | collective-permute-start | bytes 5384 | tf_op jit(solution)/shard_map/ppermute | solution.py:286
  56.8 10.8 %collective-permute-done.2 = s32[224,2]{0,1:T(2,128)S(1)} collective-permute-done((s32[224,2]{0,1:T(2,128)S(1)}, s32[224,2]{0,1:T(2,128)S(1)}, u32[]{:S(2)}, u32[]{:S(2)}) %collective-permute-start.2) | collective-permute-done | bytes 1824 | tf_op jit(solution)/shard_map/ppermute | solution.py:286
  67.7 3.5 %all-to-all-start.1 = ((bf16[4,256,256]{2,1,0:T(8,128)(2,1)}), bf16[4,256,256]{2,1,0:T(8,128)(2,1)S(1)}, u32[]{:S(2)}, u32[]{:S(2)}) async-start(bf16[4,256,256]{2,1,0:T(8,128)(2,1)} %get-tuple-element.14), calls=%async_computation.1 | async-start | bytes 1048576 | tf_op jit(solution)/shard_map/all_to_all | solution.py:317
  71.2 10.5 %frames.3 = (bf16[704,1536]{1,0:T(8,128)(2,1)}, f32[224,128]{1,0:T(8,128)S(1)}, f32[12,224,128]{2,1,0:T(8,128)}) custom-call(s32[1]{0:T(128)} %bitcast.11.block_ref, s32[1,4]{1,0:T(1,128)S(1)} %copy-done.5, bf16[4,256,256]{2,1,0:T(8,128)(2,1)S(1)} %all-to-all-done.4.att_ref, bf16[1024,1536]{1,0:T(8,128)(2,1)} %proj_ref.3, f32[12,31,128]{2,1,0:T(8,128)S(1)} %bitcast.29, ...), custom_call_target="tpu_custom_call" | custom-call | flops 11000000512 | tf_op jit(solution)/shard_map/frames/pallas_call | solution.py:326
  82.3 2.8 %all-to-all-done.1.att_ref = bf16[4,256,256]{2,1,0:T(8,128)(2,1)S(1)} async-done(((bf16[4,256,256]{2,1,0:T(8,128)(2,1)}), bf16[4,256,256]{2,1,0:T(8,128)(2,1)S(1)}, u32[]{:S(2)}, u32[]{:S(2)}) %all-to-all-start.1) | async-done | bytes 524320 | tf_op jit(solution)/shard_map/all_to_all | solution.py:317
  85.1 4.5 %all-to-all-start.5 = ((bf16[8,88,1536]{2,1,0:T(8,128)(2,1)}), bf16[8,88,1536]{2,1,0:T(8,128)(2,1)}, u32[]{:S(2)}, u32[]{:S(2)}) async-start(bf16[8,88,1536]{2,1,0:T(8,128)(2,1)} %bitcast.39), calls=%async_computation.5 | async-start | bytes 4325376 | tf_op jit(solution)/shard_map/all_to_all | solution.py:344
  89.8 2.0 collective-permute-start.1
  91.9 13.3 %frames.2 = (bf16[704,1536]{1,0:T(8,128)(2,1)}, f32[224,128]{1,0:T(8,128)S(1)}, f32[12,224,128]{2,1,0:T(8,128)S(1)}) custom-call(s32[1]{0:T(128)} %bitcast.block_ref, s32[1,4]{1,0:T(1,128)S(1)} %copy-done.5, bf16[4,256,256]{2,1,0:T(8,128)(2,1)S(1)} %all-to-all-done.1.att_ref, bf16[1024,1536]{1,0:T(8,128)(2,1)} %proj_ref.3, f32[12,31,128]{2,1,0:T(8,128)S(1)} %bitcast.30, ...), custom_call_target="tpu_custom_call" | custom-call | flops 11000000512 | tf_op jit(solution)/shard_map/frames/pallas_call | solution.py:326
  105.2 1.1 copy-done.6
  106.2 10.7 %all-to-all-done.5 = bf16[8,88,1536]{2,1,0:T(8,128)(2,1)} async-done(((bf16[8,88,1536]{2,1,0:T(8,128)(2,1)}), bf16[8,88,1536]{2,1,0:T(8,128)(2,1)}, u32[]{:S(2)}, u32[]{:S(2)}) %all-to-all-start.5) | async-done | bytes 2162720 | tf_op jit(solution)/shard_map/all_to_all | solution.py:344
  117.0 4.6 %all-to-all-start.2 = ((bf16[8,88,1536]{2,1,0:T(8,128)(2,1)}), bf16[8,88,1536]{2,1,0:T(8,128)(2,1)}, u32[]{:S(2)}, u32[]{:S(2)}) async-start(bf16[8,88,1536]{2,1,0:T(8,128)(2,1)} %bitcast.40), calls=%async_computation.2 | async-start | bytes 4325376 | tf_op jit(solution)/shard_map/all_to_all | solution.py:344
  121.5 5.6 %collective-permute-done.refs_1_ = bf16[512,1536]{1,0:T(8,128)(2,1)} collective-permute-done((bf16[512,1536]{1,0:T(8,128)(2,1)S(1)}, bf16[512,1536]{1,0:T(8,128)(2,1)}, u32[]{:S(2)}, u32[]{:S(2)}) %collective-permute-start) | collective-permute-done | bytes 1572896 | tf_op jit(solution)/shard_map/ppermute | solution.py:291
  127.2 33.2 %collective-permute-done.1.refs_3_ = bf16[512,1536]{1,0:T(8,128)(2,1)} collective-permute-done((bf16[512,1536]{1,0:T(8,128)(2,1)}, bf16[512,1536]{1,0:T(8,128)(2,1)}, u32[]{:S(2)}, u32[]{:S(2)}) %collective-permute-start.1) | collective-permute-done | bytes 1572896 | tf_op jit(solution)/shard_map/ppermute | solution.py:292
  160.3 8.9 %experts.3 = bf16[704,1536]{1,0:T(8,128)(2,1)} custom-call(bf16[704,1536]{1,0:T(8,128)(2,1)} %bitcast.14.x_ref, bf16[512,1536]{1,0:T(8,128)(2,1)S(1)} %bitcast.36, bf16[512,1536]{1,0:T(8,128)(2,1)} %collective-permute-done.refs_1_, bf16[512,1536]{1,0:T(8,128)(2,1)} %bitcast.44, bf16[512,1536]{1,0:T(8,128)(2,1)} %collective-permute-done.1.refs_3_), custom_call_target="tpu_custom_call" | custom-call | flops 7699999744 | tf_op jit(solution)/shard_map/experts/pallas_call | solution.py:350
  169.3 3.9 %all-to-all-start.6 = ((bf16[8,88,1536]{2,1,0:T(8,128)(2,1)}), bf16[8,88,1536]{2,1,0:T(8,128)(2,1)S(1)}, u32[]{:S(2)}, u32[]{:S(2)}) async-start(bf16[8,88,1536]{2,1,0:T(8,128)(2,1)} %bitcast.42), calls=%async_computation.6 | async-start | bytes 4325376 | tf_op jit(solution)/shard_map/all_to_all | solution.py:361
  173.1 1.4 copy-done.4
  174.5 9.0 %experts.2 = bf16[704,1536]{1,0:T(8,128)(2,1)} custom-call(bf16[704,1536]{1,0:T(8,128)(2,1)} %bitcast.6.x_ref, bf16[512,1536]{1,0:T(8,128)(2,1)S(1)} %bitcast.37, bf16[512,1536]{1,0:T(8,128)(2,1)} %collective-permute-done.refs_1_, bf16[512,1536]{1,0:T(8,128)(2,1)} %bitcast.45, bf16[512,1536]{1,0:T(8,128)(2,1)} %collective-permute-done.1.refs_3_), custom_call_target="tpu_custom_call" | custom-call | flops 7699999744 | tf_op jit(solution)/shard_map/experts/pallas_call | solution.py:350
  183.5 17.0 %all-to-all-done.6 = bf16[8,88,1536]{2,1,0:T(8,128)(2,1)S(1)} async-done(((bf16[8,88,1536]{2,1,0:T(8,128)(2,1)}), bf16[8,88,1536]{2,1,0:T(8,128)(2,1)S(1)}, u32[]{:S(2)}, u32[]{:S(2)}) %all-to-all-start.6) | async-done | bytes 2162720 | tf_op jit(solution)/shard_map/all_to_all | solution.py:361
  200.5 1.3 copy-done
  201.8 3.7 %all-to-all-start.3 = ((bf16[8,88,1536]{2,1,0:T(8,128)(2,1)}), bf16[8,88,1536]{2,1,0:T(8,128)(2,1)S(1)}, u32[]{:S(2)}, u32[]{:S(2)}) async-start(bf16[8,88,1536]{2,1,0:T(8,128)(2,1)} %bitcast.41), calls=%async_computation.3 | async-start | bytes 4325376 | tf_op jit(solution)/shard_map/all_to_all | solution.py:361
  205.6 1.6 copy-done.1
  208.0 3.2 %collective-permute-start.3 = (bf16[224,1536]{1,0:T(8,128)(2,1)S(1)}, bf16[224,1536]{1,0:T(8,128)(2,1)S(1)}, u32[]{:S(2)}, u32[]{:S(2)}) collective-permute-start(bf16[224,1536]{1,0:T(8,128)(2,1)S(1)} %theirs.1), channel_id=1, source_target_pairs={{0,2},{1,3},{2,0},{3,1},{4,6},{5,7},{6,4},{7,5},{8,10},{9,11},{10,... | collective-permute-start | bytes 2064392 | tf_op jit(solution)/shard_map/ppermute | solution.py:380
  211.2 21.6 %all-to-all-done.3 = bf16[8,88,1536]{2,1,0:T(8,128)(2,1)S(1)} async-done(((bf16[8,88,1536]{2,1,0:T(8,128)(2,1)}), bf16[8,88,1536]{2,1,0:T(8,128)(2,1)S(1)}, u32[]{:S(2)}, u32[]{:S(2)}) %all-to-all-start.3) | async-done | bytes 2162720 | tf_op jit(solution)/shard_map/all_to_all | solution.py:361
  232.9 8.8 %collective-permute-done.3.part_ref = bf16[224,1536]{1,0:T(8,128)(2,1)S(1)} collective-permute-done((bf16[224,1536]{1,0:T(8,128)(2,1)S(1)}, bf16[224,1536]{1,0:T(8,128)(2,1)S(1)}, u32[]{:S(2)}, u32[]{:S(2)}) %collective-permute-start.3) | collective-permute-done | bytes 688160 | tf_op jit(solution)/shard_map/ppermute | solution.py:380
  241.7 1.3 copy-done.7
  243.9 1.7 mine.1
  (35 shorter events, 3.1 us)
Async XLA Ops:
  2.7 6.5 %copy-start.14 = (f32[16]{0:T(128)S(1)}, f32[16]{0:T(128)}, u32[]{:S(2)}) copy-start(f32[16]{0:T(128)} %param.14) | copy-start | bytes 196
  2.7 39.2 %copy-start.5 = (s32[1,4]{1,0:T(1,128)S(1)}, s32[1,4]{1,0:T(1,128)}, u32[]{:S(2)}) copy-start(s32[1,4]{1,0:T(1,128)} %len_ref.5) | copy-start | bytes 52
  2.7 39.2 %all-to-all-start = ((bf16[4,3,224,256]{3,2,1,0:T(8,128)(2,1)}), bf16[4,3,224,256]{3,2,1,0:T(8,128)(2,1)S(1)}, u32[]{:S(2)}, u32[]{:S(2)}) async-start(bf16[4,3,224,256]{3,2,1,0:T(8,128)(2,1)} %bitcast.25), calls=%async_computation | async-start | bytes 2752512 | tf_op jit(solution)/shard_map/all_to_all | solution.py:284
  9.2 44.3 %copy-start.2 = (s32[1,224,2]{1,2,0:T(2,128)S(1)}, s32[1,224,2]{1,2,0:T(2,128)}, u32[]{:S(2)}) copy-start(s32[1,224,2]{1,2,0:T(2,128)} %param.21) | copy-start | bytes 5380
  9.2 47.2 %copy-start.12 = (f32[31,1536]{1,0:T(8,128)S(1)}, f32[31,1536]{1,0:T(8,128)}, u32[]{:S(2)}) copy-start(f32[31,1536]{1,0:T(8,128)} %param.16) | copy-start | bytes 571396
  49.9 6.6 %copy-start.13 = (bf16[1536,8]{0,1:T(8,128)(2,1)S(1)}, bf16[1536,8]{0,1:T(8,128)(2,1)}, u32[]{:S(2)}) copy-start(bf16[1536,8]{0,1:T(8,128)(2,1)} %param.17) | copy-start | bytes 73732
  49.9 17.8 %all-to-all-start.4 = ((bf16[4,256,256]{2,1,0:T(8,128)(2,1)}), bf16[4,256,256]{2,1,0:T(8,128)(2,1)S(1)}, u32[]{:S(2)}, u32[]{:S(2)}) async-start(bf16[4,256,256]{2,1,0:T(8,128)(2,1)} %get-tuple-element.20), calls=%async_computation.4 | async-start | bytes 1048576 | tf_op jit(solution)/shard_map/all_to_all | solution.py:317
  53.5 14.0 %collective-permute-start.2 = (s32[224,2]{0,1:T(2,128)S(1)}, s32[224,2]{0,1:T(2,128)S(1)}, u32[]{:S(2)}, u32[]{:S(2)}) collective-permute-start(s32[224,2]{0,1:T(2,128)S(1)} %bitcast.31), channel_id=1, source_target_pairs={{0,2},{1,3},{2,0},{3,1},{4,6},{5,7},{6,4},{7,5},{8,10},{9,11},{10,... | collective-permute-start | bytes 5384 | tf_op jit(solution)/shard_map/ppermute | solution.py:286
  67.7 17.4 %all-to-all-start.1 = ((bf16[4,256,256]{2,1,0:T(8,128)(2,1)}), bf16[4,256,256]{2,1,0:T(8,128)(2,1)S(1)}, u32[]{:S(2)}, u32[]{:S(2)}) async-start(bf16[4,256,256]{2,1,0:T(8,128)(2,1)} %get-tuple-element.14), calls=%async_computation.1 | async-start | bytes 1048576 | tf_op jit(solution)/shard_map/all_to_all | solution.py:317
  81.7 0.6 copy-start.10
  85.1 4.6 %copy-start.3 = (bf16[1,512,1536]{2,1,0:T(8,128)(2,1)S(1)}, bf16[1,512,1536]{2,1,0:T(8,128)(2,1)}, u32[]{:S(2)}) copy-start(bf16[1,512,1536]{2,1,0:T(8,128)(2,1)} %param.18) | copy-start | bytes 4718596
  85.1 31.9 %all-to-all-start.5 = ((bf16[8,88,1536]{2,1,0:T(8,128)(2,1)}), bf16[8,88,1536]{2,1,0:T(8,128)(2,1)}, u32[]{:S(2)}, u32[]{:S(2)}) async-start(bf16[8,88,1536]{2,1,0:T(8,128)(2,1)} %bitcast.39), calls=%async_computation.5 | async-start | bytes 4325376 | tf_op jit(solution)/shard_map/all_to_all | solution.py:344
  89.8 37.4 %collective-permute-start = (bf16[512,1536]{1,0:T(8,128)(2,1)S(1)}, bf16[512,1536]{1,0:T(8,128)(2,1)}, u32[]{:S(2)}, u32[]{:S(2)}) collective-permute-start(bf16[512,1536]{1,0:T(8,128)(2,1)S(1)} %bitcast.35), channel_id=1, source_target_pairs={{0,1},{1,0},{2,3},{3,2},{4,5},{5,4},{6,7},{7,6},{8,9},{9,8},{10,11... | collective-permute-start | bytes 4718600 | tf_op jit(solution)/shard_map/ppermute | solution.py:291
  89.8 70.5 %collective-permute-start.1 = (bf16[512,1536]{1,0:T(8,128)(2,1)}, bf16[512,1536]{1,0:T(8,128)(2,1)}, u32[]{:S(2)}, u32[]{:S(2)}) collective-permute-start(bf16[512,1536]{1,0:T(8,128)(2,1)} %bitcast.43), channel_id=1, source_target_pairs={{0,1},{1,0},{2,3},{3,2},{4,5},{5,4},{6,7},{7,6},{8,9},{9,8},{10,11... | collective-permute-start | bytes 4718600 | tf_op jit(solution)/shard_map/ppermute | solution.py:292
  105.2 1.1 copy-start.6
  106.2 10.7 %copy-start.8 = (f32[224,128]{1,0:T(8,128)}, f32[224,128]{1,0:T(8,128)S(1)}, u32[]{:S(2)}) copy-start(f32[224,128]{1,0:T(8,128)S(1)} %get-tuple-element.15.info_ref) | copy-start | bytes 344068
  117.0 52.3 %all-to-all-start.2 = ((bf16[8,88,1536]{2,1,0:T(8,128)(2,1)}), bf16[8,88,1536]{2,1,0:T(8,128)(2,1)}, u32[]{:S(2)}, u32[]{:S(2)}) async-start(bf16[8,88,1536]{2,1,0:T(8,128)(2,1)} %bitcast.40), calls=%async_computation.2 | async-start | bytes 4325376 | tf_op jit(solution)/shard_map/all_to_all | solution.py:344
  169.3 31.2 %all-to-all-start.6 = ((bf16[8,88,1536]{2,1,0:T(8,128)(2,1)}), bf16[8,88,1536]{2,1,0:T(8,128)(2,1)S(1)}, u32[]{:S(2)}, u32[]{:S(2)}) async-start(bf16[8,88,1536]{2,1,0:T(8,128)(2,1)} %bitcast.42), calls=%async_computation.6 | async-start | bytes 4325376 | tf_op jit(solution)/shard_map/all_to_all | solution.py:361
  173.1 1.4 copy-start.4
  200.5 1.3 copy-start
  201.8 3.7 %copy-start.11 = (f32[224,128]{1,0:T(8,128)S(1)}, f32[224,128]{1,0:T(8,128)}, u32[]{:S(2)}) copy-start(f32[224,128]{1,0:T(8,128)} %copy-done.10) | copy-start | bytes 344068
  201.8 31.0 %all-to-all-start.3 = ((bf16[8,88,1536]{2,1,0:T(8,128)(2,1)}), bf16[8,88,1536]{2,1,0:T(8,128)(2,1)S(1)}, u32[]{:S(2)}, u32[]{:S(2)}) async-start(bf16[8,88,1536]{2,1,0:T(8,128)(2,1)} %bitcast.41), calls=%async_computation.3 | async-start | bytes 4325376 | tf_op jit(solution)/shard_map/all_to_all | solution.py:361
  205.6 1.6 copy-start.1
  208.0 33.6 %collective-permute-start.3 = (bf16[224,1536]{1,0:T(8,128)(2,1)S(1)}, bf16[224,1536]{1,0:T(8,128)(2,1)S(1)}, u32[]{:S(2)}, u32[]{:S(2)}) collective-permute-start(bf16[224,1536]{1,0:T(8,128)(2,1)S(1)} %theirs.1), channel_id=1, source_target_pairs={{0,2},{1,3},{2,0},{3,1},{4,6},{5,7},{6,4},{7,5},{8,10},{9,11},{10,... | collective-permute-start | bytes 2064392 | tf_op jit(solution)/shard_map/ppermute | solution.py:380
  241.7 1.3 copy-start.7
  243.0 0.9 copy-start.9

commit v3 on v2

--- a/solution.py
+++ b/solution.py
@@ -49,6 +49,13 @@
     right = jnp.sum(jnp.where(low, 0.0, square), axis=1, keepdims=True)
     factor = jnp.where(low, lax.rsqrt(left + 1e-06), lax.rsqrt(right + 1e-06))
     return lifted * factor
+
+
+def pack_kernel(q_ref, k_ref, v_ref, o_ref):
+    width = o_ref.shape[3]
+    for which, ref in enumerate((q_ref, k_ref, v_ref)):
+        for target in range(o_ref.shape[0]):
+            o_ref[target, which] = ref[:, target * width : (target + 1) * width]
 
 
 def attend_kernel(count, rows, heads, scale_ref, len_ref, x_ref, oa_ref, ob_ref, k_ref, v_ref, a_ref
@@ -279,21 +286,23 @@
     me = lax.axis_index("tm").astype(jnp.int32)
     partner = [(i, (i + half) % count) for i in range(count)]
 
-    packed = jnp.stack([query_rows[0], key_rows[0], value_rows[0]])
-    packed = jnp.transpose(packed.reshape(3, rows, count, width), (2, 0, 1, 3))
+    packed = pl.pallas_call(
+        pack_kernel,
+        out_shape=jax.ShapeDtypeStruct((count, 3, rows, width), BF16),
+        in_specs=[VMEM, VMEM, VMEM],
+        out_specs=VMEM,
+        compiler_params=params(16),
+        cost_estimate=cost(1),
+        name="pack",
+    )(query_rows[0], key_rows[0], value_rows[0])
     arrived = lax.all_to_all(packed, "tm", split_axis=0, concat_axis=0, tiled=True)
     scales = lax.dynamic_slice_in_dim(head_scale, me * heads, heads)
     partner_routes = lax.ppermute(routes[0], "tm", partner)
 
     own_in, own_out, _ = lax.optimization_barrier((expert_in[0], expert_out[0], arrived))
-    if half == 2:
-        swap = [(i, i ^ 1) for i in range(count)]
-        ins = [own_in, lax.ppermute(own_in, "tm", swap)]
-        outs = [own_out, lax.ppermute(own_out, "tm", swap)]
-    else:
-        groups = [list(range(half)), list(range(half, count))]
-        ins = [lax.all_gather(own_in, "tm", axis=0, tiled=True, axis_index_groups=groups)]
-        outs = [lax.all_gather(own_out, "tm", axis=0, tiled=True, axis_index_groups=groups)]
+    groups = [list(range(half)), list(range(half, count))]
+    ins = [lax.all_gather(own_in, "tm", axis=0, tiled=True, axis_index_groups=groups)]
+    outs = [lax.all_gather(own_out, "tm", axis=0, tiled=True, axis_index_groups=groups)]
 
     tiles = max(1, width // LANES)
     total = count * rows

time: 246 us -> 249 us (1.012)
  waiting for transfers between devices: 143 us -> 102 us
  blocking collectives: 0 us -> 38.9 us
  between operations: 0.18 us -> 13.6 us
  starting transfers between devices: 38.4 us -> 31 us
  local copies, waits for them, and re-layouts: 10.2 us -> 12.8 us
    all_to_all x0 -> x1, blocking collectives: none -> 38.9 us  [body(): lax.all_to_all(packed, 'tm', split_axis=0, concat_axis=0, tiled=True)]
    ppermute x2 -> x0, waiting for transfers between devices: 38.8 us -> none  [the longest x1 33.2 us: body(): outs = [own_out, lax.ppermute(own_out, 'tm', swap)]]
    all_to_all x1 -> x0, waiting for transfers between devices: 32.7 us -> none  [body(): lax.all_to_all(packed, 'tm', split_axis=0, concat_axis=0, tiled=True)]
    all_gather x0 -> x2, waiting for transfers between devices: none -> 18.7 us  [the longest x1 18.6 us: body(): lax.all_gather(own_out, 'tm', axis=0, tiled=True, axis_index_groups=groups)]
    all_to_all x1 -> x0, starting transfers between devices: 6.45 us -> none  [body(): lax.all_to_all(packed, 'tm', split_axis=0, concat_axis=0, tiled=True)]
    all_to_all x2, waiting for transfers between devices: 2.79 us -> 6.86 us  [body(): lax.all_to_all(one, 'tm', split_axis=0, concat_axis=0, tiled=True)]
    unnamed x31 -> x33, local copies, waits for them, and re-layouts: 8.56 us -> 12.4 us
    ppermute x1, waiting for transfers between devices: 10.8 us -> 14.4 us  [body(): partner_routes = lax.ppermute(routes[0], 'tm', partner)]
  transfers between devices with their start and end apart: 11 -> 10, of which waited for: 9 -> 7; matrix products, arithmetic and copies ran while one was open for 0% -> 0% of each run, Pallas kernels for 17% -> 20%
where the time goes in v3:
time: 249 us
  waiting for transfers between devices  102 us (41%)
  Pallas kernels  50.6 us (20%)
  blocking collectives  38.9 us (16%)
  starting transfers between devices  31 us (12%)
  between operations  13.6 us (5%)
  local copies, waits for them, and re-layouts  12.8 us (5%)
    all_to_all x2, waiting for transfers between devices, run_expert(): lax.all_to_all(produced.reshape(experts, capacity, D), 'dp', split_axis=0...  40.1 us
    all_to_all x1, blocking collectives, body(): lax.all_to_all(packed, 'tm', split_axis=0, concat_axis=0, tiled=True)  38.9 us
    pallas_call x2, Pallas kernels, send_frames(): pl.pallas_call(functools.partial(frame_kernel, count, rows, experts, capa...  23.5 us
    all_gather x1, waiting for transfers between devices, body(): lax.all_gather(own_out, 'tm', axis=0, tiled=True, axis_index_groups=groups)  18.6 us
    pallas_call x2, Pallas kernels, run_expert(): pl.pallas_call(functools.partial(expert_kernel, pieces), grid=(2,), out_s...  16.4 us
    ppermute x1, waiting for transfers between devices, body(): partner_routes = lax.ppermute(routes[0], 'tm', partner)  14.4 us
    all_to_all x2, waiting for transfers between devices, send_frames(): lax.all_to_all(outgoing.reshape(experts, capacity, D), 'dp', split_axis=0...  13 us
    unnamed x33, local copies, waits for them, and re-layouts  12.4 us
  transfers between devices with their start and end apart: 10, of which 7 were waited for; matrix products, arithmetic and copies ran while one was open for 0% of the time, Pallas kernels for 20%

profile of v3, /device:TPU:0, one launch (start us, length us, event | category | flops | bytes accessed | tf_op | source)
XLA Modules:
  0.0 248.6 jit_solution(8727845999835248659)
XLA Ops:
  6.5 1.0 copy-done.5
  7.6 1.0 copy-done.6
  8.6 1.0 copy-done.7
  9.7 38.9 %all_to_all.35.x_ref = bf16[4,3,224,256]{3,2,1,0:T(8,128)(2,1)S(1)} all-to-all(bf16[4,3,224,256]{3,2,1,0:T(8,128)(2,1)S(1)} %pack.1), channel_id=1, replica_groups=mesh['dp'=8,'tm'=4] {'tm'}, dimensions={0} | all-to-all | bytes 2752512 | tf_op jit(solution)/shard_map/all_to_all | solution.py:298
  48.7 8.0 %attend.1 = (bf16[4,256,256]{2,1,0:T(8,128)(2,1)}, bf16[4,256,256]{2,1,0:T(8,128)(2,1)}) custom-call(f32[4]{0:T(128)S(1)} %dynamic_slice.3.scale_ref, s32[1,4]{1,0:T(1,128)S(1)} %copy-done.8, bf16[4,3,224,256]{3,2,1,0:T(8,128)(2,1)S(1)} %all_to_all.35.x_ref), custom_call_target="tpu_custom_call" | custom-call | flops 8800000000 | tf_op jit(solution)/shard_map/attend/pallas_call | solution.py:310
  56.7 3.5 %all-to-all-start.4 = ((bf16[4,256,256]{2,1,0:T(8,128)(2,1)}), bf16[4,256,256]{2,1,0:T(8,128)(2,1)S(1)}, u32[]{:S(2)}, u32[]{:S(2)}) async-start(bf16[4,256,256]{2,1,0:T(8,128)(2,1)} %get-tuple-element.20), calls=%async_computation.4 | async-start | bytes 1048576 | tf_op jit(solution)/shard_map/all_to_all | solution.py:326
  60.3 2.8 %collective-permute-start = (s32[224,2]{0,1:T(2,128)S(1)}, s32[224,2]{0,1:T(2,128)S(1)}, u32[]{:S(2)}, u32[]{:S(2)}) collective-permute-start(s32[224,2]{0,1:T(2,128)S(1)} %bitcast.29), channel_id=1, source_target_pairs={{0,2},{1,3},{2,0},{3,1},{4,6},{5,7},{6,4},{7,5},{8,10},{9,11},{10,... | collective-permute-start | bytes 5384 | tf_op jit(solution)/shard_map/ppermute | solution.py:300
  63.5 14.4 %collective-permute-done = s32[224,2]{0,1:T(2,128)S(1)} collective-permute-done((s32[224,2]{0,1:T(2,128)S(1)}, s32[224,2]{0,1:T(2,128)S(1)}, u32[]{:S(2)}, u32[]{:S(2)}) %collective-permute-start) | collective-permute-done | bytes 1824 | tf_op jit(solution)/shard_map/ppermute | solution.py:300
  78.1 6.0 %all-to-all-start.1 = ((bf16[4,256,256]{2,1,0:T(8,128)(2,1)}), bf16[4,256,256]{2,1,0:T(8,128)(2,1)S(1)}, u32[]{:S(2)}, u32[]{:S(2)}) async-start(bf16[4,256,256]{2,1,0:T(8,128)(2,1)} %get-tuple-element.14), calls=%async_computation.1 | async-start | bytes 1048576 | tf_op jit(solution)/shard_map/all_to_all | solution.py:326
  84.0 10.4 %frames.3 = (bf16[704,1536]{1,0:T(8,128)(2,1)}, f32[224,128]{1,0:T(8,128)S(1)}, f32[12,224,128]{2,1,0:T(8,128)}) custom-call(s32[1]{0:T(128)} %bitcast.13.block_ref, s32[1,4]{1,0:T(1,128)S(1)} %copy-done.8, bf16[4,256,256]{2,1,0:T(8,128)(2,1)S(1)} %all-to-all-done.4.att_ref, bf16[1024,1536]{1,0:T(8,128)(2,1)} %proj_ref.3, f32[12,31,128]{2,1,0:T(8,128)S(1)} %bitcast.27, ...), custom_call_target="tpu_custom_call" | custom-call | flops 11000000512 | tf_op jit(solution)/shard_map/frames/pallas_call | solution.py:335
  94.5 6.9 %all-to-all-done.1.att_ref = bf16[4,256,256]{2,1,0:T(8,128)(2,1)S(1)} async-done(((bf16[4,256,256]{2,1,0:T(8,128)(2,1)}), bf16[4,256,256]{2,1,0:T(8,128)(2,1)S(1)}, u32[]{:S(2)}, u32[]{:S(2)}) %all-to-all-start.1) | async-done | bytes 524320 | tf_op jit(solution)/shard_map/all_to_all | solution.py:326
  101.3 4.4 %all-to-all-start.5 = ((bf16[8,88,1536]{2,1,0:T(8,128)(2,1)}), bf16[8,88,1536]{2,1,0:T(8,128)(2,1)}, u32[]{:S(2)}, u32[]{:S(2)}) async-start(bf16[8,88,1536]{2,1,0:T(8,128)(2,1)} %bitcast.36), calls=%async_computation.5 | async-start | bytes 4325376 | tf_op jit(solution)/shard_map/all_to_all | solution.py:353
  105.8 13.1 %frames.2 = (bf16[704,1536]{1,0:T(8,128)(2,1)}, f32[224,128]{1,0:T(8,128)S(1)}, f32[12,224,128]{2,1,0:T(8,128)S(1)}) custom-call(s32[1]{0:T(128)} %bitcast.block_ref, s32[1,4]{1,0:T(1,128)S(1)} %copy-done.8, bf16[4,256,256]{2,1,0:T(8,128)(2,1)S(1)} %all-to-all-done.1.att_ref, bf16[1024,1536]{1,0:T(8,128)(2,1)} %proj_ref.3, f32[12,31,128]{2,1,0:T(8,128)S(1)} %bitcast.28, ...), custom_call_target="tpu_custom_call" | custom-call | flops 11000000512 | tf_op jit(solution)/shard_map/frames/pallas_call | solution.py:335
  119.0 1.1 copy-done.9
  120.0 13.0 %all-to-all-done.5 = bf16[8,88,1536]{2,1,0:T(8,128)(2,1)} async-done(((bf16[8,88,1536]{2,1,0:T(8,128)(2,1)}), bf16[8,88,1536]{2,1,0:T(8,128)(2,1)}, u32[]{:S(2)}, u32[]{:S(2)}) %all-to-all-start.5) | async-done | bytes 2162720 | tf_op jit(solution)/shard_map/all_to_all | solution.py:353
  133.0 4.5 %all-to-all-start.2 = ((bf16[8,88,1536]{2,1,0:T(8,128)(2,1)}), bf16[8,88,1536]{2,1,0:T(8,128)(2,1)}, u32[]{:S(2)}, u32[]{:S(2)}) async-start(bf16[8,88,1536]{2,1,0:T(8,128)(2,1)} %bitcast.37), calls=%async_computation.2 | async-start | bytes 4325376 | tf_op jit(solution)/shard_map/all_to_all | solution.py:353
  137.6 18.6 %all-gather.5.cloned.1.call-done.refs_1_ = bf16[1024,1536]{1,0:T(8,128)(2,1)} async-done(((bf16[512,1536]{1,0:T(8,128)(2,1)}), bf16[1024,1536]{1,0:T(8,128)(2,1)}) %all-gather.5.cloned.1.call-update) | async-done | bytes 3145744 | tf_op jit(solution)/shard_map/all_gather | solution.py:305
  156.3 8.2 %experts.3 = bf16[704,1536]{1,0:T(8,128)(2,1)S(1)} custom-call(bf16[704,1536]{1,0:T(8,128)(2,1)} %bitcast.16.x_ref, bf16[1024,1536]{1,0:T(8,128)(2,1)} %all-gather.3.cloned.1.call-done.refs_0_, bf16[1024,1536]{1,0:T(8,128)(2,1)} %all-gather.5.cloned.1.call-done.refs_1_), custom_call_target="tpu_custom_call" | custom-call | flops 7699999744 | tf_op jit(solution)/shard_map/experts/pallas_call | solution.py:359
  164.5 1.4 copy-done.3
  165.9 3.7 %all-to-all-start.6 = ((bf16[8,88,1536]{2,1,0:T(8,128)(2,1)}), bf16[8,88,1536]{2,1,0:T(8,128)(2,1)S(1)}, u32[]{:S(2)}, u32[]{:S(2)}) async-start(bf16[8,88,1536]{2,1,0:T(8,128)(2,1)} %bitcast.26), calls=%async_computation.6 | async-start | bytes 4325376 | tf_op jit(solution)/shard_map/all_to_all | solution.py:370
  169.5 8.2 %experts.2 = bf16[704,1536]{1,0:T(8,128)(2,1)S(1)} custom-call(bf16[704,1536]{1,0:T(8,128)(2,1)} %bitcast.8.x_ref, bf16[1024,1536]{1,0:T(8,128)(2,1)} %all-gather.3.cloned.1.call-done.refs_0_, bf16[1024,1536]{1,0:T(8,128)(2,1)} %all-gather.5.cloned.1.call-done.refs_1_), custom_call_target="tpu_custom_call" | custom-call | flops 7699999744 | tf_op jit(solution)/shard_map/experts/pallas_call | solution.py:359
  177.8 1.4 copy-done.2
  179.1 17.8 %all-to-all-done.6 = bf16[8,88,1536]{2,1,0:T(8,128)(2,1)S(1)} async-done(((bf16[8,88,1536]{2,1,0:T(8,128)(2,1)}), bf16[8,88,1536]{2,1,0:T(8,128)(2,1)S(1)}, u32[]{:S(2)}, u32[]{:S(2)}) %all-to-all-start.6) | async-done | bytes 2162720 | tf_op jit(solution)/shard_map/all_to_all | solution.py:370
  196.9 1.3 copy-done
  198.2 3.6 %all-to-all-start.3 = ((bf16[8,88,1536]{2,1,0:T(8,128)(2,1)}), bf16[8,88,1536]{2,1,0:T(8,128)(2,1)S(1)}, u32[]{:S(2)}, u32[]{:S(2)}) async-start(bf16[8,88,1536]{2,1,0:T(8,128)(2,1)} %bitcast.25), calls=%async_computation.3 | async-start | bytes 4325376 | tf_op jit(solution)/shard_map/all_to_all | solution.py:370
  201.9 1.6 copy-done.1
  204.3 2.5 collective-permute-start.1
  206.8 22.4 %all-to-all-done.3 = bf16[8,88,1536]{2,1,0:T(8,128)(2,1)S(1)} async-done(((bf16[8,88,1536]{2,1,0:T(8,128)(2,1)}), bf16[8,88,1536]{2,1,0:T(8,128)(2,1)S(1)}, u32[]{:S(2)}, u32[]{:S(2)}) %all-to-all-start.3) | async-done | bytes 2162720 | tf_op jit(solution)/shard_map/all_to_all | solution.py:370
  229.1 8.6 %collective-permute-done.1.part_ref = bf16[224,1536]{1,0:T(8,128)(2,1)S(1)} collective-permute-done((bf16[224,1536]{1,0:T(8,128)(2,1)S(1)}, bf16[224,1536]{1,0:T(8,128)(2,1)S(1)}, u32[]{:S(2)}, u32[]{:S(2)}) %collective-permute-start.1) | collective-permute-done | bytes 688160 | tf_op jit(solution)/shard_map/ppermute | solution.py:389
  237.8 1.3 copy-done.10
  239.1 0.9 copy-done.12
  240.0 1.7 mine.1
  (37 shorter events, 1.7 us)
Async XLA Ops:
  6.5 131.1 %all-gather.3.cloned.1.call-start = ((), (), s32[]{:S(2)}) async-start(), calls=%async_computation.7 | async-start | bytes 4718592 | tf_op jit(solution)/shard_map/all_gather | solution.py:304
  6.5 1.0 copy-start.5
  7.6 1.0 copy-start.6
  8.6 1.0 copy-start.7
  9.7 38.9 %copy-start.15 = (f32[16]{0:T(128)S(1)}, f32[16]{0:T(128)}, u32[]{:S(2)}) copy-start(f32[16]{0:T(128)} %param.14) | copy-start | bytes 196
  9.7 39.0 %copy-start.8 = (s32[1,4]{1,0:T(1,128)S(1)}, s32[1,4]{1,0:T(1,128)}, u32[]{:S(2)}) copy-start(s32[1,4]{1,0:T(1,128)} %len_ref.5) | copy-start | bytes 52
  48.7 11.6 %copy-start.4 = (s32[1,224,2]{1,2,0:T(2,128)S(1)}, s32[1,224,2]{1,2,0:T(2,128)}, u32[]{:S(2)}) copy-start(s32[1,224,2]{1,2,0:T(2,128)} %param.21) | copy-start | bytes 5380
  48.7 14.4 %copy-start.13 = (f32[31,1536]{1,0:T(8,128)S(1)}, f32[31,1536]{1,0:T(8,128)}, u32[]{:S(2)}) copy-start(f32[31,1536]{1,0:T(8,128)} %param.16) | copy-start | bytes 571396
  48.7 14.6 %copy-start.14 = (bf16[1536,8]{0,1:T(8,128)(2,1)S(1)}, bf16[1536,8]{0,1:T(8,128)(2,1)}, u32[]{:S(2)}) copy-start(bf16[1536,8]{0,1:T(8,128)(2,1)} %param.17) | copy-start | bytes 73732
  56.7 21.3 %all-to-all-start.4 = ((bf16[4,256,256]{2,1,0:T(8,128)(2,1)}), bf16[4,256,256]{2,1,0:T(8,128)(2,1)S(1)}, u32[]{:S(2)}, u32[]{:S(2)}) async-start(bf16[4,256,256]{2,1,0:T(8,128)(2,1)} %get-tuple-element.20), calls=%async_computation.4 | async-start | bytes 1048576 | tf_op jit(solution)/shard_map/all_to_all | solution.py:326
  60.2 96.0 %all-gather.5.cloned.1.call-start = ((), (), s32[]{:S(2)}) async-start(), calls=%async_computation.8 | async-start | bytes 4718592 | tf_op jit(solution)/shard_map/all_gather | solution.py:305
  60.3 17.6 %collective-permute-start = (s32[224,2]{0,1:T(2,128)S(1)}, s32[224,2]{0,1:T(2,128)S(1)}, u32[]{:S(2)}, u32[]{:S(2)}) collective-permute-start(s32[224,2]{0,1:T(2,128)S(1)} %bitcast.29), channel_id=1, source_target_pairs={{0,2},{1,3},{2,0},{3,1},{4,6},{5,7},{6,4},{7,5},{8,10},{9,11},{10,... | collective-permute-start | bytes 5384 | tf_op jit(solution)/shard_map/ppermute | solution.py:300
  78.1 23.3 %all-to-all-start.1 = ((bf16[4,256,256]{2,1,0:T(8,128)(2,1)}), bf16[4,256,256]{2,1,0:T(8,128)(2,1)S(1)}, u32[]{:S(2)}, u32[]{:S(2)}) async-start(bf16[4,256,256]{2,1,0:T(8,128)(2,1)} %get-tuple-element.14), calls=%async_computation.1 | async-start | bytes 1048576 | tf_op jit(solution)/shard_map/all_to_all | solution.py:326
  101.3 31.7 %all-to-all-start.5 = ((bf16[8,88,1536]{2,1,0:T(8,128)(2,1)}), bf16[8,88,1536]{2,1,0:T(8,128)(2,1)}, u32[]{:S(2)}, u32[]{:S(2)}) async-start(bf16[8,88,1536]{2,1,0:T(8,128)(2,1)} %bitcast.36), calls=%async_computation.5 | async-start | bytes 4325376 | tf_op jit(solution)/shard_map/all_to_all | solution.py:353
  119.0 1.1 copy-start.9
  120.0 13.0 %copy-start.11 = (f32[224,128]{1,0:T(8,128)}, f32[224,128]{1,0:T(8,128)S(1)}, u32[]{:S(2)}) copy-start(f32[224,128]{1,0:T(8,128)S(1)} %get-tuple-element.15.info_ref) | copy-start | bytes 344068
  133.0 32.8 %all-to-all-start.2 = ((bf16[8,88,1536]{2,1,0:T(8,128)(2,1)}), bf16[8,88,1536]{2,1,0:T(8,128)(2,1)}, u32[]{:S(2)}, u32[]{:S(2)}) async-start(bf16[8,88,1536]{2,1,0:T(8,128)(2,1)} %bitcast.37), calls=%async_computation.2 | async-start | bytes 4325376 | tf_op jit(solution)/shard_map/all_to_all | solution.py:353
  164.4 1.4 copy-start.3
  165.9 31.0 %all-to-all-start.6 = ((bf16[8,88,1536]{2,1,0:T(8,128)(2,1)}), bf16[8,88,1536]{2,1,0:T(8,128)(2,1)S(1)}, u32[]{:S(2)}, u32[]{:S(2)}) async-start(bf16[8,88,1536]{2,1,0:T(8,128)(2,1)} %bitcast.26), calls=%async_computation.6 | async-start | bytes 4325376 | tf_op jit(solution)/shard_map/all_to_all | solution.py:370
  177.8 1.4 copy-start.2
  196.9 1.3 copy-start
  198.2 30.9 %all-to-all-start.3 = ((bf16[8,88,1536]{2,1,0:T(8,128)(2,1)}), bf16[8,88,1536]{2,1,0:T(8,128)(2,1)S(1)}, u32[]{:S(2)}, u32[]{:S(2)}) async-start(bf16[8,88,1536]{2,1,0:T(8,128)(2,1)} %bitcast.25), calls=%async_computation.3 | async-start | bytes 4325376 | tf_op jit(solution)/shard_map/all_to_all | solution.py:370
  201.9 1.6 copy-start.1
  204.3 33.5 %collective-permute-start.1 = (bf16[224,1536]{1,0:T(8,128)(2,1)S(1)}, bf16[224,1536]{1,0:T(8,128)(2,1)S(1)}, u32[]{:S(2)}, u32[]{:S(2)}) collective-permute-start(bf16[224,1536]{1,0:T(8,128)(2,1)S(1)} %theirs.1), channel_id=1, source_target_pairs={{0,2},{1,3},{2,0},{3,1},{4,6},{5,7},{6,4},{7,5},{8,10},{9,11},{10,... | collective-permute-start | bytes 2064392 | tf_op jit(solution)/shard_map/ppermute | solution.py:389
  237.8 1.3 copy-start.10
  239.1 0.9 copy-start.12
Sparse Core Ops, SparseCore 0:
  48.7 60.9 all-gather.2
  111.3 44.9 all-gather.4

commit v4 on v3

v4 whole, which is shorter than its diff:
```python
import functools

import jax
import jax.numpy as jnp
from jax import lax
from jax.experimental import pallas as pl
from jax.experimental.pallas import tpu as pltpu
from jax.sharding import PartitionSpec as P

D = 1536
HEADS = 16
HEAD_DIM = 64
KERNEL = 31
TOPK = 2
RECS = 4
HALO = 16
LANES = 128
APART = 64.0
LOG2E = 1.4426950408889634
F32 = jnp.float32
BF16 = jnp.bfloat16
VMEM = pl.BlockSpec(memory_space=pltpu.VMEM)
SMEM = pl.BlockSpec(memory_space=pltpu.SMEM)


def params(mib):
    return pltpu.CompilerParams(vmem_limit_bytes=mib << 20)


def cost(micros):
    return pl.CostEstimate(flops=micros * 1_100_000_000, bytes_accessed=0, transcendentals=0)


def labels_of(frames, len_ref):
    first = len_ref[0, 0]
    second = first + len_ref[0, 1]
    third = second + len_ref[0, 2]
    return (
        (frames >= first).astype(F32)
        + (frames >= second).astype(F32)
        + (frames >= third).astype(F32)
    )


def unit_tile(tile, low):
    lifted = tile.astype(F32)
    square = lifted * lifted
    left = jnp.sum(jnp.where(low, square, 0.0), axis=1, keepdims=True)
    right = jnp.sum(jnp.where(low, 0.0, square), axis=1, keepdims=True)
    factor = jnp.where(low, lax.rsqrt(left + 1e-06), lax.rsqrt(right + 1e-06))
    return lifted * factor


def pack_kernel(place, q_ref, k_ref, v_ref, me_ref, *o_refs):
    width = o_refs[0].shape[2]
    for r, o_ref in enumerate(o_refs):
        target = place(me_ref[0], r)
        for which, ref in enumerate((q_ref, k_ref, v_ref)):
            if isinstance(target, int):
                o_ref[which] = ref[:, target * width : (target + 1) * width]
            else:
                o_ref[which] = ref[:, pl.ds(pl.multiple_of(target * width, LANES), width)]


def attend_kernel(count, rows, heads, place, me_ref, scale_ref, len_ref, *refs):
    x_refs, oa_refs, ob_refs = refs[:count], refs[count : 2 * count], refs[2 * count : 3 * count]
    k_ref, v_ref, a_ref = refs[3 * count :]
    me = me_ref[0]
    width = heads * HEAD_DIM
    tiles = max(1, width // LANES)
    half = count // 2
    window = rows + 2 * HALO

    def tile_of(r, which, tile):
        if width >= LANES:
            return x_refs[r][which, :, tile * LANES : (tile + 1) * LANES]
        piece = x_refs[r][which]
        return jnp.concatenate([piece, jnp.zeros((rows, LANES - width), BF16)], axis=1)

    low = lax.broadcasted_iota(jnp.int32, (rows, LANES), 1) < HEAD_DIM
    lane = lax.broadcasted_iota(jnp.int32, (rows, LANES), 1).astype(F32)
    row = lax.broadcasted_iota(jnp.int32, (rows, LANES), 0)

    edge = jnp.zeros((HALO, width), BF16)
    a_ref[0:HALO, :] = edge
    a_ref[HALO + count * rows :, :] = edge
    for r in range(count):
        at = slice(r * rows, (r + 1) * rows)
        label = labels_of(row + place(me, r) * rows, len_ref)
        other = jnp.where((lane >= 1.0) & (lane <= 4.0) & (lane != label + 1.0), -APART, 0.0)
        extra = jnp.where(lane == 0.0, -1.0, other).astype(BF16)
        for tile in range(tiles):
            k_ref[tile, at, 0:LANES] = unit_tile(tile_of(r, 1, tile), low).astype(BF16)
            k_ref[tile, at, LANES:] = extra
            v_ref[tile, at, 0:LANES] = tile_of(r, 2, tile)
            v_ref[tile, at, LANES:] = jnp.ones((rows, LANES), BF16)

    for r in range(count):
        block = place(me, r)
        label = labels_of(row + block * rows, len_ref)
        extra = jnp.where((lane == 0.0) | (lane == label + 1.0), 1.0, 0.0).astype(BF16)
        for tile in range(tiles):
            unit = unit_tile(tile_of(r, 0, tile), low)
            parts = []
            for side in range(min(2, heads)):
                head = tile * 2 + side
                kept = jnp.where(low if side == 0 else ~low, unit, 0.0).astype(BF16)
                query = jnp.concatenate([kept, extra], axis=1)
                scores = lax.dot_general(
                    query, k_ref[tile], (((1,), (1,)), ((), ())), preferred_element_type=F32
                )
                weights = jnp.exp2(scores * (scale_ref[head] * LOG2E)).astype(BF16)
                summed = jnp.dot(weights, v_ref[tile], preferred_element_type=F32)
                parts.append(summed[:, 0:LANES] / summed[:, LANES:])
            done = parts[0] if len(parts) == 1 else jnp.where(low, parts[0], parts[1])
            start = pl.multiple_of(HALO + block * rows, HALO)
            wide = min(LANES, width)
            a_ref[pl.ds(start, rows), tile * LANES : tile * LANES + wide] = done[:, 0:wide].astype(BF16)

    for r in range(count):
        target = place(me, r)
        for o_ref, block in ((oa_refs[r], target ^ half), (ob_refs[r], target)):
            o_ref[...] = a_ref[pl.ds(pl.multiple_of(block * rows, HALO), window), :]


def normalize(values):
    average = jnp.mean(values, axis=-1, keepdims=True)
    centered = values - average
    spread = jnp.mean(centered * centered, axis=-1, keepdims=True)
    return centered * lax.rsqrt(spread + 1e-05)


def frame_kernel(
    count,
    rows,
    experts,
    capacity,
    place,
    flip,
    me_ref,
    expert_ref,
    len_ref,
    proj_ref,
    taps_ref,
    router_ref,
    routes_ref,
    turned_ref,
    *refs,
):
    att_refs, out_refs = refs[:count], refs[count : count + experts]
    info_ref, second_ref, x_ref, first_ref, lab_ref = refs[count + experts :]
    me = me_ref[0]
    width = att_refs[0].shape[1]
    window = rows + 2 * HALO
    half = (KERNEL - 1) // 2
    tiles = D // LANES
    step = 56
    first = jnp.zeros((window, D), F32)
    for r in range(count):
        begin = pl.multiple_of(place(me, r) * width, HEAD_DIM)
        first = first + jnp.dot(
            att_refs[r][...], proj_ref[pl.ds(begin, width), :], preferred_element_type=F32
        )
    normed = normalize(first).astype(BF16).astype(F32)
    origin = (me ^ flip) * rows
    frames = lax.broadcasted_iota(jnp.int32, (window, LANES), 0) + (origin - HALO)
    lab_ref[...] = labels_of(frames, len_ref)
    for tile in range(tiles):
        at = slice(tile * LANES, (tile + 1) * LANES)
        x_ref[tile] = normed[:, at]
        first_ref[tile] = first[HALO : HALO + rows, at]

    starts = [len_ref[0, 0], len_ref[0, 0] + len_ref[0, 1]]
    starts.append(starts[1] + len_ref[0, 2])
    for begin in range(0, rows, step):
        low = origin + begin - half
        high = low + step + 2 * half
        crossed = functools.reduce(
            jnp.logical_or, [(low < start) & (start < high) for start in starts]
        )

        def columns(tile, masked):
            total = jnp.zeros((step, LANES), F32)
            own = lab_ref[HALO + begin : HALO + begin + step, :] if masked else None
            for tap in range(KERNEL):
                source = HALO - half + begin + tap
                term = taps_ref[tile, tap : tap + 1, :] * x_ref[tile, source : source + step, :]
                if masked:
                    term = jnp.where(lab_ref[source : source + step, :] == own, term, 0.0)
                total = total + term
            gated = total / (1.0 + jnp.exp(-total))
            second_ref[tile, begin : begin + step, :] = (
                first_ref[tile, begin : begin + step, :] + gated
            )

        @pl.when(crossed)
        def _():
            lax.fori_loop(0, tiles, lambda tile, c: (columns(tile, True), c)[1], 0)

        @pl.when(jnp.logical_not(crossed))
        def _():
            lax.fori_loop(0, tiles, lambda tile, c: (columns(tile, False), c)[1], 0)

    second = jnp.concatenate([second_ref[tile] for tile in range(tiles)], axis=1)
    mixed = normalize(second).astype(BF16)

    logits = jnp.dot(mixed, router_ref[...], preferred_element_type=F32)
    lane = lax.broadcasted_iota(jnp.int32, (rows, experts), 1)
    named = [lane == routes_ref[:, pick : pick + 1] for pick in range(TOPK)]
    picked = [jnp.sum(jnp.where(one, logits, 0.0), axis=1, keepdims=True) for one in named]
    top = jnp.maximum(picked[0], picked[1])
    raised = [jnp.exp(one - top) for one in picked]
    mass = raised[0] + raised[1]
    down = lax.broadcasted_iota(jnp.int32, (rows, rows), 0)
    across = lax.broadcasted_iota(jnp.int32, (rows, rows), 1)
    picks = jnp.where(named[0] | named[1], 1.0, 0.0).astype(BF16)
    earlier = jnp.where(across < down, 1.0, 0.0).astype(BF16)
    ranks = jnp.dot(earlier, picks, preferred_element_type=F32)
    column = lax.broadcasted_iota(jnp.int32, (rows, LANES), 1)
    info = jnp.zeros((rows, LANES), F32)
    for pick in range(TOPK):
        rank = jnp.sum(jnp.where(named[pick], ranks, 0.0), axis=1, keepdims=True)
        place_of = routes_ref[:, pick : pick + 1] ^ expert_ref[0]
        slot = rank + (place_of * capacity).astype(F32)
        info = jnp.where(column == pick, slot, info)
        info = jnp.where(column == TOPK + pick, raised[pick] / mass, info)
    info_ref[...] = info

    expert = lax.broadcasted_iota(jnp.int32, (experts, rows), 0) ^ expert_ref[0]
    chosen = (expert == turned_ref[0:1, :]) | (expert == turned_ref[1:2, :])
    later = jnp.where(down < across, 1.0, 0.0).astype(BF16)
    order = jnp.dot(jnp.where(chosen, 1.0, 0.0).astype(BF16), later, preferred_element_type=F32)
    order = jnp.where(chosen, order, -1.0)
    slot = lax.broadcasted_iota(jnp.int32, (capacity, rows), 0).astype(F32)
    for e in range(0, experts, 2):
        select = jnp.concatenate(
            [jnp.where(slot == order[e + k : e + k + 1, :], 1.0, 0.0) for k in range(2)], axis=0
        ).astype(BF16)
        moved = jnp.dot(select, mixed, preferred_element_type=F32)
        out_refs[e][...] = moved[0:capacity].astype(BF16)
        out_refs[e + 1][...] = moved[capacity:].astype(BF16)


def joined(left_ref, right_ref):
    both = [left_ref[...].astype(F32), right_ref[...].astype(F32)]
    return jnp.concatenate(both, axis=0).astype(BF16)


def expert_kernel(experts, pieces, *refs):
    x_refs, refs = refs[:experts], refs[experts:]
    ins, outs, o_refs = refs[:pieces], refs[pieces : 2 * pieces], refs[2 * pieces :]
    capacity = x_refs[0].shape[0]
    for e in range(0, experts, 2):
        tokens = joined(x_refs[e], x_refs[e + 1])
        total = jnp.zeros((2 * capacity, D), F32)
        for piece_in, piece_out in zip(ins, outs):
            raw = lax.dot_general(
                tokens, piece_in[...], (((1,), (1,)), ((), ())), preferred_element_type=F32
            )
            hidden = (raw / (1.0 + jnp.exp(-raw))).astype(BF16)
            total = total + jnp.dot(hidden, piece_out[...], preferred_element_type=F32)
        o_refs[e][...] = total[0:capacity].astype(BF16)
        o_refs[e + 1][...] = total[capacity:].astype(BF16)


def mixture_of(info, back_refs):
    capacity = back_refs[0].shape[0]
    total = jnp.zeros((info.shape[0], D), F32)
    column = lax.broadcasted_iota(jnp.int32, (info.shape[0], 2 * capacity), 1).astype(F32)
    for e in range(0, len(back_refs), 2):
        spread = jnp.where(column == info[:, 0:1] - e * capacity, info[:, 2:3], 0.0)
        spread = jnp.where(column == info[:, 1:2] - e * capacity, info[:, 3:4], spread)
        total = total + jnp.dot(
            spread.astype(BF16), joined(back_refs[e], back_refs[e + 1]), preferred_element_type=F32
        )
    return total


def theirs_kernel(info_ref, *refs):
    refs[-1][...] = mixture_of(info_ref[...], refs[:-1]).astype(BF16)


def mine_kernel(info_ref, second_ref, part_ref, *refs):
    o_ref = refs[-1]
    mixture = mixture_of(info_ref[...], refs[:-1])
    for tile in range(D // LANES):
        at = slice(tile * LANES, (tile + 1) * LANES)
        both = mixture[:, at] + part_ref[:, at].astype(F32)
        o_ref[:, at] = (second_ref[tile] + 0.5 * both).astype(BF16)


def crossed(count, direct, me, r):
    return me ^ r if direct else r


def trade(arrays, axis, direct=True):
    count = len(arrays)
    if not direct:
        mixed = lax.all_to_all(jnp.stack(arrays), axis, split_axis=0, concat_axis=0, tiled=True)
        return [mixed[r] for r in range(count)]
    moved = {
        r: lax.ppermute(arrays[r], axis, [(i, i ^ r) for i in range(count)])
        for r in range(count - 1, 0, -1)
    }
    return [arrays[0]] + [moved[r] for r in range(1, count)]


def tied(arrays, marker):
    return lax.optimization_barrier((*arrays, marker))[:-1]


def body(
    query_rows,
    key_rows,
    value_rows,
    head_scale,
    out_proj,
    conv_taps,
    router,
    expert_in,
    expert_out,
    lengths,
    routes,
):
    rows = query_rows.shape[1]
    experts = lax.axis_size("dp")
    count = lax.axis_size("tm")
    half = count // 2
    heads = HEADS // count
    width = heads * HEAD_DIM
    window = rows + 2 * HALO
    capacity = -(-(3 * rows // experts) // 8) * 8
    direct = width % LANES == 0
    me = lax.axis_index("tm").astype(jnp.int32).reshape(1)
    expert = lax.axis_index("dp").astype(jnp.int32).reshape(1)
    partner = [(i, i ^ half) for i in range(count)]
    place = functools.partial(crossed, count, direct)

    packed = pl.pallas_call(
        functools.partial(pack_kernel, place),
        out_shape=(jax.ShapeDtypeStruct((3, rows, width), BF16),) * count,
        in_specs=[VMEM, VMEM, VMEM, SMEM],
        out_specs=(VMEM,) * count,
        compiler_params=params(16),
        cost_estimate=cost(1),
        name="pack",
    )(query_rows[0], key_rows[0], value_rows[0], me)
    arrived = trade(packed, "tm", direct)
    scales = lax.dynamic_slice_in_dim(head_scale, me[0] * heads, heads)
    partner_routes = lax.ppermute(routes[0], "tm", partner)

    tiles = max(1, width // LANES)
    total = count * rows
    sent = jax.ShapeDtypeStruct((window, width), BF16)
    attended = pl.pallas_call(
        functools.partial(attend_kernel, count, rows, heads, place),
        out_shape=(sent,) * (2 * count),
        in_specs=[SMEM, SMEM, SMEM] + [VMEM] * count,
        out_specs=(VMEM,) * (2 * count),
        scratch_shapes=[
            pltpu.VMEM((tiles, total, 2 * LANES), BF16),
            pltpu.VMEM((tiles, total, 2 * LANES), BF16),
            pltpu.VMEM((total + 2 * HALO, width), BF16),
        ],
        compiler_params=params(32),
        cost_estimate=cost(1),
        name="attend",
    )(me, scales, lengths, *arrived)
    gathered_a = trade(attended[:count], "tm", direct)
    gathered_b = trade(attended[count:], "tm", direct)

    if half == 2:
        swap = [(i, i ^ 1) for i in range(count)]
        units = expert_in.shape[1]
        cut = units // 2
        (early,) = tied((expert_in[0, :cut],), packed[1])
        late = tied((expert_in[0, cut:], expert_out[0, :cut], expert_out[0, cut:]), gathered_a[-1])
        moved = [lax.ppermute(one, "tm", swap) for one in (early, *late)]
        ins = [expert_in[0], moved[0], moved[1]]
        outs = [expert_out[0], moved[2], moved[3]]
    else:
        groups = [list(range(half)), list(range(half, count))]
        ins = [lax.all_gather(expert_in[0], "tm", axis=0, tiled=True, axis_index_groups=groups)]
        outs = [lax.all_gather(expert_out[0], "tm", axis=0, tiled=True, axis_index_groups=groups)]

    taps = jnp.transpose(conv_taps.reshape(KERNEL, D // LANES, LANES), (1, 0, 2))
    pieces = len(ins)
    chunk = jax.ShapeDtypeStruct((capacity, D), BF16)

    def send_frames(windows, flip, block_routes):
        made = pl.pallas_call(
            functools.partial(frame_kernel, count, rows, experts, capacity, place, flip),
            out_shape=(chunk,) * experts
            + (
                jax.ShapeDtypeStruct((rows, LANES), F32),
                jax.ShapeDtypeStruct((D // LANES, rows, LANES), F32),
            ),
            in_specs=[SMEM, SMEM, SMEM] + [VMEM] * (5 + count),
            out_specs=(VMEM,) * (experts + 2),
            scratch_shapes=[
                pltpu.VMEM((D // LANES, window, LANES), F32),
                pltpu.VMEM((D // LANES, rows, LANES), F32),
                pltpu.VMEM((window, LANES), F32),
            ],
            compiler_params=params(32),
            cost_estimate=cost(1),
            name="frames",
        )(me, expert, lengths, out_proj, taps, router, block_routes, block_routes.T, *windows)
        return trade(made[:experts], "dp"), made[experts], made[experts + 1]

    def run_expert(tokens):
        produced = pl.pallas_call(
            functools.partial(expert_kernel, experts, pieces),
            out_shape=(chunk,) * experts,
            in_specs=[VMEM] * (experts + 2 * pieces),
            out_specs=(VMEM,) * experts,
            compiler_params=params(32),
            cost_estimate=cost(1),
            name="experts",
        )(*tokens, *ins, *outs)
        return trade(produced, "dp")

    tokens_a, info_a, _ = send_frames(gathered_a, half, partner_routes)
    tokens_b, info_b, second = send_frames(gathered_b, 0, routes[0])
    back_a = run_expert(tokens_a)
    back_b = run_expert(tokens_b)

    theirs = pl.pallas_call(
        theirs_kernel,
        out_shape=jax.ShapeDtypeStruct((rows, D), BF16),
        in_specs=[VMEM] * (1 + experts),
        out_specs=VMEM,
        compiler_params=params(24),
        cost_estimate=cost(1),
        name="theirs",
    )(info_a, *back_a)
    received = lax.ppermute(theirs, "tm", partner)
    out = pl.pallas_call(
        mine_kernel,
        out_shape=jax.ShapeDtypeStruct((rows, D), BF16),
        in_specs=[VMEM] * (3 + experts),
        out_specs=VMEM,
        compiler_params=params(24),
        cost_estimate=cost(1),
        name="mine",
    )(info_b, second, received, *back_b)
    return out[None]


def solution(mesh):
    return jax.shard_map(
        body,
        mesh=mesh,
        in_specs=(
            P("dp", "tm", None),
            P("dp", "tm", None),
            P("dp", "tm", None),
            P(),
            P(),
            P(),
            P(),
            P("dp", "tm", None),
            P("dp", "tm", None),
            P("dp", None),
            P("dp", "tm", None),
        ),
        out_specs=P("dp", "tm", None),
        check_vma=False,
    )
```

time: 249 us -> 262 us (1.052)
  blocking collectives: 38.9 us -> 0 us
  starting transfers between devices: 31 us -> 60.4 us
  waiting for transfers between devices: 102 us -> 128 us
  local copies, waits for them, and re-layouts: 12.8 us -> 26.9 us
  between operations: 13.6 us -> 0.25 us
  Pallas kernels: 50.6 us -> 46.4 us
    ppermute x0 -> x41, waiting for transfers between devices: none -> 119 us  [the longest x37 90 us: trade(): lax.ppermute(arrays[r], axis, [(i, i ^ r) for i in range(count)])]
    all_to_all x6 -> x0, waiting for transfers between devices: 60 us -> none  [the longest x2 40.1 us: run_expert(): lax.all_to_all(produced.reshape(experts, capacity, D), 'dp', split_axis=0...]
    ppermute x0 -> x41, starting transfers between devices: none -> 55.3 us  [the longest x37 48.6 us: trade(): lax.ppermute(arrays[r], axis, [(i, i ^ r) for i in range(count)])]
    all_to_all x1 -> x0, blocking collectives: 38.9 us -> none  [body(): lax.all_to_all(packed, 'tm', split_axis=0, concat_axis=0, tiled=True)]
    all_to_all x6 -> x0, starting transfers between devices: 25.6 us -> none  [the longest x2 9.47 us: body(): lax.all_to_all(one, 'tm', split_axis=0, concat_axis=0, tiled=True)]
    all_gather x2 -> x0, waiting for transfers between devices: 18.7 us -> none  [the longest x1 18.6 us: body(): lax.all_gather(own_out, 'tm', axis=0, tiled=True, axis_index_groups=groups)]
    unnamed x33 -> x85, local copies, waits for them, and re-layouts: 12.4 us -> 22.8 us
    ppermute x1, waiting for transfers between devices: 8.64 us -> 0.01 us  [body(): received = lax.ppermute(theirs, 'tm', partner)]
  transfers between devices with their start and end apart: 10 -> 43, of which waited for: 7 -> 16; matrix products, arithmetic and copies ran while one was open for 0% -> 2% of each run, Pallas kernels for 20% -> 15%
where the time goes in v4:
time: 262 us
  waiting for transfers between devices  128 us (49%)
  starting transfers between devices  60.4 us (23%)
  Pallas kernels  46.4 us (18%)
  local copies, waits for them, and re-layouts  26.9 us (10%)
    ppermute x37, waiting for transfers between devices, trade(): lax.ppermute(arrays[r], axis, [(i, i ^ r) for i in range(count)])  90 us
    ppermute x37, starting transfers between devices, trade(): lax.ppermute(arrays[r], axis, [(i, i ^ r) for i in range(count)])  48.6 us
    ppermute x4, waiting for transfers between devices, body(): moved = [lax.ppermute(one, 'tm', swap) for one in (early, *late)]  29.5 us
    unnamed x85, local copies, waits for them, and re-layouts  22.8 us
    pallas_call x2, Pallas kernels, run_expert(): pl.pallas_call(functools.partial(expert_kernel, experts, pieces), out_sha...  19.2 us
    pallas_call x2, Pallas kernels, send_frames(): pl.pallas_call(functools.partial(frame_kernel, count, rows, experts, capa...  17.9 us
    ppermute x1, waiting for transfers between devices, body(): partner_routes = lax.ppermute(routes[0], 'tm', partner)  8.29 us
    ppermute x4, starting transfers between devices, body(): moved = [lax.ppermute(one, 'tm', swap) for one in (early, *late)]  6.68 us
  transfers between devices with their start and end apart: 43, of which 16 were waited for; matrix products, arithmetic and copies ran while one was open for 2% of the time, Pallas kernels for 15%

profile of v4, /device:TPU:0, one launch (start us, length us, event | category | flops | bytes accessed | tf_op | source)
XLA Modules:
  0.0 261.8 jit_solution(15270132235805556084)
XLA Ops:
  3.2 4.1 %collective-permute-start.1 = (bf16[3,224,256]{2,1,0:T(8,128)(2,1)S(1)}, bf16[3,224,256]{2,1,0:T(8,128)(2,1)S(1)}, u32[]{:S(2)}, u32[]{:S(2)}) collective-permute-start(bf16[3,224,256]{2,1,0:T(8,128)(2,1)S(1)} %get-tuple-element.58), channel_id=1, source_target_pairs={{0,2},{1,3},{2,0},{3,1},{4,6},{5,7},{6,4},{7,5},{8,10},{9,11},{10,... | collective-permute-start | bytes 1032200 | tf_op jit(solution)/shard_map/ppermute | solution.py:302
  9.0 22.0 %collective-permute-done.1.refs_2_ = bf16[3,224,256]{2,1,0:T(8,128)(2,1)S(1)} collective-permute-done((bf16[3,224,256]{2,1,0:T(8,128)(2,1)S(1)}, bf16[3,224,256]{2,1,0:T(8,128)(2,1)S(1)}, u32[]{:S(2)}, u32[]{:S(2)}) %collective-permute-start.1) | collective-permute-done | bytes 344096 | tf_op jit(solution)/shard_map/ppermute | solution.py:302
  31.6 6.3 %attend.1 = (bf16[256,256]{1,0:T(8,128)(2,1)S(1)}, bf16[256,256]{1,0:T(8,128)(2,1)S(1)}, bf16[256,256]{1,0:T(8,128)(2,1)S(1)}, bf16[256,256]{1,0:T(8,128)(2,1)S(...) custom-call(s32[1]{0:T(128)} %bitcast.me_ref, ...), custom_call_target="tpu_custom_call" | custom-call | flops 1100000000 | tf_op jit(solution)/shard_map/attend/pallas_call | solution.py:355
  39.1 6.8 %collective-permute-start.7 = (bf16[256,256]{1,0:T(8,128)(2,1)S(1)}, bf16[256,256]{1,0:T(8,128)(2,1)S(1)}, u32[]{:S(2)}, u32[]{:S(2)}) collective-permute-start(bf16[256,256]{1,0:T(8,128)(2,1)S(1)} %get-tuple-element.67), channel_id=1, source_target_pairs={{0,1},{1,0},{2,3},{3,2},{4,5},{5,4},{6,7},{7,6},{8,9},{9,8},{10,11... | collective-permute-start | bytes 393224 | tf_op jit(solution)/shard_map/ppermute | solution.py:302
  45.9 1.9 collective-permute-start.8
  49.3 2.0 collective-permute-start.6
  52.2 8.3 %collective-permute-done.6 = s32[224,2]{0,1:T(2,128)S(1)} collective-permute-done((s32[224,2]{0,1:T(2,128)S(1)}, s32[224,2]{0,1:T(2,128)S(1)}, u32[]{:S(2)}, u32[]{:S(2)}) %collective-permute-start.6) | collective-permute-done | bytes 1824 | tf_op jit(solution)/shard_map/ppermute | solution.py:350
  61.2 3.2 %collective-permute-start.5 = (bf16[256,256]{1,0:T(8,128)(2,1)}, bf16[256,256]{1,0:T(8,128)(2,1)}, u32[]{:S(2)}, u32[]{:S(2)}) collective-permute-start(bf16[256,256]{1,0:T(8,128)(2,1)} %get-tuple-element.63), channel_id=1, source_target_pairs={{0,3},{1,2},{2,1},{3,0},{4,7},{5,6},{6,5},{7,4},{8,11},{9,10},{10,... | collective-permute-start | bytes 393224 | tf_op jit(solution)/shard_map/ppermute | solution.py:302
  74.9 9.5 %frames.3 = (bf16[88,1536]{1,0:T(8,128)(2,1)S(1)}, bf16[88,1536]{1,0:T(8,128)(2,1)S(1)}, bf16[88,1536]{1,0:T(8,128)(2,1)S(1)}, bf16[88,1536]{1,0:T(8,128)(2,1)S(...) custom-call(s32[1]{0:T(128)} %bitcast.me_ref, ...), custom_call_target="tpu_custom_call" | custom-call | flops 1100000000 | tf_op jit(solution)/shard_map/frames/pallas_call | solution.py:391
  90.3 2.2 collective-permute-start.17
  94.4 2.2 collective-permute-start.18
  96.6 1.9 collective-permute-done.12.refs_3_
  99.3 2.2 collective-permute-start.19
  104.4 8.3 %collective-permute-done.15.refs_6_ = bf16[88,1536]{1,0:T(8,128)(2,1)S(1)} collective-permute-done((bf16[88,1536]{1,0:T(8,128)(2,1)S(1)}, bf16[88,1536]{1,0:T(8,128)(2,1)S(1)}, u32[]{:S(2)}, u32[]{:S(2)}) %collective-permute-start.15) | collective-permute-done | bytes 270368 | tf_op jit(solution)/shard_map/ppermute | solution.py:302
  119.2 8.4 %frames.2 = (bf16[88,1536]{1,0:T(8,128)(2,1)S(1)}, bf16[88,1536]{1,0:T(8,128)(2,1)S(1)}, bf16[88,1536]{1,0:T(8,128)(2,1)S(1)}, bf16[88,1536]{1,0:T(8,128)(2,1)S(...) custom-call(s32[1]{0:T(128)} %bitcast.me_ref, ...), custom_call_target="tpu_custom_call" | custom-call | flops 1100000000 | tf_op jit(solution)/shard_map/frames/pallas_call | solution.py:391
  127.7 3.3 %collective-permute-start.29 = (bf16[88,1536]{1,0:T(8,128)(2,1)S(1)}, bf16[88,1536]{1,0:T(8,128)(2,1)S(1)}, u32[]{:S(2)}, u32[]{:S(2)}) collective-permute-start(bf16[88,1536]{1,0:T(8,128)(2,1)S(1)} %get-tuple-element.92), channel_id=1, source_target_pairs={{0,4},{4,0},{8,12},{12,8},{16,20},{20,16},{24,28},{28,24},{1,5},{5... | collective-permute-start | bytes 811016 | tf_op jit(solution)/shard_map/ppermute | solution.py:302
  132.0 12.9 %collective-permute-done.19.refs_12_ = bf16[256,1536]{1,0:T(8,128)(2,1)} collective-permute-done((bf16[256,1536]{1,0:T(8,128)(2,1)}, bf16[256,1536]{1,0:T(8,128)(2,1)}, u32[]{:S(2)}, u32[]{:S(2)}) %collective-permute-start.19) | collective-permute-done | bytes 786464 | tf_op jit(solution)/shard_map/ppermute | solution.py:378
  145.0 16.6 %collective-permute-done.20.refs_13_ = bf16[256,1536]{1,0:T(8,128)(2,1)} collective-permute-done((bf16[256,1536]{1,0:T(8,128)(2,1)}, bf16[256,1536]{1,0:T(8,128)(2,1)}, u32[]{:S(2)}, u32[]{:S(2)}) %collective-permute-start.20) | collective-permute-done | bytes 786464 | tf_op jit(solution)/shard_map/ppermute | solution.py:378
  161.6 9.6 %experts.2 = (bf16[88,1536]{1,0:T(8,128)(2,1)S(1)}, bf16[88,1536]{1,0:T(8,128)(2,1)S(1)}, bf16[88,1536]{1,0:T(8,128)(2,1)S(1)}, bf16[88,1536]{1,0:T(8,128)(2,1)S...) custom-call(bf16[88,1536]{1,0:T(8,128)(2,1)S(1)} %copy-done.9, ...), custom_call_target="tpu_custom_call" | custom-call | flops 1100000000 | tf_op jit(solution)/shard_map/experts/pallas_call | solution.py:412
  176.2 4.5 %collective-permute-done.22.refs_2_ = bf16[88,1536]{1,0:T(8,128)(2,1)S(1)} collective-permute-done((bf16[88,1536]{1,0:T(8,128)(2,1)S(1)}, bf16[88,1536]{1,0:T(8,128)(2,1)S(1)}, u32[]{:S(2)}, u32[]{:S(2)}) %collective-permute-start.22) | collective-permute-done | bytes 270368 | tf_op jit(solution)/shard_map/ppermute | solution.py:302
  180.8 4.7 %collective-permute-done.23.refs_3_ = bf16[88,1536]{1,0:T(8,128)(2,1)S(1)} collective-permute-done((bf16[88,1536]{1,0:T(8,128)(2,1)S(1)}, bf16[88,1536]{1,0:T(8,128)(2,1)S(1)}, u32[]{:S(2)}, u32[]{:S(2)}) %collective-permute-start.23) | collective-permute-done | bytes 270368 | tf_op jit(solution)/shard_map/ppermute | solution.py:302
  185.5 2.1 collective-permute-start.31
  188.0 10.9 %collective-permute-done.25.refs_5_ = bf16[88,1536]{1,0:T(8,128)(2,1)S(1)} collective-permute-done((bf16[88,1536]{1,0:T(8,128)(2,1)S(1)}, bf16[88,1536]{1,0:T(8,128)(2,1)S(1)}, u32[]{:S(2)}, u32[]{:S(2)}) %collective-permute-start.25) | collective-permute-done | bytes 270368 | tf_op jit(solution)/shard_map/ppermute | solution.py:302
  198.9 2.2 collective-permute-start.33
  203.6 3.0 %collective-permute-start.28 = (bf16[224,1536]{1,0:T(8,128)(2,1)S(1)}, bf16[224,1536]{1,0:T(8,128)(2,1)S(1)}, u32[]{:S(2)}, u32[]{:S(2)}) collective-permute-start(bf16[224,1536]{1,0:T(8,128)(2,1)S(1)} %theirs.1), channel_id=1, source_target_pairs={{0,2},{1,3},{2,0},{3,1},{4,6},{5,7},{6,4},{7,5},{8,10},{9,11},{10,... | collective-permute-start | bytes 2064392 | tf_op jit(solution)/shard_map/ppermute | solution.py:437
  206.7 10.5 %collective-permute-done.32.refs_4_ = bf16[88,1536]{1,0:T(8,128)(2,1)S(1)} collective-permute-done((bf16[88,1536]{1,0:T(8,128)(2,1)S(1)}, bf16[88,1536]{1,0:T(8,128)(2,1)S(1)}, u32[]{:S(2)}, u32[]{:S(2)}) %collective-permute-start.32) | collective-permute-done | bytes 270368 | tf_op jit(solution)/shard_map/ppermute | solution.py:302
  217.2 4.7 %collective-permute-done.33.refs_5_ = bf16[88,1536]{1,0:T(8,128)(2,1)S(1)} collective-permute-done((bf16[88,1536]{1,0:T(8,128)(2,1)S(1)}, bf16[88,1536]{1,0:T(8,128)(2,1)S(1)}, u32[]{:S(2)}, u32[]{:S(2)}) %collective-permute-start.33) | collective-permute-done | bytes 270368 | tf_op jit(solution)/shard_map/ppermute | solution.py:302
  221.9 9.7 %experts.3 = (bf16[88,1536]{1,0:T(8,128)(2,1)S(1)}, bf16[88,1536]{1,0:T(8,128)(2,1)S(1)}, bf16[88,1536]{1,0:T(8,128)(2,1)S(1)}, bf16[88,1536]{1,0:T(8,128)(2,1)S...) custom-call(bf16[88,1536]{1,0:T(8,128)(2,1)S(1)} %get-tuple-element., ...), custom_call_target="tpu_custom_call" | custom-call | flops 1100000000 | tf_op jit(solution)/shard_map/experts/pallas_call | solution.py:412
  235.8 5.8 %collective-permute-done.37.refs_2_ = bf16[88,1536]{1,0:T(8,128)(2,1)S(1)} collective-permute-done((bf16[88,1536]{1,0:T(8,128)(2,1)S(1)}, bf16[88,1536]{1,0:T(8,128)(2,1)S(1)}, u32[]{:S(2)}, u32[]{:S(2)}) %collective-permute-start.37) | collective-permute-done | bytes 270368 | tf_op jit(solution)/shard_map/ppermute | solution.py:302
  242.9 3.5 %collective-permute-done.38.refs_3_ = bf16[88,1536]{1,0:T(8,128)(2,1)S(1)} collective-permute-done((bf16[88,1536]{1,0:T(8,128)(2,1)S(1)}, bf16[88,1536]{1,0:T(8,128)(2,1)S(1)}, u32[]{:S(2)}, u32[]{:S(2)}) %collective-permute-start.38) | collective-permute-done | bytes 270368 | tf_op jit(solution)/shard_map/ppermute | solution.py:302
  246.4 2.0 collective-permute-start.42
  248.5 11.4 %collective-permute-done.40.refs_5_ = bf16[88,1536]{1,0:T(8,128)(2,1)S(1)} collective-permute-done((bf16[88,1536]{1,0:T(8,128)(2,1)S(1)}, bf16[88,1536]{1,0:T(8,128)(2,1)S(1)}, u32[]{:S(2)}, u32[]{:S(2)}) %collective-permute-start.40) | collective-permute-done | bytes 270368 | tf_op jit(solution)/shard_map/ppermute | solution.py:302
  (153 shorter events, 54.7 us)
Async XLA Ops:
  3.2 27.8 %collective-permute-start.1 = (bf16[3,224,256]{2,1,0:T(8,128)(2,1)S(1)}, bf16[3,224,256]{2,1,0:T(8,128)(2,1)S(1)}, u32[]{:S(2)}, u32[]{:S(2)}) collective-permute-start(bf16[3,224,256]{2,1,0:T(8,128)(2,1)S(1)} %get-tuple-element.58), channel_id=1, source_target_pairs={{0,2},{1,3},{2,0},{3,1},{4,6},{5,7},{6,4},{7,5},{8,10},{9,11},{10,... | collective-permute-start | bytes 1032200 | tf_op jit(solution)/shard_map/ppermute | solution.py:302
  7.3 23.7 %collective-permute-start.2 = (bf16[3,224,256]{2,1,0:T(8,128)(2,1)S(1)}, bf16[3,224,256]{2,1,0:T(8,128)(2,1)S(1)}, u32[]{:S(2)}, u32[]{:S(2)}) collective-permute-start(bf16[3,224,256]{2,1,0:T(8,128)(2,1)S(1)} %get-tuple-element.59), channel_id=1, source_target_pairs={{0,3},{1,2},{2,1},{3,0},{4,7},{5,6},{6,5},{7,4},{8,11},{9,10},{10,... | collective-permute-start | bytes 1032200 | tf_op jit(solution)/shard_map/ppermute | solution.py:302
  8.7 22.8 %collective-permute-start = (bf16[3,224,256]{2,1,0:T(8,128)(2,1)S(1)}, bf16[3,224,256]{2,1,0:T(8,128)(2,1)S(1)}, u32[]{:S(2)}, u32[]{:S(2)}) collective-permute-start(bf16[3,224,256]{2,1,0:T(8,128)(2,1)S(1)} %get-tuple-element.57), channel_id=1, source_target_pairs={{0,1},{1,0},{2,3},{3,2},{4,5},{5,4},{6,7},{7,6},{8,9},{9,8},{10,11... | collective-permute-start | bytes 1032200 | tf_op jit(solution)/shard_map/ppermute | solution.py:302
  39.1 21.4 %collective-permute-start.7 = (bf16[256,256]{1,0:T(8,128)(2,1)S(1)}, bf16[256,256]{1,0:T(8,128)(2,1)S(1)}, u32[]{:S(2)}, u32[]{:S(2)}) collective-permute-start(bf16[256,256]{1,0:T(8,128)(2,1)S(1)} %get-tuple-element.67), channel_id=1, source_target_pairs={{0,1},{1,0},{2,3},{3,2},{4,5},{5,4},{6,7},{7,6},{8,9},{9,8},{10,11... | collective-permute-start | bytes 393224 | tf_op jit(solution)/shard_map/ppermute | solution.py:302
  45.9 20.3 %collective-permute-start.8 = (bf16[256,256]{1,0:T(8,128)(2,1)S(1)}, bf16[256,256]{1,0:T(8,128)(2,1)S(1)}, u32[]{:S(2)}, u32[]{:S(2)}) collective-permute-start(bf16[256,256]{1,0:T(8,128)(2,1)S(1)} %get-tuple-element.68), channel_id=1, source_target_pairs={{0,2},{1,3},{2,0},{3,1},{4,6},{5,7},{6,4},{7,5},{8,10},{9,11},{10,... | collective-permute-start | bytes 393224 | tf_op jit(solution)/shard_map/ppermute | solution.py:302
  47.8 19.0 %collective-permute-start.9 = (bf16[256,256]{1,0:T(8,128)(2,1)S(1)}, bf16[256,256]{1,0:T(8,128)(2,1)S(1)}, u32[]{:S(2)}, u32[]{:S(2)}) collective-permute-start(bf16[256,256]{1,0:T(8,128)(2,1)S(1)} %get-tuple-element.69), channel_id=1, source_target_pairs={{0,3},{1,2},{2,1},{3,0},{4,7},{5,6},{6,5},{7,4},{8,11},{9,10},{10,... | collective-permute-start | bytes 393224 | tf_op jit(solution)/shard_map/ppermute | solution.py:302
  51.3 33.7 %collective-permute-start.3 = (bf16[256,256]{1,0:T(8,128)(2,1)}, bf16[256,256]{1,0:T(8,128)(2,1)}, u32[]{:S(2)}, u32[]{:S(2)}) collective-permute-start(bf16[256,256]{1,0:T(8,128)(2,1)} %get-tuple-element.61), channel_id=1, source_target_pairs={{0,1},{1,0},{2,3},{3,2},{4,5},{5,4},{6,7},{7,6},{8,9},{9,8},{10,11... | collective-permute-start | bytes 393224 | tf_op jit(solution)/shard_map/ppermute | solution.py:302
  60.5 25.7 %collective-permute-start.4 = (bf16[256,256]{1,0:T(8,128)(2,1)}, bf16[256,256]{1,0:T(8,128)(2,1)}, u32[]{:S(2)}, u32[]{:S(2)}) collective-permute-start(bf16[256,256]{1,0:T(8,128)(2,1)} %get-tuple-element.62), channel_id=1, source_target_pairs={{0,2},{1,3},{2,0},{3,1},{4,6},{5,7},{6,4},{7,5},{8,10},{9,11},{10,... | collective-permute-start | bytes 393224 | tf_op jit(solution)/shard_map/ppermute | solution.py:302
  61.2 25.7 %collective-permute-start.5 = (bf16[256,256]{1,0:T(8,128)(2,1)}, bf16[256,256]{1,0:T(8,128)(2,1)}, u32[]{:S(2)}, u32[]{:S(2)}) collective-permute-start(bf16[256,256]{1,0:T(8,128)(2,1)} %get-tuple-element.63), channel_id=1, source_target_pairs={{0,3},{1,2},{2,1},{3,0},{4,7},{5,6},{6,5},{7,4},{8,11},{9,10},{10,... | collective-permute-start | bytes 393224 | tf_op jit(solution)/shard_map/ppermute | solution.py:302
  85.1 13.5 %collective-permute-start.12 = (bf16[88,1536]{1,0:T(8,128)(2,1)S(1)}, bf16[88,1536]{1,0:T(8,128)(2,1)S(1)}, u32[]{:S(2)}, u32[]{:S(2)}) collective-permute-start(bf16[88,1536]{1,0:T(8,128)(2,1)S(1)} %get-tuple-element.74), channel_id=1, source_target_pairs={{0,12},{4,8},{8,4},{12,0},{16,28},{20,24},{24,20},{28,16},{1,13},{... | collective-permute-start | bytes 811016 | tf_op jit(solution)/shard_map/ppermute | solution.py:302
  86.2 15.3 %collective-permute-start.13 = (bf16[88,1536]{1,0:T(8,128)(2,1)S(1)}, bf16[88,1536]{1,0:T(8,128)(2,1)S(1)}, u32[]{:S(2)}, u32[]{:S(2)}) collective-permute-start(bf16[88,1536]{1,0:T(8,128)(2,1)S(1)} %get-tuple-element.75), channel_id=1, source_target_pairs={{0,16},{4,20},{8,24},{12,28},{16,0},{20,4},{24,8},{28,12},{1,17},{... | collective-permute-start | bytes 811016 | tf_op jit(solution)/shard_map/ppermute | solution.py:302
  86.9 15.4 %collective-permute-start.14 = (bf16[88,1536]{1,0:T(8,128)(2,1)S(1)}, bf16[88,1536]{1,0:T(8,128)(2,1)S(1)}, u32[]{:S(2)}, u32[]{:S(2)}) collective-permute-start(bf16[88,1536]{1,0:T(8,128)(2,1)S(1)} %get-tuple-element.76), channel_id=1, source_target_pairs={{0,20},{4,16},{8,28},{12,24},{16,4},{20,0},{24,12},{28,8},{1,21},{... | collective-permute-start | bytes 811016 | tf_op jit(solution)/shard_map/ppermute | solution.py:302
  90.3 40.7 %collective-permute-start.17 = (bf16[256,1536]{1,0:T(8,128)(2,1)}, bf16[256,1536]{1,0:T(8,128)(2,1)}, u32[]{:S(2)}, u32[]{:S(2)}) collective-permute-start(bf16[256,1536]{1,0:T(8,128)(2,1)} %get-tuple-element.79), channel_id=1, source_target_pairs={{0,1},{1,0},{2,3},{3,2},{4,5},{5,4},{6,7},{7,6},{8,9},{9,8},{10,11... | collective-permute-start | bytes 2359304 | tf_op jit(solution)/shard_map/ppermute | solution.py:378
  94.4 37.6 %collective-permute-start.18 = (bf16[256,1536]{1,0:T(8,128)(2,1)}, bf16[256,1536]{1,0:T(8,128)(2,1)}, u32[]{:S(2)}, u32[]{:S(2)}) collective-permute-start(bf16[256,1536]{1,0:T(8,128)(2,1)} %get-tuple-element.80), channel_id=1, source_target_pairs={{0,1},{1,0},{2,3},{3,2},{4,5},{5,4},{6,7},{7,6},{8,9},{9,8},{10,11... | collective-permute-start | bytes 2359304 | tf_op jit(solution)/shard_map/ppermute | solution.py:378
  99.3 45.7 %collective-permute-start.19 = (bf16[256,1536]{1,0:T(8,128)(2,1)}, bf16[256,1536]{1,0:T(8,128)(2,1)}, u32[]{:S(2)}, u32[]{:S(2)}) collective-permute-start(bf16[256,1536]{1,0:T(8,128)(2,1)} %get-tuple-element.81), channel_id=1, source_target_pairs={{0,1},{1,0},{2,3},{3,2},{4,5},{5,4},{6,7},{7,6},{8,9},{9,8},{10,11... | collective-permute-start | bytes 2359304 | tf_op jit(solution)/shard_map/ppermute | solution.py:378
  102.2 59.3 %collective-permute-start.20 = (bf16[256,1536]{1,0:T(8,128)(2,1)}, bf16[256,1536]{1,0:T(8,128)(2,1)}, u32[]{:S(2)}, u32[]{:S(2)}) collective-permute-start(bf16[256,1536]{1,0:T(8,128)(2,1)} %get-tuple-element.82), channel_id=1, source_target_pairs={{0,1},{1,0},{2,3},{3,2},{4,5},{5,4},{6,7},{7,6},{8,9},{9,8},{10,11... | collective-permute-start | bytes 2359304 | tf_op jit(solution)/shard_map/ppermute | solution.py:378
  113.4 14.3 %collective-permute-start.16 = (bf16[88,1536]{1,0:T(8,128)(2,1)}, bf16[88,1536]{1,0:T(8,128)(2,1)}, u32[]{:S(2)}, u32[]{:S(2)}) collective-permute-start(bf16[88,1536]{1,0:T(8,128)(2,1)} %get-tuple-element.78), channel_id=1, source_target_pairs={{0,28},{4,24},{8,20},{12,16},{16,12},{20,8},{24,4},{28,0},{1,29},{... | collective-permute-start | bytes 811016 | tf_op jit(solution)/shard_map/ppermute | solution.py:302
  127.7 45.5 %collective-permute-start.29 = (bf16[88,1536]{1,0:T(8,128)(2,1)S(1)}, bf16[88,1536]{1,0:T(8,128)(2,1)S(1)}, u32[]{:S(2)}, u32[]{:S(2)}) collective-permute-start(bf16[88,1536]{1,0:T(8,128)(2,1)S(1)} %get-tuple-element.92), channel_id=1, source_target_pairs={{0,4},{4,0},{8,12},{12,8},{16,20},{20,16},{24,28},{28,24},{1,5},{5... | collective-permute-start | bytes 811016 | tf_op jit(solution)/shard_map/ppermute | solution.py:302
  131.0 43.7 %collective-permute-start.30 = (bf16[88,1536]{1,0:T(8,128)(2,1)S(1)}, bf16[88,1536]{1,0:T(8,128)(2,1)S(1)}, u32[]{:S(2)}, u32[]{:S(2)}) collective-permute-start(bf16[88,1536]{1,0:T(8,128)(2,1)S(1)} %get-tuple-element.93), channel_id=1, source_target_pairs={{0,8},{4,12},{8,0},{12,4},{16,24},{20,28},{24,16},{28,20},{1,9},{5... | collective-permute-start | bytes 811016 | tf_op jit(solution)/shard_map/ppermute | solution.py:302
  173.1 14.5 %collective-permute-start.24 = (bf16[88,1536]{1,0:T(8,128)(2,1)S(1)}, bf16[88,1536]{1,0:T(8,128)(2,1)S(1)}, u32[]{:S(2)}, u32[]{:S(2)}) collective-permute-start(bf16[88,1536]{1,0:T(8,128)(2,1)S(1)} %get-tuple-element.87), channel_id=1, source_target_pairs={{0,16},{4,20},{8,24},{12,28},{16,0},{20,4},{24,8},{28,12},{1,17},{... | collective-permute-start | bytes 811016 | tf_op jit(solution)/shard_map/ppermute | solution.py:302
  174.7 24.2 %collective-permute-start.25 = (bf16[88,1536]{1,0:T(8,128)(2,1)S(1)}, bf16[88,1536]{1,0:T(8,128)(2,1)S(1)}, u32[]{:S(2)}, u32[]{:S(2)}) collective-permute-start(bf16[88,1536]{1,0:T(8,128)(2,1)S(1)} %get-tuple-element.88), channel_id=1, source_target_pairs={{0,20},{4,16},{8,28},{12,24},{16,4},{20,0},{24,12},{28,8},{1,21},{... | collective-permute-start | bytes 811016 | tf_op jit(solution)/shard_map/ppermute | solution.py:302
  174.8 26.3 %collective-permute-start.26 = (bf16[88,1536]{1,0:T(8,128)(2,1)S(1)}, bf16[88,1536]{1,0:T(8,128)(2,1)S(1)}, u32[]{:S(2)}, u32[]{:S(2)}) collective-permute-start(bf16[88,1536]{1,0:T(8,128)(2,1)S(1)} %get-tuple-element.89), channel_id=1, source_target_pairs={{0,24},{4,28},{8,16},{12,20},{16,8},{20,12},{24,0},{28,4},{1,25},{... | collective-permute-start | bytes 811016 | tf_op jit(solution)/shard_map/ppermute | solution.py:302
  180.6 21.9 %collective-permute-start.27 = (bf16[88,1536]{1,0:T(8,128)(2,1)S(1)}, bf16[88,1536]{1,0:T(8,128)(2,1)S(1)}, u32[]{:S(2)}, u32[]{:S(2)}) collective-permute-start(bf16[88,1536]{1,0:T(8,128)(2,1)S(1)} %get-tuple-element.90), channel_id=1, source_target_pairs={{0,28},{4,24},{8,20},{12,16},{16,12},{20,8},{24,4},{28,0},{1,29},{... | collective-permute-start | bytes 811016 | tf_op jit(solution)/shard_map/ppermute | solution.py:302
  185.5 18.1 %collective-permute-start.31 = (bf16[88,1536]{1,0:T(8,128)(2,1)S(1)}, bf16[88,1536]{1,0:T(8,128)(2,1)S(1)}, u32[]{:S(2)}, u32[]{:S(2)}) collective-permute-start(bf16[88,1536]{1,0:T(8,128)(2,1)S(1)} %get-tuple-element.94), channel_id=1, source_target_pairs={{0,12},{4,8},{8,4},{12,0},{16,28},{20,24},{24,20},{28,16},{1,13},{... | collective-permute-start | bytes 811016 | tf_op jit(solution)/shard_map/ppermute | solution.py:302
  187.6 29.6 %collective-permute-start.32 = (bf16[88,1536]{1,0:T(8,128)(2,1)S(1)}, bf16[88,1536]{1,0:T(8,128)(2,1)S(1)}, u32[]{:S(2)}, u32[]{:S(2)}) collective-permute-start(bf16[88,1536]{1,0:T(8,128)(2,1)S(1)} %get-tuple-element.95), channel_id=1, source_target_pairs={{0,16},{4,20},{8,24},{12,28},{16,0},{20,4},{24,8},{28,12},{1,17},{... | collective-permute-start | bytes 811016 | tf_op jit(solution)/shard_map/ppermute | solution.py:302
  198.9 22.9 %collective-permute-start.33 = (bf16[88,1536]{1,0:T(8,128)(2,1)S(1)}, bf16[88,1536]{1,0:T(8,128)(2,1)S(1)}, u32[]{:S(2)}, u32[]{:S(2)}) collective-permute-start(bf16[88,1536]{1,0:T(8,128)(2,1)S(1)} %get-tuple-element.96), channel_id=1, source_target_pairs={{0,20},{4,16},{8,28},{12,24},{16,4},{20,0},{24,12},{28,8},{1,21},{... | collective-permute-start | bytes 811016 | tf_op jit(solution)/shard_map/ppermute | solution.py:302
  201.1 20.7 %collective-permute-start.34 = (bf16[88,1536]{1,0:T(8,128)(2,1)S(1)}, bf16[88,1536]{1,0:T(8,128)(2,1)S(1)}, u32[]{:S(2)}, u32[]{:S(2)}) collective-permute-start(bf16[88,1536]{1,0:T(8,128)(2,1)S(1)} %get-tuple-element.97), channel_id=1, source_target_pairs={{0,24},{4,28},{8,16},{12,20},{16,8},{20,12},{24,0},{28,4},{1,25},{... | collective-permute-start | bytes 811016 | tf_op jit(solution)/shard_map/ppermute | solution.py:302
  202.5 19.4 %collective-permute-start.35 = (bf16[88,1536]{1,0:T(8,128)(2,1)S(1)}, bf16[88,1536]{1,0:T(8,128)(2,1)S(1)}, u32[]{:S(2)}, u32[]{:S(2)}) collective-permute-start(bf16[88,1536]{1,0:T(8,128)(2,1)S(1)} %get-tuple-element.98), channel_id=1, source_target_pairs={{0,28},{4,24},{8,20},{12,16},{16,12},{20,8},{24,4},{28,0},{1,29},{... | collective-permute-start | bytes 811016 | tf_op jit(solution)/shard_map/ppermute | solution.py:302
  203.6 56.2 %collective-permute-start.28 = (bf16[224,1536]{1,0:T(8,128)(2,1)S(1)}, bf16[224,1536]{1,0:T(8,128)(2,1)S(1)}, u32[]{:S(2)}, u32[]{:S(2)}) collective-permute-start(bf16[224,1536]{1,0:T(8,128)(2,1)S(1)} %theirs.1), channel_id=1, source_target_pairs={{0,2},{1,3},{2,0},{3,1},{4,6},{5,7},{6,4},{7,5},{8,10},{9,11},{10,... | collective-permute-start | bytes 2064392 | tf_op jit(solution)/shard_map/ppermute | solution.py:437
  233.8 14.7 %collective-permute-start.39 = (bf16[88,1536]{1,0:T(8,128)(2,1)S(1)}, bf16[88,1536]{1,0:T(8,128)(2,1)S(1)}, u32[]{:S(2)}, u32[]{:S(2)}) collective-permute-start(bf16[88,1536]{1,0:T(8,128)(2,1)S(1)} %get-tuple-element.103), channel_id=1, source_target_pairs={{0,16},{4,20},{8,24},{12,28},{16,0},{20,4},{24,8},{28,12},{1,17},{... | collective-permute-start | bytes 811016 | tf_op jit(solution)/shard_map/ppermute | solution.py:302
  235.3 24.6 %collective-permute-start.40 = (bf16[88,1536]{1,0:T(8,128)(2,1)S(1)}, bf16[88,1536]{1,0:T(8,128)(2,1)S(1)}, u32[]{:S(2)}, u32[]{:S(2)}) collective-permute-start(bf16[88,1536]{1,0:T(8,128)(2,1)S(1)} %get-tuple-element.104), channel_id=1, source_target_pairs={{0,20},{4,16},{8,28},{12,24},{16,4},{20,0},{24,12},{28,8},{1,21},{... | collective-permute-start | bytes 811016 | tf_op jit(solution)/shard_map/ppermute | solution.py:302
  241.6 18.2 %collective-permute-start.41 = (bf16[88,1536]{1,0:T(8,128)(2,1)S(1)}, bf16[88,1536]{1,0:T(8,128)(2,1)S(1)}, u32[]{:S(2)}, u32[]{:S(2)}) collective-permute-start(bf16[88,1536]{1,0:T(8,128)(2,1)S(1)} %get-tuple-element.105), channel_id=1, source_target_pairs={{0,24},{4,28},{8,16},{12,20},{16,8},{20,12},{24,0},{28,4},{1,25},{... | collective-permute-start | bytes 811016 | tf_op jit(solution)/shard_map/ppermute | solution.py:302
  (53 other events, 615.9 us)

commit v5 on v4

--- a/solution.py
+++ b/solution.py
@@ -51,15 +51,24 @@
     return lifted * factor
 
 
-def pack_kernel(place, q_ref, k_ref, v_ref, me_ref, *o_refs):
+def pack_kernel(place, me_ref, q_ref, k_ref, v_ref, *refs):
+    o_refs, sem_ref = refs[:-1], refs[-1]
     width = o_refs[0].shape[2]
-    for r, o_ref in enumerate(o_refs):
+    copies = []
+    for r in range(len(o_refs) - 1, -1, -1):
         target = place(me_ref[0], r)
         for which, ref in enumerate((q_ref, k_ref, v_ref)):
-            if isinstance(target, int):
-                o_ref[which] = ref[:, target * width : (target + 1) * width]
+            if width % LANES == 0:
+                columns = pl.ds(pl.multiple_of(target * width, LANES), width)
+                copy = pltpu.make_async_copy(
+                    ref.at[:, columns], o_refs[r].at[which], sem_ref.at[r * 3 + which]
+                )
+                copy.start()
+                copies.append(copy)
             else:
-                o_ref[which] = ref[:, pl.ds(pl.multiple_of(target * width, LANES), width)]
+                o_refs[r][which] = ref[:, target * width : (target + 1) * width]
+    for copy in copies:
+        copy.wait()
 
 
 def attend_kernel(count, rows, heads, place, me_ref, scale_ref, len_ref, *refs):
@@ -147,9 +156,10 @@
     turned_ref,
     *refs,
 ):
-    att_refs, out_refs = refs[:count], refs[count : count + experts]
-    info_ref, second_ref, x_ref, first_ref, lab_ref = refs[count + experts :]
+    att_refs, out_refs = refs[:count], refs[count:-5]
+    info_ref, second_ref, x_ref, first_ref, lab_ref = refs[-5:]
     me = me_ref[0]
+    turn = expert_ref[0] if len(out_refs) > 1 else 0
     width = att_refs[0].shape[1]
     window = rows + 2 * HALO
     half = (KERNEL - 1) // 2
@@ -220,60 +230,60 @@
     info = jnp.zeros((rows, LANES), F32)
     for pick in range(TOPK):
         rank = jnp.sum(jnp.where(named[pick], ranks, 0.0), axis=1, keepdims=True)
-        place_of = routes_ref[:, pick : pick + 1] ^ expert_ref[0]
+        place_of = routes_ref[:, pick : pick + 1] ^ turn
         slot = rank + (place_of * capacity).astype(F32)
         info = jnp.where(column == pick, slot, info)
         info = jnp.where(column == TOPK + pick, raised[pick] / mass, info)
     info_ref[...] = info
 
-    expert = lax.broadcasted_iota(jnp.int32, (experts, rows), 0) ^ expert_ref[0]
+    expert = lax.broadcasted_iota(jnp.int32, (experts, rows), 0) ^ turn
     chosen = (expert == turned_ref[0:1, :]) | (expert == turned_ref[1:2, :])
     later = jnp.where(down < across, 1.0, 0.0).astype(BF16)
     order = jnp.dot(jnp.where(chosen, 1.0, 0.0).astype(BF16), later, preferred_element_type=F32)
     order = jnp.where(chosen, order, -1.0)
     slot = lax.broadcasted_iota(jnp.int32, (capacity, rows), 0).astype(F32)
-    for e in range(0, experts, 2):
-        select = jnp.concatenate(
-            [jnp.where(slot == order[e + k : e + k + 1, :], 1.0, 0.0) for k in range(2)], axis=0
-        ).astype(BF16)
-        moved = jnp.dot(select, mixed, preferred_element_type=F32)
-        out_refs[e][...] = moved[0:capacity].astype(BF16)
-        out_refs[e + 1][...] = moved[capacity:].astype(BF16)
-
-
-def joined(left_ref, right_ref):
-    both = [left_ref[...].astype(F32), right_ref[...].astype(F32)]
-    return jnp.concatenate(both, axis=0).astype(BF16)
-
-
-def expert_kernel(experts, pieces, *refs):
-    x_refs, refs = refs[:experts], refs[experts:]
-    ins, outs, o_refs = refs[:pieces], refs[pieces : 2 * pieces], refs[2 * pieces :]
-    capacity = x_refs[0].shape[0]
-    for e in range(0, experts, 2):
-        tokens = joined(x_refs[e], x_refs[e + 1])
-        total = jnp.zeros((2 * capacity, D), F32)
-        for piece_in, piece_out in zip(ins, outs):
-            raw = lax.dot_general(
-                tokens, piece_in[...], (((1,), (1,)), ((), ())), preferred_element_type=F32
-            )
-            hidden = (raw / (1.0 + jnp.exp(-raw))).astype(BF16)
-            total = total + jnp.dot(hidden, piece_out[...], preferred_element_type=F32)
-        o_refs[e][...] = total[0:capacity].astype(BF16)
-        o_refs[e + 1][...] = total[capacity:].astype(BF16)
+    select = jnp.concatenate(
+        [jnp.where(slot == order[e : e + 1, :], 1.0, 0.0) for e in range(experts)], axis=0
+    ).astype(BF16)
+    scatter(out_refs, jnp.dot(select, mixed, preferred_element_type=F32))
+
+
+def joined(refs):
+    if len(refs) == 1:
+        return refs[0][...]
+    return jnp.concatenate([ref[...].astype(F32) for ref in refs], axis=0).astype(BF16)
+
+
+def scatter(refs, values):
+    tall = values.shape[0] // len(refs)
+    for e, ref in enumerate(refs):
+        ref[...] = values[e * tall : (e + 1) * tall].astype(BF16)
+
+
+def expert_kernel(chunks, me_ref, in_ref, *refs):
+    x_refs, out_refs, o_refs = refs[:chunks], refs[chunks:-chunks], refs[-chunks:]
+    tokens = joined(x_refs)
+    total = jnp.zeros((tokens.shape[0], D), F32)
+    units = out_refs[0].shape[0]
+    for place, out_ref in enumerate(out_refs):
+        begin = 0 if len(out_refs) == 1 else pl.multiple_of(((me_ref[0] & 1) ^ place) * units, 16)
+        raw = lax.dot_general(
+            tokens,
+            in_ref[pl.ds(begin, units), :],
+            (((1,), (1,)), ((), ())),
+            preferred_element_type=F32,
+        )
+        hidden = (raw / (1.0 + jnp.exp(-raw))).astype(BF16)
+        total = total + jnp.dot(hidden, out_ref[...], preferred_element_type=F32)
+    scatter(o_refs, total)
 
 
 def mixture_of(info, back_refs):
-    capacity = back_refs[0].shape[0]
-    total = jnp.zeros((info.shape[0], D), F32)
-    column = lax.broadcasted_iota(jnp.int32, (info.shape[0], 2 * capacity), 1).astype(F32)
-    for e in range(0, len(back_refs), 2):
-        spread = jnp.where(column == info[:, 0:1] - e * capacity, info[:, 2:3], 0.0)
-        spread = jnp.where(column == info[:, 1:2] - e * capacity, info[:, 3:4], spread)
-        total = total + jnp.dot(
-            spread.astype(BF16), joined(back_refs[e], back_refs[e + 1]), preferred_element_type=F32
-        )
-    return total
+    back = joined(back_refs)
+    column = lax.broadcasted_iota(jnp.int32, (info.shape[0], back.shape[0]), 1).astype(F32)
+    spread = jnp.where(column == info[:, 0:1], info[:, 2:3], 0.0)
+    spread = jnp.where(column == info[:, 1:2], info[:, 3:4], spread).astype(BF16)
+    return jnp.dot(spread, back, preferred_element_type=F32)
 
 
 def theirs_kernel(info_ref, *refs):
@@ -339,12 +349,13 @@
     packed = pl.pallas_call(
         functools.partial(pack_kernel, place),
         out_shape=(jax.ShapeDtypeStruct((3, rows, width), BF16),) * count,
-        in_specs=[VMEM, VMEM, VMEM, SMEM],
+        in_specs=[SMEM] + [pl.BlockSpec(memory_space=pltpu.HBM) if direct else VMEM] * 3,
         out_specs=(VMEM,) * count,
-        compiler_params=params(16),
+        scratch_shapes=[pltpu.SemaphoreType.DMA((3 * count,))],
+        compiler_params=params(60),
         cost_estimate=cost(1),
         name="pack",
-    )(query_rows[0], key_rows[0], value_rows[0], me)
+    )(me, query_rows[0], key_rows[0], value_rows[0])
     arrived = trade(packed, "tm", direct)
     scales = lax.dynamic_slice_in_dim(head_scale, me[0] * heads, heads)
     partner_routes = lax.ppermute(routes[0], "tm", partner)
@@ -362,75 +373,89 @@
             pltpu.VMEM((tiles, total, 2 * LANES), BF16),
             pltpu.VMEM((total + 2 * HALO, width), BF16),
         ],
-        compiler_params=params(32),
-        cost_estimate=cost(1),
+        compiler_params=params(16),
+        cost_estimate=cost(6),
         name="attend",
     )(me, scales, lengths, *arrived)
     gathered_a = trade(attended[:count], "tm", direct)
     gathered_b = trade(attended[count:], "tm", direct)
 
+    groups = [list(range(i, i + half)) for i in (0, half)]
+    (early,) = tied((expert_in[0],), arrived[-1])
+    (late,) = tied((expert_out[0],), gathered_a[-1])
+    ins = lax.all_gather(early, "tm", axis=0, tiled=True, axis_index_groups=groups)
     if half == 2:
-        swap = [(i, i ^ 1) for i in range(count)]
-        units = expert_in.shape[1]
-        cut = units // 2
-        (early,) = tied((expert_in[0, :cut],), packed[1])
-        late = tied((expert_in[0, cut:], expert_out[0, :cut], expert_out[0, cut:]), gathered_a[-1])
-        moved = [lax.ppermute(one, "tm", swap) for one in (early, *late)]
-        ins = [expert_in[0], moved[0], moved[1]]
-        outs = [expert_out[0], moved[2], moved[3]]
+        outs = [late, lax.ppermute(late, "tm", [(i, i ^ 1) for i in range(count)])]
     else:
-        groups = [list(range(half)), list(range(half, count))]
-        ins = [lax.all_gather(expert_in[0], "tm", axis=0, tiled=True, axis_index_groups=groups)]
-        outs = [lax.all_gather(expert_out[0], "tm", axis=0, tiled=True, axis_index_groups=groups)]
+        outs = [lax.all_gather(late, "tm", axis=0, tiled=True, axis_index_groups=groups)]
 
     taps = jnp.transpose(conv_taps.reshape(KERNEL, D // LANES, LANES), (1, 0, 2))
-    pieces = len(ins)
-    chunk = jax.ShapeDtypeStruct((capacity, D), BF16)
-
-    def send_frames(windows, flip, block_routes):
+    slots = experts * capacity
+
+    def chunks_of(split):
+        if split:
+            return (jax.ShapeDtypeStruct((capacity, D), BF16),) * experts
+        return (jax.ShapeDtypeStruct((slots, D), BF16),)
+
+    def route(arrays):
+        if len(arrays) > 1:
+            return trade(arrays, "dp")
+        whole = arrays[0].reshape(experts, capacity, D)
+        moved = lax.all_to_all(whole, "dp", split_axis=0, concat_axis=0, tiled=True)
+        return [moved.reshape(slots, D)]
+
+    def send_frames(windows, flip, split, block_routes):
+        chunks = chunks_of(split)
         made = pl.pallas_call(
             functools.partial(frame_kernel, count, rows, experts, capacity, place, flip),
-            out_shape=(chunk,) * experts
+            out_shape=chunks
             + (
                 jax.ShapeDtypeStruct((rows, LANES), F32),
                 jax.ShapeDtypeStruct((D // LANES, rows, LANES), F32),
             ),
             in_specs=[SMEM, SMEM, SMEM] + [VMEM] * (5 + count),
-            out_specs=(VMEM,) * (experts + 2),
+            out_specs=(VMEM,) * (len(chunks) + 2),
             scratch_shapes=[
                 pltpu.VMEM((D // LANES, window, LANES), F32),
                 pltpu.VMEM((D // LANES, rows, LANES), F32),
                 pltpu.VMEM((window, LANES), F32),
             ],
-            compiler_params=params(32),
-            cost_estimate=cost(1),
+            compiler_params=params(24),
+            cost_estimate=cost(10),
             name="frames",
         )(me, expert, lengths, out_proj, taps, router, block_routes, block_routes.T, *windows)
-        return trade(made[:experts], "dp"), made[experts], made[experts + 1]
+        return made[:-2], made[-2], made[-1]
 
     def run_expert(tokens):
+        split = len(tokens) > 1
+        chunks = chunks_of(split)
         produced = pl.pallas_call(
-            functools.partial(expert_kernel, experts, pieces),
-            out_shape=(chunk,) * experts,
-            in_specs=[VMEM] * (experts + 2 * pieces),
-            out_specs=(VMEM,) * experts,
-            compiler_params=params(32),
-            cost_estimate=cost(1),
+            functools.partial(expert_kernel, len(tokens)),
+            out_shape=chunks,
+            in_specs=[SMEM] + [VMEM] * (1 + len(tokens) + len(outs)),
+            out_specs=(VMEM,) * len(chunks),
+            compiler_params=params(24),
+            cost_estimate=cost(8),
             name="experts",
-        )(*tokens, *ins, *outs)
-        return trade(produced, "dp")
-
-    tokens_a, info_a, _ = send_frames(gathered_a, half, partner_routes)
-    tokens_b, info_b, second = send_frames(gathered_b, 0, routes[0])
-    back_a = run_expert(tokens_a)
-    back_b = run_expert(tokens_b)
+        )(me, ins, *tokens, *outs)
+        return produced
+
+    outgoing_a, info_a, _ = send_frames(gathered_a, half, False, partner_routes)
+    tokens_a = route(outgoing_a)
+    gathered_b = tied(gathered_b, outgoing_a[0])
+    outgoing_b, info_b, second = send_frames(gathered_b, 0, True, routes[0])
+    tokens_b = route(outgoing_b)
+    produced_a = run_expert(tokens_a)
+    back_a = route(produced_a)
+    tokens_b = tied(tokens_b, produced_a[0])
+    back_b = route(run_expert(tokens_b))
 
     theirs = pl.pallas_call(
         theirs_kernel,
         out_shape=jax.ShapeDtypeStruct((rows, D), BF16),
-        in_specs=[VMEM] * (1 + experts),
+        in_specs=[VMEM] * (1 + len(back_a)),
         out_specs=VMEM,
-        compiler_params=params(24),
+        compiler_params=params(16),
         cost_estimate=cost(1),
         name="theirs",
     )(info_a, *back_a)
@@ -438,9 +463,9 @@
     out = pl.pallas_call(
         mine_kernel,
         out_shape=jax.ShapeDtypeStruct((rows, D), BF16),
-        in_specs=[VMEM] * (3 + experts),
+        in_specs=[VMEM] * (3 + len(back_b)),
         out_specs=VMEM,
-        compiler_params=params(24),
+        compiler_params=params(16),
         cost_estimate=cost(1),
         name="mine",
     )(info_b, second, received, *back_b)

time: 262 us -> 262 us (level)
  starting transfers between devices: 60.4 us -> 42.6 us
  between operations: 0.25 us -> 13.7 us
  local copies, waits for them, and re-layouts: 26.9 us -> 40.1 us
  Pallas kernels: 46.4 us -> 38.3 us
    ppermute x37 -> x23, starting transfers between devices: 48.6 us -> 31.4 us  [trade(): lax.ppermute(arrays[r], axis, [(i, i ^ r) for i in range(count)])]
    unnamed x85 -> x111, local copies, waits for them, and re-layouts: 22.8 us -> 39 us
    ppermute x37 -> x23, waiting for transfers between devices: 90 us -> 78.6 us  [trade(): lax.ppermute(arrays[r], axis, [(i, i ^ r) for i in range(count)])]
    pallas_call x2, Pallas kernels: 19.2 us -> 9.87 us  [run_expert(): pl.pallas_call(functools.partial(expert_kernel, len(tokens)), out_shape=c...]
    all_to_all x0 -> x2, starting transfers between devices: none -> 7.76 us  [route(): moved = lax.all_to_all(whole, 'dp', split_axis=0, concat_axis=0, tiled=True)]
    ppermute x4 -> x1, waiting for transfers between devices: 29.5 us -> 35.3 us  [body(): outs = [late, lax.ppermute(late, 'tm', [(i, i ^ 1) for i in range(count)])]]
    ppermute x1, waiting for transfers between devices: 8.29 us -> 12.5 us  [body(): partner_routes = lax.ppermute(routes[0], 'tm', partner)]
    ppermute x4 -> x1, starting transfers between devices: 6.68 us -> 3.3 us  [body(): outs = [late, lax.ppermute(late, 'tm', [(i, i ^ 1) for i in range(count)])]]
  transfers between devices with their start and end apart: 43 -> 29, of which waited for: 16 -> 14; matrix products, arithmetic and copies ran while one was open for 2% -> 1% of each run, Pallas kernels for 15% -> 11%
where the time goes in v5:
time: 262 us; the launch traced here: 261 us
  waiting for transfers between devices  126 us (48%)
  starting transfers between devices  42.6 us (16%)
  local copies, waits for them, and re-layouts  40.1 us (15%)
  Pallas kernels  38.3 us (15%)
  between operations  13.7 us (5%)
    ppermute x23, waiting for transfers between devices, trade(): lax.ppermute(arrays[r], axis, [(i, i ^ r) for i in range(count)])  78.6 us
    unnamed x111, local copies, waits for them, and re-layouts  39 us
    ppermute x1, waiting for transfers between devices, body(): outs = [late, lax.ppermute(late, 'tm', [(i, i ^ 1) for i in range(count)])]  35.3 us
    ppermute x23, starting transfers between devices, trade(): lax.ppermute(arrays[r], axis, [(i, i ^ r) for i in range(count)])  31.4 us
    pallas_call x2, Pallas kernels, send_frames(): pl.pallas_call(functools.partial(frame_kernel, count, rows, experts, capa...  17.8 us
    ppermute x1, waiting for transfers between devices, body(): partner_routes = lax.ppermute(routes[0], 'tm', partner)  12.5 us
    pallas_call x2, Pallas kernels, run_expert(): pl.pallas_call(functools.partial(expert_kernel, len(tokens)), out_shape=c...  9.87 us
    all_to_all x2, starting transfers between devices, route(): moved = lax.all_to_all(whole, 'dp', split_axis=0, concat_axis=0, tiled=True)  7.76 us
  transfers between devices with their start and end apart: 29, of which 14 were waited for; matrix products, arithmetic and copies ran while one was open for 1% of the time, Pallas kernels for 11%

profile of v5, /device:TPU:0, one launch (start us, length us, event | category | flops | bytes accessed | tf_op | source)
XLA Modules:
  0.0 261.1 jit_solution(4451841536853943211)
XLA Ops:
  6.5 2.6 pack.1
  9.1 5.1 %collective-permute-start.2 = (bf16[3,224,256]{2,1,0:T(8,128)(2,1)}, bf16[3,224,256]{2,1,0:T(8,128)(2,1)S(1)}, u32[]{:S(2)}, u32[]{:S(2)}) collective-permute-start(bf16[3,224,256]{2,1,0:T(8,128)(2,1)} %get-tuple-element.54), channel_id=1, source_target_pairs={{0,3},{1,2},{2,1},{3,0},{4,7},{5,6},{6,5},{7,4},{8,11},{9,10},{10,... | collective-permute-start | bytes 1032200 | tf_op jit(solution)/shard_map/ppermute | solution.py:312
  15.0 8.5 %collective-permute-done.2.refs_3_ = bf16[3,224,256]{2,1,0:T(8,128)(2,1)S(1)} collective-permute-done((bf16[3,224,256]{2,1,0:T(8,128)(2,1)}, bf16[3,224,256]{2,1,0:T(8,128)(2,1)S(1)}, u32[]{:S(2)}, u32[]{:S(2)}) %collective-permute-start.2) | collective-permute-done | bytes 344096 | tf_op jit(solution)/shard_map/ppermute | solution.py:312
  23.5 7.6 %collective-permute-done.refs_1_ = bf16[3,224,256]{2,1,0:T(8,128)(2,1)S(1)} collective-permute-done((bf16[3,224,256]{2,1,0:T(8,128)(2,1)}, bf16[3,224,256]{2,1,0:T(8,128)(2,1)S(1)}, u32[]{:S(2)}, u32[]{:S(2)}) %collective-permute-start) | collective-permute-done | bytes 344096 | tf_op jit(solution)/shard_map/ppermute | solution.py:312
  31.0 12.9 %collective-permute-done.1.refs_2_ = bf16[3,224,256]{2,1,0:T(8,128)(2,1)S(1)} collective-permute-done((bf16[3,224,256]{2,1,0:T(8,128)(2,1)}, bf16[3,224,256]{2,1,0:T(8,128)(2,1)S(1)}, u32[]{:S(2)}, u32[]{:S(2)}) %collective-permute-start.1) | collective-permute-done | bytes 344096 | tf_op jit(solution)/shard_map/ppermute | solution.py:312
  44.9 5.5 %attend.1 = (bf16[256,256]{1,0:T(8,128)(2,1)S(1)}, bf16[256,256]{1,0:T(8,128)(2,1)S(1)}, bf16[256,256]{1,0:T(8,128)(2,1)S(1)}, bf16[256,256]{1,0:T(8,128)(2,1)S(...) custom-call(s32[1]{0:T(128)} %bitcast.me_ref, ...), custom_call_target="tpu_custom_call" | custom-call | flops 6600000000 | tf_op jit(solution)/shard_map/attend/pallas_call | solution.py:366
  53.0 3.1 %collective-permute-start.8 = (bf16[256,256]{1,0:T(8,128)(2,1)S(1)}, bf16[256,256]{1,0:T(8,128)(2,1)S(1)}, u32[]{:S(2)}, u32[]{:S(2)}) collective-permute-start(bf16[256,256]{1,0:T(8,128)(2,1)S(1)} %get-tuple-element.61), channel_id=1, source_target_pairs={{0,2},{1,3},{2,0},{3,1},{4,6},{5,7},{6,4},{7,5},{8,10},{9,11},{10,... | collective-permute-start | bytes 393224 | tf_op jit(solution)/shard_map/ppermute | solution.py:312
  58.0 12.5 %collective-permute-done.6 = s32[224,2]{0,1:T(2,128)S(1)} collective-permute-done((s32[224,2]{0,1:T(2,128)S(1)}, s32[224,2]{0,1:T(2,128)S(1)}, u32[]{:S(2)}, u32[]{:S(2)}) %collective-permute-start.6) | collective-permute-done | bytes 1824 | tf_op jit(solution)/shard_map/ppermute | solution.py:361
  70.6 2.7 %collective-permute-done.9.refs_3_ = bf16[256,256]{1,0:T(8,128)(2,1)S(1)} collective-permute-done((bf16[256,256]{1,0:T(8,128)(2,1)S(1)}, bf16[256,256]{1,0:T(8,128)(2,1)S(1)}, u32[]{:S(2)}, u32[]{:S(2)}) %collective-permute-start.9) | collective-permute-done | bytes 131104 | tf_op jit(solution)/shard_map/ppermute | solution.py:312
  73.3 1.9 copy-done.9
  75.2 9.9 %frames.2 = (bf16[704,1536]{1,0:T(8,128)(2,1)}, f32[224,128]{1,0:T(8,128)S(1)}, f32[12,224,128]{2,1,0:T(8,128)}) custom-call(s32[1]{0:T(128)} %bitcast.me_ref, s32[1]{0:T(128)} %bitcast.1.expert_ref, s32[1,4]{1,0:T(1,128)S(1)} %copy-done.44, bf16[1024,1536]{1,0:T(8,128)(2,1)S(1)} %copy-done.9, f32[12,31,128]{2,1,0:T(8,128)S(1)} %bitcast.22, ...), custom_call_target="tpu_custom_call" | custom-call | flops 11000000512 | tf_op jit(solution)/shard_map/frames/pallas_call | solution.py:409
  85.8 3.8 %all-to-all-start = ((bf16[8,88,1536]{2,1,0:T(8,128)(2,1)}), bf16[8,88,1536]{2,1,0:T(8,128)(2,1)S(1)}, u32[]{:S(2)}, u32[]{:S(2)}) async-start(bf16[8,88,1536]{2,1,0:T(8,128)(2,1)} %bitcast.10), calls=%async_computation | async-start | bytes 4325376 | tf_op jit(solution)/shard_map/all_to_all | solution.py:404
  89.6 3.3 %collective-permute-start.10 = (bf16[512,1536]{1,0:T(8,128)(2,1)}, bf16[512,1536]{1,0:T(8,128)(2,1)S(1)}, u32[]{:S(2)}, u32[]{:S(2)}) collective-permute-start(bf16[512,1536]{1,0:T(8,128)(2,1)} %bitcast.28), channel_id=1, source_target_pairs={{0,1},{1,0},{2,3},{3,2},{4,5},{5,4},{6,7},{7,6},{8,9},{9,8},{10,11... | collective-permute-start | bytes 4718600 | tf_op jit(solution)/shard_map/ppermute | solution.py:388
  92.9 35.3 %collective-permute-done.10.refs_2_.refs_9_ = bf16[512,1536]{1,0:T(8,128)(2,1)S(1)} collective-permute-done((bf16[512,1536]{1,0:T(8,128)(2,1)}, bf16[512,1536]{1,0:T(8,128)(2,1)S(1)}, u32[]{:S(2)}, u32[]{:S(2)}) %collective-permute-start.10) | collective-permute-done | bytes 1572896 | tf_op jit(solution)/shard_map/ppermute | solution.py:388
  129.3 1.9 copy-done.11
  134.0 4.9 %experts.2 = bf16[704,1536]{1,0:T(8,128)(2,1)S(1)} custom-call(s32[1]{0:T(128)} %bitcast.me_ref, bf16[1024,1536]{1,0:T(8,128)(2,1)S(1)} %copy-done.11, bf16[704,1536]{1,0:T(8,128)(2,1)S(1)} %bitcast.21, bf16[512,1536]{1,0:T(8,128)(2,1)S(1)} %bitcast.29, bf16[512,1536]{1,0:T(8,128)(2,1)S(1)} %copy-done.16), custom_call_target="tpu_custom_call" | custom-call | flops 8800000000 | tf_op jit(solution)/shard_map/experts/pallas_call | solution.py:432
  140.4 4.0 %all-to-all-start.1 = ((bf16[8,88,1536]{2,1,0:T(8,128)(2,1)}), bf16[8,88,1536]{2,1,0:T(8,128)(2,1)S(1)}, u32[]{:S(2)}, u32[]{:S(2)}) async-start(bf16[8,88,1536]{2,1,0:T(8,128)(2,1)} %bitcast.20), calls=%async_computation.1 | async-start | bytes 4325376 | tf_op jit(solution)/shard_map/all_to_all | solution.py:404
  144.3 1.8 collective-permute-start.3
  146.2 2.6 %collective-permute-start.5 = (bf16[256,256]{1,0:T(8,128)(2,1)S(1)}, bf16[256,256]{1,0:T(8,128)(2,1)S(1)}, u32[]{:S(2)}, u32[]{:S(2)}) collective-permute-start(bf16[256,256]{1,0:T(8,128)(2,1)S(1)} %copy-done.33), channel_id=1, source_target_pairs={{0,3},{1,2},{2,1},{3,0},{4,7},{5,6},{6,5},{7,4},{8,11},{9,10},{10,... | collective-permute-start | bytes 393224 | tf_op jit(solution)/shard_map/ppermute | solution.py:312
  151.5 7.2 %collective-permute-done.4.refs_2_ = bf16[256,256]{1,0:T(8,128)(2,1)S(1)} collective-permute-done((bf16[256,256]{1,0:T(8,128)(2,1)S(1)}, bf16[256,256]{1,0:T(8,128)(2,1)S(1)}, u32[]{:S(2)}, u32[]{:S(2)}) %collective-permute-start.4) | collective-permute-done | bytes 131104 | tf_op jit(solution)/shard_map/ppermute | solution.py:312
  162.8 1.9 copy-done.10
  168.3 7.9 %frames.3 = (bf16[88,1536]{1,0:T(8,128)(2,1)S(1)}, bf16[88,1536]{1,0:T(8,128)(2,1)S(1)}, bf16[88,1536]{1,0:T(8,128)(2,1)S(1)}, bf16[88,1536]{1,0:T(8,128)(2,1)S(...) custom-call(s32[1]{0:T(128)} %bitcast.me_ref, ...), custom_call_target="tpu_custom_call" | custom-call | flops 11000000512 | tf_op jit(solution)/shard_map/frames/pallas_call | solution.py:409
  178.2 3.2 %collective-permute-start.13 = (bf16[88,1536]{1,0:T(8,128)(2,1)S(1)}, bf16[88,1536]{1,0:T(8,128)(2,1)S(1)}, u32[]{:S(2)}, u32[]{:S(2)}) collective-permute-start(bf16[88,1536]{1,0:T(8,128)(2,1)S(1)} %get-tuple-element.75), channel_id=1, source_target_pairs={{0,8},{4,12},{8,0},{12,4},{16,24},{20,28},{24,16},{28,20},{1,9},{5... | collective-permute-start | bytes 811016 | tf_op jit(solution)/shard_map/ppermute | solution.py:312
  181.5 2.4 collective-permute-start.15
  185.8 2.9 %collective-permute-done.13.refs_2_ = bf16[88,1536]{1,0:T(8,128)(2,1)S(1)} collective-permute-done((bf16[88,1536]{1,0:T(8,128)(2,1)S(1)}, bf16[88,1536]{1,0:T(8,128)(2,1)S(1)}, u32[]{:S(2)}, u32[]{:S(2)}) %collective-permute-start.13) | collective-permute-done | bytes 270368 | tf_op jit(solution)/shard_map/ppermute | solution.py:312
  190.8 3.3 %collective-permute-done.14.refs_3_ = bf16[88,1536]{1,0:T(8,128)(2,1)S(1)} collective-permute-done((bf16[88,1536]{1,0:T(8,128)(2,1)S(1)}, bf16[88,1536]{1,0:T(8,128)(2,1)S(1)}, u32[]{:S(2)}, u32[]{:S(2)}) %collective-permute-start.14) | collective-permute-done | bytes 270368 | tf_op jit(solution)/shard_map/ppermute | solution.py:312
  195.6 11.9 %collective-permute-done.16.refs_5_ = bf16[88,1536]{1,0:T(8,128)(2,1)S(1)} collective-permute-done((bf16[88,1536]{1,0:T(8,128)(2,1)S(1)}, bf16[88,1536]{1,0:T(8,128)(2,1)S(1)}, u32[]{:S(2)}, u32[]{:S(2)}) %collective-permute-start.16) | collective-permute-done | bytes 270368 | tf_op jit(solution)/shard_map/ppermute | solution.py:312
  219.3 4.9 %experts.3 = (bf16[88,1536]{1,0:T(8,128)(2,1)S(1)}, bf16[88,1536]{1,0:T(8,128)(2,1)S(1)}, bf16[88,1536]{1,0:T(8,128)(2,1)S(1)}, bf16[88,1536]{1,0:T(8,128)(2,1)S...) custom-call(s32[1]{0:T(128)} %bitcast.me_ref, ...), custom_call_target="tpu_custom_call" | custom-call | flops 8800000000 | tf_op jit(solution)/shard_map/experts/pallas_call | solution.py:432
  228.4 5.8 %collective-permute-done.20.refs_2_ = bf16[88,1536]{1,0:T(8,128)(2,1)S(1)} collective-permute-done((bf16[88,1536]{1,0:T(8,128)(2,1)S(1)}, bf16[88,1536]{1,0:T(8,128)(2,1)S(1)}, u32[]{:S(2)}, u32[]{:S(2)}) %collective-permute-start.20) | collective-permute-done | bytes 270368 | tf_op jit(solution)/shard_map/ppermute | solution.py:312
  235.5 3.1 %collective-permute-done.21.refs_3_ = bf16[88,1536]{1,0:T(8,128)(2,1)S(1)} collective-permute-done((bf16[88,1536]{1,0:T(8,128)(2,1)S(1)}, bf16[88,1536]{1,0:T(8,128)(2,1)S(1)}, u32[]{:S(2)}, u32[]{:S(2)}) %collective-permute-start.21) | collective-permute-done | bytes 270368 | tf_op jit(solution)/shard_map/ppermute | solution.py:312
  238.6 2.4 collective-permute-start.25
  241.0 11.5 %collective-permute-done.23.refs_5_ = bf16[88,1536]{1,0:T(8,128)(2,1)S(1)} collective-permute-done((bf16[88,1536]{1,0:T(8,128)(2,1)S(1)}, bf16[88,1536]{1,0:T(8,128)(2,1)S(1)}, u32[]{:S(2)}, u32[]{:S(2)}) %collective-permute-start.23) | collective-permute-done | bytes 270368 | tf_op jit(solution)/shard_map/ppermute | solution.py:312
  (151 shorter events, 49.2 us)
Async XLA Ops:
  6.5 122.8 %all-gather.2.cloned.1.call-start = ((), (), s32[]{:S(2)}) async-start(), calls=%async_computation.2 | async-start | bytes 4718592 | tf_op jit(solution)/shard_map/all_gather | solution.py:386
  6.5 37.4 %copy-start.44 = (s32[1,4]{1,0:T(1,128)S(1)}, s32[1,4]{1,0:T(1,128)}, u32[]{:S(2)}) copy-start(s32[1,4]{1,0:T(1,128)} %len_ref.5) | copy-start | bytes 52
  9.1 14.3 %collective-permute-start.2 = (bf16[3,224,256]{2,1,0:T(8,128)(2,1)}, bf16[3,224,256]{2,1,0:T(8,128)(2,1)S(1)}, u32[]{:S(2)}, u32[]{:S(2)}) collective-permute-start(bf16[3,224,256]{2,1,0:T(8,128)(2,1)} %get-tuple-element.54), channel_id=1, source_target_pairs={{0,3},{1,2},{2,1},{3,0},{4,7},{5,6},{6,5},{7,4},{8,11},{9,10},{10,... | collective-permute-start | bytes 1032200 | tf_op jit(solution)/shard_map/ppermute | solution.py:312
  14.3 16.8 %collective-permute-start = (bf16[3,224,256]{2,1,0:T(8,128)(2,1)}, bf16[3,224,256]{2,1,0:T(8,128)(2,1)S(1)}, u32[]{:S(2)}, u32[]{:S(2)}) collective-permute-start(bf16[3,224,256]{2,1,0:T(8,128)(2,1)} %get-tuple-element.52), channel_id=1, source_target_pairs={{0,1},{1,0},{2,3},{3,2},{4,5},{5,4},{6,7},{7,6},{8,9},{9,8},{10,11... | collective-permute-start | bytes 1032200 | tf_op jit(solution)/shard_map/ppermute | solution.py:312
  14.3 29.6 %collective-permute-start.1 = (bf16[3,224,256]{2,1,0:T(8,128)(2,1)}, bf16[3,224,256]{2,1,0:T(8,128)(2,1)S(1)}, u32[]{:S(2)}, u32[]{:S(2)}) collective-permute-start(bf16[3,224,256]{2,1,0:T(8,128)(2,1)} %get-tuple-element.53), channel_id=1, source_target_pairs={{0,2},{1,3},{2,0},{3,1},{4,6},{5,7},{6,4},{7,5},{8,10},{9,11},{10,... | collective-permute-start | bytes 1032200 | tf_op jit(solution)/shard_map/ppermute | solution.py:312
  53.0 17.6 %collective-permute-start.7 = (bf16[256,256]{1,0:T(8,128)(2,1)S(1)}, bf16[256,256]{1,0:T(8,128)(2,1)S(1)}, u32[]{:S(2)}, u32[]{:S(2)}) collective-permute-start(bf16[256,256]{1,0:T(8,128)(2,1)S(1)} %get-tuple-element.60), channel_id=1, source_target_pairs={{0,1},{1,0},{2,3},{3,2},{4,5},{5,4},{6,7},{7,6},{8,9},{9,8},{10,11... | collective-permute-start | bytes 393224 | tf_op jit(solution)/shard_map/ppermute | solution.py:312
  53.0 17.6 %collective-permute-start.8 = (bf16[256,256]{1,0:T(8,128)(2,1)S(1)}, bf16[256,256]{1,0:T(8,128)(2,1)S(1)}, u32[]{:S(2)}, u32[]{:S(2)}) collective-permute-start(bf16[256,256]{1,0:T(8,128)(2,1)S(1)} %get-tuple-element.61), channel_id=1, source_target_pairs={{0,2},{1,3},{2,0},{3,1},{4,6},{5,7},{6,4},{7,5},{8,10},{9,11},{10,... | collective-permute-start | bytes 393224 | tf_op jit(solution)/shard_map/ppermute | solution.py:312
  56.1 17.2 %collective-permute-start.9 = (bf16[256,256]{1,0:T(8,128)(2,1)S(1)}, bf16[256,256]{1,0:T(8,128)(2,1)S(1)}, u32[]{:S(2)}, u32[]{:S(2)}) collective-permute-start(bf16[256,256]{1,0:T(8,128)(2,1)S(1)} %get-tuple-element.62), channel_id=1, source_target_pairs={{0,3},{1,2},{2,1},{3,0},{4,7},{5,6},{6,5},{7,4},{8,11},{9,10},{10,... | collective-permute-start | bytes 393224 | tf_op jit(solution)/shard_map/ppermute | solution.py:312
  57.4 13.1 %collective-permute-start.6 = (s32[224,2]{0,1:T(2,128)S(1)}, s32[224,2]{0,1:T(2,128)S(1)}, u32[]{:S(2)}, u32[]{:S(2)}) collective-permute-start(s32[224,2]{0,1:T(2,128)S(1)} %bitcast.24), channel_id=1, source_target_pairs={{0,2},{1,3},{2,0},{3,1},{4,6},{5,7},{6,4},{7,5},{8,10},{9,11},{10,... | collective-permute-start | bytes 5384 | tf_op jit(solution)/shard_map/ppermute | solution.py:361
  57.7 27.4 %copy-start.3 = (f32[31,12,128]{2,0,1:T(8,128)}, f32[31,12,128]{2,0,1:T(8,128)S(1)}, u32[]{:S(2)}) copy-start(f32[31,12,128]{2,0,1:T(8,128)S(1)} %copy.22) | copy-start | bytes 571396
  85.8 43.5 %all-to-all-start = ((bf16[8,88,1536]{2,1,0:T(8,128)(2,1)}), bf16[8,88,1536]{2,1,0:T(8,128)(2,1)S(1)}, u32[]{:S(2)}, u32[]{:S(2)}) async-start(bf16[8,88,1536]{2,1,0:T(8,128)(2,1)} %bitcast.10), calls=%async_computation | async-start | bytes 4325376 | tf_op jit(solution)/shard_map/all_to_all | solution.py:404
  89.6 38.6 %collective-permute-start.10 = (bf16[512,1536]{1,0:T(8,128)(2,1)}, bf16[512,1536]{1,0:T(8,128)(2,1)S(1)}, u32[]{:S(2)}, u32[]{:S(2)}) collective-permute-start(bf16[512,1536]{1,0:T(8,128)(2,1)} %bitcast.28), channel_id=1, source_target_pairs={{0,1},{1,0},{2,3},{3,2},{4,5},{5,4},{6,7},{7,6},{8,9},{9,8},{10,11... | collective-permute-start | bytes 4718600 | tf_op jit(solution)/shard_map/ppermute | solution.py:388
  140.4 69.3 %all-to-all-start.1 = ((bf16[8,88,1536]{2,1,0:T(8,128)(2,1)}), bf16[8,88,1536]{2,1,0:T(8,128)(2,1)S(1)}, u32[]{:S(2)}, u32[]{:S(2)}) async-start(bf16[8,88,1536]{2,1,0:T(8,128)(2,1)} %bitcast.20), calls=%async_computation.1 | async-start | bytes 4325376 | tf_op jit(solution)/shard_map/all_to_all | solution.py:404
  144.3 6.5 %collective-permute-start.3 = (bf16[256,256]{1,0:T(8,128)(2,1)S(1)}, bf16[256,256]{1,0:T(8,128)(2,1)S(1)}, u32[]{:S(2)}, u32[]{:S(2)}) collective-permute-start(bf16[256,256]{1,0:T(8,128)(2,1)S(1)} %copy-done.37), channel_id=1, source_target_pairs={{0,1},{1,0},{2,3},{3,2},{4,5},{5,4},{6,7},{7,6},{8,9},{9,8},{10,11... | collective-permute-start | bytes 393224 | tf_op jit(solution)/shard_map/ppermute | solution.py:312
  146.1 12.5 %collective-permute-start.4 = (bf16[256,256]{1,0:T(8,128)(2,1)S(1)}, bf16[256,256]{1,0:T(8,128)(2,1)S(1)}, u32[]{:S(2)}, u32[]{:S(2)}) collective-permute-start(bf16[256,256]{1,0:T(8,128)(2,1)S(1)} %copy-done.35), channel_id=1, source_target_pairs={{0,2},{1,3},{2,0},{3,1},{4,6},{5,7},{6,4},{7,5},{8,10},{9,11},{10,... | collective-permute-start | bytes 393224 | tf_op jit(solution)/shard_map/ppermute | solution.py:312
  146.2 13.2 %collective-permute-start.5 = (bf16[256,256]{1,0:T(8,128)(2,1)S(1)}, bf16[256,256]{1,0:T(8,128)(2,1)S(1)}, u32[]{:S(2)}, u32[]{:S(2)}) collective-permute-start(bf16[256,256]{1,0:T(8,128)(2,1)S(1)} %copy-done.33), channel_id=1, source_target_pairs={{0,3},{1,2},{2,1},{3,0},{4,7},{5,6},{6,5},{7,4},{8,11},{9,10},{10,... | collective-permute-start | bytes 393224 | tf_op jit(solution)/shard_map/ppermute | solution.py:312
  177.6 6.3 %collective-permute-start.12 = (bf16[88,1536]{1,0:T(8,128)(2,1)S(1)}, bf16[88,1536]{1,0:T(8,128)(2,1)S(1)}, u32[]{:S(2)}, u32[]{:S(2)}) collective-permute-start(bf16[88,1536]{1,0:T(8,128)(2,1)S(1)} %get-tuple-element.74), channel_id=1, source_target_pairs={{0,4},{4,0},{8,12},{12,8},{16,20},{20,16},{24,28},{28,24},{1,5},{5... | collective-permute-start | bytes 811016 | tf_op jit(solution)/shard_map/ppermute | solution.py:312
  178.2 10.5 %collective-permute-start.13 = (bf16[88,1536]{1,0:T(8,128)(2,1)S(1)}, bf16[88,1536]{1,0:T(8,128)(2,1)S(1)}, u32[]{:S(2)}, u32[]{:S(2)}) collective-permute-start(bf16[88,1536]{1,0:T(8,128)(2,1)S(1)} %get-tuple-element.75), channel_id=1, source_target_pairs={{0,8},{4,12},{8,0},{12,4},{16,24},{20,28},{24,16},{28,20},{1,9},{5... | collective-permute-start | bytes 811016 | tf_op jit(solution)/shard_map/ppermute | solution.py:312
  181.4 12.8 %collective-permute-start.14 = (bf16[88,1536]{1,0:T(8,128)(2,1)S(1)}, bf16[88,1536]{1,0:T(8,128)(2,1)S(1)}, u32[]{:S(2)}, u32[]{:S(2)}) collective-permute-start(bf16[88,1536]{1,0:T(8,128)(2,1)S(1)} %get-tuple-element.76), channel_id=1, source_target_pairs={{0,12},{4,8},{8,4},{12,0},{16,28},{20,24},{24,20},{28,16},{1,13},{... | collective-permute-start | bytes 811016 | tf_op jit(solution)/shard_map/ppermute | solution.py:312
  181.5 13.3 %collective-permute-start.15 = (bf16[88,1536]{1,0:T(8,128)(2,1)S(1)}, bf16[88,1536]{1,0:T(8,128)(2,1)S(1)}, u32[]{:S(2)}, u32[]{:S(2)}) collective-permute-start(bf16[88,1536]{1,0:T(8,128)(2,1)S(1)} %get-tuple-element.77), channel_id=1, source_target_pairs={{0,16},{4,20},{8,24},{12,28},{16,0},{20,4},{24,8},{28,12},{1,17},{... | collective-permute-start | bytes 811016 | tf_op jit(solution)/shard_map/ppermute | solution.py:312
  183.9 23.6 %collective-permute-start.16 = (bf16[88,1536]{1,0:T(8,128)(2,1)S(1)}, bf16[88,1536]{1,0:T(8,128)(2,1)S(1)}, u32[]{:S(2)}, u32[]{:S(2)}) collective-permute-start(bf16[88,1536]{1,0:T(8,128)(2,1)S(1)} %get-tuple-element.78), channel_id=1, source_target_pairs={{0,20},{4,16},{8,28},{12,24},{16,4},{20,0},{24,12},{28,8},{1,21},{... | collective-permute-start | bytes 811016 | tf_op jit(solution)/shard_map/ppermute | solution.py:312
  184.6 23.6 %collective-permute-start.17 = (bf16[88,1536]{1,0:T(8,128)(2,1)S(1)}, bf16[88,1536]{1,0:T(8,128)(2,1)S(1)}, u32[]{:S(2)}, u32[]{:S(2)}) collective-permute-start(bf16[88,1536]{1,0:T(8,128)(2,1)S(1)} %get-tuple-element.79), channel_id=1, source_target_pairs={{0,24},{4,28},{8,16},{12,20},{16,8},{20,12},{24,0},{28,4},{1,25},{... | collective-permute-start | bytes 811016 | tf_op jit(solution)/shard_map/ppermute | solution.py:312
  189.4 19.5 %collective-permute-start.18 = (bf16[88,1536]{1,0:T(8,128)(2,1)S(1)}, bf16[88,1536]{1,0:T(8,128)(2,1)S(1)}, u32[]{:S(2)}, u32[]{:S(2)}) collective-permute-start(bf16[88,1536]{1,0:T(8,128)(2,1)S(1)} %get-tuple-element.80), channel_id=1, source_target_pairs={{0,28},{4,24},{8,20},{12,16},{16,12},{20,8},{24,4},{28,0},{1,29},{... | collective-permute-start | bytes 811016 | tf_op jit(solution)/shard_map/ppermute | solution.py:312
  211.5 41.0 %copy-start.7 = (f32[224,128]{1,0:T(8,128)S(1)}, f32[224,128]{1,0:T(8,128)}, u32[]{:S(2)}) copy-start(f32[224,128]{1,0:T(8,128)} %copy-done.6) | copy-start | bytes 344068
  211.6 41.0 %collective-permute-start.11 = (bf16[224,1536]{1,0:T(8,128)(2,1)S(1)}, bf16[224,1536]{1,0:T(8,128)(2,1)S(1)}, u32[]{:S(2)}, u32[]{:S(2)}) collective-permute-start(bf16[224,1536]{1,0:T(8,128)(2,1)S(1)} %theirs.1), channel_id=1, source_target_pairs={{0,2},{1,3},{2,0},{3,1},{4,6},{5,7},{6,4},{7,5},{8,10},{9,11},{10,... | collective-permute-start | bytes 2064392 | tf_op jit(solution)/shard_map/ppermute | solution.py:462
  224.3 3.8 %collective-permute-start.19 = (bf16[88,1536]{1,0:T(8,128)(2,1)S(1)}, bf16[88,1536]{1,0:T(8,128)(2,1)S(1)}, u32[]{:S(2)}, u32[]{:S(2)}) collective-permute-start(bf16[88,1536]{1,0:T(8,128)(2,1)S(1)} %get-tuple-element.90), channel_id=1, source_target_pairs={{0,4},{4,0},{8,12},{12,8},{16,20},{20,16},{24,28},{28,24},{1,5},{5... | collective-permute-start | bytes 811016 | tf_op jit(solution)/shard_map/ppermute | solution.py:312
  224.9 9.3 %collective-permute-start.20 = (bf16[88,1536]{1,0:T(8,128)(2,1)S(1)}, bf16[88,1536]{1,0:T(8,128)(2,1)S(1)}, u32[]{:S(2)}, u32[]{:S(2)}) collective-permute-start(bf16[88,1536]{1,0:T(8,128)(2,1)S(1)} %get-tuple-element.91), channel_id=1, source_target_pairs={{0,8},{4,12},{8,0},{12,4},{16,24},{20,28},{24,16},{28,20},{1,9},{5... | collective-permute-start | bytes 811016 | tf_op jit(solution)/shard_map/ppermute | solution.py:312
  225.9 12.6 %collective-permute-start.21 = (bf16[88,1536]{1,0:T(8,128)(2,1)S(1)}, bf16[88,1536]{1,0:T(8,128)(2,1)S(1)}, u32[]{:S(2)}, u32[]{:S(2)}) collective-permute-start(bf16[88,1536]{1,0:T(8,128)(2,1)S(1)} %get-tuple-element.92), channel_id=1, source_target_pairs={{0,12},{4,8},{8,4},{12,0},{16,28},{20,24},{24,20},{28,16},{1,13},{... | collective-permute-start | bytes 811016 | tf_op jit(solution)/shard_map/ppermute | solution.py:312
  226.3 14.7 %collective-permute-start.22 = (bf16[88,1536]{1,0:T(8,128)(2,1)S(1)}, bf16[88,1536]{1,0:T(8,128)(2,1)S(1)}, u32[]{:S(2)}, u32[]{:S(2)}) collective-permute-start(bf16[88,1536]{1,0:T(8,128)(2,1)S(1)} %get-tuple-element.93), channel_id=1, source_target_pairs={{0,16},{4,20},{8,24},{12,28},{16,0},{20,4},{24,8},{28,12},{1,17},{... | collective-permute-start | bytes 811016 | tf_op jit(solution)/shard_map/ppermute | solution.py:312
  228.1 24.5 %collective-permute-start.23 = (bf16[88,1536]{1,0:T(8,128)(2,1)S(1)}, bf16[88,1536]{1,0:T(8,128)(2,1)S(1)}, u32[]{:S(2)}, u32[]{:S(2)}) collective-permute-start(bf16[88,1536]{1,0:T(8,128)(2,1)S(1)} %get-tuple-element.94), channel_id=1, source_target_pairs={{0,20},{4,16},{8,28},{12,24},{16,4},{20,0},{24,12},{28,8},{1,21},{... | collective-permute-start | bytes 811016 | tf_op jit(solution)/shard_map/ppermute | solution.py:312
  234.2 18.3 %collective-permute-start.24 = (bf16[88,1536]{1,0:T(8,128)(2,1)S(1)}, bf16[88,1536]{1,0:T(8,128)(2,1)S(1)}, u32[]{:S(2)}, u32[]{:S(2)}) collective-permute-start(bf16[88,1536]{1,0:T(8,128)(2,1)S(1)} %get-tuple-element.95), channel_id=1, source_target_pairs={{0,24},{4,28},{8,16},{12,20},{16,8},{20,12},{24,0},{28,4},{1,25},{... | collective-permute-start | bytes 811016 | tf_op jit(solution)/shard_map/ppermute | solution.py:312
  238.6 13.9 %collective-permute-start.25 = (bf16[88,1536]{1,0:T(8,128)(2,1)S(1)}, bf16[88,1536]{1,0:T(8,128)(2,1)S(1)}, u32[]{:S(2)}, u32[]{:S(2)}) collective-permute-start(bf16[88,1536]{1,0:T(8,128)(2,1)S(1)} %get-tuple-element.96), channel_id=1, source_target_pairs={{0,28},{4,24},{8,20},{12,16},{16,12},{20,8},{24,4},{28,0},{1,29},{... | collective-permute-start | bytes 811016 | tf_op jit(solution)/shard_map/ppermute | solution.py:312
  (52 other events, 135.9 us)
Sparse Core Ops, SparseCore 0:
  23.6 62.5 all-gather.1

commit v6 on v5

--- a/solution.py
+++ b/solution.py
@@ -260,18 +260,14 @@
         ref[...] = values[e * tall : (e + 1) * tall].astype(BF16)
 
 
-def expert_kernel(chunks, me_ref, in_ref, *refs):
-    x_refs, out_refs, o_refs = refs[:chunks], refs[chunks:-chunks], refs[-chunks:]
+def expert_kernel(chunks, pieces, *refs):
+    x_refs, o_refs = refs[:chunks], refs[-chunks:]
+    in_refs, out_refs = refs[chunks : chunks + pieces], refs[chunks + pieces : chunks + 2 * pieces]
     tokens = joined(x_refs)
     total = jnp.zeros((tokens.shape[0], D), F32)
-    units = out_refs[0].shape[0]
-    for place, out_ref in enumerate(out_refs):
-        begin = 0 if len(out_refs) == 1 else pl.multiple_of(((me_ref[0] & 1) ^ place) * units, 16)
+    for in_ref, out_ref in zip(in_refs, out_refs):
         raw = lax.dot_general(
-            tokens,
-            in_ref[pl.ds(begin, units), :],
-            (((1,), (1,)), ((), ())),
-            preferred_element_type=F32,
+            tokens, in_ref[...], (((1,), (1,)), ((), ())), preferred_element_type=F32
         )
         hidden = (raw / (1.0 + jnp.exp(-raw))).astype(BF16)
         total = total + jnp.dot(hidden, out_ref[...], preferred_element_type=F32)
@@ -315,8 +311,8 @@
     return [arrays[0]] + [moved[r] for r in range(1, count)]
 
 
-def tied(arrays, marker):
-    return lax.optimization_barrier((*arrays, marker))[:-1]
+def after(arrays, markers):
+    return lax.optimization_barrier((*arrays, *markers))[: len(arrays)]
 
 
 def body(
@@ -373,20 +369,21 @@
             pltpu.VMEM((tiles, total, 2 * LANES), BF16),
             pltpu.VMEM((total + 2 * HALO, width), BF16),
         ],
-        compiler_params=params(16),
+        compiler_params=params(10),
         cost_estimate=cost(6),
         name="attend",
     )(me, scales, lengths, *arrived)
     gathered_a = trade(attended[:count], "tm", direct)
     gathered_b = trade(attended[count:], "tm", direct)
 
-    groups = [list(range(i, i + half)) for i in (0, half)]
-    (early,) = tied((expert_in[0],), arrived[-1])
-    (late,) = tied((expert_out[0],), gathered_a[-1])
-    ins = lax.all_gather(early, "tm", axis=0, tiled=True, axis_index_groups=groups)
+    early, late = after((expert_in[0], expert_out[0]), gathered_b)
     if half == 2:
-        outs = [late, lax.ppermute(late, "tm", [(i, i ^ 1) for i in range(count)])]
+        swap = [(i, i ^ 1) for i in range(count)]
+        ins = [early, lax.ppermute(early, "tm", swap)]
+        outs = [late, lax.ppermute(late, "tm", swap)]
     else:
+        groups = [list(range(i, i + half)) for i in (0, half)]
+        ins = [lax.all_gather(early, "tm", axis=0, tiled=True, axis_index_groups=groups)]
         outs = [lax.all_gather(late, "tm", axis=0, tiled=True, axis_index_groups=groups)]
 
     taps = jnp.transpose(conv_taps.reshape(KERNEL, D // LANES, LANES), (1, 0, 2))
@@ -420,7 +417,7 @@
                 pltpu.VMEM((D // LANES, rows, LANES), F32),
                 pltpu.VMEM((window, LANES), F32),
             ],
-            compiler_params=params(24),
+            compiler_params=params(16),
             cost_estimate=cost(10),
             name="frames",
         )(me, expert, lengths, out_proj, taps, router, block_routes, block_routes.T, *windows)
@@ -430,32 +427,33 @@
         split = len(tokens) > 1
         chunks = chunks_of(split)
         produced = pl.pallas_call(
-            functools.partial(expert_kernel, len(tokens)),
+            functools.partial(expert_kernel, len(tokens), len(ins)),
             out_shape=chunks,
-            in_specs=[SMEM] + [VMEM] * (1 + len(tokens) + len(outs)),
+            in_specs=[VMEM] * (len(tokens) + len(ins) + len(outs)),
             out_specs=(VMEM,) * len(chunks),
-            compiler_params=params(24),
+            compiler_params=params(20),
             cost_estimate=cost(8),
             name="experts",
-        )(me, ins, *tokens, *outs)
+        )(*tokens, *ins, *outs)
         return produced
 
     outgoing_a, info_a, _ = send_frames(gathered_a, half, False, partner_routes)
-    tokens_a = route(outgoing_a)
-    gathered_b = tied(gathered_b, outgoing_a[0])
+    tokens_a = route(after(outgoing_a, gathered_b))
+    gathered_b = after(gathered_b, (outgoing_a[0], ins[-1]))
     outgoing_b, info_b, second = send_frames(gathered_b, 0, True, routes[0])
     tokens_b = route(outgoing_b)
-    produced_a = run_expert(tokens_a)
+    produced_a = run_expert(after(tokens_a, tokens_b))
     back_a = route(produced_a)
-    tokens_b = tied(tokens_b, produced_a[0])
-    back_b = route(run_expert(tokens_b))
+    produced_b = run_expert(after(tokens_b, produced_a))
+    back_b = route(produced_b)
+    back_a = after(back_a, back_b[1:2])
 
     theirs = pl.pallas_call(
         theirs_kernel,
         out_shape=jax.ShapeDtypeStruct((rows, D), BF16),
         in_specs=[VMEM] * (1 + len(back_a)),
         out_specs=VMEM,
-        compiler_params=params(16),
+        compiler_params=params(8),
         cost_estimate=cost(1),
         name="theirs",
     )(info_a, *back_a)
@@ -465,7 +463,7 @@
         out_shape=jax.ShapeDtypeStruct((rows, D), BF16),
         in_specs=[VMEM] * (3 + len(back_b)),
         out_specs=VMEM,
-        compiler_params=params(16),
+        compiler_params=params(12),
         cost_estimate=cost(1),
         name="mine",
     )(info_b, second, received, *back_b)

time: 262 us -> 250 us (0.954)
  between operations: 13.7 us -> 0.3 us
  waiting for transfers between devices: 126 us -> 116 us
  Pallas kernels: 38.3 us -> 44.9 us
  starting transfers between devices: 42.6 us -> 46.6 us
    ppermute x1 -> x2, waiting for transfers between devices: 35.3 us -> 0.01 us  [the longest x1 0.01 us: body(): outs = [late, lax.ppermute(late, 'tm', swap)]]
    ppermute x1, waiting for transfers between devices: 12.5 us -> 35.8 us  [body(): partner_routes = lax.ppermute(routes[0], 'tm', partner)]
    pallas_call x2, Pallas kernels: 9.87 us -> 14.6 us  [run_expert(): pl.pallas_call(functools.partial(expert_kernel, len(tokens), len(ins)), o...]
    ppermute x23, waiting for transfers between devices: 78.6 us -> 74.5 us  [trade(): lax.ppermute(arrays[r], axis, [(i, i ^ r) for i in range(count)])]
    all_to_all x2, waiting for transfers between devices: 0.01 us -> 3.69 us  [route(): moved = lax.all_to_all(whole, 'dp', split_axis=0, concat_axis=0, tiled=True)]
    ppermute x23, starting transfers between devices: 31.4 us -> 34.5 us  [trade(): lax.ppermute(arrays[r], axis, [(i, i ^ r) for i in range(count)])]
    unnamed x111 -> x121, local copies, waits for them, and re-layouts: 39 us -> 39.5 us
  transfers between devices with their start and end apart: 29 -> 29, of which waited for: 14 -> 15; matrix products, arithmetic and copies ran while one was open for 1% -> 1% of each run, Pallas kernels for 11% -> 11%
where the time goes in v6:
time: 250 us; the launch traced here: 248 us
  waiting for transfers between devices  116 us (46%)
  starting transfers between devices  46.6 us (19%)
  Pallas kernels  44.9 us (18%)
  local copies, waits for them, and re-layouts  40.5 us (16%)
    ppermute x23, waiting for transfers between devices, trade(): lax.ppermute(arrays[r], axis, [(i, i ^ r) for i in range(count)])  74.5 us
    unnamed x121, local copies, waits for them, and re-layouts  39.5 us
    ppermute x1, waiting for transfers between devices, body(): partner_routes = lax.ppermute(routes[0], 'tm', partner)  35.8 us
    ppermute x23, starting transfers between devices, trade(): lax.ppermute(arrays[r], axis, [(i, i ^ r) for i in range(count)])  34.5 us
    pallas_call x2, Pallas kernels, send_frames(): pl.pallas_call(functools.partial(frame_kernel, count, rows, experts, capa...  19.7 us
    pallas_call x2, Pallas kernels, run_expert(): pl.pallas_call(functools.partial(expert_kernel, len(tokens), len(ins)), o...  14.6 us
    all_to_all x2, starting transfers between devices, route(): moved = lax.all_to_all(whole, 'dp', split_axis=0, concat_axis=0, tiled=True)  7.33 us
    pallas_call x1, Pallas kernels, body(): pl.pallas_call(functools.partial(attend_kernel, count, rows, heads, place...  5.5 us
  transfers between devices with their start and end apart: 29, of which 15 were waited for; matrix products, arithmetic and copies ran while one was open for 1% of the time, Pallas kernels for 11%

profile of v6, /device:TPU:0, one launch (start us, length us, event | category | flops | bytes accessed | tf_op | source)
XLA Modules:
  0.0 248.2 jit_solution(6888397626180801333)
XLA Ops:
  0.0 2.6 %pack.1 = (bf16[3,224,256]{2,1,0:T(8,128)(2,1)}, bf16[3,224,256]{2,1,0:T(8,128)(2,1)}, bf16[3,224,256]{2,1,0:T(8,128)(2,1)}, bf16[3,224,256]{2,1,0:T(8,128)(2,1)}) custom-call(s32[1]{0:T(128)} %bitcast.me_ref, bf16[224,1024]{1,0:T(8,128)(2,1)} %bitcast.31, bf16[224,1024]{1,0:T(8,128)(2,1)} %bitcast.32, bf16[224,1024]{1,0:T(8,128)(2,1)} %bitcast.33), custom_call_target="tpu_custom_call" | custom-call | flops 1100000000 | tf_op jit(solution)/shard_map/pack/pallas_call | solution.py:345
  2.6 3.1 %collective-permute-start = (bf16[3,224,256]{2,1,0:T(8,128)(2,1)}, bf16[3,224,256]{2,1,0:T(8,128)(2,1)S(1)}, u32[]{:S(2)}, u32[]{:S(2)}) collective-permute-start(bf16[3,224,256]{2,1,0:T(8,128)(2,1)} %get-tuple-element.55), channel_id=1, source_target_pairs={{0,1},{1,0},{2,3},{3,2},{4,5},{5,4},{6,7},{7,6},{8,9},{9,8},{10,11... | collective-permute-start | bytes 1032200 | tf_op jit(solution)/shard_map/ppermute | solution.py:308
  5.7 2.6 %collective-permute-start.1 = (bf16[3,224,256]{2,1,0:T(8,128)(2,1)}, bf16[3,224,256]{2,1,0:T(8,128)(2,1)S(1)}, u32[]{:S(2)}, u32[]{:S(2)}) collective-permute-start(bf16[3,224,256]{2,1,0:T(8,128)(2,1)} %get-tuple-element.56), channel_id=1, source_target_pairs={{0,2},{1,3},{2,0},{3,1},{4,6},{5,7},{6,4},{7,5},{8,10},{9,11},{10,... | collective-permute-start | bytes 1032200 | tf_op jit(solution)/shard_map/ppermute | solution.py:308
  8.4 12.2 %collective-permute-done.refs_1_ = bf16[3,224,256]{2,1,0:T(8,128)(2,1)S(1)} collective-permute-done((bf16[3,224,256]{2,1,0:T(8,128)(2,1)}, bf16[3,224,256]{2,1,0:T(8,128)(2,1)S(1)}, u32[]{:S(2)}, u32[]{:S(2)}) %collective-permute-start) | collective-permute-done | bytes 344096 | tf_op jit(solution)/shard_map/ppermute | solution.py:308
  20.6 12.0 %collective-permute-done.1.refs_2_ = bf16[3,224,256]{2,1,0:T(8,128)(2,1)S(1)} collective-permute-done((bf16[3,224,256]{2,1,0:T(8,128)(2,1)}, bf16[3,224,256]{2,1,0:T(8,128)(2,1)S(1)}, u32[]{:S(2)}, u32[]{:S(2)}) %collective-permute-start.1) | collective-permute-done | bytes 344096 | tf_op jit(solution)/shard_map/ppermute | solution.py:308
  33.5 5.5 %attend.1 = (bf16[256,256]{1,0:T(8,128)(2,1)S(1)}, bf16[256,256]{1,0:T(8,128)(2,1)S(1)}, bf16[256,256]{1,0:T(8,128)(2,1)S(1)}, bf16[256,256]{1,0:T(8,128)(2,1)S(...) custom-call(s32[1]{0:T(128)} %bitcast.me_ref, ...), custom_call_target="tpu_custom_call" | custom-call | flops 6600000000 | tf_op jit(solution)/shard_map/attend/pallas_call | solution.py:362
  39.7 6.5 %collective-permute-start.3 = (bf16[256,256]{1,0:T(8,128)(2,1)S(1)}, bf16[256,256]{1,0:T(8,128)(2,1)S(1)}, u32[]{:S(2)}, u32[]{:S(2)}) collective-permute-start(bf16[256,256]{1,0:T(8,128)(2,1)S(1)} %get-tuple-element.59), channel_id=1, source_target_pairs={{0,1},{1,0},{2,3},{3,2},{4,5},{5,4},{6,7},{7,6},{8,9},{9,8},{10,11... | collective-permute-start | bytes 393224 | tf_op jit(solution)/shard_map/ppermute | solution.py:308
  51.1 6.9 %collective-permute-done.4.refs_2_ = bf16[256,256]{1,0:T(8,128)(2,1)S(1)} collective-permute-done((bf16[256,256]{1,0:T(8,128)(2,1)S(1)}, bf16[256,256]{1,0:T(8,128)(2,1)S(1)}, u32[]{:S(2)}, u32[]{:S(2)}) %collective-permute-start.4) | collective-permute-done | bytes 131104 | tf_op jit(solution)/shard_map/ppermute | solution.py:308
  61.3 2.3 collective-permute-start.8
  65.7 35.8 %collective-permute-done.6 = s32[224,2]{0,1:T(2,128)S(1)} collective-permute-done((s32[224,2]{0,1:T(2,128)S(1)}, s32[224,2]{0,1:T(2,128)S(1)}, u32[]{:S(2)}, u32[]{:S(2)}) %collective-permute-start.6) | collective-permute-done | bytes 1824 | tf_op jit(solution)/shard_map/ppermute | solution.py:357
  101.7 3.5 %collective-permute-done.9.refs_3_ = bf16[256,256]{1,0:T(8,128)(2,1)S(1)} collective-permute-done((bf16[256,256]{1,0:T(8,128)(2,1)S(1)}, bf16[256,256]{1,0:T(8,128)(2,1)S(1)}, u32[]{:S(2)}, u32[]{:S(2)}) %collective-permute-start.9) | collective-permute-done | bytes 131104 | tf_op jit(solution)/shard_map/ppermute | solution.py:308
  105.1 1.9 copy-done.13
  107.0 9.0 %frames.2 = (bf16[704,1536]{1,0:T(8,128)(2,1)}, f32[224,128]{1,0:T(8,128)S(1)}, f32[12,224,128]{2,1,0:T(8,128)}) custom-call(s32[1]{0:T(128)} %bitcast.me_ref, s32[1]{0:T(128)} %bitcast.1.expert_ref, s32[1,4]{1,0:T(1,128)S(1)} %copy-done.49, bf16[1024,1536]{1,0:T(8,128)(2,1)S(1)} %copy-done.13, f32[12,31,128]{2,1,0:T(8,128)S(1)} %bitcast.22, ...), custom_call_target="tpu_custom_call" | custom-call | flops 11000000512 | tf_op jit(solution)/shard_map/frames/pallas_call | solution.py:406
  116.7 3.7 %all-to-all-start = ((bf16[8,88,1536]{2,1,0:T(8,128)(2,1)}), bf16[8,88,1536]{2,1,0:T(8,128)(2,1)S(1)}, u32[]{:S(2)}, u32[]{:S(2)}) async-start(bf16[8,88,1536]{2,1,0:T(8,128)(2,1)} %bitcast.11), calls=%async_computation | async-start | bytes 4325376 | tf_op jit(solution)/shard_map/all_to_all | solution.py:401
  120.4 2.4 collective-permute-start.18
  126.5 1.9 copy-done.14
  132.0 10.6 %frames.3 = (bf16[88,1536]{1,0:T(8,128)(2,1)S(1)}, bf16[88,1536]{1,0:T(8,128)(2,1)S(1)}, bf16[88,1536]{1,0:T(8,128)(2,1)S(1)}, bf16[88,1536]{1,0:T(8,128)(2,1)S(...) custom-call(s32[1]{0:T(128)} %bitcast.me_ref, ...), custom_call_target="tpu_custom_call" | custom-call | flops 11000000512 | tf_op jit(solution)/shard_map/frames/pallas_call | solution.py:406
  148.3 4.9 %collective-permute-done.12.refs_2_ = bf16[88,1536]{1,0:T(8,128)(2,1)S(1)} collective-permute-done((bf16[88,1536]{1,0:T(8,128)(2,1)S(1)}, bf16[88,1536]{1,0:T(8,128)(2,1)S(1)}, u32[]{:S(2)}, u32[]{:S(2)}) %collective-permute-start.12) | collective-permute-done | bytes 270368 | tf_op jit(solution)/shard_map/ppermute | solution.py:308
  153.9 2.2 collective-permute-start.16
  156.2 2.1 collective-permute-done.13.refs_3_
  159.0 2.7 %collective-permute-start.17 = (bf16[88,1536]{1,0:T(8,128)(2,1)S(1)}, bf16[88,1536]{1,0:T(8,128)(2,1)S(1)}, u32[]{:S(2)}, u32[]{:S(2)}) collective-permute-start(bf16[88,1536]{1,0:T(8,128)(2,1)S(1)} %get-tuple-element.83), channel_id=1, source_target_pairs={{0,28},{4,24},{8,20},{12,16},{16,12},{20,8},{24,4},{28,0},{1,29},{... | collective-permute-start | bytes 811016 | tf_op jit(solution)/shard_map/ppermute | solution.py:308
  162.4 9.1 %collective-permute-done.15.refs_5_ = bf16[88,1536]{1,0:T(8,128)(2,1)S(1)} collective-permute-done((bf16[88,1536]{1,0:T(8,128)(2,1)S(1)}, bf16[88,1536]{1,0:T(8,128)(2,1)S(1)}, u32[]{:S(2)}, u32[]{:S(2)}) %collective-permute-start.15) | collective-permute-done | bytes 270368 | tf_op jit(solution)/shard_map/ppermute | solution.py:308
  175.2 7.3 %experts.2 = bf16[704,1536]{1,0:T(8,128)(2,1)S(1)} custom-call(bf16[704,1536]{1,0:T(8,128)(2,1)S(1)} %bitcast.19, bf16[512,1536]{1,0:T(8,128)(2,1)} %bitcast.9.refs_1_.refs_8_, bf16[512,1536]{1,0:T(8,128)(2,1)} %collective-permute-done.10.refs_2_.refs_9_, bf16[512,1536]{1,0:T(8,128)(2,1)S(1)} %bitcast.29, ...), custom_call_target="tpu_custom_call" | custom-call | flops 8800000000 | tf_op jit(solution)/shard_map/experts/pallas_call | solution.py:429
  183.8 3.6 %all-to-all-start.1 = ((bf16[8,88,1536]{2,1,0:T(8,128)(2,1)}), bf16[8,88,1536]{2,1,0:T(8,128)(2,1)S(1)}, u32[]{:S(2)}, u32[]{:S(2)}) async-start(bf16[8,88,1536]{2,1,0:T(8,128)(2,1)} %bitcast.21), calls=%async_computation.1 | async-start | bytes 4325376 | tf_op jit(solution)/shard_map/all_to_all | solution.py:401
  196.5 7.3 %experts.3 = (bf16[88,1536]{1,0:T(8,128)(2,1)S(1)}, bf16[88,1536]{1,0:T(8,128)(2,1)S(1)}, bf16[88,1536]{1,0:T(8,128)(2,1)S(1)}, bf16[88,1536]{1,0:T(8,128)(2,1)S...) custom-call(bf16[88,1536]{1,0:T(8,128)(2,1)S(1)} %copy-done.54, ...), custom_call_target="tpu_custom_call" | custom-call | flops 8800000000 | tf_op jit(solution)/shard_map/experts/pallas_call | solution.py:429
  211.0 3.7 %all-to-all-done.1 = bf16[8,88,1536]{2,1,0:T(8,128)(2,1)S(1)} async-done(((bf16[8,88,1536]{2,1,0:T(8,128)(2,1)}), bf16[8,88,1536]{2,1,0:T(8,128)(2,1)S(1)}, u32[]{:S(2)}, u32[]{:S(2)}) %all-to-all-start.1) | async-done | bytes 2162720 | tf_op jit(solution)/shard_map/all_to_all | solution.py:401
  218.5 2.3 collective-permute-start.24
  220.8 5.9 %collective-permute-done.21.refs_2_ = bf16[88,1536]{1,0:T(8,128)(2,1)S(1)} collective-permute-done((bf16[88,1536]{1,0:T(8,128)(2,1)S(1)}, bf16[88,1536]{1,0:T(8,128)(2,1)S(1)}, u32[]{:S(2)}, u32[]{:S(2)}) %collective-permute-start.21) | collective-permute-done | bytes 270368 | tf_op jit(solution)/shard_map/ppermute | solution.py:308
  227.3 3.2 %collective-permute-done.22.refs_3_ = bf16[88,1536]{1,0:T(8,128)(2,1)S(1)} collective-permute-done((bf16[88,1536]{1,0:T(8,128)(2,1)S(1)}, bf16[88,1536]{1,0:T(8,128)(2,1)S(1)}, u32[]{:S(2)}, u32[]{:S(2)}) %collective-permute-start.22) | collective-permute-done | bytes 270368 | tf_op jit(solution)/shard_map/ppermute | solution.py:308
  230.5 2.3 collective-permute-start.26
  232.8 11.8 %collective-permute-done.24.refs_5_ = bf16[88,1536]{1,0:T(8,128)(2,1)S(1)} collective-permute-done((bf16[88,1536]{1,0:T(8,128)(2,1)S(1)}, bf16[88,1536]{1,0:T(8,128)(2,1)S(1)}, u32[]{:S(2)}, u32[]{:S(2)}) %collective-permute-start.24) | collective-permute-done | bytes 270368 | tf_op jit(solution)/shard_map/ppermute | solution.py:308
  244.6 1.9 collective-permute-done.20.part_ref
  (160 shorter events, 55.1 us)
Async XLA Ops:
  0.0 32.6 %copy-start.49 = (s32[1,4]{1,0:T(1,128)S(1)}, s32[1,4]{1,0:T(1,128)}, u32[]{:S(2)}) copy-start(s32[1,4]{1,0:T(1,128)} %len_ref.5) | copy-start | bytes 52
  2.6 18.0 %collective-permute-start = (bf16[3,224,256]{2,1,0:T(8,128)(2,1)}, bf16[3,224,256]{2,1,0:T(8,128)(2,1)S(1)}, u32[]{:S(2)}, u32[]{:S(2)}) collective-permute-start(bf16[3,224,256]{2,1,0:T(8,128)(2,1)} %get-tuple-element.55), channel_id=1, source_target_pairs={{0,1},{1,0},{2,3},{3,2},{4,5},{5,4},{6,7},{7,6},{8,9},{9,8},{10,11... | collective-permute-start | bytes 1032200 | tf_op jit(solution)/shard_map/ppermute | solution.py:308
  5.7 26.8 %collective-permute-start.1 = (bf16[3,224,256]{2,1,0:T(8,128)(2,1)}, bf16[3,224,256]{2,1,0:T(8,128)(2,1)S(1)}, u32[]{:S(2)}, u32[]{:S(2)}) collective-permute-start(bf16[3,224,256]{2,1,0:T(8,128)(2,1)} %get-tuple-element.56), channel_id=1, source_target_pairs={{0,2},{1,3},{2,0},{3,1},{4,6},{5,7},{6,4},{7,5},{8,10},{9,11},{10,... | collective-permute-start | bytes 1032200 | tf_op jit(solution)/shard_map/ppermute | solution.py:308
  8.3 24.3 %collective-permute-start.2 = (bf16[3,224,256]{2,1,0:T(8,128)(2,1)}, bf16[3,224,256]{2,1,0:T(8,128)(2,1)S(1)}, u32[]{:S(2)}, u32[]{:S(2)}) collective-permute-start(bf16[3,224,256]{2,1,0:T(8,128)(2,1)} %get-tuple-element.57), channel_id=1, source_target_pairs={{0,3},{1,2},{2,1},{3,0},{4,7},{5,6},{6,5},{7,4},{8,11},{9,10},{10,... | collective-permute-start | bytes 1032200 | tf_op jit(solution)/shard_map/ppermute | solution.py:308
  39.7 10.7 %collective-permute-start.3 = (bf16[256,256]{1,0:T(8,128)(2,1)S(1)}, bf16[256,256]{1,0:T(8,128)(2,1)S(1)}, u32[]{:S(2)}, u32[]{:S(2)}) collective-permute-start(bf16[256,256]{1,0:T(8,128)(2,1)S(1)} %get-tuple-element.59), channel_id=1, source_target_pairs={{0,1},{1,0},{2,3},{3,2},{4,5},{5,4},{6,7},{7,6},{8,9},{9,8},{10,11... | collective-permute-start | bytes 393224 | tf_op jit(solution)/shard_map/ppermute | solution.py:308
  46.2 11.8 %collective-permute-start.4 = (bf16[256,256]{1,0:T(8,128)(2,1)S(1)}, bf16[256,256]{1,0:T(8,128)(2,1)S(1)}, u32[]{:S(2)}, u32[]{:S(2)}) collective-permute-start(bf16[256,256]{1,0:T(8,128)(2,1)S(1)} %get-tuple-element.60), channel_id=1, source_target_pairs={{0,2},{1,3},{2,0},{3,1},{4,6},{5,7},{6,4},{7,5},{8,10},{9,11},{10,... | collective-permute-start | bytes 393224 | tf_op jit(solution)/shard_map/ppermute | solution.py:308
  47.2 11.4 %collective-permute-start.5 = (bf16[256,256]{1,0:T(8,128)(2,1)S(1)}, bf16[256,256]{1,0:T(8,128)(2,1)S(1)}, u32[]{:S(2)}, u32[]{:S(2)}) collective-permute-start(bf16[256,256]{1,0:T(8,128)(2,1)S(1)} %get-tuple-element.61), channel_id=1, source_target_pairs={{0,3},{1,2},{2,1},{3,0},{4,7},{5,6},{6,5},{7,4},{8,11},{9,10},{10,... | collective-permute-start | bytes 393224 | tf_op jit(solution)/shard_map/ppermute | solution.py:308
  59.3 64.3 %collective-permute-start.10 = (bf16[512,1536]{1,0:T(8,128)(2,1)}, bf16[512,1536]{1,0:T(8,128)(2,1)}, u32[]{:S(2)}, u32[]{:S(2)}) collective-permute-start(bf16[512,1536]{1,0:T(8,128)(2,1)} %bitcast.9.refs_1_.refs_8_), channel_id=1, source_target_pairs={{0,1},{1,0},{2,3},{3,2},{4,5},{5,4},{6,7},{7,6},{8,9},{9,8},{10,11... | collective-permute-start | bytes 4718600 | tf_op jit(solution)/shard_map/ppermute | solution.py:382
  60.6 41.0 %collective-permute-start.7 = (bf16[256,256]{1,0:T(8,128)(2,1)S(1)}, bf16[256,256]{1,0:T(8,128)(2,1)S(1)}, u32[]{:S(2)}, u32[]{:S(2)}) collective-permute-start(bf16[256,256]{1,0:T(8,128)(2,1)S(1)} %get-tuple-element.63), channel_id=1, source_target_pairs={{0,1},{1,0},{2,3},{3,2},{4,5},{5,4},{6,7},{7,6},{8,9},{9,8},{10,11... | collective-permute-start | bytes 393224 | tf_op jit(solution)/shard_map/ppermute | solution.py:308
  61.3 40.3 %collective-permute-start.8 = (bf16[256,256]{1,0:T(8,128)(2,1)S(1)}, bf16[256,256]{1,0:T(8,128)(2,1)S(1)}, u32[]{:S(2)}, u32[]{:S(2)}) collective-permute-start(bf16[256,256]{1,0:T(8,128)(2,1)S(1)} %get-tuple-element.64), channel_id=1, source_target_pairs={{0,2},{1,3},{2,0},{3,1},{4,6},{5,7},{6,4},{7,5},{8,10},{9,11},{10,... | collective-permute-start | bytes 393224 | tf_op jit(solution)/shard_map/ppermute | solution.py:308
  63.6 41.5 %collective-permute-start.9 = (bf16[256,256]{1,0:T(8,128)(2,1)S(1)}, bf16[256,256]{1,0:T(8,128)(2,1)S(1)}, u32[]{:S(2)}, u32[]{:S(2)}) collective-permute-start(bf16[256,256]{1,0:T(8,128)(2,1)S(1)} %get-tuple-element.65), channel_id=1, source_target_pairs={{0,3},{1,2},{2,1},{3,0},{4,7},{5,6},{6,5},{7,4},{8,11},{9,10},{10,... | collective-permute-start | bytes 393224 | tf_op jit(solution)/shard_map/ppermute | solution.py:308
  65.0 36.5 %collective-permute-start.6 = (s32[224,2]{0,1:T(2,128)S(1)}, s32[224,2]{0,1:T(2,128)S(1)}, u32[]{:S(2)}, u32[]{:S(2)}) collective-permute-start(s32[224,2]{0,1:T(2,128)S(1)} %bitcast.24), channel_id=1, source_target_pairs={{0,2},{1,3},{2,0},{3,1},{4,6},{5,7},{6,4},{7,5},{8,10},{9,11},{10,... | collective-permute-start | bytes 5384 | tf_op jit(solution)/shard_map/ppermute | solution.py:357
  65.5 50.6 %copy-start.7 = (f32[31,12,128]{2,0,1:T(8,128)}, f32[31,12,128]{2,0,1:T(8,128)S(1)}, u32[]{:S(2)}) copy-start(f32[31,12,128]{2,0,1:T(8,128)S(1)} %copy.22) | copy-start | bytes 571396
  65.7 50.4 %copy-start.1 = (bf16[1536,8]{1,0:T(8,128)(2,1)}, bf16[1536,8]{1,0:T(8,128)(2,1)S(1)}, u32[]{:S(2)}) copy-start(bf16[1536,8]{1,0:T(8,128)(2,1)S(1)} %copy.19.router_ref) | copy-start | bytes 73732
  116.7 57.0 %all-to-all-start = ((bf16[8,88,1536]{2,1,0:T(8,128)(2,1)}), bf16[8,88,1536]{2,1,0:T(8,128)(2,1)S(1)}, u32[]{:S(2)}, u32[]{:S(2)}) async-start(bf16[8,88,1536]{2,1,0:T(8,128)(2,1)} %bitcast.11), calls=%async_computation | async-start | bytes 4325376 | tf_op jit(solution)/shard_map/all_to_all | solution.py:401
  120.4 53.3 %collective-permute-start.18 = (bf16[512,1536]{1,0:T(8,128)(2,1)}, bf16[512,1536]{1,0:T(8,128)(2,1)}, u32[]{:S(2)}, u32[]{:S(2)}) collective-permute-start(bf16[512,1536]{1,0:T(8,128)(2,1)} %bitcast.28), channel_id=1, source_target_pairs={{0,1},{1,0},{2,3},{3,2},{4,5},{5,4},{6,7},{7,6},{8,9},{9,8},{10,11... | collective-permute-start | bytes 4718600 | tf_op jit(solution)/shard_map/ppermute | solution.py:383
  144.0 3.2 %collective-permute-start.11 = (bf16[88,1536]{1,0:T(8,128)(2,1)S(1)}, bf16[88,1536]{1,0:T(8,128)(2,1)S(1)}, u32[]{:S(2)}, u32[]{:S(2)}) collective-permute-start(bf16[88,1536]{1,0:T(8,128)(2,1)S(1)} %get-tuple-element.77), channel_id=1, source_target_pairs={{0,4},{4,0},{8,12},{12,8},{16,20},{20,16},{24,28},{28,24},{1,5},{5... | collective-permute-start | bytes 811016 | tf_op jit(solution)/shard_map/ppermute | solution.py:308
  144.0 9.3 %collective-permute-start.12 = (bf16[88,1536]{1,0:T(8,128)(2,1)S(1)}, bf16[88,1536]{1,0:T(8,128)(2,1)S(1)}, u32[]{:S(2)}, u32[]{:S(2)}) collective-permute-start(bf16[88,1536]{1,0:T(8,128)(2,1)S(1)} %get-tuple-element.78), channel_id=1, source_target_pairs={{0,8},{4,12},{8,0},{12,4},{16,24},{20,28},{24,16},{28,20},{1,9},{5... | collective-permute-start | bytes 811016 | tf_op jit(solution)/shard_map/ppermute | solution.py:308
  144.0 14.3 %collective-permute-start.13 = (bf16[88,1536]{1,0:T(8,128)(2,1)S(1)}, bf16[88,1536]{1,0:T(8,128)(2,1)S(1)}, u32[]{:S(2)}, u32[]{:S(2)}) collective-permute-start(bf16[88,1536]{1,0:T(8,128)(2,1)S(1)} %get-tuple-element.79), channel_id=1, source_target_pairs={{0,12},{4,8},{8,4},{12,0},{16,28},{20,24},{24,20},{28,16},{1,13},{... | collective-permute-start | bytes 811016 | tf_op jit(solution)/shard_map/ppermute | solution.py:308
  145.8 15.9 %collective-permute-start.14 = (bf16[88,1536]{1,0:T(8,128)(2,1)S(1)}, bf16[88,1536]{1,0:T(8,128)(2,1)S(1)}, u32[]{:S(2)}, u32[]{:S(2)}) collective-permute-start(bf16[88,1536]{1,0:T(8,128)(2,1)S(1)} %get-tuple-element.80), channel_id=1, source_target_pairs={{0,16},{4,20},{8,24},{12,28},{16,0},{20,4},{24,8},{28,12},{1,17},{... | collective-permute-start | bytes 811016 | tf_op jit(solution)/shard_map/ppermute | solution.py:308
  147.9 23.6 %collective-permute-start.15 = (bf16[88,1536]{1,0:T(8,128)(2,1)S(1)}, bf16[88,1536]{1,0:T(8,128)(2,1)S(1)}, u32[]{:S(2)}, u32[]{:S(2)}) collective-permute-start(bf16[88,1536]{1,0:T(8,128)(2,1)S(1)} %get-tuple-element.81), channel_id=1, source_target_pairs={{0,20},{4,16},{8,28},{12,24},{16,4},{20,0},{24,12},{28,8},{1,21},{... | collective-permute-start | bytes 811016 | tf_op jit(solution)/shard_map/ppermute | solution.py:308
  153.9 18.3 %collective-permute-start.16 = (bf16[88,1536]{1,0:T(8,128)(2,1)S(1)}, bf16[88,1536]{1,0:T(8,128)(2,1)S(1)}, u32[]{:S(2)}, u32[]{:S(2)}) collective-permute-start(bf16[88,1536]{1,0:T(8,128)(2,1)S(1)} %get-tuple-element.82), channel_id=1, source_target_pairs={{0,24},{4,28},{8,16},{12,20},{16,8},{20,12},{24,0},{28,4},{1,25},{... | collective-permute-start | bytes 811016 | tf_op jit(solution)/shard_map/ppermute | solution.py:308
  159.0 14.1 %collective-permute-start.17 = (bf16[88,1536]{1,0:T(8,128)(2,1)S(1)}, bf16[88,1536]{1,0:T(8,128)(2,1)S(1)}, u32[]{:S(2)}, u32[]{:S(2)}) collective-permute-start(bf16[88,1536]{1,0:T(8,128)(2,1)S(1)} %get-tuple-element.83), channel_id=1, source_target_pairs={{0,28},{4,24},{8,20},{12,16},{16,12},{20,8},{24,4},{28,0},{1,29},{... | collective-permute-start | bytes 811016 | tf_op jit(solution)/shard_map/ppermute | solution.py:308
  183.8 30.9 %all-to-all-start.1 = ((bf16[8,88,1536]{2,1,0:T(8,128)(2,1)}), bf16[8,88,1536]{2,1,0:T(8,128)(2,1)S(1)}, u32[]{:S(2)}, u32[]{:S(2)}) async-start(bf16[8,88,1536]{2,1,0:T(8,128)(2,1)} %bitcast.21), calls=%async_computation.1 | async-start | bytes 4325376 | tf_op jit(solution)/shard_map/all_to_all | solution.py:401
  208.8 1.6 collective-permute-start.19
  216.5 29.9 %collective-permute-start.20 = (bf16[224,1536]{1,0:T(8,128)(2,1)S(1)}, bf16[224,1536]{1,0:T(8,128)(2,1)S(1)}, u32[]{:S(2)}, u32[]{:S(2)}) collective-permute-start(bf16[224,1536]{1,0:T(8,128)(2,1)S(1)} %theirs.1), channel_id=1, source_target_pairs={{0,2},{1,3},{2,0},{3,1},{4,6},{5,7},{6,4},{7,5},{8,10},{9,11},{10,... | collective-permute-start | bytes 2064392 | tf_op jit(solution)/shard_map/ppermute | solution.py:460
  217.3 9.4 %collective-permute-start.21 = (bf16[88,1536]{1,0:T(8,128)(2,1)S(1)}, bf16[88,1536]{1,0:T(8,128)(2,1)S(1)}, u32[]{:S(2)}, u32[]{:S(2)}) collective-permute-start(bf16[88,1536]{1,0:T(8,128)(2,1)S(1)} %copy-done.40), channel_id=1, source_target_pairs={{0,8},{4,12},{8,0},{12,4},{16,24},{20,28},{24,16},{28,20},{1,9},{5... | collective-permute-start | bytes 811016 | tf_op jit(solution)/shard_map/ppermute | solution.py:308
  217.8 12.7 %collective-permute-start.22 = (bf16[88,1536]{1,0:T(8,128)(2,1)S(1)}, bf16[88,1536]{1,0:T(8,128)(2,1)S(1)}, u32[]{:S(2)}, u32[]{:S(2)}) collective-permute-start(bf16[88,1536]{1,0:T(8,128)(2,1)S(1)} %copy-done.36), channel_id=1, source_target_pairs={{0,12},{4,8},{8,4},{12,0},{16,28},{20,24},{24,20},{28,16},{1,13},{... | collective-permute-start | bytes 811016 | tf_op jit(solution)/shard_map/ppermute | solution.py:308
  217.8 15.0 %collective-permute-start.23 = (bf16[88,1536]{1,0:T(8,128)(2,1)S(1)}, bf16[88,1536]{1,0:T(8,128)(2,1)S(1)}, u32[]{:S(2)}, u32[]{:S(2)}) collective-permute-start(bf16[88,1536]{1,0:T(8,128)(2,1)S(1)} %copy-done.32), channel_id=1, source_target_pairs={{0,16},{4,20},{8,24},{12,28},{16,0},{20,4},{24,8},{28,12},{1,17},{... | collective-permute-start | bytes 811016 | tf_op jit(solution)/shard_map/ppermute | solution.py:308
  218.5 26.1 %collective-permute-start.24 = (bf16[88,1536]{1,0:T(8,128)(2,1)S(1)}, bf16[88,1536]{1,0:T(8,128)(2,1)S(1)}, u32[]{:S(2)}, u32[]{:S(2)}) collective-permute-start(bf16[88,1536]{1,0:T(8,128)(2,1)S(1)} %copy-done.28), channel_id=1, source_target_pairs={{0,20},{4,16},{8,28},{12,24},{16,4},{20,0},{24,12},{28,8},{1,21},{... | collective-permute-start | bytes 811016 | tf_op jit(solution)/shard_map/ppermute | solution.py:308
  226.7 17.9 %collective-permute-start.25 = (bf16[88,1536]{1,0:T(8,128)(2,1)S(1)}, bf16[88,1536]{1,0:T(8,128)(2,1)S(1)}, u32[]{:S(2)}, u32[]{:S(2)}) collective-permute-start(bf16[88,1536]{1,0:T(8,128)(2,1)S(1)} %copy-done.24), channel_id=1, source_target_pairs={{0,24},{4,28},{8,16},{12,20},{16,8},{20,12},{24,0},{28,4},{1,25},{... | collective-permute-start | bytes 811016 | tf_op jit(solution)/shard_map/ppermute | solution.py:308
  230.5 14.1 %collective-permute-start.26 = (bf16[88,1536]{1,0:T(8,128)(2,1)S(1)}, bf16[88,1536]{1,0:T(8,128)(2,1)S(1)}, u32[]{:S(2)}, u32[]{:S(2)}) collective-permute-start(bf16[88,1536]{1,0:T(8,128)(2,1)S(1)} %copy-done.20), channel_id=1, source_target_pairs={{0,28},{4,24},{8,20},{12,16},{16,12},{20,8},{24,4},{28,0},{1,29},{... | collective-permute-start | bytes 811016 | tf_op jit(solution)/shard_map/ppermute | solution.py:308
  (57 other events, 269.7 us)

commit v7 on v6

--- a/solution.py
+++ b/solution.py
@@ -260,17 +260,18 @@
         ref[...] = values[e * tall : (e + 1) * tall].astype(BF16)
 
 
-def expert_kernel(chunks, pieces, *refs):
+def expert_kernel(chunks, spans, *refs):
     x_refs, o_refs = refs[:chunks], refs[-chunks:]
-    in_refs, out_refs = refs[chunks : chunks + pieces], refs[chunks + pieces : chunks + 2 * pieces]
+    in_refs, out_refs = refs[chunks : chunks + len(spans)], refs[chunks + len(spans) : -chunks]
     tokens = joined(x_refs)
     total = jnp.zeros((tokens.shape[0], D), F32)
-    for in_ref, out_ref in zip(in_refs, out_refs):
+    for in_ref, (place, begin) in zip(in_refs, spans):
         raw = lax.dot_general(
             tokens, in_ref[...], (((1,), (1,)), ((), ())), preferred_element_type=F32
         )
         hidden = (raw / (1.0 + jnp.exp(-raw))).astype(BF16)
-        total = total + jnp.dot(hidden, out_ref[...], preferred_element_type=F32)
+        matching = out_refs[place][begin : begin + in_ref.shape[0], :]
+        total = total + jnp.dot(hidden, matching, preferred_element_type=F32)
     scatter(o_refs, total)
 
 
@@ -376,15 +377,21 @@
     gathered_a = trade(attended[:count], "tm", direct)
     gathered_b = trade(attended[count:], "tm", direct)
 
-    early, late = after((expert_in[0], expert_out[0]), gathered_b)
+    shards = after((expert_in[0], expert_out[0]), gathered_a + gathered_b)
     if half == 2:
         swap = [(i, i ^ 1) for i in range(count)]
-        ins = [early, lax.ppermute(early, "tm", swap)]
-        outs = [late, lax.ppermute(late, "tm", swap)]
+        cut = expert_in.shape[1] // 2
+        pieces = (shards[0][:cut], shards[0][cut:], shards[1])
+        moved = [lax.ppermute(one, "tm", swap) for one in pieces]
+        ins, outs = [shards[0], moved[0], moved[1]], [shards[1], moved[2]]
+        spans = ((0, 0), (1, 0), (1, cut))
     else:
         groups = [list(range(i, i + half)) for i in (0, half)]
-        ins = [lax.all_gather(early, "tm", axis=0, tiled=True, axis_index_groups=groups)]
-        outs = [lax.all_gather(late, "tm", axis=0, tiled=True, axis_index_groups=groups)]
+        moved = [
+            lax.all_gather(one, "tm", axis=0, tiled=True, axis_index_groups=groups)
+            for one in shards
+        ]
+        ins, outs, spans = moved[:1], moved[1:], ((0, 0),)
 
     taps = jnp.transpose(conv_taps.reshape(KERNEL, D // LANES, LANES), (1, 0, 2))
     slots = experts * capacity
@@ -427,7 +434,7 @@
         split = len(tokens) > 1
         chunks = chunks_of(split)
         produced = pl.pallas_call(
-            functools.partial(expert_kernel, len(tokens), len(ins)),
+            functools.partial(expert_kernel, len(tokens), spans),
             out_shape=chunks,
             in_specs=[VMEM] * (len(tokens) + len(ins) + len(outs)),
             out_specs=(VMEM,) * len(chunks),
@@ -439,14 +446,13 @@
 
     outgoing_a, info_a, _ = send_frames(gathered_a, half, False, partner_routes)
     tokens_a = route(after(outgoing_a, gathered_b))
-    gathered_b = after(gathered_b, (outgoing_a[0], ins[-1]))
-    outgoing_b, info_b, second = send_frames(gathered_b, 0, True, routes[0])
+    gathered_b = after(gathered_b, (outgoing_a[0], moved[0]))
+    outgoing_b, info_b, second = send_frames(gathered_b, 0, False, routes[0])
     tokens_b = route(outgoing_b)
-    produced_a = run_expert(after(tokens_a, tokens_b))
-    back_a = route(produced_a)
+    produced_a = run_expert(tokens_a)
+    back_a = route(after(produced_a, tokens_b))
     produced_b = run_expert(after(tokens_b, produced_a))
-    back_b = route(produced_b)
-    back_a = after(back_a, back_b[1:2])
+    back_a = after(back_a, produced_b)
 
     theirs = pl.pallas_call(
         theirs_kernel,
@@ -458,6 +464,7 @@
         name="theirs",
     )(info_a, *back_a)
     received = lax.ppermute(theirs, "tm", partner)
+    back_b = route(after(produced_b, (theirs,)))
     out = pl.pallas_call(
         mine_kernel,
         out_shape=jax.ShapeDtypeStruct((rows, D), BF16),

time: 250 us -> 253 us (1.012)
  waiting for transfers between devices: 116 us -> 122 us
  local copies, waits for them, and re-layouts: 40.5 us -> 37.9 us
    ppermute x2 -> x3, waiting for transfers between devices: 0.01 us -> 42.2 us  [body(): moved = [lax.ppermute(one, 'tm', swap) for one in pieces]]
    ppermute x23 -> x9, waiting for transfers between devices: 74.5 us -> 37.9 us  [trade(): lax.ppermute(arrays[r], axis, [(i, i ^ r) for i in range(count)])]
    ppermute x1, waiting for transfers between devices: 35.8 us -> 0.01 us  [body(): partner_routes = lax.ppermute(routes[0], 'tm', partner)]
    ppermute x1, waiting for transfers between devices: 1.86 us -> 30.9 us  [body(): received = lax.ppermute(theirs, 'tm', partner)]
    ppermute x23 -> x9, starting transfers between devices: 34.5 us -> 21 us  [trade(): lax.ppermute(arrays[r], axis, [(i, i ^ r) for i in range(count)])]
    all_to_all x2 -> x4, starting transfers between devices: 7.33 us -> 16 us  [route(): moved = lax.all_to_all(whole, 'dp', split_axis=0, concat_axis=0, tiled=True)]
    all_to_all x2 -> x4, waiting for transfers between devices: 3.69 us -> 10.9 us  [route(): moved = lax.all_to_all(whole, 'dp', split_axis=0, concat_axis=0, tiled=True)]
    unnamed x121 -> x83, local copies, waits for them, and re-layouts: 39.5 us -> 34.2 us
  transfers between devices with their start and end apart: 29 -> 18, of which waited for: 15 -> 8; matrix products, arithmetic and copies ran while one was open for 1% -> 2% of each run, Pallas kernels for 11% -> 11%
where the time goes in v7:
time: 253 us; the launch traced here: 252 us
  waiting for transfers between devices  122 us (48%)
  Pallas kernels  46.8 us (18%)
  starting transfers between devices  44.8 us (18%)
  local copies, waits for them, and re-layouts  37.9 us (15%)
    ppermute x3, waiting for transfers between devices, body(): moved = [lax.ppermute(one, 'tm', swap) for one in pieces]  42.2 us
    ppermute x9, waiting for transfers between devices, trade(): lax.ppermute(arrays[r], axis, [(i, i ^ r) for i in range(count)])  37.9 us
    unnamed x83, local copies, waits for them, and re-layouts  34.2 us
    ppermute x1, waiting for transfers between devices, body(): received = lax.ppermute(theirs, 'tm', partner)  30.9 us
    ppermute x9, starting transfers between devices, trade(): lax.ppermute(arrays[r], axis, [(i, i ^ r) for i in range(count)])  21 us
    pallas_call x2, Pallas kernels, run_expert(): pl.pallas_call(functools.partial(expert_kernel, len(tokens), spans), out_...  19.4 us
    pallas_call x2, Pallas kernels, send_frames(): pl.pallas_call(functools.partial(frame_kernel, count, rows, experts, capa...  16.8 us
    all_to_all x4, starting transfers between devices, route(): moved = lax.all_to_all(whole, 'dp', split_axis=0, concat_axis=0, tiled=True)  16 us
  transfers between devices with their start and end apart: 18, of which 8 were waited for; matrix products, arithmetic and copies ran while one was open for 2% of the time, Pallas kernels for 11%

profile of v7, /device:TPU:0, one launch (start us, length us, event | category | flops | bytes accessed | tf_op | source)
XLA Modules:
  0.0 251.7 jit_solution(11195238766702214557)
XLA Ops:
  0.0 2.6 %pack.1 = (bf16[3,224,256]{2,1,0:T(8,128)(2,1)}, bf16[3,224,256]{2,1,0:T(8,128)(2,1)}, bf16[3,224,256]{2,1,0:T(8,128)(2,1)}, bf16[3,224,256]{2,1,0:T(8,128)(2,1)}) custom-call(s32[1]{0:T(128)} %bitcast.me_ref, bf16[224,1024]{1,0:T(8,128)(2,1)} %bitcast.42, bf16[224,1024]{1,0:T(8,128)(2,1)} %bitcast.43, bf16[224,1024]{1,0:T(8,128)(2,1)} %bitcast.44), custom_call_target="tpu_custom_call" | custom-call | flops 1100000000 | tf_op jit(solution)/shard_map/pack/pallas_call | solution.py:346
  2.6 3.1 %collective-permute-start = (bf16[3,224,256]{2,1,0:T(8,128)(2,1)}, bf16[3,224,256]{2,1,0:T(8,128)(2,1)S(1)}, u32[]{:S(2)}, u32[]{:S(2)}) collective-permute-start(bf16[3,224,256]{2,1,0:T(8,128)(2,1)} %get-tuple-element.34), channel_id=1, source_target_pairs={{0,1},{1,0},{2,3},{3,2},{4,5},{5,4},{6,7},{7,6},{8,9},{9,8},{10,11... | collective-permute-start | bytes 1032200 | tf_op jit(solution)/shard_map/ppermute | solution.py:309
  5.7 2.6 %collective-permute-start.1 = (bf16[3,224,256]{2,1,0:T(8,128)(2,1)}, bf16[3,224,256]{2,1,0:T(8,128)(2,1)S(1)}, u32[]{:S(2)}, u32[]{:S(2)}) collective-permute-start(bf16[3,224,256]{2,1,0:T(8,128)(2,1)} %get-tuple-element.35), channel_id=1, source_target_pairs={{0,2},{1,3},{2,0},{3,1},{4,6},{5,7},{6,4},{7,5},{8,10},{9,11},{10,... | collective-permute-start | bytes 1032200 | tf_op jit(solution)/shard_map/ppermute | solution.py:309
  8.4 12.2 %collective-permute-done.refs_1_ = bf16[3,224,256]{2,1,0:T(8,128)(2,1)S(1)} collective-permute-done((bf16[3,224,256]{2,1,0:T(8,128)(2,1)}, bf16[3,224,256]{2,1,0:T(8,128)(2,1)S(1)}, u32[]{:S(2)}, u32[]{:S(2)}) %collective-permute-start) | collective-permute-done | bytes 344096 | tf_op jit(solution)/shard_map/ppermute | solution.py:309
  20.6 12.0 %collective-permute-done.1.refs_2_ = bf16[3,224,256]{2,1,0:T(8,128)(2,1)S(1)} collective-permute-done((bf16[3,224,256]{2,1,0:T(8,128)(2,1)}, bf16[3,224,256]{2,1,0:T(8,128)(2,1)S(1)}, u32[]{:S(2)}, u32[]{:S(2)}) %collective-permute-start.1) | collective-permute-done | bytes 344096 | tf_op jit(solution)/shard_map/ppermute | solution.py:309
  33.5 5.5 %attend.1 = (bf16[256,256]{1,0:T(8,128)(2,1)S(1)}, bf16[256,256]{1,0:T(8,128)(2,1)S(1)}, bf16[256,256]{1,0:T(8,128)(2,1)S(1)}, bf16[256,256]{1,0:T(8,128)(2,1)S(...) custom-call(s32[1]{0:T(128)} %bitcast.me_ref, ...), custom_call_target="tpu_custom_call" | custom-call | flops 6600000000 | tf_op jit(solution)/shard_map/attend/pallas_call | solution.py:363
  39.7 6.5 %collective-permute-start.3 = (bf16[256,256]{1,0:T(8,128)(2,1)S(1)}, bf16[256,256]{1,0:T(8,128)(2,1)S(1)}, u32[]{:S(2)}, u32[]{:S(2)}) collective-permute-start(bf16[256,256]{1,0:T(8,128)(2,1)S(1)} %get-tuple-element.38), channel_id=1, source_target_pairs={{0,1},{1,0},{2,3},{3,2},{4,5},{5,4},{6,7},{7,6},{8,9},{9,8},{10,11... | collective-permute-start | bytes 393224 | tf_op jit(solution)/shard_map/ppermute | solution.py:309
  47.2 1.9 collective-permute-start.4
  49.1 2.5 collective-permute-start.5
  51.6 1.9 collective-permute-start.8
  53.5 2.5 collective-permute-start.9
  56.5 3.9 %collective-permute-done.4.refs_2_ = bf16[256,256]{1,0:T(8,128)(2,1)S(1)} collective-permute-done((bf16[256,256]{1,0:T(8,128)(2,1)S(1)}, bf16[256,256]{1,0:T(8,128)(2,1)S(1)}, u32[]{:S(2)}, u32[]{:S(2)}) %collective-permute-start.4) | collective-permute-done | bytes 131104 | tf_op jit(solution)/shard_map/ppermute | solution.py:309
  60.5 9.8 %collective-permute-done.8.refs_2_ = bf16[256,256]{1,0:T(8,128)(2,1)S(1)} collective-permute-done((bf16[256,256]{1,0:T(8,128)(2,1)S(1)}, bf16[256,256]{1,0:T(8,128)(2,1)S(1)}, u32[]{:S(2)}, u32[]{:S(2)}) %collective-permute-start.8) | collective-permute-done | bytes 131104 | tf_op jit(solution)/shard_map/ppermute | solution.py:309
  70.3 1.9 copy-done.16
  72.2 7.6 %frames.2 = (bf16[704,1536]{1,0:T(8,128)(2,1)S(1)}, f32[224,128]{1,0:T(8,128)S(1)}, f32[12,224,128]{2,1,0:T(8,128)}) custom-call(s32[1]{0:T(128)} %bitcast.me_ref, s32[1]{0:T(128)} %bitcast.1.expert_ref, s32[1,4]{1,0:T(1,128)S(1)} %copy-done.32, bf16[1024,1536]{1,0:T(8,128)(2,1)S(1)} %copy-done.16, f32[12,31,128]{2,1,0:T(8,128)S(1)} %bitcast.33, ...), custom_call_target="tpu_custom_call" | custom-call | flops 11000000512 | tf_op jit(solution)/shard_map/frames/pallas_call | solution.py:413
  81.8 3.7 %all-to-all-start = ((bf16[8,88,1536]{2,1,0:T(8,128)(2,1)}), bf16[8,88,1536]{2,1,0:T(8,128)(2,1)S(1)}, u32[]{:S(2)}, u32[]{:S(2)}) async-start(bf16[8,88,1536]{2,1,0:T(8,128)(2,1)} %bitcast.25), calls=%async_computation | async-start | bytes 4325376 | tf_op jit(solution)/shard_map/all_to_all | solution.py:408
  85.5 2.6 %fusion = (bf16[256,1536]{1,0:T(8,128)(2,1)}, bf16[256,1536]{1,0:T(8,128)(2,1)}) fusion(bf16[512,1536]{1,0:T(8,128)(2,1)} %bitcast.30), kind=kLoop, calls=%fused_computation.1 | loop fusion | bytes 3145728 | tf_op jit(solution)/shard_map/slice | solution.py:384
  88.1 3.4 %collective-permute-start.10 = (bf16[256,1536]{1,0:T(8,128)(2,1)}, bf16[256,1536]{1,0:T(8,128)(2,1)S(1)}, u32[]{:S(2)}, u32[]{:S(2)}) collective-permute-start(bf16[256,1536]{1,0:T(8,128)(2,1)} %get-tuple-element.62), channel_id=1, source_target_pairs={{0,1},{1,0},{2,3},{3,2},{4,5},{5,4},{6,7},{7,6},{8,9},{9,8},{10,11... | collective-permute-start | bytes 2359304 | tf_op jit(solution)/shard_map/ppermute | solution.py:385
  92.3 17.8 %collective-permute-done.10.refs_2_ = bf16[256,1536]{1,0:T(8,128)(2,1)S(1)} collective-permute-done((bf16[256,1536]{1,0:T(8,128)(2,1)}, bf16[256,1536]{1,0:T(8,128)(2,1)S(1)}, u32[]{:S(2)}, u32[]{:S(2)}) %collective-permute-start.10) | collective-permute-done | bytes 786464 | tf_op jit(solution)/shard_map/ppermute | solution.py:385
  113.9 1.9 copy-done.17
  119.4 9.2 %frames.3 = (bf16[704,1536]{1,0:T(8,128)(2,1)S(1)}, f32[224,128]{1,0:T(8,128)S(1)}, f32[12,224,128]{2,1,0:T(8,128)S(1)}) custom-call(s32[1]{0:T(128)} %bitcast.me_ref, s32[1]{0:T(128)} %bitcast.1.expert_ref, s32[1,4]{1,0:T(1,128)S(1)} %copy-done.32, bf16[1024,1536]{1,0:T(8,128)(2,1)S(1)} %copy-done.17, f32[12,31,128]{2,1,0:T(8,128)S(1)} %bitcast.34, ...), custom_call_target="tpu_custom_call" | custom-call | flops 11000000512 | tf_op jit(solution)/shard_map/frames/pallas_call | solution.py:413
  130.6 4.8 %all-to-all-start.1 = ((bf16[8,88,1536]{2,1,0:T(8,128)(2,1)}), bf16[8,88,1536]{2,1,0:T(8,128)(2,1)}, u32[]{:S(2)}, u32[]{:S(2)}) async-start(bf16[8,88,1536]{2,1,0:T(8,128)(2,1)} %bitcast.26), calls=%async_computation.1 | async-start | bytes 4325376 | tf_op jit(solution)/shard_map/all_to_all | solution.py:408
  136.1 24.4 %collective-permute-done.11.refs_3_ = bf16[256,1536]{1,0:T(8,128)(2,1)S(1)} collective-permute-done((bf16[256,1536]{1,0:T(8,128)(2,1)}, bf16[256,1536]{1,0:T(8,128)(2,1)S(1)}, u32[]{:S(2)}, u32[]{:S(2)}) %collective-permute-start.11) | collective-permute-done | bytes 786464 | tf_op jit(solution)/shard_map/ppermute | solution.py:385
  160.5 1.4 copy-done.4
  164.5 9.4 %experts.2 = bf16[704,1536]{1,0:T(8,128)(2,1)S(1)} custom-call(bf16[704,1536]{1,0:T(8,128)(2,1)S(1)} %bitcast.24, bf16[512,1536]{1,0:T(8,128)(2,1)S(1)} %bitcast.31, bf16[256,1536]{1,0:T(8,128)(2,1)S(1)} %copy-done.21, bf16[256,1536]{1,0:T(8,128)(2,1)S(1)} %collective-permute-done.11.refs_3_, bf16[512,1536]{1,0:T(8,128)(2,1)S(1)} %bitcast.40, ...), custom_call_target="tpu_custom_call" | custom-call | flops 8800000000 | tf_op jit(solution)/shard_map/experts/pallas_call | solution.py:436
  176.1 3.8 %all-to-all-start.2 = ((bf16[8,88,1536]{2,1,0:T(8,128)(2,1)}), bf16[8,88,1536]{2,1,0:T(8,128)(2,1)S(1)}, u32[]{:S(2)}, u32[]{:S(2)}) async-start(bf16[8,88,1536]{2,1,0:T(8,128)(2,1)} %bitcast.29), calls=%async_computation.2 | async-start | bytes 4325376 | tf_op jit(solution)/shard_map/all_to_all | solution.py:408
  185.0 10.0 %experts.3 = bf16[704,1536]{1,0:T(8,128)(2,1)S(1)} custom-call(bf16[704,1536]{1,0:T(8,128)(2,1)} %bitcast.14.refs_0_, bf16[512,1536]{1,0:T(8,128)(2,1)S(1)} %bitcast.32, bf16[256,1536]{1,0:T(8,128)(2,1)S(1)} %copy-done.22, bf16[256,1536]{1,0:T(8,128)(2,1)S(1)} %copy-done.24, bf16[512,1536]{1,0:T(8,128)(2,1)S(1)} %bitcast.41, ...), custom_call_target="tpu_custom_call" | custom-call | flops 8800000000 | tf_op jit(solution)/shard_map/experts/pallas_call | solution.py:436
  196.4 10.9 %all-to-all-done.2 = bf16[8,88,1536]{2,1,0:T(8,128)(2,1)S(1)} async-done(((bf16[8,88,1536]{2,1,0:T(8,128)(2,1)}), bf16[8,88,1536]{2,1,0:T(8,128)(2,1)S(1)}, u32[]{:S(2)}, u32[]{:S(2)}) %all-to-all-start.2) | async-done | bytes 2162720 | tf_op jit(solution)/shard_map/all_to_all | solution.py:408
  209.9 3.6 %all-to-all-start.3 = ((bf16[8,88,1536]{2,1,0:T(8,128)(2,1)}), bf16[8,88,1536]{2,1,0:T(8,128)(2,1)S(1)}, u32[]{:S(2)}, u32[]{:S(2)}) async-start(bf16[8,88,1536]{2,1,0:T(8,128)(2,1)} %bitcast.27), calls=%async_computation.3 | async-start | bytes 4325376 | tf_op jit(solution)/shard_map/all_to_all | solution.py:408
  213.5 2.8 %collective-permute-start.13 = (bf16[224,1536]{1,0:T(8,128)(2,1)}, bf16[224,1536]{1,0:T(8,128)(2,1)S(1)}, u32[]{:S(2)}, u32[]{:S(2)}) collective-permute-start(bf16[224,1536]{1,0:T(8,128)(2,1)} %copy-done.25), channel_id=1, source_target_pairs={{0,2},{1,3},{2,0},{3,1},{4,6},{5,7},{6,4},{7,5},{8,10},{9,11},{10,... | collective-permute-start | bytes 2064392 | tf_op jit(solution)/shard_map/ppermute | solution.py:466
  216.3 30.9 %collective-permute-done.13.part_ref = bf16[224,1536]{1,0:T(8,128)(2,1)S(1)} collective-permute-done((bf16[224,1536]{1,0:T(8,128)(2,1)}, bf16[224,1536]{1,0:T(8,128)(2,1)S(1)}, u32[]{:S(2)}, u32[]{:S(2)}) %collective-permute-start.13) | collective-permute-done | bytes 688160 | tf_op jit(solution)/shard_map/ppermute | solution.py:466
  250.0 1.7 mine.1
  (101 shorter events, 32.6 us)
Async XLA Ops:
  0.0 8.3 %copy-start.40 = (f32[16]{0:T(128)S(1)}, f32[16]{0:T(128)}, u32[]{:S(2)}) copy-start(f32[16]{0:T(128)} %param.14) | copy-start | bytes 196
  0.0 32.5 %copy-start.32 = (s32[1,4]{1,0:T(1,128)S(1)}, s32[1,4]{1,0:T(1,128)}, u32[]{:S(2)}) copy-start(s32[1,4]{1,0:T(1,128)} %len_ref.5) | copy-start | bytes 52
  2.6 18.0 %collective-permute-start = (bf16[3,224,256]{2,1,0:T(8,128)(2,1)}, bf16[3,224,256]{2,1,0:T(8,128)(2,1)S(1)}, u32[]{:S(2)}, u32[]{:S(2)}) collective-permute-start(bf16[3,224,256]{2,1,0:T(8,128)(2,1)} %get-tuple-element.34), channel_id=1, source_target_pairs={{0,1},{1,0},{2,3},{3,2},{4,5},{5,4},{6,7},{7,6},{8,9},{9,8},{10,11... | collective-permute-start | bytes 1032200 | tf_op jit(solution)/shard_map/ppermute | solution.py:309
  5.7 26.8 %collective-permute-start.1 = (bf16[3,224,256]{2,1,0:T(8,128)(2,1)}, bf16[3,224,256]{2,1,0:T(8,128)(2,1)S(1)}, u32[]{:S(2)}, u32[]{:S(2)}) collective-permute-start(bf16[3,224,256]{2,1,0:T(8,128)(2,1)} %get-tuple-element.35), channel_id=1, source_target_pairs={{0,2},{1,3},{2,0},{3,1},{4,6},{5,7},{6,4},{7,5},{8,10},{9,11},{10,... | collective-permute-start | bytes 1032200 | tf_op jit(solution)/shard_map/ppermute | solution.py:309
  8.3 24.3 %collective-permute-start.2 = (bf16[3,224,256]{2,1,0:T(8,128)(2,1)}, bf16[3,224,256]{2,1,0:T(8,128)(2,1)S(1)}, u32[]{:S(2)}, u32[]{:S(2)}) collective-permute-start(bf16[3,224,256]{2,1,0:T(8,128)(2,1)} %get-tuple-element.36), channel_id=1, source_target_pairs={{0,3},{1,2},{2,1},{3,0},{4,7},{5,6},{6,5},{7,4},{8,11},{9,10},{10,... | collective-permute-start | bytes 1032200 | tf_op jit(solution)/shard_map/ppermute | solution.py:309
  33.5 12.7 %copy-start.15 = (s32[1,224,2]{1,2,0:T(2,128)S(1)}, s32[1,224,2]{1,2,0:T(2,128)}, u32[]{:S(2)}) copy-start(s32[1,224,2]{1,2,0:T(2,128)} %param.21) | copy-start | bytes 5380
  33.5 22.5 %copy-start.38 = (f32[31,1536]{1,0:T(8,128)S(1)}, f32[31,1536]{1,0:T(8,128)}, u32[]{:S(2)}) copy-start(f32[31,1536]{1,0:T(8,128)} %param.16) | copy-start | bytes 571396
  33.5 22.6 %copy-start.39 = (bf16[1536,8]{0,1:T(8,128)(2,1)S(1)}, bf16[1536,8]{0,1:T(8,128)(2,1)}, u32[]{:S(2)}) copy-start(bf16[1536,8]{0,1:T(8,128)(2,1)} %param.17) | copy-start | bytes 73732
  39.7 13.8 %collective-permute-start.3 = (bf16[256,256]{1,0:T(8,128)(2,1)S(1)}, bf16[256,256]{1,0:T(8,128)(2,1)S(1)}, u32[]{:S(2)}, u32[]{:S(2)}) collective-permute-start(bf16[256,256]{1,0:T(8,128)(2,1)S(1)} %get-tuple-element.38), channel_id=1, source_target_pairs={{0,1},{1,0},{2,3},{3,2},{4,5},{5,4},{6,7},{7,6},{8,9},{9,8},{10,11... | collective-permute-start | bytes 393224 | tf_op jit(solution)/shard_map/ppermute | solution.py:309
  46.2 5.4 %collective-permute-start.6 = (s32[224,2]{0,1:T(2,128)S(1)}, s32[224,2]{0,1:T(2,128)S(1)}, u32[]{:S(2)}, u32[]{:S(2)}) collective-permute-start(s32[224,2]{0,1:T(2,128)S(1)} %bitcast.35), channel_id=1, source_target_pairs={{0,2},{1,3},{2,0},{3,1},{4,6},{5,7},{6,4},{7,5},{8,10},{9,11},{10,... | collective-permute-start | bytes 5384 | tf_op jit(solution)/shard_map/ppermute | solution.py:358
  47.2 13.2 %collective-permute-start.4 = (bf16[256,256]{1,0:T(8,128)(2,1)S(1)}, bf16[256,256]{1,0:T(8,128)(2,1)S(1)}, u32[]{:S(2)}, u32[]{:S(2)}) collective-permute-start(bf16[256,256]{1,0:T(8,128)(2,1)S(1)} %get-tuple-element.39), channel_id=1, source_target_pairs={{0,2},{1,3},{2,0},{3,1},{4,6},{5,7},{6,4},{7,5},{8,10},{9,11},{10,... | collective-permute-start | bytes 393224 | tf_op jit(solution)/shard_map/ppermute | solution.py:309
  49.1 11.3 %collective-permute-start.5 = (bf16[256,256]{1,0:T(8,128)(2,1)S(1)}, bf16[256,256]{1,0:T(8,128)(2,1)S(1)}, u32[]{:S(2)}, u32[]{:S(2)}) collective-permute-start(bf16[256,256]{1,0:T(8,128)(2,1)S(1)} %get-tuple-element.40), channel_id=1, source_target_pairs={{0,3},{1,2},{2,1},{3,0},{4,7},{5,6},{6,5},{7,4},{8,11},{9,10},{10,... | collective-permute-start | bytes 393224 | tf_op jit(solution)/shard_map/ppermute | solution.py:309
  51.6 8.9 %collective-permute-start.7 = (bf16[256,256]{1,0:T(8,128)(2,1)S(1)}, bf16[256,256]{1,0:T(8,128)(2,1)S(1)}, u32[]{:S(2)}, u32[]{:S(2)}) collective-permute-start(bf16[256,256]{1,0:T(8,128)(2,1)S(1)} %get-tuple-element.42), channel_id=1, source_target_pairs={{0,1},{1,0},{2,3},{3,2},{4,5},{5,4},{6,7},{7,6},{8,9},{9,8},{10,11... | collective-permute-start | bytes 393224 | tf_op jit(solution)/shard_map/ppermute | solution.py:309
  51.6 18.6 %collective-permute-start.8 = (bf16[256,256]{1,0:T(8,128)(2,1)S(1)}, bf16[256,256]{1,0:T(8,128)(2,1)S(1)}, u32[]{:S(2)}, u32[]{:S(2)}) collective-permute-start(bf16[256,256]{1,0:T(8,128)(2,1)S(1)} %get-tuple-element.43), channel_id=1, source_target_pairs={{0,2},{1,3},{2,0},{3,1},{4,6},{5,7},{6,4},{7,5},{8,10},{9,11},{10,... | collective-permute-start | bytes 393224 | tf_op jit(solution)/shard_map/ppermute | solution.py:309
  53.5 26.2 %copy-start.26 = (bf16[256,256]{1,0:T(8,128)(2,1)}, bf16[256,256]{1,0:T(8,128)(2,1)S(1)}, u32[]{:S(2)}) copy-start(bf16[256,256]{1,0:T(8,128)(2,1)S(1)} %collective-permute-done.3.refs_1_) | copy-start | bytes 393220
  53.5 16.7 %collective-permute-start.9 = (bf16[256,256]{1,0:T(8,128)(2,1)S(1)}, bf16[256,256]{1,0:T(8,128)(2,1)S(1)}, u32[]{:S(2)}, u32[]{:S(2)}) collective-permute-start(bf16[256,256]{1,0:T(8,128)(2,1)S(1)} %get-tuple-element.44), channel_id=1, source_target_pairs={{0,3},{1,2},{2,1},{3,0},{4,7},{5,6},{6,5},{7,4},{8,11},{9,10},{10,... | collective-permute-start | bytes 393224 | tf_op jit(solution)/shard_map/ppermute | solution.py:309
  56.1 23.6 %copy-start.10 = (f32[31,12,128]{2,0,1:T(8,128)}, f32[31,12,128]{2,0,1:T(8,128)S(1)}, u32[]{:S(2)}) copy-start(f32[31,12,128]{2,0,1:T(8,128)S(1)} %copy.22) | copy-start | bytes 571396
  56.4 23.4 %copy-start.8 = (bf16[1536,8]{1,0:T(8,128)(2,1)}, bf16[1536,8]{1,0:T(8,128)(2,1)S(1)}, u32[]{:S(2)}) copy-start(bf16[1536,8]{1,0:T(8,128)(2,1)S(1)} %copy.19.router_ref) | copy-start | bytes 73732
  60.5 19.3 %copy-start.28 = (bf16[256,256]{1,0:T(8,128)(2,1)}, bf16[256,256]{1,0:T(8,128)(2,1)S(1)}, u32[]{:S(2)}) copy-start(bf16[256,256]{1,0:T(8,128)(2,1)S(1)} %collective-permute-done.4.refs_2_) | copy-start | bytes 393220
  60.5 19.3 %copy-start.30 = (bf16[256,256]{1,0:T(8,128)(2,1)}, bf16[256,256]{1,0:T(8,128)(2,1)S(1)}, u32[]{:S(2)}) copy-start(bf16[256,256]{1,0:T(8,128)(2,1)S(1)} %collective-permute-done.5.refs_3_) | copy-start | bytes 393220
  70.3 1.9 copy-start.16
  81.8 48.8 %all-to-all-start = ((bf16[8,88,1536]{2,1,0:T(8,128)(2,1)}), bf16[8,88,1536]{2,1,0:T(8,128)(2,1)S(1)}, u32[]{:S(2)}, u32[]{:S(2)}) async-start(bf16[8,88,1536]{2,1,0:T(8,128)(2,1)} %bitcast.25), calls=%async_computation | async-start | bytes 4325376 | tf_op jit(solution)/shard_map/all_to_all | solution.py:408
  88.1 22.0 %collective-permute-start.10 = (bf16[256,1536]{1,0:T(8,128)(2,1)}, bf16[256,1536]{1,0:T(8,128)(2,1)S(1)}, u32[]{:S(2)}, u32[]{:S(2)}) collective-permute-start(bf16[256,1536]{1,0:T(8,128)(2,1)} %get-tuple-element.62), channel_id=1, source_target_pairs={{0,1},{1,0},{2,3},{3,2},{4,5},{5,4},{6,7},{7,6},{8,9},{9,8},{10,11... | collective-permute-start | bytes 2359304 | tf_op jit(solution)/shard_map/ppermute | solution.py:385
  92.3 68.2 %collective-permute-start.12 = (bf16[512,1536]{1,0:T(8,128)(2,1)}, bf16[512,1536]{1,0:T(8,128)(2,1)}, u32[]{:S(2)}, u32[]{:S(2)}) collective-permute-start(bf16[512,1536]{1,0:T(8,128)(2,1)} %bitcast.39), channel_id=1, source_target_pairs={{0,1},{1,0},{2,3},{3,2},{4,5},{5,4},{6,7},{7,6},{8,9},{9,8},{10,11... | collective-permute-start | bytes 4718600 | tf_op jit(solution)/shard_map/ppermute | solution.py:385
  113.9 1.9 copy-start.17
  130.6 45.5 %all-to-all-start.1 = ((bf16[8,88,1536]{2,1,0:T(8,128)(2,1)}), bf16[8,88,1536]{2,1,0:T(8,128)(2,1)}, u32[]{:S(2)}, u32[]{:S(2)}) async-start(bf16[8,88,1536]{2,1,0:T(8,128)(2,1)} %bitcast.26), calls=%async_computation.1 | async-start | bytes 4325376 | tf_op jit(solution)/shard_map/all_to_all | solution.py:408
  135.4 25.1 %collective-permute-start.11 = (bf16[256,1536]{1,0:T(8,128)(2,1)}, bf16[256,1536]{1,0:T(8,128)(2,1)S(1)}, u32[]{:S(2)}, u32[]{:S(2)}) collective-permute-start(bf16[256,1536]{1,0:T(8,128)(2,1)} %get-tuple-element.61), channel_id=1, source_target_pairs={{0,1},{1,0},{2,3},{3,2},{4,5},{5,4},{6,7},{7,6},{8,9},{9,8},{10,11... | collective-permute-start | bytes 2359304 | tf_op jit(solution)/shard_map/ppermute | solution.py:385
  160.5 1.4 copy-start.4
  161.9 1.4 copy-start.18
  176.1 31.2 %all-to-all-start.2 = ((bf16[8,88,1536]{2,1,0:T(8,128)(2,1)}), bf16[8,88,1536]{2,1,0:T(8,128)(2,1)S(1)}, u32[]{:S(2)}, u32[]{:S(2)}) async-start(bf16[8,88,1536]{2,1,0:T(8,128)(2,1)} %bitcast.29), calls=%async_computation.2 | async-start | bytes 4325376 | tf_op jit(solution)/shard_map/all_to_all | solution.py:408
  209.9 38.1 %all-to-all-start.3 = ((bf16[8,88,1536]{2,1,0:T(8,128)(2,1)}), bf16[8,88,1536]{2,1,0:T(8,128)(2,1)S(1)}, u32[]{:S(2)}, u32[]{:S(2)}) async-start(bf16[8,88,1536]{2,1,0:T(8,128)(2,1)} %bitcast.27), calls=%async_computation.3 | async-start | bytes 4325376 | tf_op jit(solution)/shard_map/all_to_all | solution.py:408
  213.5 33.7 %collective-permute-start.13 = (bf16[224,1536]{1,0:T(8,128)(2,1)}, bf16[224,1536]{1,0:T(8,128)(2,1)S(1)}, u32[]{:S(2)}, u32[]{:S(2)}) collective-permute-start(bf16[224,1536]{1,0:T(8,128)(2,1)} %copy-done.25), channel_id=1, source_target_pairs={{0,2},{1,3},{2,0},{3,1},{4,6},{5,7},{6,4},{7,5},{8,10},{9,11},{10,... | collective-permute-start | bytes 2064392 | tf_op jit(solution)/shard_map/ppermute | solution.py:466
  (27 other events, 27.4 us)

commit v8 on v7

--- a/solution.py
+++ b/solution.py
@@ -72,8 +72,7 @@
 
 
 def attend_kernel(count, rows, heads, place, me_ref, scale_ref, len_ref, *refs):
-    x_refs, oa_refs, ob_refs = refs[:count], refs[count : 2 * count], refs[2 * count : 3 * count]
-    k_ref, v_ref, a_ref = refs[3 * count :]
+    x_refs, (o_ref, k_ref, v_ref, a_ref) = refs[:count], refs[count:]
     me = me_ref[0]
     width = heads * HEAD_DIM
     tiles = max(1, width // LANES)
@@ -126,10 +125,9 @@
             wide = min(LANES, width)
             a_ref[pl.ds(start, rows), tile * LANES : tile * LANES + wide] = done[:, 0:wide].astype(BF16)
 
-    for r in range(count):
-        target = place(me, r)
-        for o_ref, block in ((oa_refs[r], target ^ half), (ob_refs[r], target)):
-            o_ref[...] = a_ref[pl.ds(pl.multiple_of(block * rows, HALO), window), :]
+    for target in range(count):
+        for which, block in enumerate((target ^ half, target)):
+            o_ref[target, which] = a_ref[block * rows : block * rows + window, :]
 
 
 def normalize(values):
@@ -144,7 +142,6 @@
     rows,
     experts,
     capacity,
-    place,
     flip,
     me_ref,
     expert_ref,
@@ -156,21 +153,17 @@
     turned_ref,
     *refs,
 ):
-    att_refs, out_refs = refs[:count], refs[count:-5]
+    att_ref, out_refs = refs[0], refs[1:-5]
     info_ref, second_ref, x_ref, first_ref, lab_ref = refs[-5:]
     me = me_ref[0]
     turn = expert_ref[0] if len(out_refs) > 1 else 0
-    width = att_refs[0].shape[1]
     window = rows + 2 * HALO
     half = (KERNEL - 1) // 2
     tiles = D // LANES
     step = 56
-    first = jnp.zeros((window, D), F32)
-    for r in range(count):
-        begin = pl.multiple_of(place(me, r) * width, HEAD_DIM)
-        first = first + jnp.dot(
-            att_refs[r][...], proj_ref[pl.ds(begin, width), :], preferred_element_type=F32
-        )
+    which = 0 if flip else 1
+    attended = jnp.concatenate([att_ref[source, which] for source in range(count)], axis=1)
+    first = jnp.dot(attended, proj_ref[...], preferred_element_type=F32)
     normed = normalize(first).astype(BF16).astype(F32)
     origin = (me ^ flip) * rows
     frames = lax.broadcasted_iota(jnp.int32, (window, LANES), 0) + (origin - HALO)
@@ -260,18 +253,22 @@
         ref[...] = values[e * tall : (e + 1) * tall].astype(BF16)
 
 
-def expert_kernel(chunks, spans, *refs):
-    x_refs, o_refs = refs[:chunks], refs[-chunks:]
-    in_refs, out_refs = refs[chunks : chunks + len(spans)], refs[chunks + len(spans) : -chunks]
+def expert_kernel(chunks, units, spans, *refs):
+    x_refs, w_refs, o_refs = refs[:chunks], refs[chunks:-chunks], refs[-chunks:]
     tokens = joined(x_refs)
-    total = jnp.zeros((tokens.shape[0], D), F32)
-    for in_ref, (place, begin) in zip(in_refs, spans):
+    total = None
+    for (into, first), (out, second) in spans:
         raw = lax.dot_general(
-            tokens, in_ref[...], (((1,), (1,)), ((), ())), preferred_element_type=F32
+            tokens,
+            w_refs[into][first : first + units, :],
+            (((1,), (1,)), ((), ())),
+            preferred_element_type=F32,
         )
         hidden = (raw / (1.0 + jnp.exp(-raw))).astype(BF16)
-        matching = out_refs[place][begin : begin + in_ref.shape[0], :]
-        total = total + jnp.dot(hidden, matching, preferred_element_type=F32)
+        product = jnp.dot(
+            hidden, w_refs[out][second : second + units, :], preferred_element_type=F32
+        )
+        total = product if total is None else total + product
     scatter(o_refs, total)
 
 
@@ -359,39 +356,36 @@
 
     tiles = max(1, width // LANES)
     total = count * rows
-    sent = jax.ShapeDtypeStruct((window, width), BF16)
     attended = pl.pallas_call(
         functools.partial(attend_kernel, count, rows, heads, place),
-        out_shape=(sent,) * (2 * count),
+        out_shape=jax.ShapeDtypeStruct((count, 2, window, width), BF16),
         in_specs=[SMEM, SMEM, SMEM] + [VMEM] * count,
-        out_specs=(VMEM,) * (2 * count),
+        out_specs=VMEM,
         scratch_shapes=[
             pltpu.VMEM((tiles, total, 2 * LANES), BF16),
             pltpu.VMEM((tiles, total, 2 * LANES), BF16),
             pltpu.VMEM((total + 2 * HALO, width), BF16),
         ],
-        compiler_params=params(10),
+        compiler_params=params(16),
         cost_estimate=cost(6),
         name="attend",
     )(me, scales, lengths, *arrived)
-    gathered_a = trade(attended[:count], "tm", direct)
-    gathered_b = trade(attended[count:], "tm", direct)
-
-    shards = after((expert_in[0], expert_out[0]), gathered_a + gathered_b)
+    windows = lax.all_to_all(attended, "tm", split_axis=0, concat_axis=0, tiled=True)
+
+    units = expert_in.shape[1]
+    (shard,) = after((jnp.concatenate([expert_in[0], expert_out[0]]),), (attended,))
     if half == 2:
-        swap = [(i, i ^ 1) for i in range(count)]
-        cut = expert_in.shape[1] // 2
-        pieces = (shards[0][:cut], shards[0][cut:], shards[1])
-        moved = [lax.ppermute(one, "tm", swap) for one in pieces]
-        ins, outs = [shards[0], moved[0], moved[1]], [shards[1], moved[2]]
-        spans = ((0, 0), (1, 0), (1, cut))
+        moved = lax.ppermute(shard, "tm", [(i, i ^ 1) for i in range(count)])
+        weights = [expert_in[0], expert_out[0], moved]
+        spans = (((0, 0), (1, 0)), ((2, 0), (2, units)))
     else:
         groups = [list(range(i, i + half)) for i in (0, half)]
-        moved = [
+        weights = [
             lax.all_gather(one, "tm", axis=0, tiled=True, axis_index_groups=groups)
-            for one in shards
+            for one in (shard[:units], shard[units:])
         ]
-        ins, outs, spans = moved[:1], moved[1:], ((0, 0),)
+        units = units * half
+        spans = (((0, 0), (1, 0)),)
 
     taps = jnp.transpose(conv_taps.reshape(KERNEL, D // LANES, LANES), (1, 0, 2))
     slots = experts * capacity
@@ -411,44 +405,44 @@
     def send_frames(windows, flip, split, block_routes):
         chunks = chunks_of(split)
         made = pl.pallas_call(
-            functools.partial(frame_kernel, count, rows, experts, capacity, place, flip),
+            functools.partial(frame_kernel, count, rows, experts, capacity, flip),
             out_shape=chunks
             + (
                 jax.ShapeDtypeStruct((rows, LANES), F32),
                 jax.ShapeDtypeStruct((D // LANES, rows, LANES), F32),
             ),
-            in_specs=[SMEM, SMEM, SMEM] + [VMEM] * (5 + count),
+            in_specs=[SMEM, SMEM, SMEM] + [VMEM] * 6,
             out_specs=(VMEM,) * (len(chunks) + 2),
             scratch_shapes=[
                 pltpu.VMEM((D // LANES, window, LANES), F32),
                 pltpu.VMEM((D // LANES, rows, LANES), F32),
                 pltpu.VMEM((window, LANES), F32),
             ],
-            compiler_params=params(16),
+            compiler_params=params(56),
             cost_estimate=cost(10),
             name="frames",
-        )(me, expert, lengths, out_proj, taps, router, block_routes, block_routes.T, *windows)
+        )(me, expert, lengths, out_proj, taps, router, block_routes, block_routes.T, windows)
         return made[:-2], made[-2], made[-1]
 
     def run_expert(tokens):
         split = len(tokens) > 1
         chunks = chunks_of(split)
         produced = pl.pallas_call(
-            functools.partial(expert_kernel, len(tokens), spans),
+            functools.partial(expert_kernel, len(tokens), units, spans),
             out_shape=chunks,
-            in_specs=[VMEM] * (len(tokens) + len(ins) + len(outs)),
+            in_specs=[VMEM] * (len(tokens) + len(weights)),
             out_specs=(VMEM,) * len(chunks),
-            compiler_params=params(20),
+            compiler_params=params(56),
             cost_estimate=cost(8),
             name="experts",
-        )(*tokens, *ins, *outs)
+        )(*tokens, *weights)
         return produced
 
-    outgoing_a, info_a, _ = send_frames(gathered_a, half, False, partner_routes)
-    tokens_a = route(after(outgoing_a, gathered_b))
-    gathered_b = after(gathered_b, (outgoing_a[0], moved[0]))
-    outgoing_b, info_b, second = send_frames(gathered_b, 0, False, routes[0])
-    tokens_b = route(outgoing_b)
+    outgoing_a, info_a, _ = send_frames(windows, half, False, partner_routes)
+    tokens_a = route(outgoing_a)
+    (windows,) = after((windows,), outgoing_a)
+    outgoing_b, info_b, second = send_frames(windows, 0, False, routes[0])
+    tokens_b = route(after(outgoing_b, tokens_a))
     produced_a = run_expert(tokens_a)
     back_a = route(after(produced_a, tokens_b))
     produced_b = run_expert(after(tokens_b, produced_a))
@@ -459,7 +453,7 @@
         out_shape=jax.ShapeDtypeStruct((rows, D), BF16),
         in_specs=[VMEM] * (1 + len(back_a)),
         out_specs=VMEM,
-        compiler_params=params(8),
+        compiler_params=params(56),
         cost_estimate=cost(1),
         name="theirs",
     )(info_a, *back_a)
@@ -470,7 +464,7 @@
         out_shape=jax.ShapeDtypeStruct((rows, D), BF16),
         in_specs=[VMEM] * (3 + len(back_b)),
         out_specs=VMEM,
-        compiler_params=params(12),
+        compiler_params=params(56),
         cost_estimate=cost(1),
         name="mine",
     )(info_b, second, received, *back_b)

time: 253 us -> 233 us (0.921)
  local copies, waits for them, and re-layouts: 37.9 us -> 8.22 us
  Pallas kernels: 46.8 us -> 60.6 us
  starting transfers between devices: 44.8 us -> 33.8 us
  waiting for transfers between devices: 122 us -> 128 us
    unnamed x83 -> x21, local copies, waits for them, and re-layouts: 34.2 us -> 4.88 us
    all_to_all x4, waiting for transfers between devices: 10.9 us -> 30.6 us  [route(): moved = lax.all_to_all(whole, 'dp', split_axis=0, concat_axis=0, tiled=True)]
    ppermute x3 -> x1, waiting for transfers between devices: 42.2 us -> 22.7 us  [body(): moved = lax.ppermute(shard, 'tm', [(i, i ^ 1) for i in range(count)])]
    ppermute x1, waiting for transfers between devices: 0.01 us -> 17.6 us  [body(): partner_routes = lax.ppermute(routes[0], 'tm', partner)]
    ppermute x9 -> x3, starting transfers between devices: 21 us -> 5.68 us  [trade(): lax.ppermute(arrays[r], axis, [(i, i ^ r) for i in range(count)])]
    ppermute x9 -> x3, waiting for transfers between devices: 37.9 us -> 24.2 us  [trade(): lax.ppermute(arrays[r], axis, [(i, i ^ r) for i in range(count)])]
    all_to_all x0 -> x1, starting transfers between devices: none -> 8.79 us  [body(): lax.all_to_all(attended, 'tm', split_axis=0, concat_axis=0, tiled=True)]
    pallas_call x2, Pallas kernels: 16.8 us -> 24.5 us  [send_frames(): pl.pallas_call(functools.partial(frame_kernel, count, rows, experts, capa...]
  transfers between devices with their start and end apart: 18 -> 11, of which waited for: 8 -> 7; matrix products, arithmetic and copies ran while one was open for 2% -> 3% of each run, Pallas kernels for 11% -> 19%
where the time goes in v8:
time: 233 us
  waiting for transfers between devices  128 us (55%)
  Pallas kernels  60.6 us (26%)
  starting transfers between devices  33.8 us (15%)
  local copies, waits for them, and re-layouts  8.22 us (4%)
    ppermute x1, waiting for transfers between devices, body(): received = lax.ppermute(theirs, 'tm', partner)  33 us
    all_to_all x4, waiting for transfers between devices, route(): moved = lax.all_to_all(whole, 'dp', split_axis=0, concat_axis=0, tiled=True)  30.6 us
    pallas_call x2, Pallas kernels, send_frames(): pl.pallas_call(functools.partial(frame_kernel, count, rows, experts, capa...  24.5 us
    ppermute x3, waiting for transfers between devices, trade(): lax.ppermute(arrays[r], axis, [(i, i ^ r) for i in range(count)])  24.2 us
    ppermute x1, waiting for transfers between devices, body(): moved = lax.ppermute(shard, 'tm', [(i, i ^ 1) for i in range(count)])  22.7 us
    pallas_call x2, Pallas kernels, run_expert(): pl.pallas_call(functools.partial(expert_kernel, len(tokens), units, spans...  19.6 us
    ppermute x1, waiting for transfers between devices, body(): partner_routes = lax.ppermute(routes[0], 'tm', partner)  17.6 us
    all_to_all x4, starting transfers between devices, route(): moved = lax.all_to_all(whole, 'dp', split_axis=0, concat_axis=0, tiled=True)  16.2 us
  transfers between devices with their start and end apart: 11, of which 7 were waited for; matrix products, arithmetic and copies ran while one was open for 3% of the time, Pallas kernels for 19%

profile of v8, /device:TPU:0, one launch (start us, length us, event | category | flops | bytes accessed | tf_op | source)
XLA Modules:
  0.0 232.8 jit_solution(12171003669679017145)
XLA Ops:
  0.0 2.6 %pack.1 = (bf16[3,224,256]{2,1,0:T(8,128)(2,1)}, bf16[3,224,256]{2,1,0:T(8,128)(2,1)}, bf16[3,224,256]{2,1,0:T(8,128)(2,1)}, bf16[3,224,256]{2,1,0:T(8,128)(2,1)}) custom-call(s32[1]{0:T(128)} %bitcast.me_ref, bf16[224,1024]{1,0:T(8,128)(2,1)} %bitcast.41, bf16[224,1024]{1,0:T(8,128)(2,1)} %bitcast.42, bf16[224,1024]{1,0:T(8,128)(2,1)} %bitcast.43), custom_call_target="tpu_custom_call" | custom-call | flops 1100000000 | tf_op jit(solution)/shard_map/pack/pallas_call | solution.py:343
  2.6 3.1 %collective-permute-start = (bf16[3,224,256]{2,1,0:T(8,128)(2,1)}, bf16[3,224,256]{2,1,0:T(8,128)(2,1)S(1)}, u32[]{:S(2)}, u32[]{:S(2)}) collective-permute-start(bf16[3,224,256]{2,1,0:T(8,128)(2,1)} %get-tuple-element.22), channel_id=1, source_target_pairs={{0,1},{1,0},{2,3},{3,2},{4,5},{5,4},{6,7},{7,6},{8,9},{9,8},{10,11... | collective-permute-start | bytes 1032200 | tf_op jit(solution)/shard_map/ppermute | solution.py:306
  5.7 2.6 %collective-permute-start.1 = (bf16[3,224,256]{2,1,0:T(8,128)(2,1)}, bf16[3,224,256]{2,1,0:T(8,128)(2,1)S(1)}, u32[]{:S(2)}, u32[]{:S(2)}) collective-permute-start(bf16[3,224,256]{2,1,0:T(8,128)(2,1)} %get-tuple-element.23), channel_id=1, source_target_pairs={{0,2},{1,3},{2,0},{3,1},{4,6},{5,7},{6,4},{7,5},{8,10},{9,11},{10,... | collective-permute-start | bytes 1032200 | tf_op jit(solution)/shard_map/ppermute | solution.py:306
  8.4 12.2 %collective-permute-done.refs_1_ = bf16[3,224,256]{2,1,0:T(8,128)(2,1)S(1)} collective-permute-done((bf16[3,224,256]{2,1,0:T(8,128)(2,1)}, bf16[3,224,256]{2,1,0:T(8,128)(2,1)S(1)}, u32[]{:S(2)}, u32[]{:S(2)}) %collective-permute-start) | collective-permute-done | bytes 344096 | tf_op jit(solution)/shard_map/ppermute | solution.py:306
  20.6 12.0 %collective-permute-done.1.refs_2_ = bf16[3,224,256]{2,1,0:T(8,128)(2,1)S(1)} collective-permute-done((bf16[3,224,256]{2,1,0:T(8,128)(2,1)}, bf16[3,224,256]{2,1,0:T(8,128)(2,1)S(1)}, u32[]{:S(2)}, u32[]{:S(2)}) %collective-permute-start.1) | collective-permute-done | bytes 344096 | tf_op jit(solution)/shard_map/ppermute | solution.py:306
  32.6 1.0 copy-done.1
  33.6 6.5 %attend.1 = bf16[4,2,256,256]{3,2,1,0:T(8,128)(2,1)} custom-call(s32[1]{0:T(128)} %bitcast.me_ref, f32[4]{0:T(128)S(1)} %dynamic_slice.3.scale_ref, s32[1,4]{1,0:T(1,128)S(1)} %copy-done, bf16[3,224,256]{2,1,0:T(8,128)(2,1)S(1)} %copy-done.1, bf16[3,224,256]{2,1,0:T(8,128)(2,1)S(1)} %collective-permute-done.refs_1_, ...), custom_call_target="tpu_custom_call" | custom-call | flops 6600000000 | tf_op jit(solution)/shard_map/attend/pallas_call | solution.py:359
  40.1 8.8 %all-to-all-start = ((bf16[4,2,256,256]{3,2,1,0:T(8,128)(2,1)}), bf16[4,2,256,256]{3,2,1,0:T(8,128)(2,1)}, u32[]{:S(2)}, u32[]{:S(2)}) async-start(bf16[4,2,256,256]{3,2,1,0:T(8,128)(2,1)} %attend.1), calls=%async_computation | async-start | bytes 2097152 | tf_op jit(solution)/shard_map/all_to_all | solution.py:373
  48.8 3.1 %collective-permute-start.3 = (s32[224,2]{0,1:T(2,128)S(1)}, s32[224,2]{0,1:T(2,128)S(1)}, u32[]{:S(2)}, u32[]{:S(2)}) collective-permute-start(s32[224,2]{0,1:T(2,128)S(1)} %bitcast.38), channel_id=1, source_target_pairs={{0,2},{1,3},{2,0},{3,1},{4,6},{5,7},{6,4},{7,5},{8,10},{9,11},{10,... | collective-permute-start | bytes 5384 | tf_op jit(solution)/shard_map/ppermute | solution.py:355
  51.9 2.1 pad_maximum_fusion
  54.0 1.0 reshape.35
  55.0 0.7 copy.22
  55.7 0.9 copy.19.router_ref
  56.6 17.6 %collective-permute-done.3 = s32[224,2]{0,1:T(2,128)S(1)} collective-permute-done((s32[224,2]{0,1:T(2,128)S(1)}, s32[224,2]{0,1:T(2,128)S(1)}, u32[]{:S(2)}, u32[]{:S(2)}) %collective-permute-start.3) | collective-permute-done | bytes 1824 | tf_op jit(solution)/shard_map/ppermute | solution.py:355
  74.2 0.8 copy.18.routes_ref
  75.0 11.0 %frames.2 = (bf16[704,1536]{1,0:T(8,128)(2,1)}, f32[224,128]{1,0:T(8,128)}, f32[12,224,128]{2,1,0:T(8,128)}) custom-call(s32[1]{0:T(128)} %bitcast.me_ref, s32[1]{0:T(128)} %bitcast.1.expert_ref, s32[1,4]{1,0:T(1,128)} %len_ref.5, bf16[1024,1536]{1,0:T(8,128)(2,1)} %proj_ref.3, f32[12,31,128]{2,1,0:T(8,128)} %bitcast.35, bf16[1536,8]{1,0:T(8,128)(2,1)} %copy.19.router_ref, ...), custom_call_target="tpu_custom_call" | custom-call | flops 11000000512 | tf_op jit(solution)/shard_map/frames/pallas_call | solution.py:407
  86.0 4.4 %all-to-all-start.1 = ((bf16[8,88,1536]{2,1,0:T(8,128)(2,1)}), bf16[8,88,1536]{2,1,0:T(8,128)(2,1)}, u32[]{:S(2)}, u32[]{:S(2)}) async-start(bf16[8,88,1536]{2,1,0:T(8,128)(2,1)} %bitcast.26), calls=%async_computation.1 | async-start | bytes 4325376 | tf_op jit(solution)/shard_map/all_to_all | solution.py:402
  90.4 0.8 copy.20.routes_ref
  91.1 13.5 %frames.3 = (bf16[704,1536]{1,0:T(8,128)(2,1)}, f32[224,128]{1,0:T(8,128)}, f32[12,224,128]{2,1,0:T(8,128)}) custom-call(s32[1]{0:T(128)} %bitcast.me_ref, s32[1]{0:T(128)} %bitcast.1.expert_ref, s32[1,4]{1,0:T(1,128)} %len_ref.5, bf16[1024,1536]{1,0:T(8,128)(2,1)} %proj_ref.3, f32[12,31,128]{2,1,0:T(8,128)} %bitcast.36, bf16[1536,8]{1,0:T(8,128)(2,1)} %copy.19.router_ref, ...), custom_call_target="tpu_custom_call" | custom-call | flops 11000000512 | tf_op jit(solution)/shard_map/frames/pallas_call | solution.py:407
  104.7 13.0 %all-to-all-done.1 = bf16[8,88,1536]{2,1,0:T(8,128)(2,1)} async-done(((bf16[8,88,1536]{2,1,0:T(8,128)(2,1)}), bf16[8,88,1536]{2,1,0:T(8,128)(2,1)}, u32[]{:S(2)}, u32[]{:S(2)}) %all-to-all-start.1) | async-done | bytes 2162720 | tf_op jit(solution)/shard_map/all_to_all | solution.py:402
  117.7 4.4 %all-to-all-start.2 = ((bf16[8,88,1536]{2,1,0:T(8,128)(2,1)}), bf16[8,88,1536]{2,1,0:T(8,128)(2,1)}, u32[]{:S(2)}, u32[]{:S(2)}) async-start(bf16[8,88,1536]{2,1,0:T(8,128)(2,1)} %bitcast.24), calls=%async_computation.2 | async-start | bytes 4325376 | tf_op jit(solution)/shard_map/all_to_all | solution.py:402
  122.1 22.7 %collective-permute-done.4.refs_3_ = bf16[1024,1536]{1,0:T(8,128)(2,1)} collective-permute-done((bf16[1024,1536]{1,0:T(8,128)(2,1)S(1)}, bf16[1024,1536]{1,0:T(8,128)(2,1)}, u32[]{:S(2)}, u32[]{:S(2)}) %collective-permute-start.4) | collective-permute-done | bytes 3145760 | tf_op jit(solution)/shard_map/ppermute | solution.py:378
  144.8 9.8 %experts.2 = bf16[704,1536]{1,0:T(8,128)(2,1)} custom-call(bf16[704,1536]{1,0:T(8,128)(2,1)} %bitcast.10.refs_0_, bf16[512,1536]{1,0:T(8,128)(2,1)} %bitcast.30, bf16[512,1536]{1,0:T(8,128)(2,1)} %bitcast.33, bf16[1024,1536]{1,0:T(8,128)(2,1)} %collective-permute-done.4.refs_3_), custom_call_target="tpu_custom_call" | custom-call | flops 8800000000 | tf_op jit(solution)/shard_map/experts/pallas_call | solution.py:430
  154.6 3.7 %all-to-all-start.3 = ((bf16[8,88,1536]{2,1,0:T(8,128)(2,1)}), bf16[8,88,1536]{2,1,0:T(8,128)(2,1)S(1)}, u32[]{:S(2)}, u32[]{:S(2)}) async-start(bf16[8,88,1536]{2,1,0:T(8,128)(2,1)} %bitcast.28), calls=%async_computation.3 | async-start | bytes 4325376 | tf_op jit(solution)/shard_map/all_to_all | solution.py:402
  158.3 9.8 %experts.3 = bf16[704,1536]{1,0:T(8,128)(2,1)} custom-call(bf16[704,1536]{1,0:T(8,128)(2,1)} %bitcast.14.refs_0_, bf16[512,1536]{1,0:T(8,128)(2,1)} %bitcast.31, bf16[512,1536]{1,0:T(8,128)(2,1)} %bitcast.34, bf16[1024,1536]{1,0:T(8,128)(2,1)} %collective-permute-done.4.refs_3_), custom_call_target="tpu_custom_call" | custom-call | flops 8800000000 | tf_op jit(solution)/shard_map/experts/pallas_call | solution.py:430
  168.1 17.5 %all-to-all-done.3 = bf16[8,88,1536]{2,1,0:T(8,128)(2,1)S(1)} async-done(((bf16[8,88,1536]{2,1,0:T(8,128)(2,1)}), bf16[8,88,1536]{2,1,0:T(8,128)(2,1)S(1)}, u32[]{:S(2)}, u32[]{:S(2)}) %all-to-all-start.3) | async-done | bytes 2162720 | tf_op jit(solution)/shard_map/all_to_all | solution.py:402
  185.7 1.4 copy-done.3
  187.0 3.3 %theirs.1 = bf16[224,1536]{1,0:T(8,128)(2,1)} custom-call(f32[224,128]{1,0:T(8,128)} %get-tuple-element.29.info_ref, bf16[704,1536]{1,0:T(8,128)(2,1)} %bitcast.27), custom_call_target="tpu_custom_call" | custom-call | flops 1100000000 | tf_op jit(solution)/shard_map/theirs/pallas_call | solution.py:451
  190.4 3.7 %all-to-all-start.4 = ((bf16[8,88,1536]{2,1,0:T(8,128)(2,1)}), bf16[8,88,1536]{2,1,0:T(8,128)(2,1)S(1)}, u32[]{:S(2)}, u32[]{:S(2)}) async-start(bf16[8,88,1536]{2,1,0:T(8,128)(2,1)} %bitcast.25), calls=%async_computation.4 | async-start | bytes 4325376 | tf_op jit(solution)/shard_map/all_to_all | solution.py:402
  194.2 33.0 %collective-permute-done.5.part_ref = bf16[224,1536]{1,0:T(8,128)(2,1)S(1)} collective-permute-done((bf16[224,1536]{1,0:T(8,128)(2,1)S(1)}, bf16[224,1536]{1,0:T(8,128)(2,1)S(1)}, u32[]{:S(2)}, u32[]{:S(2)}) %collective-permute-start.5) | collective-permute-done | bytes 688160 | tf_op jit(solution)/shard_map/ppermute | solution.py:460
  227.2 0.9 copy-done.4
  228.8 4.0 %mine.1 = bf16[224,1536]{1,0:T(8,128)(2,1)} custom-call(f32[224,128]{1,0:T(8,128)} %get-tuple-element.27.info_ref, f32[12,224,128]{2,1,0:T(8,128)} %get-tuple-element.28.second_ref, bf16[224,1536]{1,0:T(8,128)(2,1)} %copy-done.4, bf16[704,1536]{1,0:T(8,128)(2,1)} %bitcast.23), custom_call_target="tpu_custom_call" | custom-call | flops 1100000000 | tf_op jit(solution)/shard_map/mine/pallas_call | solution.py:462
  (25 shorter events, 0.9 us)
Async XLA Ops:
  0.0 8.3 %copy-start.9 = (f32[16]{0:T(128)S(1)}, f32[16]{0:T(128)}, u32[]{:S(2)}) copy-start(f32[16]{0:T(128)} %param.14) | copy-start | bytes 196
  0.0 32.6 %copy-start = (s32[1,4]{1,0:T(1,128)S(1)}, s32[1,4]{1,0:T(1,128)}, u32[]{:S(2)}) copy-start(s32[1,4]{1,0:T(1,128)} %len_ref.5) | copy-start | bytes 52
  2.6 18.0 %collective-permute-start = (bf16[3,224,256]{2,1,0:T(8,128)(2,1)}, bf16[3,224,256]{2,1,0:T(8,128)(2,1)S(1)}, u32[]{:S(2)}, u32[]{:S(2)}) collective-permute-start(bf16[3,224,256]{2,1,0:T(8,128)(2,1)} %get-tuple-element.22), channel_id=1, source_target_pairs={{0,1},{1,0},{2,3},{3,2},{4,5},{5,4},{6,7},{7,6},{8,9},{9,8},{10,11... | collective-permute-start | bytes 1032200 | tf_op jit(solution)/shard_map/ppermute | solution.py:306
  5.7 26.8 %collective-permute-start.1 = (bf16[3,224,256]{2,1,0:T(8,128)(2,1)}, bf16[3,224,256]{2,1,0:T(8,128)(2,1)S(1)}, u32[]{:S(2)}, u32[]{:S(2)}) collective-permute-start(bf16[3,224,256]{2,1,0:T(8,128)(2,1)} %get-tuple-element.23), channel_id=1, source_target_pairs={{0,2},{1,3},{2,0},{3,1},{4,6},{5,7},{6,4},{7,5},{8,10},{9,11},{10,... | collective-permute-start | bytes 1032200 | tf_op jit(solution)/shard_map/ppermute | solution.py:306
  8.3 24.3 %collective-permute-start.2 = (bf16[3,224,256]{2,1,0:T(8,128)(2,1)}, bf16[3,224,256]{2,1,0:T(8,128)(2,1)S(1)}, u32[]{:S(2)}, u32[]{:S(2)}) collective-permute-start(bf16[3,224,256]{2,1,0:T(8,128)(2,1)} %get-tuple-element.24), channel_id=1, source_target_pairs={{0,3},{1,2},{2,1},{3,0},{4,7},{5,6},{6,5},{7,4},{8,11},{9,10},{10,... | collective-permute-start | bytes 1032200 | tf_op jit(solution)/shard_map/ppermute | solution.py:306
  32.6 1.0 copy-start.1
  33.6 15.3 %copy-start.6 = (s32[1,224,2]{1,2,0:T(2,128)S(1)}, s32[1,224,2]{1,2,0:T(2,128)}, u32[]{:S(2)}) copy-start(s32[1,224,2]{1,2,0:T(2,128)} %param.21) | copy-start | bytes 5380
  40.1 34.9 %all-to-all-start = ((bf16[4,2,256,256]{3,2,1,0:T(8,128)(2,1)}), bf16[4,2,256,256]{3,2,1,0:T(8,128)(2,1)}, u32[]{:S(2)}, u32[]{:S(2)}) async-start(bf16[4,2,256,256]{3,2,1,0:T(8,128)(2,1)} %attend.1), calls=%async_computation | async-start | bytes 2097152 | tf_op jit(solution)/shard_map/all_to_all | solution.py:373
  48.8 25.3 %collective-permute-start.3 = (s32[224,2]{0,1:T(2,128)S(1)}, s32[224,2]{0,1:T(2,128)S(1)}, u32[]{:S(2)}, u32[]{:S(2)}) collective-permute-start(s32[224,2]{0,1:T(2,128)S(1)} %bitcast.38), channel_id=1, source_target_pairs={{0,2},{1,3},{2,0},{3,1},{4,6},{5,7},{6,4},{7,5},{8,10},{9,11},{10,... | collective-permute-start | bytes 5384 | tf_op jit(solution)/shard_map/ppermute | solution.py:355
  51.9 3.8 %copy-start.5 = (bf16[1536,8]{0,1:T(8,128)(2,1)S(1)}, bf16[1536,8]{0,1:T(8,128)(2,1)}, u32[]{:S(2)}) copy-start(bf16[1536,8]{0,1:T(8,128)(2,1)} %param.17) | copy-start | bytes 73732
  74.2 0.8 copy-start.7
  75.0 69.8 %collective-permute-start.4 = (bf16[1024,1536]{1,0:T(8,128)(2,1)S(1)}, bf16[1024,1536]{1,0:T(8,128)(2,1)}, u32[]{:S(2)}, u32[]{:S(2)}) collective-permute-start(bf16[1024,1536]{1,0:T(8,128)(2,1)S(1)} %pad_maximum_fusion), channel_id=1, source_target_pairs={{0,1},{1,0},{2,3},{3,2},{4,5},{5,4},{6,7},{7,6},{8,9},{9,8},{10,11... | collective-permute-start | bytes 9437192 | tf_op jit(solution)/shard_map/ppermute | solution.py:378
  86.0 31.7 %all-to-all-start.1 = ((bf16[8,88,1536]{2,1,0:T(8,128)(2,1)}), bf16[8,88,1536]{2,1,0:T(8,128)(2,1)}, u32[]{:S(2)}, u32[]{:S(2)}) async-start(bf16[8,88,1536]{2,1,0:T(8,128)(2,1)} %bitcast.26), calls=%async_computation.1 | async-start | bytes 4325376 | tf_op jit(solution)/shard_map/all_to_all | solution.py:402
  117.7 36.9 %all-to-all-start.2 = ((bf16[8,88,1536]{2,1,0:T(8,128)(2,1)}), bf16[8,88,1536]{2,1,0:T(8,128)(2,1)}, u32[]{:S(2)}, u32[]{:S(2)}) async-start(bf16[8,88,1536]{2,1,0:T(8,128)(2,1)} %bitcast.24), calls=%async_computation.2 | async-start | bytes 4325376 | tf_op jit(solution)/shard_map/all_to_all | solution.py:402
  154.6 31.1 %all-to-all-start.3 = ((bf16[8,88,1536]{2,1,0:T(8,128)(2,1)}), bf16[8,88,1536]{2,1,0:T(8,128)(2,1)S(1)}, u32[]{:S(2)}, u32[]{:S(2)}) async-start(bf16[8,88,1536]{2,1,0:T(8,128)(2,1)} %bitcast.28), calls=%async_computation.3 | async-start | bytes 4325376 | tf_op jit(solution)/shard_map/all_to_all | solution.py:402
  185.7 1.4 copy-start.3
  190.4 3.7 %copy-start.8 = (bf16[224,1536]{1,0:T(8,128)(2,1)S(1)}, bf16[224,1536]{1,0:T(8,128)(2,1)}, u32[]{:S(2)}) copy-start(bf16[224,1536]{1,0:T(8,128)(2,1)} %theirs.1) | copy-start | bytes 2064388
  190.4 36.9 %all-to-all-start.4 = ((bf16[8,88,1536]{2,1,0:T(8,128)(2,1)}), bf16[8,88,1536]{2,1,0:T(8,128)(2,1)S(1)}, u32[]{:S(2)}, u32[]{:S(2)}) async-start(bf16[8,88,1536]{2,1,0:T(8,128)(2,1)} %bitcast.25), calls=%async_computation.4 | async-start | bytes 4325376 | tf_op jit(solution)/shard_map/all_to_all | solution.py:402
  194.1 33.1 %collective-permute-start.5 = (bf16[224,1536]{1,0:T(8,128)(2,1)S(1)}, bf16[224,1536]{1,0:T(8,128)(2,1)S(1)}, u32[]{:S(2)}, u32[]{:S(2)}) collective-permute-start(bf16[224,1536]{1,0:T(8,128)(2,1)S(1)} %copy-done.8), channel_id=1, source_target_pairs={{0,2},{1,3},{2,0},{3,1},{4,6},{5,7},{6,4},{7,5},{8,10},{9,11},{10,... | collective-permute-start | bytes 2064392 | tf_op jit(solution)/shard_map/ppermute | solution.py:460
  227.2 0.9 copy-start.4
  227.2 1.6 copy-start.2

commit v9 on v8

--- a/solution.py
+++ b/solution.py
@@ -72,7 +72,8 @@
 
 
 def attend_kernel(count, rows, heads, place, me_ref, scale_ref, len_ref, *refs):
-    x_refs, (o_ref, k_ref, v_ref, a_ref) = refs[:count], refs[count:]
+    x_refs, o_refs = refs[:count], refs[count : 2 * count]
+    k_ref, v_ref, a_ref = refs[2 * count :]
     me = me_ref[0]
     width = heads * HEAD_DIM
     tiles = max(1, width // LANES)
@@ -125,9 +126,11 @@
             wide = min(LANES, width)
             a_ref[pl.ds(start, rows), tile * LANES : tile * LANES + wide] = done[:, 0:wide].astype(BF16)
 
-    for target in range(count):
+    for r in range(count):
+        target = place(me, r)
         for which, block in enumerate((target ^ half, target)):
-            o_ref[target, which] = a_ref[block * rows : block * rows + window, :]
+            begin = pl.multiple_of(block * rows, HALO)
+            o_refs[r][which] = a_ref[pl.ds(begin, window), :]
 
 
 def normalize(values):
@@ -142,6 +145,7 @@
     rows,
     experts,
     capacity,
+    place,
     flip,
     me_ref,
     expert_ref,
@@ -153,17 +157,23 @@
     turned_ref,
     *refs,
 ):
-    att_ref, out_refs = refs[0], refs[1:-5]
+    att_refs, out_refs = refs[:count], refs[count:-5]
     info_ref, second_ref, x_ref, first_ref, lab_ref = refs[-5:]
     me = me_ref[0]
-    turn = expert_ref[0] if len(out_refs) > 1 else 0
+    turn = 0 if flip else expert_ref[0]
     window = rows + 2 * HALO
     half = (KERNEL - 1) // 2
     tiles = D // LANES
     step = 56
     which = 0 if flip else 1
-    attended = jnp.concatenate([att_ref[source, which] for source in range(count)], axis=1)
-    first = jnp.dot(attended, proj_ref[...], preferred_element_type=F32)
+    width = att_refs[0].shape[2]
+    first = None
+    for r in range(count):
+        begin = pl.multiple_of(place(me, r) * width, HEAD_DIM)
+        term = jnp.dot(
+            att_refs[r][which], proj_ref[pl.ds(begin, width), :], preferred_element_type=F32
+        )
+        first = term if first is None else first + term
     normed = normalize(first).astype(BF16).astype(F32)
     origin = (me ^ flip) * rows
     frames = lax.broadcasted_iota(jnp.int32, (window, LANES), 0) + (origin - HALO)
@@ -229,7 +239,7 @@
         info = jnp.where(column == TOPK + pick, raised[pick] / mass, info)
     info_ref[...] = info
 
-    expert = lax.broadcasted_iota(jnp.int32, (experts, rows), 0) ^ turn
+    expert = lax.broadcasted_iota(jnp.int32, (experts, rows), 0)
     chosen = (expert == turned_ref[0:1, :]) | (expert == turned_ref[1:2, :])
     later = jnp.where(down < across, 1.0, 0.0).astype(BF16)
     order = jnp.dot(jnp.where(chosen, 1.0, 0.0).astype(BF16), later, preferred_element_type=F32)
@@ -238,7 +248,7 @@
     select = jnp.concatenate(
         [jnp.where(slot == order[e : e + 1, :], 1.0, 0.0) for e in range(experts)], axis=0
     ).astype(BF16)
-    scatter(out_refs, jnp.dot(select, mixed, preferred_element_type=F32))
+    out_refs[0][...] = jnp.dot(select, mixed, preferred_element_type=F32).astype(BF16)
 
 
 def joined(refs):
@@ -247,15 +257,10 @@
     return jnp.concatenate([ref[...].astype(F32) for ref in refs], axis=0).astype(BF16)
 
 
-def scatter(refs, values):
-    tall = values.shape[0] // len(refs)
-    for e, ref in enumerate(refs):
-        ref[...] = values[e * tall : (e + 1) * tall].astype(BF16)
-
-
-def expert_kernel(chunks, units, spans, *refs):
-    x_refs, w_refs, o_refs = refs[:chunks], refs[chunks:-chunks], refs[-chunks:]
-    tokens = joined(x_refs)
+def expert_kernel(chunks, units, spans, expert_ref, x_ref, *refs):
+    pieces = len(refs) - chunks - (chunks > 1)
+    w_refs, o_refs = refs[:pieces], refs[pieces : pieces + chunks]
+    tokens = x_ref[...]
     total = None
     for (into, first), (out, second) in spans:
         raw = lax.dot_general(
@@ -269,7 +274,14 @@
             hidden, w_refs[out][second : second + units, :], preferred_element_type=F32
         )
         total = product if total is None else total + product
-    scatter(o_refs, total)
+    if chunks == 1:
+        o_refs[0][...] = total.astype(BF16)
+        return
+    refs[-1][...] = total
+    tall = o_refs[0].shape[0]
+    for r, o_ref in enumerate(o_refs):
+        begin = pl.multiple_of((expert_ref[0] ^ r) * tall, 8)
+        o_ref[...] = refs[-1][pl.ds(begin, tall), :].astype(BF16)
 
 
 def mixture_of(info, back_refs):
@@ -358,9 +370,9 @@
     total = count * rows
     attended = pl.pallas_call(
         functools.partial(attend_kernel, count, rows, heads, place),
-        out_shape=jax.ShapeDtypeStruct((count, 2, window, width), BF16),
+        out_shape=(jax.ShapeDtypeStruct((2, window, width), BF16),) * count,
         in_specs=[SMEM, SMEM, SMEM] + [VMEM] * count,
-        out_specs=VMEM,
+        out_specs=(VMEM,) * count,
         scratch_shapes=[
             pltpu.VMEM((tiles, total, 2 * LANES), BF16),
             pltpu.VMEM((tiles, total, 2 * LANES), BF16),
@@ -370,10 +382,10 @@
         cost_estimate=cost(6),
         name="attend",
     )(me, scales, lengths, *arrived)
-    windows = lax.all_to_all(attended, "tm", split_axis=0, concat_axis=0, tiled=True)
+    windows = trade(attended, "tm", direct)
 
     units = expert_in.shape[1]
-    (shard,) = after((jnp.concatenate([expert_in[0], expert_out[0]]),), (attended,))
+    (shard,) = after((jnp.concatenate([expert_in[0], expert_out[0]]),), windows)
     if half == 2:
         moved = lax.ppermute(shard, "tm", [(i, i ^ 1) for i in range(count)])
         weights = [expert_in[0], expert_out[0], moved]
@@ -402,16 +414,16 @@
         moved = lax.all_to_all(whole, "dp", split_axis=0, concat_axis=0, tiled=True)
         return [moved.reshape(slots, D)]
 
-    def send_frames(windows, flip, split, block_routes):
-        chunks = chunks_of(split)
+    def send_frames(windows, flip, block_routes):
+        chunks = chunks_of(False)
         made = pl.pallas_call(
-            functools.partial(frame_kernel, count, rows, experts, capacity, flip),
+            functools.partial(frame_kernel, count, rows, experts, capacity, place, flip),
             out_shape=chunks
             + (
                 jax.ShapeDtypeStruct((rows, LANES), F32),
                 jax.ShapeDtypeStruct((D // LANES, rows, LANES), F32),
             ),
-            in_specs=[SMEM, SMEM, SMEM] + [VMEM] * 6,
+            in_specs=[SMEM, SMEM, SMEM] + [VMEM] * (5 + count),
             out_specs=(VMEM,) * (len(chunks) + 2),
             scratch_shapes=[
                 pltpu.VMEM((D // LANES, window, LANES), F32),
@@ -421,50 +433,50 @@
             compiler_params=params(56),
             cost_estimate=cost(10),
             name="frames",
-        )(me, expert, lengths, out_proj, taps, router, block_routes, block_routes.T, windows)
+        )(me, expert, lengths, out_proj, taps, router, block_routes, block_routes.T, *windows)
         return made[:-2], made[-2], made[-1]
 
-    def run_expert(tokens):
-        split = len(tokens) > 1
+    def run_expert(tokens, split):
         chunks = chunks_of(split)
         produced = pl.pallas_call(
-            functools.partial(expert_kernel, len(tokens), units, spans),
+            functools.partial(expert_kernel, len(chunks), units, spans),
             out_shape=chunks,
-            in_specs=[VMEM] * (len(tokens) + len(weights)),
+            in_specs=[SMEM, VMEM] + [VMEM] * len(weights),
             out_specs=(VMEM,) * len(chunks),
+            scratch_shapes=[pltpu.VMEM((slots, D), F32)] * split,
             compiler_params=params(56),
             cost_estimate=cost(8),
             name="experts",
-        )(*tokens, *weights)
+        )(expert, *tokens, *weights)
         return produced
 
-    outgoing_a, info_a, _ = send_frames(windows, half, False, partner_routes)
+    outgoing_a, info_a, _ = send_frames(windows, half, partner_routes)
     tokens_a = route(outgoing_a)
-    (windows,) = after((windows,), outgoing_a)
-    outgoing_b, info_b, second = send_frames(windows, 0, False, routes[0])
+    windows = after(windows, outgoing_a)
+    outgoing_b, info_b, second = send_frames(windows, 0, routes[0])
     tokens_b = route(after(outgoing_b, tokens_a))
-    produced_a = run_expert(tokens_a)
+    produced_a = run_expert(tokens_a, False)
     back_a = route(after(produced_a, tokens_b))
-    produced_b = run_expert(after(tokens_b, produced_a))
-    back_a = after(back_a, produced_b)
+    produced_b = run_expert(after(tokens_b, produced_a), True)
+    back_b = route(produced_b)
+    back_a = after(back_a, back_b[1:2])
 
     theirs = pl.pallas_call(
         theirs_kernel,
         out_shape=jax.ShapeDtypeStruct((rows, D), BF16),
         in_specs=[VMEM] * (1 + len(back_a)),
         out_specs=VMEM,
-        compiler_params=params(56),
+        compiler_params=params(16),
         cost_estimate=cost(1),
         name="theirs",
     )(info_a, *back_a)
     received = lax.ppermute(theirs, "tm", partner)
-    back_b = route(after(produced_b, (theirs,)))
     out = pl.pallas_call(
         mine_kernel,
         out_shape=jax.ShapeDtypeStruct((rows, D), BF16),
         in_specs=[VMEM] * (3 + len(back_b)),
         out_specs=VMEM,
-        compiler_params=params(56),
+        compiler_params=params(16),
         cost_estimate=cost(1),
         name="mine",
     )(info_b, second, received, *back_b)

time: 233 us -> 213 us (0.914)
  waiting for transfers between devices: 128 us -> 107 us
  starting transfers between devices: 33.8 us -> 41.9 us
  Pallas kernels: 60.6 us -> 53 us
    ppermute x3 -> x13, waiting for transfers between devices: 24.2 us -> 59.1 us  [trade(): lax.ppermute(arrays[r], axis, [(i, i ^ r) for i in range(count)])]
    ppermute x1, waiting for transfers between devices: 33 us -> 0.01 us  [body(): received = lax.ppermute(theirs, 'tm', partner)]
    ppermute x1, waiting for transfers between devices: 17.6 us -> 0.01 us  [body(): partner_routes = lax.ppermute(routes[0], 'tm', partner)]
    ppermute x3 -> x13, starting transfers between devices: 5.68 us -> 21.6 us  [trade(): lax.ppermute(arrays[r], axis, [(i, i ^ r) for i in range(count)])]
    all_to_all x1 -> x0, starting transfers between devices: 8.79 us -> none  [body(): lax.all_to_all(attended, 'tm', split_axis=0, concat_axis=0, tiled=True)]
    ppermute x1, waiting for transfers between devices: 22.7 us -> 17.7 us  [body(): moved = lax.ppermute(shard, 'tm', [(i, i ^ 1) for i in range(count)])]
    all_to_all x4 -> x3, starting transfers between devices: 16.2 us -> 11.7 us  [route(): moved = lax.all_to_all(whole, 'dp', split_axis=0, concat_axis=0, tiled=True)]
    ppermute x1, starting transfers between devices: 0.01 us -> 3.58 us  [body(): moved = lax.ppermute(shard, 'tm', [(i, i ^ 1) for i in range(count)])]
  transfers between devices with their start and end apart: 11 -> 19, of which waited for: 7 -> 11; matrix products, arithmetic and copies ran while one was open for 3% -> 2% of each run, Pallas kernels for 19% -> 23%
where the time goes in v9:
time: 213 us; the launch traced here: 212 us
  waiting for transfers between devices  107 us (50%)
  Pallas kernels  53 us (25%)
  starting transfers between devices  41.9 us (20%)
  local copies, waits for them, and re-layouts  8.19 us (4%)
    ppermute x13, waiting for transfers between devices, trade(): lax.ppermute(arrays[r], axis, [(i, i ^ r) for i in range(count)])  59.1 us
    all_to_all x3, waiting for transfers between devices, route(): moved = lax.all_to_all(whole, 'dp', split_axis=0, concat_axis=0, tiled=True)  30.4 us
    pallas_call x2, Pallas kernels, send_frames(): pl.pallas_call(functools.partial(frame_kernel, count, rows, experts, capa...  22.7 us
    ppermute x13, starting transfers between devices, trade(): lax.ppermute(arrays[r], axis, [(i, i ^ r) for i in range(count)])  21.6 us
    pallas_call x2, Pallas kernels, run_expert(): pl.pallas_call(functools.partial(expert_kernel, len(chunks), units, spans...  19.6 us
    ppermute x1, waiting for transfers between devices, body(): moved = lax.ppermute(shard, 'tm', [(i, i ^ 1) for i in range(count)])  17.7 us
    all_to_all x3, starting transfers between devices, route(): moved = lax.all_to_all(whole, 'dp', split_axis=0, concat_axis=0, tiled=True)  11.7 us
    unnamed x53, local copies, waits for them, and re-layouts  5.78 us
  transfers between devices with their start and end apart: 19, of which 11 were waited for; matrix products, arithmetic and copies ran while one was open for 2% of the time, Pallas kernels for 23%

profile of v9, /device:TPU:0, one launch (start us, length us, event | category | flops | bytes accessed | tf_op | source)
XLA Modules:
  0.0 212.4 jit_solution(15753232493689221573)
XLA Ops:
  0.0 2.6 %pack.1 = (bf16[3,224,256]{2,1,0:T(8,128)(2,1)}, bf16[3,224,256]{2,1,0:T(8,128)(2,1)}, bf16[3,224,256]{2,1,0:T(8,128)(2,1)}, bf16[3,224,256]{2,1,0:T(8,128)(2,1)}) custom-call(s32[1]{0:T(128)} %bitcast.me_ref, bf16[224,1024]{1,0:T(8,128)(2,1)} %bitcast.38, bf16[224,1024]{1,0:T(8,128)(2,1)} %bitcast.39, bf16[224,1024]{1,0:T(8,128)(2,1)} %bitcast.40), custom_call_target="tpu_custom_call" | custom-call | flops 1100000000 | tf_op jit(solution)/shard_map/pack/pallas_call | solution.py:355
  2.6 3.1 %collective-permute-start = (bf16[3,224,256]{2,1,0:T(8,128)(2,1)}, bf16[3,224,256]{2,1,0:T(8,128)(2,1)S(1)}, u32[]{:S(2)}, u32[]{:S(2)}) collective-permute-start(bf16[3,224,256]{2,1,0:T(8,128)(2,1)} %get-tuple-element.36), channel_id=1, source_target_pairs={{0,1},{1,0},{2,3},{3,2},{4,5},{5,4},{6,7},{7,6},{8,9},{9,8},{10,11... | collective-permute-start | bytes 1032200 | tf_op jit(solution)/shard_map/ppermute | solution.py:318
  5.7 2.6 %collective-permute-start.1 = (bf16[3,224,256]{2,1,0:T(8,128)(2,1)}, bf16[3,224,256]{2,1,0:T(8,128)(2,1)S(1)}, u32[]{:S(2)}, u32[]{:S(2)}) collective-permute-start(bf16[3,224,256]{2,1,0:T(8,128)(2,1)} %get-tuple-element.37), channel_id=1, source_target_pairs={{0,2},{1,3},{2,0},{3,1},{4,6},{5,7},{6,4},{7,5},{8,10},{9,11},{10,... | collective-permute-start | bytes 1032200 | tf_op jit(solution)/shard_map/ppermute | solution.py:318
  8.3 1.9 collective-permute-start.6
  10.3 10.3 %collective-permute-done.refs_1_ = bf16[3,224,256]{2,1,0:T(8,128)(2,1)S(1)} collective-permute-done((bf16[3,224,256]{2,1,0:T(8,128)(2,1)}, bf16[3,224,256]{2,1,0:T(8,128)(2,1)S(1)}, u32[]{:S(2)}, u32[]{:S(2)}) %collective-permute-start) | collective-permute-done | bytes 344096 | tf_op jit(solution)/shard_map/ppermute | solution.py:318
  20.6 12.0 %collective-permute-done.1.refs_2_ = bf16[3,224,256]{2,1,0:T(8,128)(2,1)S(1)} collective-permute-done((bf16[3,224,256]{2,1,0:T(8,128)(2,1)}, bf16[3,224,256]{2,1,0:T(8,128)(2,1)S(1)}, u32[]{:S(2)}, u32[]{:S(2)}) %collective-permute-start.1) | collective-permute-done | bytes 344096 | tf_op jit(solution)/shard_map/ppermute | solution.py:318
  33.6 5.5 %attend.1 = (bf16[2,256,256]{2,1,0:T(8,128)(2,1)S(1)}, bf16[2,256,256]{2,1,0:T(8,128)(2,1)S(1)}, bf16[2,256,256]{2,1,0:T(8,128)(2,1)S(1)}, bf16[2,256,256]{2,1,0:T(8,128)(2,1)S(1)}) custom-call(s32[1]{0:T(128)} %bitcast.me_ref, f32[4]{0:T(128)S(1)} %dynamic_slice.3.scale_ref, s32[1,4]{1,0:T(1,128)S(1)} %copy-done.5, bf16[3,224,256]{2,1,0:T(8,128)(2,1)S(1)} %copy-done.7, ...), custom_call_target="tpu_custom_call" | custom-call | flops 6600000000 | tf_op jit(solution)/shard_map/attend/pallas_call | solution.py:371
  39.8 6.5 %collective-permute-start.3 = (bf16[2,256,256]{2,1,0:T(8,128)(2,1)S(1)}, bf16[2,256,256]{2,1,0:T(8,128)(2,1)S(1)}, u32[]{:S(2)}, u32[]{:S(2)}) collective-permute-start(bf16[2,256,256]{2,1,0:T(8,128)(2,1)S(1)} %get-tuple-element.40), channel_id=1, source_target_pairs={{0,1},{1,0},{2,3},{3,2},{4,5},{5,4},{6,7},{7,6},{8,9},{9,8},{10,11... | collective-permute-start | bytes 786440 | tf_op jit(solution)/shard_map/ppermute | solution.py:318
  47.4 1.5 collective-permute-start.5
  48.9 1.9 pad_maximum_fusion
  53.2 2.4 %collective-permute-done.3.refs_1_ = bf16[2,256,256]{2,1,0:T(8,128)(2,1)S(1)} collective-permute-done((bf16[2,256,256]{2,1,0:T(8,128)(2,1)S(1)}, bf16[2,256,256]{2,1,0:T(8,128)(2,1)S(1)}, u32[]{:S(2)}, u32[]{:S(2)}) %collective-permute-start.3) | collective-permute-done | bytes 262176 | tf_op jit(solution)/shard_map/ppermute | solution.py:318
  55.6 12.2 %collective-permute-done.4.refs_2_ = bf16[2,256,256]{2,1,0:T(8,128)(2,1)S(1)} collective-permute-done((bf16[2,256,256]{2,1,0:T(8,128)(2,1)S(1)}, bf16[2,256,256]{2,1,0:T(8,128)(2,1)S(1)}, u32[]{:S(2)}, u32[]{:S(2)}) %collective-permute-start.4) | collective-permute-done | bytes 262176 | tf_op jit(solution)/shard_map/ppermute | solution.py:318
  67.8 3.6 %collective-permute-start.7 = (bf16[1024,1536]{1,0:T(8,128)(2,1)}, bf16[1024,1536]{1,0:T(8,128)(2,1)}, u32[]{:S(2)}, u32[]{:S(2)}) collective-permute-start(bf16[1024,1536]{1,0:T(8,128)(2,1)} %pad_maximum_fusion), channel_id=1, source_target_pairs={{0,1},{1,0},{2,3},{3,2},{4,5},{5,4},{6,7},{7,6},{8,9},{9,8},{10,11... | collective-permute-start | bytes 9437192 | tf_op jit(solution)/shard_map/ppermute | solution.py:390
  71.4 11.6 %frames.2 = (bf16[704,1536]{1,0:T(8,128)(2,1)}, f32[224,128]{1,0:T(8,128)}, f32[12,224,128]{2,1,0:T(8,128)}) custom-call(s32[1]{0:T(128)} %bitcast.me_ref, s32[1]{0:T(128)} %bitcast.1.expert_ref, s32[1,4]{1,0:T(1,128)} %len_ref.5, bf16[1024,1536]{1,0:T(8,128)(2,1)} %proj_ref.3, f32[12,31,128]{2,1,0:T(8,128)} %bitcast.32, bf16[1536,8]{1,0:T(8,128)(2,1)} %copy.19.router_ref, ...), custom_call_target="tpu_custom_call" | custom-call | flops 11000000512 | tf_op jit(solution)/shard_map/frames/pallas_call | solution.py:419
  83.0 3.6 %all-to-all-start = ((bf16[8,88,1536]{2,1,0:T(8,128)(2,1)}), bf16[8,88,1536]{2,1,0:T(8,128)(2,1)S(1)}, u32[]{:S(2)}, u32[]{:S(2)}) async-start(bf16[8,88,1536]{2,1,0:T(8,128)(2,1)} %bitcast.25), calls=%async_computation | async-start | bytes 4325376 | tf_op jit(solution)/shard_map/all_to_all | solution.py:414
  87.4 11.1 %frames.3 = (bf16[704,1536]{1,0:T(8,128)(2,1)}, f32[224,128]{1,0:T(8,128)}, f32[12,224,128]{2,1,0:T(8,128)}) custom-call(s32[1]{0:T(128)} %bitcast.me_ref, s32[1]{0:T(128)} %bitcast.1.expert_ref, s32[1,4]{1,0:T(1,128)} %len_ref.5, bf16[1024,1536]{1,0:T(8,128)(2,1)} %proj_ref.3, f32[12,31,128]{2,1,0:T(8,128)} %bitcast.33, bf16[1536,8]{1,0:T(8,128)(2,1)} %copy.19.router_ref, ...), custom_call_target="tpu_custom_call" | custom-call | flops 11000000512 | tf_op jit(solution)/shard_map/frames/pallas_call | solution.py:419
  98.5 15.4 %all-to-all-done = bf16[8,88,1536]{2,1,0:T(8,128)(2,1)S(1)} async-done(((bf16[8,88,1536]{2,1,0:T(8,128)(2,1)}), bf16[8,88,1536]{2,1,0:T(8,128)(2,1)S(1)}, u32[]{:S(2)}, u32[]{:S(2)}) %all-to-all-start) | async-done | bytes 2162720 | tf_op jit(solution)/shard_map/all_to_all | solution.py:414
  113.9 1.4 copy-done.9
  115.3 4.4 %all-to-all-start.1 = ((bf16[8,88,1536]{2,1,0:T(8,128)(2,1)}), bf16[8,88,1536]{2,1,0:T(8,128)(2,1)}, u32[]{:S(2)}, u32[]{:S(2)}) async-start(bf16[8,88,1536]{2,1,0:T(8,128)(2,1)} %bitcast.24), calls=%async_computation.1 | async-start | bytes 4325376 | tf_op jit(solution)/shard_map/all_to_all | solution.py:414
  119.7 17.7 %collective-permute-done.7.refs_2_ = bf16[1024,1536]{1,0:T(8,128)(2,1)} collective-permute-done((bf16[1024,1536]{1,0:T(8,128)(2,1)}, bf16[1024,1536]{1,0:T(8,128)(2,1)}, u32[]{:S(2)}, u32[]{:S(2)}) %collective-permute-start.7) | collective-permute-done | bytes 3145760 | tf_op jit(solution)/shard_map/ppermute | solution.py:390
  137.4 9.8 %experts.2 = bf16[704,1536]{1,0:T(8,128)(2,1)} custom-call(s32[1]{0:T(128)} %bitcast.1.expert_ref, bf16[704,1536]{1,0:T(8,128)(2,1)} %bitcast.22, bf16[512,1536]{1,0:T(8,128)(2,1)} %bitcast.26, bf16[512,1536]{1,0:T(8,128)(2,1)} %bitcast.29, bf16[1024,1536]{1,0:T(8,128)(2,1)} %collective-permute-done.7.refs_2_), custom_call_target="tpu_custom_call" | custom-call | flops 8800000000 | tf_op jit(solution)/shard_map/experts/pallas_call | solution.py:441
  147.2 3.7 %all-to-all-start.2 = ((bf16[8,88,1536]{2,1,0:T(8,128)(2,1)}), bf16[8,88,1536]{2,1,0:T(8,128)(2,1)S(1)}, u32[]{:S(2)}, u32[]{:S(2)}) async-start(bf16[8,88,1536]{2,1,0:T(8,128)(2,1)} %bitcast.23), calls=%async_computation.2 | async-start | bytes 4325376 | tf_op jit(solution)/shard_map/all_to_all | solution.py:414
  150.9 9.8 %experts.3 = (bf16[88,1536]{1,0:T(8,128)(2,1)}, bf16[88,1536]{1,0:T(8,128)(2,1)}, bf16[88,1536]{1,0:T(8,128)(2,1)}, bf16[88,1536]{1,0:T(8,128)(2,1)}, bf16[88,15...) custom-call(s32[1]{0:T(128)} %bitcast.1.expert_ref, ...), custom_call_target="tpu_custom_call" | custom-call | flops 8800000000 | tf_op jit(solution)/shard_map/experts/pallas_call | solution.py:441
  161.2 1.4 collective-permute-done.8.refs_1_
  163.3 15.0 %all-to-all-done.2 = bf16[8,88,1536]{2,1,0:T(8,128)(2,1)S(1)} async-done(((bf16[8,88,1536]{2,1,0:T(8,128)(2,1)}), bf16[8,88,1536]{2,1,0:T(8,128)(2,1)S(1)}, u32[]{:S(2)}, u32[]{:S(2)}) %all-to-all-start.2) | async-done | bytes 2162720 | tf_op jit(solution)/shard_map/all_to_all | solution.py:414
  180.1 3.2 %collective-permute-start.9 = (bf16[224,1536]{1,0:T(8,128)(2,1)S(1)}, bf16[224,1536]{1,0:T(8,128)(2,1)S(1)}, u32[]{:S(2)}, u32[]{:S(2)}) collective-permute-start(bf16[224,1536]{1,0:T(8,128)(2,1)S(1)} %theirs.1), channel_id=1, source_target_pairs={{0,2},{1,3},{2,0},{3,1},{4,6},{5,7},{6,4},{7,5},{8,10},{9,11},{10,... | collective-permute-start | bytes 2064392 | tf_op jit(solution)/shard_map/ppermute | solution.py:473
  184.5 2.3 %collective-permute-start.13 = (bf16[88,1536]{1,0:T(8,128)(2,1)S(1)}, bf16[88,1536]{1,0:T(8,128)(2,1)S(1)}, u32[]{:S(2)}, u32[]{:S(2)}) collective-permute-start(bf16[88,1536]{1,0:T(8,128)(2,1)S(1)} %copy-done.18), channel_id=1, source_target_pairs={{0,20},{4,16},{8,28},{12,24},{16,4},{20,0},{24,12},{28,8},{1,21},{... | collective-permute-start | bytes 811016 | tf_op jit(solution)/shard_map/ppermute | solution.py:318
  186.8 5.9 %collective-permute-done.10.refs_2_ = bf16[88,1536]{1,0:T(8,128)(2,1)S(1)} collective-permute-done((bf16[88,1536]{1,0:T(8,128)(2,1)S(1)}, bf16[88,1536]{1,0:T(8,128)(2,1)S(1)}, u32[]{:S(2)}, u32[]{:S(2)}) %collective-permute-start.10) | collective-permute-done | bytes 270368 | tf_op jit(solution)/shard_map/ppermute | solution.py:318
  193.3 3.2 %collective-permute-done.11.refs_3_ = bf16[88,1536]{1,0:T(8,128)(2,1)S(1)} collective-permute-done((bf16[88,1536]{1,0:T(8,128)(2,1)S(1)}, bf16[88,1536]{1,0:T(8,128)(2,1)S(1)}, u32[]{:S(2)}, u32[]{:S(2)}) %collective-permute-start.11) | collective-permute-done | bytes 270368 | tf_op jit(solution)/shard_map/ppermute | solution.py:318
  196.5 2.3 %collective-permute-start.15 = (bf16[88,1536]{1,0:T(8,128)(2,1)S(1)}, bf16[88,1536]{1,0:T(8,128)(2,1)S(1)}, u32[]{:S(2)}, u32[]{:S(2)}) collective-permute-start(bf16[88,1536]{1,0:T(8,128)(2,1)S(1)} %copy-done.16), channel_id=1, source_target_pairs={{0,28},{4,24},{8,20},{12,16},{16,12},{20,8},{24,4},{28,0},{1,29},{... | collective-permute-start | bytes 811016 | tf_op jit(solution)/shard_map/ppermute | solution.py:318
  198.8 11.8 %collective-permute-done.13.refs_5_ = bf16[88,1536]{1,0:T(8,128)(2,1)S(1)} collective-permute-done((bf16[88,1536]{1,0:T(8,128)(2,1)S(1)}, bf16[88,1536]{1,0:T(8,128)(2,1)S(1)}, u32[]{:S(2)}, u32[]{:S(2)}) %collective-permute-start.13) | collective-permute-done | bytes 270368 | tf_op jit(solution)/shard_map/ppermute | solution.py:318
  210.7 1.7 mine.1
  (73 shorter events, 10.9 us)
Async XLA Ops:
  0.0 8.3 %copy-start.14 = (s32[1,224,2]{1,2,0:T(2,128)S(1)}, s32[1,224,2]{1,2,0:T(2,128)}, u32[]{:S(2)}) copy-start(s32[1,224,2]{1,2,0:T(2,128)} %param.21) | copy-start | bytes 5380
  0.0 10.2 %copy-start.25 = (f32[16]{0:T(128)S(1)}, f32[16]{0:T(128)}, u32[]{:S(2)}) copy-start(f32[16]{0:T(128)} %param.14) | copy-start | bytes 196
  0.0 32.6 %copy-start.5 = (s32[1,4]{1,0:T(1,128)S(1)}, s32[1,4]{1,0:T(1,128)}, u32[]{:S(2)}) copy-start(s32[1,4]{1,0:T(1,128)} %len_ref.5) | copy-start | bytes 52
  2.6 18.0 %collective-permute-start = (bf16[3,224,256]{2,1,0:T(8,128)(2,1)}, bf16[3,224,256]{2,1,0:T(8,128)(2,1)S(1)}, u32[]{:S(2)}, u32[]{:S(2)}) collective-permute-start(bf16[3,224,256]{2,1,0:T(8,128)(2,1)} %get-tuple-element.36), channel_id=1, source_target_pairs={{0,1},{1,0},{2,3},{3,2},{4,5},{5,4},{6,7},{7,6},{8,9},{9,8},{10,11... | collective-permute-start | bytes 1032200 | tf_op jit(solution)/shard_map/ppermute | solution.py:318
  5.7 26.9 %collective-permute-start.1 = (bf16[3,224,256]{2,1,0:T(8,128)(2,1)}, bf16[3,224,256]{2,1,0:T(8,128)(2,1)S(1)}, u32[]{:S(2)}, u32[]{:S(2)}) collective-permute-start(bf16[3,224,256]{2,1,0:T(8,128)(2,1)} %get-tuple-element.37), channel_id=1, source_target_pairs={{0,2},{1,3},{2,0},{3,1},{4,6},{5,7},{6,4},{7,5},{8,10},{9,11},{10,... | collective-permute-start | bytes 1032200 | tf_op jit(solution)/shard_map/ppermute | solution.py:318
  8.3 24.3 %collective-permute-start.2 = (bf16[3,224,256]{2,1,0:T(8,128)(2,1)}, bf16[3,224,256]{2,1,0:T(8,128)(2,1)S(1)}, u32[]{:S(2)}, u32[]{:S(2)}) collective-permute-start(bf16[3,224,256]{2,1,0:T(8,128)(2,1)} %get-tuple-element.38), channel_id=1, source_target_pairs={{0,3},{1,2},{2,1},{3,0},{4,7},{5,6},{6,5},{7,4},{8,11},{9,10},{10,... | collective-permute-start | bytes 1032200 | tf_op jit(solution)/shard_map/ppermute | solution.py:318
  8.3 44.1 %collective-permute-start.6 = (s32[224,2]{0,1:T(2,128)S(1)}, s32[224,2]{0,1:T(2,128)S(1)}, u32[]{:S(2)}, u32[]{:S(2)}) collective-permute-start(s32[224,2]{0,1:T(2,128)S(1)} %bitcast.35), channel_id=1, source_target_pairs={{0,2},{1,3},{2,0},{3,1},{4,6},{5,7},{6,4},{7,5},{8,10},{9,11},{10,... | collective-permute-start | bytes 5384 | tf_op jit(solution)/shard_map/ppermute | solution.py:367
  33.6 15.3 %copy-start.10 = (bf16[1,512,1536]{2,1,0:T(8,128)(2,1)S(1)}, bf16[1,512,1536]{2,1,0:T(8,128)(2,1)}, u32[]{:S(2)}) copy-start(bf16[1,512,1536]{2,1,0:T(8,128)(2,1)} %param.18) | copy-start | bytes 4718596
  33.6 15.3 %copy-start.11 = (bf16[1,512,1536]{2,1,0:T(8,128)(2,1)S(1)}, bf16[1,512,1536]{2,1,0:T(8,128)(2,1)}, u32[]{:S(2)}) copy-start(bf16[1,512,1536]{2,1,0:T(8,128)(2,1)} %param.19) | copy-start | bytes 4718596
  39.8 15.8 %collective-permute-start.3 = (bf16[2,256,256]{2,1,0:T(8,128)(2,1)S(1)}, bf16[2,256,256]{2,1,0:T(8,128)(2,1)S(1)}, u32[]{:S(2)}, u32[]{:S(2)}) collective-permute-start(bf16[2,256,256]{2,1,0:T(8,128)(2,1)S(1)} %get-tuple-element.40), channel_id=1, source_target_pairs={{0,1},{1,0},{2,3},{3,2},{4,5},{5,4},{6,7},{7,6},{8,9},{9,8},{10,11... | collective-permute-start | bytes 786440 | tf_op jit(solution)/shard_map/ppermute | solution.py:318
  46.4 21.4 %collective-permute-start.4 = (bf16[2,256,256]{2,1,0:T(8,128)(2,1)S(1)}, bf16[2,256,256]{2,1,0:T(8,128)(2,1)S(1)}, u32[]{:S(2)}, u32[]{:S(2)}) collective-permute-start(bf16[2,256,256]{2,1,0:T(8,128)(2,1)S(1)} %get-tuple-element.41), channel_id=1, source_target_pairs={{0,2},{1,3},{2,0},{3,1},{4,6},{5,7},{6,4},{7,5},{8,10},{9,11},{10,... | collective-permute-start | bytes 786440 | tf_op jit(solution)/shard_map/ppermute | solution.py:318
  47.4 20.4 %collective-permute-start.5 = (bf16[2,256,256]{2,1,0:T(8,128)(2,1)S(1)}, bf16[2,256,256]{2,1,0:T(8,128)(2,1)S(1)}, u32[]{:S(2)}, u32[]{:S(2)}) collective-permute-start(bf16[2,256,256]{2,1,0:T(8,128)(2,1)S(1)} %get-tuple-element.42), channel_id=1, source_target_pairs={{0,3},{1,2},{2,1},{3,0},{4,7},{5,6},{6,5},{7,4},{8,11},{9,10},{10,... | collective-permute-start | bytes 786440 | tf_op jit(solution)/shard_map/ppermute | solution.py:318
  52.5 18.9 %copy-start.15 = (s32[224,2]{0,1:T(2,128)}, s32[224,2]{0,1:T(2,128)S(1)}, u32[]{:S(2)}) copy-start(s32[224,2]{0,1:T(2,128)S(1)} %collective-permute-done.6) | copy-start | bytes 5380
  55.6 15.7 %copy-start.22 = (bf16[2,256,256]{2,1,0:T(8,128)(2,1)}, bf16[2,256,256]{2,1,0:T(8,128)(2,1)S(1)}, u32[]{:S(2)}) copy-start(bf16[2,256,256]{2,1,0:T(8,128)(2,1)S(1)} %collective-permute-done.3.refs_1_) | copy-start | bytes 786436
  67.8 69.7 %collective-permute-start.7 = (bf16[1024,1536]{1,0:T(8,128)(2,1)}, bf16[1024,1536]{1,0:T(8,128)(2,1)}, u32[]{:S(2)}, u32[]{:S(2)}) collective-permute-start(bf16[1024,1536]{1,0:T(8,128)(2,1)} %pad_maximum_fusion), channel_id=1, source_target_pairs={{0,1},{1,0},{2,3},{3,2},{4,5},{5,4},{6,7},{7,6},{8,9},{9,8},{10,11... | collective-permute-start | bytes 9437192 | tf_op jit(solution)/shard_map/ppermute | solution.py:390
  83.0 30.9 %all-to-all-start = ((bf16[8,88,1536]{2,1,0:T(8,128)(2,1)}), bf16[8,88,1536]{2,1,0:T(8,128)(2,1)S(1)}, u32[]{:S(2)}, u32[]{:S(2)}) async-start(bf16[8,88,1536]{2,1,0:T(8,128)(2,1)} %bitcast.25), calls=%async_computation | async-start | bytes 4325376 | tf_op jit(solution)/shard_map/all_to_all | solution.py:414
  115.3 31.9 %all-to-all-start.1 = ((bf16[8,88,1536]{2,1,0:T(8,128)(2,1)}), bf16[8,88,1536]{2,1,0:T(8,128)(2,1)}, u32[]{:S(2)}, u32[]{:S(2)}) async-start(bf16[8,88,1536]{2,1,0:T(8,128)(2,1)} %bitcast.24), calls=%async_computation.1 | async-start | bytes 4325376 | tf_op jit(solution)/shard_map/all_to_all | solution.py:414
  147.2 31.1 %all-to-all-start.2 = ((bf16[8,88,1536]{2,1,0:T(8,128)(2,1)}), bf16[8,88,1536]{2,1,0:T(8,128)(2,1)S(1)}, u32[]{:S(2)}, u32[]{:S(2)}) async-start(bf16[8,88,1536]{2,1,0:T(8,128)(2,1)} %bitcast.23), calls=%async_computation.2 | async-start | bytes 4325376 | tf_op jit(solution)/shard_map/all_to_all | solution.py:414
  160.7 49.9 %copy-start = (f32[12,224,128]{2,1,0:T(8,128)S(1)}, f32[12,224,128]{2,1,0:T(8,128)}, u32[]{:S(2)}) copy-start(f32[12,224,128]{2,1,0:T(8,128)} %get-tuple-element.49.second_ref) | copy-start | bytes 4128772
  160.7 1.9 collective-permute-start.8
  178.3 32.3 %copy-start.1 = (bf16[88,1536]{1,0:T(8,128)(2,1)S(1)}, bf16[88,1536]{1,0:T(8,128)(2,1)}, u32[]{:S(2)}) copy-start(bf16[88,1536]{1,0:T(8,128)(2,1)} %get-tuple-element.58.refs_0_) | copy-start | bytes 811012
  178.3 32.4 %copy-start.3 = (bf16[88,1536]{1,0:T(8,128)(2,1)S(1)}, bf16[88,1536]{1,0:T(8,128)(2,1)}, u32[]{:S(2)}) copy-start(bf16[88,1536]{1,0:T(8,128)(2,1)} %copy-done.2) | copy-start | bytes 811012
  178.3 32.4 %copy-start.4 = (f32[224,128]{1,0:T(8,128)S(1)}, f32[224,128]{1,0:T(8,128)}, u32[]{:S(2)}) copy-start(f32[224,128]{1,0:T(8,128)} %get-tuple-element.48.info_ref) | copy-start | bytes 344068
  179.3 13.4 %copy-start.17 = (bf16[88,1536]{1,0:T(8,128)(2,1)S(1)}, bf16[88,1536]{1,0:T(8,128)(2,1)}, u32[]{:S(2)}) copy-start(bf16[88,1536]{1,0:T(8,128)(2,1)} %get-tuple-element.63) | copy-start | bytes 811012
  179.3 17.2 %copy-start.16 = (bf16[88,1536]{1,0:T(8,128)(2,1)S(1)}, bf16[88,1536]{1,0:T(8,128)(2,1)}, u32[]{:S(2)}) copy-start(bf16[88,1536]{1,0:T(8,128)(2,1)} %get-tuple-element.64) | copy-start | bytes 811012
  180.1 30.5 %collective-permute-start.9 = (bf16[224,1536]{1,0:T(8,128)(2,1)S(1)}, bf16[224,1536]{1,0:T(8,128)(2,1)S(1)}, u32[]{:S(2)}, u32[]{:S(2)}) collective-permute-start(bf16[224,1536]{1,0:T(8,128)(2,1)S(1)} %theirs.1), channel_id=1, source_target_pairs={{0,2},{1,3},{2,0},{3,1},{4,6},{5,7},{6,4},{7,5},{8,10},{9,11},{10,... | collective-permute-start | bytes 2064392 | tf_op jit(solution)/shard_map/ppermute | solution.py:473
  183.3 9.4 %collective-permute-start.10 = (bf16[88,1536]{1,0:T(8,128)(2,1)S(1)}, bf16[88,1536]{1,0:T(8,128)(2,1)S(1)}, u32[]{:S(2)}, u32[]{:S(2)}) collective-permute-start(bf16[88,1536]{1,0:T(8,128)(2,1)S(1)} %copy-done.21), channel_id=1, source_target_pairs={{0,8},{4,12},{8,0},{12,4},{16,24},{20,28},{24,16},{28,20},{1,9},{5... | collective-permute-start | bytes 811016 | tf_op jit(solution)/shard_map/ppermute | solution.py:318
  183.8 12.7 %collective-permute-start.11 = (bf16[88,1536]{1,0:T(8,128)(2,1)S(1)}, bf16[88,1536]{1,0:T(8,128)(2,1)S(1)}, u32[]{:S(2)}, u32[]{:S(2)}) collective-permute-start(bf16[88,1536]{1,0:T(8,128)(2,1)S(1)} %copy-done.20), channel_id=1, source_target_pairs={{0,12},{4,8},{8,4},{12,0},{16,28},{20,24},{24,20},{28,16},{1,13},{... | collective-permute-start | bytes 811016 | tf_op jit(solution)/shard_map/ppermute | solution.py:318
  183.8 15.0 %collective-permute-start.12 = (bf16[88,1536]{1,0:T(8,128)(2,1)S(1)}, bf16[88,1536]{1,0:T(8,128)(2,1)S(1)}, u32[]{:S(2)}, u32[]{:S(2)}) collective-permute-start(bf16[88,1536]{1,0:T(8,128)(2,1)S(1)} %copy-done.19), channel_id=1, source_target_pairs={{0,16},{4,20},{8,24},{12,28},{16,0},{20,4},{24,8},{28,12},{1,17},{... | collective-permute-start | bytes 811016 | tf_op jit(solution)/shard_map/ppermute | solution.py:318
  184.5 26.1 %collective-permute-start.13 = (bf16[88,1536]{1,0:T(8,128)(2,1)S(1)}, bf16[88,1536]{1,0:T(8,128)(2,1)S(1)}, u32[]{:S(2)}, u32[]{:S(2)}) collective-permute-start(bf16[88,1536]{1,0:T(8,128)(2,1)S(1)} %copy-done.18), channel_id=1, source_target_pairs={{0,20},{4,16},{8,28},{12,24},{16,4},{20,0},{24,12},{28,8},{1,21},{... | collective-permute-start | bytes 811016 | tf_op jit(solution)/shard_map/ppermute | solution.py:318
  192.7 17.9 %collective-permute-start.14 = (bf16[88,1536]{1,0:T(8,128)(2,1)S(1)}, bf16[88,1536]{1,0:T(8,128)(2,1)S(1)}, u32[]{:S(2)}, u32[]{:S(2)}) collective-permute-start(bf16[88,1536]{1,0:T(8,128)(2,1)S(1)} %copy-done.17), channel_id=1, source_target_pairs={{0,24},{4,28},{8,16},{12,20},{16,8},{20,12},{24,0},{28,4},{1,25},{... | collective-permute-start | bytes 811016 | tf_op jit(solution)/shard_map/ppermute | solution.py:318
  196.5 14.1 %collective-permute-start.15 = (bf16[88,1536]{1,0:T(8,128)(2,1)S(1)}, bf16[88,1536]{1,0:T(8,128)(2,1)S(1)}, u32[]{:S(2)}, u32[]{:S(2)}) collective-permute-start(bf16[88,1536]{1,0:T(8,128)(2,1)S(1)} %copy-done.16), channel_id=1, source_target_pairs={{0,28},{4,24},{8,20},{12,16},{16,12},{20,8},{24,4},{28,0},{1,29},{... | collective-permute-start | bytes 811016 | tf_op jit(solution)/shard_map/ppermute | solution.py:318
  (13 other events, 34.9 us)

commit v10 on v9

--- a/solution.py
+++ b/solution.py
@@ -157,10 +157,10 @@
     turned_ref,
     *refs,
 ):
-    att_refs, out_refs = refs[:count], refs[count:-5]
+    att_refs, out_ref = refs[:count], refs[count]
     info_ref, second_ref, x_ref, first_ref, lab_ref = refs[-5:]
     me = me_ref[0]
-    turn = 0 if flip else expert_ref[0]
+    turn = expert_ref[0]
     window = rows + 2 * HALO
     half = (KERNEL - 1) // 2
     tiles = D // LANES
@@ -248,7 +248,7 @@
     select = jnp.concatenate(
         [jnp.where(slot == order[e : e + 1, :], 1.0, 0.0) for e in range(experts)], axis=0
     ).astype(BF16)
-    out_refs[0][...] = jnp.dot(select, mixed, preferred_element_type=F32).astype(BF16)
+    out_ref[...] = jnp.dot(select, mixed, preferred_element_type=F32).astype(BF16)
 
 
 def joined(refs):
@@ -257,31 +257,42 @@
     return jnp.concatenate([ref[...].astype(F32) for ref in refs], axis=0).astype(BF16)
 
 
-def expert_kernel(chunks, units, spans, expert_ref, x_ref, *refs):
-    pieces = len(refs) - chunks - (chunks > 1)
-    w_refs, o_refs = refs[:pieces], refs[pieces : pieces + chunks]
-    tokens = x_ref[...]
+def expert_kernel(experts, units, spans, expert_ref, *refs):
+    count = (len(refs) - experts - 2) // 2
+    sources, o_refs = refs[:count], refs[count : count + experts]
+    held, (sum_ref, sem_ref) = refs[count + experts : -2], refs[-2:]
+    copies = [
+        pltpu.make_async_copy(sources[k], held[k], sem_ref.at[k]) for k in range(count)
+    ]
+    for copy in copies:
+        copy.start()
+    waiting = set(range(count))
+
+    def ready(k):
+        if k in waiting:
+            waiting.remove(k)
+            copies[k].wait()
+        return held[k]
+
+    tokens = ready(0)[...]
     total = None
     for (into, first), (out, second) in spans:
         raw = lax.dot_general(
             tokens,
-            w_refs[into][first : first + units, :],
+            ready(1 + into)[first : first + units, :],
             (((1,), (1,)), ((), ())),
             preferred_element_type=F32,
         )
         hidden = (raw / (1.0 + jnp.exp(-raw))).astype(BF16)
         product = jnp.dot(
-            hidden, w_refs[out][second : second + units, :], preferred_element_type=F32
+            hidden, ready(1 + out)[second : second + units, :], preferred_element_type=F32
         )
         total = product if total is None else total + product
-    if chunks == 1:
-        o_refs[0][...] = total.astype(BF16)
-        return
-    refs[-1][...] = total
+    sum_ref[...] = total
     tall = o_refs[0].shape[0]
     for r, o_ref in enumerate(o_refs):
         begin = pl.multiple_of((expert_ref[0] ^ r) * tall, 8)
-        o_ref[...] = refs[-1][pl.ds(begin, tall), :].astype(BF16)
+        o_ref[...] = sum_ref[pl.ds(begin, tall), :].astype(BF16)
 
 
 def mixture_of(info, back_refs):
@@ -402,29 +413,21 @@
     taps = jnp.transpose(conv_taps.reshape(KERNEL, D // LANES, LANES), (1, 0, 2))
     slots = experts * capacity
 
-    def chunks_of(split):
-        if split:
-            return (jax.ShapeDtypeStruct((capacity, D), BF16),) * experts
-        return (jax.ShapeDtypeStruct((slots, D), BF16),)
-
-    def route(arrays):
-        if len(arrays) > 1:
-            return trade(arrays, "dp")
-        whole = arrays[0].reshape(experts, capacity, D)
+    def route(array):
+        whole = array.reshape(experts, capacity, D)
         moved = lax.all_to_all(whole, "dp", split_axis=0, concat_axis=0, tiled=True)
-        return [moved.reshape(slots, D)]
+        return (moved.reshape(slots, D),)
 
     def send_frames(windows, flip, block_routes):
-        chunks = chunks_of(False)
         made = pl.pallas_call(
             functools.partial(frame_kernel, count, rows, experts, capacity, place, flip),
-            out_shape=chunks
-            + (
+            out_shape=(
+                jax.ShapeDtypeStruct((slots, D), BF16),
                 jax.ShapeDtypeStruct((rows, LANES), F32),
                 jax.ShapeDtypeStruct((D // LANES, rows, LANES), F32),
             ),
             in_specs=[SMEM, SMEM, SMEM] + [VMEM] * (5 + count),
-            out_specs=(VMEM,) * (len(chunks) + 2),
+            out_specs=(VMEM,) * 3,
             scratch_shapes=[
                 pltpu.VMEM((D // LANES, window, LANES), F32),
                 pltpu.VMEM((D // LANES, rows, LANES), F32),
@@ -434,31 +437,31 @@
             cost_estimate=cost(10),
             name="frames",
         )(me, expert, lengths, out_proj, taps, router, block_routes, block_routes.T, *windows)
-        return made[:-2], made[-2], made[-1]
-
-    def run_expert(tokens, split):
-        chunks = chunks_of(split)
-        produced = pl.pallas_call(
-            functools.partial(expert_kernel, len(chunks), units, spans),
-            out_shape=chunks,
-            in_specs=[SMEM, VMEM] + [VMEM] * len(weights),
-            out_specs=(VMEM,) * len(chunks),
-            scratch_shapes=[pltpu.VMEM((slots, D), F32)] * split,
+        return made
+
+    def run_expert(tokens):
+        operands = (*tokens, *weights)
+        return pl.pallas_call(
+            functools.partial(expert_kernel, experts, units, spans),
+            out_shape=(jax.ShapeDtypeStruct((capacity, D), BF16),) * experts,
+            in_specs=[SMEM] + [pl.BlockSpec(memory_space=pl.ANY)] * len(operands),
+            out_specs=(VMEM,) * experts,
+            scratch_shapes=[pltpu.VMEM(one.shape, BF16) for one in operands]
+            + [pltpu.VMEM((slots, D), F32), pltpu.SemaphoreType.DMA((len(operands),))],
             compiler_params=params(56),
             cost_estimate=cost(8),
             name="experts",
-        )(expert, *tokens, *weights)
-        return produced
+        )(expert, *operands)
 
     outgoing_a, info_a, _ = send_frames(windows, half, partner_routes)
     tokens_a = route(outgoing_a)
-    windows = after(windows, outgoing_a)
+    windows = after(windows, (outgoing_a,))
     outgoing_b, info_b, second = send_frames(windows, 0, routes[0])
-    tokens_b = route(after(outgoing_b, tokens_a))
-    produced_a = run_expert(tokens_a, False)
-    back_a = route(after(produced_a, tokens_b))
-    produced_b = run_expert(after(tokens_b, produced_a), True)
-    back_b = route(produced_b)
+    tokens_b = route(after((outgoing_b,), tokens_a)[0])
+    produced_a = run_expert(tokens_a)
+    back_a = trade(after(produced_a, tokens_b), "dp")
+    produced_b = run_expert(after(tokens_b, produced_a))
+    back_b = trade(produced_b, "dp")
     back_a = after(back_a, back_b[1:2])
 
     theirs = pl.pallas_call(

time: 213 us -> 211 us (level)
  starting transfers between devices: 41.9 us -> 47.2 us
  waiting for transfers between devices: 107 us -> 103 us
    all_to_all x3 -> x2, waiting for transfers between devices: 30.4 us -> 13.9 us  [route(): moved = lax.all_to_all(whole, 'dp', split_axis=0, concat_axis=0, tiled=True)]
    ppermute x13 -> x20, starting transfers between devices: 21.6 us -> 30.5 us  [trade(): lax.ppermute(arrays[r], axis, [(i, i ^ r) for i in range(count)])]
    ppermute x13 -> x20, waiting for transfers between devices: 59.1 us -> 67.4 us  [trade(): lax.ppermute(arrays[r], axis, [(i, i ^ r) for i in range(count)])]
    all_to_all x3 -> x2, starting transfers between devices: 11.7 us -> 8.11 us  [route(): moved = lax.all_to_all(whole, 'dp', split_axis=0, concat_axis=0, tiled=True)]
    ppermute x1, waiting for transfers between devices: 0.01 us -> 3.01 us  [body(): received = lax.ppermute(theirs, 'tm', partner)]
    unnamed x53 -> x57, local copies, waits for them, and re-layouts: 5.78 us -> 4.03 us
  transfers between devices with their start and end apart: 19 -> 25, of which waited for: 11 -> 14; matrix products, arithmetic and copies ran while one was open for 2% -> 2% of each run, Pallas kernels for 23% -> 22%
where the time goes in v10:
time: 211 us; the launch traced here: 210 us
  waiting for transfers between devices  103 us (49%)
  Pallas kernels  51.8 us (25%)
  starting transfers between devices  47.2 us (22%)
  local copies, waits for them, and re-layouts  6.45 us (3%)
    ppermute x20, waiting for transfers between devices, trade(): lax.ppermute(arrays[r], axis, [(i, i ^ r) for i in range(count)])  67.4 us
    ppermute x20, starting transfers between devices, trade(): lax.ppermute(arrays[r], axis, [(i, i ^ r) for i in range(count)])  30.5 us
    pallas_call x2, Pallas kernels, send_frames(): pl.pallas_call(functools.partial(frame_kernel, count, rows, experts, capa...  23.5 us
    ppermute x1, waiting for transfers between devices, body(): moved = lax.ppermute(shard, 'tm', [(i, i ^ 1) for i in range(count)])  18.5 us
    pallas_call x2, Pallas kernels, run_expert(): pl.pallas_call(functools.partial(expert_kernel, experts, units, spans), o...  17.6 us
    all_to_all x2, waiting for transfers between devices, route(): moved = lax.all_to_all(whole, 'dp', split_axis=0, concat_axis=0, tiled=True)  13.9 us
    all_to_all x2, starting transfers between devices, route(): moved = lax.all_to_all(whole, 'dp', split_axis=0, concat_axis=0, tiled=True)  8.11 us
    pallas_call x1, Pallas kernels, body(): pl.pallas_call(functools.partial(attend_kernel, count, rows, heads, place...  5.53 us
  transfers between devices with their start and end apart: 25, of which 14 were waited for; matrix products, arithmetic and copies ran while one was open for 2% of the time, Pallas kernels for 22%

profile of v10, /device:TPU:0, one launch (start us, length us, event | category | flops | bytes accessed | tf_op | source)
XLA Modules:
  0.0 210.4 jit_solution(749819249490008032)
XLA Ops:
  0.0 2.6 %pack.1 = (bf16[3,224,256]{2,1,0:T(8,128)(2,1)}, bf16[3,224,256]{2,1,0:T(8,128)(2,1)}, bf16[3,224,256]{2,1,0:T(8,128)(2,1)}, bf16[3,224,256]{2,1,0:T(8,128)(2,1)}) custom-call(s32[1]{0:T(128)} %bitcast.me_ref, bf16[224,1024]{1,0:T(8,128)(2,1)} %bitcast.35, bf16[224,1024]{1,0:T(8,128)(2,1)} %bitcast.36, bf16[224,1024]{1,0:T(8,128)(2,1)} %bitcast.37), custom_call_target="tpu_custom_call" | custom-call | flops 1100000000 | tf_op jit(solution)/shard_map/pack/pallas_call | solution.py:366
  2.6 3.1 %collective-permute-start = (bf16[3,224,256]{2,1,0:T(8,128)(2,1)}, bf16[3,224,256]{2,1,0:T(8,128)(2,1)S(1)}, u32[]{:S(2)}, u32[]{:S(2)}) collective-permute-start(bf16[3,224,256]{2,1,0:T(8,128)(2,1)} %get-tuple-element.58), channel_id=1, source_target_pairs={{0,1},{1,0},{2,3},{3,2},{4,5},{5,4},{6,7},{7,6},{8,9},{9,8},{10,11... | collective-permute-start | bytes 1032200 | tf_op jit(solution)/shard_map/ppermute | solution.py:329
  5.7 2.6 %collective-permute-start.1 = (bf16[3,224,256]{2,1,0:T(8,128)(2,1)}, bf16[3,224,256]{2,1,0:T(8,128)(2,1)S(1)}, u32[]{:S(2)}, u32[]{:S(2)}) collective-permute-start(bf16[3,224,256]{2,1,0:T(8,128)(2,1)} %get-tuple-element.59), channel_id=1, source_target_pairs={{0,2},{1,3},{2,0},{3,1},{4,6},{5,7},{6,4},{7,5},{8,10},{9,11},{10,... | collective-permute-start | bytes 1032200 | tf_op jit(solution)/shard_map/ppermute | solution.py:329
  8.3 1.9 collective-permute-start.6
  10.3 10.3 %collective-permute-done.refs_1_ = bf16[3,224,256]{2,1,0:T(8,128)(2,1)S(1)} collective-permute-done((bf16[3,224,256]{2,1,0:T(8,128)(2,1)}, bf16[3,224,256]{2,1,0:T(8,128)(2,1)S(1)}, u32[]{:S(2)}, u32[]{:S(2)}) %collective-permute-start) | collective-permute-done | bytes 344096 | tf_op jit(solution)/shard_map/ppermute | solution.py:329
  20.6 12.0 %collective-permute-done.1.refs_2_ = bf16[3,224,256]{2,1,0:T(8,128)(2,1)S(1)} collective-permute-done((bf16[3,224,256]{2,1,0:T(8,128)(2,1)}, bf16[3,224,256]{2,1,0:T(8,128)(2,1)S(1)}, u32[]{:S(2)}, u32[]{:S(2)}) %collective-permute-start.1) | collective-permute-done | bytes 344096 | tf_op jit(solution)/shard_map/ppermute | solution.py:329
  33.6 5.5 %attend.1 = (bf16[2,256,256]{2,1,0:T(8,128)(2,1)S(1)}, bf16[2,256,256]{2,1,0:T(8,128)(2,1)S(1)}, bf16[2,256,256]{2,1,0:T(8,128)(2,1)S(1)}, bf16[2,256,256]{2,1,0:T(8,128)(2,1)S(1)}) custom-call(s32[1]{0:T(128)} %bitcast.me_ref, f32[4]{0:T(128)S(1)} %dynamic_slice.3.scale_ref, s32[1,4]{1,0:T(1,128)S(1)} %copy-done.3, bf16[3,224,256]{2,1,0:T(8,128)(2,1)S(1)} %copy-done.6, ...), custom_call_target="tpu_custom_call" | custom-call | flops 6600000000 | tf_op jit(solution)/shard_map/attend/pallas_call | solution.py:382
  39.9 6.5 %collective-permute-start.3 = (bf16[2,256,256]{2,1,0:T(8,128)(2,1)S(1)}, bf16[2,256,256]{2,1,0:T(8,128)(2,1)S(1)}, u32[]{:S(2)}, u32[]{:S(2)}) collective-permute-start(bf16[2,256,256]{2,1,0:T(8,128)(2,1)S(1)} %get-tuple-element.62), channel_id=1, source_target_pairs={{0,1},{1,0},{2,3},{3,2},{4,5},{5,4},{6,7},{7,6},{8,9},{9,8},{10,11... | collective-permute-start | bytes 786440 | tf_op jit(solution)/shard_map/ppermute | solution.py:329
  48.9 1.9 pad_maximum_fusion
  53.3 2.4 %collective-permute-done.3.refs_1_ = bf16[2,256,256]{2,1,0:T(8,128)(2,1)S(1)} collective-permute-done((bf16[2,256,256]{2,1,0:T(8,128)(2,1)S(1)}, bf16[2,256,256]{2,1,0:T(8,128)(2,1)S(1)}, u32[]{:S(2)}, u32[]{:S(2)}) %collective-permute-start.3) | collective-permute-done | bytes 262176 | tf_op jit(solution)/shard_map/ppermute | solution.py:329
  55.6 12.2 %collective-permute-done.4.refs_2_ = bf16[2,256,256]{2,1,0:T(8,128)(2,1)S(1)} collective-permute-done((bf16[2,256,256]{2,1,0:T(8,128)(2,1)S(1)}, bf16[2,256,256]{2,1,0:T(8,128)(2,1)S(1)}, u32[]{:S(2)}, u32[]{:S(2)}) %collective-permute-start.4) | collective-permute-done | bytes 262176 | tf_op jit(solution)/shard_map/ppermute | solution.py:329
  67.8 3.6 %collective-permute-start.7 = (bf16[1024,1536]{1,0:T(8,128)(2,1)}, bf16[1024,1536]{1,0:T(8,128)(2,1)}, u32[]{:S(2)}, u32[]{:S(2)}) collective-permute-start(bf16[1024,1536]{1,0:T(8,128)(2,1)} %pad_maximum_fusion), channel_id=1, source_target_pairs={{0,1},{1,0},{2,3},{3,2},{4,5},{5,4},{6,7},{7,6},{8,9},{9,8},{10,11... | collective-permute-start | bytes 9437192 | tf_op jit(solution)/shard_map/ppermute | solution.py:401
  71.4 10.8 %frames.2 = (bf16[704,1536]{1,0:T(8,128)(2,1)}, f32[224,128]{1,0:T(8,128)}, f32[12,224,128]{2,1,0:T(8,128)}) custom-call(s32[1]{0:T(128)} %bitcast.me_ref, s32[1]{0:T(128)} %bitcast.1.expert_ref, s32[1,4]{1,0:T(1,128)} %len_ref.5, bf16[1024,1536]{1,0:T(8,128)(2,1)} %proj_ref.3, f32[12,31,128]{2,1,0:T(8,128)} %bitcast.29, bf16[1536,8]{1,0:T(8,128)(2,1)} %copy.19.router_ref, ...), custom_call_target="tpu_custom_call" | custom-call | flops 11000000512 | tf_op jit(solution)/shard_map/frames/pallas_call | solution.py:422
  82.2 4.5 %all-to-all-start = ((bf16[8,88,1536]{2,1,0:T(8,128)(2,1)}), bf16[8,88,1536]{2,1,0:T(8,128)(2,1)S(1)}, u32[]{:S(2)}, u32[]{:S(2)}) async-start(bf16[8,88,1536]{2,1,0:T(8,128)(2,1)} %bitcast.22), calls=%async_computation | async-start | bytes 4325376 | tf_op jit(solution)/shard_map/all_to_all | solution.py:418
  87.5 12.7 %frames.3 = (bf16[704,1536]{1,0:T(8,128)(2,1)}, f32[224,128]{1,0:T(8,128)}, f32[12,224,128]{2,1,0:T(8,128)}) custom-call(s32[1]{0:T(128)} %bitcast.me_ref, s32[1]{0:T(128)} %bitcast.1.expert_ref, s32[1,4]{1,0:T(1,128)} %len_ref.5, bf16[1024,1536]{1,0:T(8,128)(2,1)} %proj_ref.3, f32[12,31,128]{2,1,0:T(8,128)} %bitcast.30, bf16[1536,8]{1,0:T(8,128)(2,1)} %copy.19.router_ref, ...), custom_call_target="tpu_custom_call" | custom-call | flops 11000000512 | tf_op jit(solution)/shard_map/frames/pallas_call | solution.py:422
  100.2 13.9 %all-to-all-done = bf16[8,88,1536]{2,1,0:T(8,128)(2,1)S(1)} async-done(((bf16[8,88,1536]{2,1,0:T(8,128)(2,1)}), bf16[8,88,1536]{2,1,0:T(8,128)(2,1)S(1)}, u32[]{:S(2)}, u32[]{:S(2)}) %all-to-all-start) | async-done | bytes 2162720 | tf_op jit(solution)/shard_map/all_to_all | solution.py:418
  115.4 3.6 %all-to-all-start.1 = ((bf16[8,88,1536]{2,1,0:T(8,128)(2,1)}), bf16[8,88,1536]{2,1,0:T(8,128)(2,1)S(1)}, u32[]{:S(2)}, u32[]{:S(2)}) async-start(bf16[8,88,1536]{2,1,0:T(8,128)(2,1)} %bitcast.21), calls=%async_computation.1 | async-start | bytes 4325376 | tf_op jit(solution)/shard_map/all_to_all | solution.py:418
  119.0 18.5 %collective-permute-done.7.refs_3_ = bf16[1024,1536]{1,0:T(8,128)(2,1)} collective-permute-done((bf16[1024,1536]{1,0:T(8,128)(2,1)}, bf16[1024,1536]{1,0:T(8,128)(2,1)}, u32[]{:S(2)}, u32[]{:S(2)}) %collective-permute-start.7) | collective-permute-done | bytes 3145760 | tf_op jit(solution)/shard_map/ppermute | solution.py:401
  137.4 8.7 %experts.2 = (bf16[88,1536]{1,0:T(8,128)(2,1)}, bf16[88,1536]{1,0:T(8,128)(2,1)}, bf16[88,1536]{1,0:T(8,128)(2,1)}, bf16[88,1536]{1,0:T(8,128)(2,1)}, bf16[88,15...) custom-call(s32[1]{0:T(128)} %bitcast.1.expert_ref, ...), custom_call_target="tpu_custom_call" | custom-call | flops 8800000000 | tf_op jit(solution)/shard_map/experts/pallas_call | solution.py:444
  149.9 8.8 %experts.3 = (bf16[88,1536]{1,0:T(8,128)(2,1)}, bf16[88,1536]{1,0:T(8,128)(2,1)}, bf16[88,1536]{1,0:T(8,128)(2,1)}, bf16[88,1536]{1,0:T(8,128)(2,1)}, bf16[88,15...) custom-call(s32[1]{0:T(128)} %bitcast.1.expert_ref, ...), custom_call_target="tpu_custom_call" | custom-call | flops 8800000000 | tf_op jit(solution)/shard_map/experts/pallas_call | solution.py:444
  158.9 2.5 %collective-permute-start.13 = (bf16[88,1536]{1,0:T(8,128)(2,1)S(1)}, bf16[88,1536]{1,0:T(8,128)(2,1)S(1)}, u32[]{:S(2)}, u32[]{:S(2)}) collective-permute-start(bf16[88,1536]{1,0:T(8,128)(2,1)S(1)} %copy-done.23), channel_id=1, source_target_pairs={{0,24},{4,28},{8,16},{12,20},{16,8},{20,12},{24,0},{28,4},{1,25},{... | collective-permute-start | bytes 811016 | tf_op jit(solution)/shard_map/ppermute | solution.py:329
  162.4 6.8 %collective-permute-done.13.refs_6_ = bf16[88,1536]{1,0:T(8,128)(2,1)S(1)} collective-permute-done((bf16[88,1536]{1,0:T(8,128)(2,1)S(1)}, bf16[88,1536]{1,0:T(8,128)(2,1)S(1)}, u32[]{:S(2)}, u32[]{:S(2)}) %collective-permute-start.13) | collective-permute-done | bytes 270368 | tf_op jit(solution)/shard_map/ppermute | solution.py:329
  169.2 4.9 %collective-permute-done.14.refs_7_ = bf16[88,1536]{1,0:T(8,128)(2,1)S(1)} collective-permute-done((bf16[88,1536]{1,0:T(8,128)(2,1)S(1)}, bf16[88,1536]{1,0:T(8,128)(2,1)S(1)}, u32[]{:S(2)}, u32[]{:S(2)}) %collective-permute-start.14) | collective-permute-done | bytes 270368 | tf_op jit(solution)/shard_map/ppermute | solution.py:329
  174.9 3.1 %collective-permute-start.16 = (bf16[224,1536]{1,0:T(8,128)(2,1)S(1)}, bf16[224,1536]{1,0:T(8,128)(2,1)S(1)}, u32[]{:S(2)}, u32[]{:S(2)}) collective-permute-start(bf16[224,1536]{1,0:T(8,128)(2,1)S(1)} %theirs.1), channel_id=1, source_target_pairs={{0,2},{1,3},{2,0},{3,1},{4,6},{5,7},{6,4},{7,5},{8,10},{9,11},{10,... | collective-permute-start | bytes 2064392 | tf_op jit(solution)/shard_map/ppermute | solution.py:476
  179.5 1.6 collective-permute-start.19
  181.5 5.8 %collective-permute-done.17.refs_2_ = bf16[88,1536]{1,0:T(8,128)(2,1)S(1)} collective-permute-done((bf16[88,1536]{1,0:T(8,128)(2,1)S(1)}, bf16[88,1536]{1,0:T(8,128)(2,1)S(1)}, u32[]{:S(2)}, u32[]{:S(2)}) %collective-permute-start.17) | collective-permute-done | bytes 270368 | tf_op jit(solution)/shard_map/ppermute | solution.py:329
  187.4 2.4 %collective-permute-start.21 = (bf16[88,1536]{1,0:T(8,128)(2,1)S(1)}, bf16[88,1536]{1,0:T(8,128)(2,1)S(1)}, u32[]{:S(2)}, u32[]{:S(2)}) collective-permute-start(bf16[88,1536]{1,0:T(8,128)(2,1)S(1)} %copy-done.17), channel_id=1, source_target_pairs={{0,24},{4,28},{8,16},{12,20},{16,8},{20,12},{24,0},{28,4},{1,25},{... | collective-permute-start | bytes 811016 | tf_op jit(solution)/shard_map/ppermute | solution.py:329
  189.8 2.4 %collective-permute-done.18.refs_3_ = bf16[88,1536]{1,0:T(8,128)(2,1)S(1)} collective-permute-done((bf16[88,1536]{1,0:T(8,128)(2,1)S(1)}, bf16[88,1536]{1,0:T(8,128)(2,1)S(1)}, u32[]{:S(2)}, u32[]{:S(2)}) %collective-permute-start.18) | collective-permute-done | bytes 270368 | tf_op jit(solution)/shard_map/ppermute | solution.py:329
  192.2 3.2 %collective-permute-start.22 = (bf16[88,1536]{1,0:T(8,128)(2,1)S(1)}, bf16[88,1536]{1,0:T(8,128)(2,1)S(1)}, u32[]{:S(2)}, u32[]{:S(2)}) collective-permute-start(bf16[88,1536]{1,0:T(8,128)(2,1)S(1)} %copy-done.16), channel_id=1, source_target_pairs={{0,28},{4,24},{8,20},{12,16},{16,12},{20,8},{24,4},{28,0},{1,29},{... | collective-permute-start | bytes 811016 | tf_op jit(solution)/shard_map/ppermute | solution.py:329
  195.3 10.3 %collective-permute-done.20.refs_5_ = bf16[88,1536]{1,0:T(8,128)(2,1)S(1)} collective-permute-done((bf16[88,1536]{1,0:T(8,128)(2,1)S(1)}, bf16[88,1536]{1,0:T(8,128)(2,1)S(1)}, u32[]{:S(2)}, u32[]{:S(2)}) %collective-permute-start.20) | collective-permute-done | bytes 270368 | tf_op jit(solution)/shard_map/ppermute | solution.py:329
  205.6 3.0 %collective-permute-done.16.part_ref = bf16[224,1536]{1,0:T(8,128)(2,1)S(1)} collective-permute-done((bf16[224,1536]{1,0:T(8,128)(2,1)S(1)}, bf16[224,1536]{1,0:T(8,128)(2,1)S(1)}, u32[]{:S(2)}, u32[]{:S(2)}) %collective-permute-start.16) | collective-permute-done | bytes 688160 | tf_op jit(solution)/shard_map/ppermute | solution.py:476
  208.7 1.7 mine.1
  (89 shorter events, 16.4 us)
Async XLA Ops:
  0.0 32.6 %copy-start.3 = (s32[1,4]{1,0:T(1,128)S(1)}, s32[1,4]{1,0:T(1,128)}, u32[]{:S(2)}) copy-start(s32[1,4]{1,0:T(1,128)} %len_ref.5) | copy-start | bytes 52
  2.6 18.0 %collective-permute-start = (bf16[3,224,256]{2,1,0:T(8,128)(2,1)}, bf16[3,224,256]{2,1,0:T(8,128)(2,1)S(1)}, u32[]{:S(2)}, u32[]{:S(2)}) collective-permute-start(bf16[3,224,256]{2,1,0:T(8,128)(2,1)} %get-tuple-element.58), channel_id=1, source_target_pairs={{0,1},{1,0},{2,3},{3,2},{4,5},{5,4},{6,7},{7,6},{8,9},{9,8},{10,11... | collective-permute-start | bytes 1032200 | tf_op jit(solution)/shard_map/ppermute | solution.py:329
  5.7 26.9 %collective-permute-start.1 = (bf16[3,224,256]{2,1,0:T(8,128)(2,1)}, bf16[3,224,256]{2,1,0:T(8,128)(2,1)S(1)}, u32[]{:S(2)}, u32[]{:S(2)}) collective-permute-start(bf16[3,224,256]{2,1,0:T(8,128)(2,1)} %get-tuple-element.59), channel_id=1, source_target_pairs={{0,2},{1,3},{2,0},{3,1},{4,6},{5,7},{6,4},{7,5},{8,10},{9,11},{10,... | collective-permute-start | bytes 1032200 | tf_op jit(solution)/shard_map/ppermute | solution.py:329
  8.3 24.3 %collective-permute-start.2 = (bf16[3,224,256]{2,1,0:T(8,128)(2,1)}, bf16[3,224,256]{2,1,0:T(8,128)(2,1)S(1)}, u32[]{:S(2)}, u32[]{:S(2)}) collective-permute-start(bf16[3,224,256]{2,1,0:T(8,128)(2,1)} %get-tuple-element.60), channel_id=1, source_target_pairs={{0,3},{1,2},{2,1},{3,0},{4,7},{5,6},{6,5},{7,4},{8,11},{9,10},{10,... | collective-permute-start | bytes 1032200 | tf_op jit(solution)/shard_map/ppermute | solution.py:329
  8.3 44.2 %collective-permute-start.6 = (s32[224,2]{0,1:T(2,128)S(1)}, s32[224,2]{0,1:T(2,128)S(1)}, u32[]{:S(2)}, u32[]{:S(2)}) collective-permute-start(s32[224,2]{0,1:T(2,128)S(1)} %bitcast.32), channel_id=1, source_target_pairs={{0,2},{1,3},{2,0},{3,1},{4,6},{5,7},{6,4},{7,5},{8,10},{9,11},{10,... | collective-permute-start | bytes 5384 | tf_op jit(solution)/shard_map/ppermute | solution.py:378
  39.9 15.8 %collective-permute-start.3 = (bf16[2,256,256]{2,1,0:T(8,128)(2,1)S(1)}, bf16[2,256,256]{2,1,0:T(8,128)(2,1)S(1)}, u32[]{:S(2)}, u32[]{:S(2)}) collective-permute-start(bf16[2,256,256]{2,1,0:T(8,128)(2,1)S(1)} %get-tuple-element.62), channel_id=1, source_target_pairs={{0,1},{1,0},{2,3},{3,2},{4,5},{5,4},{6,7},{7,6},{8,9},{9,8},{10,11... | collective-permute-start | bytes 786440 | tf_op jit(solution)/shard_map/ppermute | solution.py:329
  46.4 21.4 %collective-permute-start.4 = (bf16[2,256,256]{2,1,0:T(8,128)(2,1)S(1)}, bf16[2,256,256]{2,1,0:T(8,128)(2,1)S(1)}, u32[]{:S(2)}, u32[]{:S(2)}) collective-permute-start(bf16[2,256,256]{2,1,0:T(8,128)(2,1)S(1)} %get-tuple-element.63), channel_id=1, source_target_pairs={{0,2},{1,3},{2,0},{3,1},{4,6},{5,7},{6,4},{7,5},{8,10},{9,11},{10,... | collective-permute-start | bytes 786440 | tf_op jit(solution)/shard_map/ppermute | solution.py:329
  47.4 20.4 %collective-permute-start.5 = (bf16[2,256,256]{2,1,0:T(8,128)(2,1)S(1)}, bf16[2,256,256]{2,1,0:T(8,128)(2,1)S(1)}, u32[]{:S(2)}, u32[]{:S(2)}) collective-permute-start(bf16[2,256,256]{2,1,0:T(8,128)(2,1)S(1)} %get-tuple-element.64), channel_id=1, source_target_pairs={{0,3},{1,2},{2,1},{3,0},{4,7},{5,6},{6,5},{7,4},{8,11},{9,10},{10,... | collective-permute-start | bytes 786440 | tf_op jit(solution)/shard_map/ppermute | solution.py:329
  67.8 69.7 %collective-permute-start.7 = (bf16[1024,1536]{1,0:T(8,128)(2,1)}, bf16[1024,1536]{1,0:T(8,128)(2,1)}, u32[]{:S(2)}, u32[]{:S(2)}) collective-permute-start(bf16[1024,1536]{1,0:T(8,128)(2,1)} %pad_maximum_fusion), channel_id=1, source_target_pairs={{0,1},{1,0},{2,3},{3,2},{4,5},{5,4},{6,7},{7,6},{8,9},{9,8},{10,11... | collective-permute-start | bytes 9437192 | tf_op jit(solution)/shard_map/ppermute | solution.py:401
  82.2 31.8 %all-to-all-start = ((bf16[8,88,1536]{2,1,0:T(8,128)(2,1)}), bf16[8,88,1536]{2,1,0:T(8,128)(2,1)S(1)}, u32[]{:S(2)}, u32[]{:S(2)}) async-start(bf16[8,88,1536]{2,1,0:T(8,128)(2,1)} %bitcast.22), calls=%async_computation | async-start | bytes 4325376 | tf_op jit(solution)/shard_map/all_to_all | solution.py:418
  115.4 30.9 %all-to-all-start.1 = ((bf16[8,88,1536]{2,1,0:T(8,128)(2,1)}), bf16[8,88,1536]{2,1,0:T(8,128)(2,1)S(1)}, u32[]{:S(2)}, u32[]{:S(2)}) async-start(bf16[8,88,1536]{2,1,0:T(8,128)(2,1)} %bitcast.21), calls=%async_computation.1 | async-start | bytes 4325376 | tf_op jit(solution)/shard_map/all_to_all | solution.py:418
  146.3 27.8 %copy-start.4 = (bf16[88,1536]{1,0:T(8,128)(2,1)S(1)}, bf16[88,1536]{1,0:T(8,128)(2,1)}, u32[]{:S(2)}) copy-start(bf16[88,1536]{1,0:T(8,128)(2,1)} %get-tuple-element.94.refs_0_) | copy-start | bytes 811012
  146.3 12.6 %collective-permute-start.8 = (bf16[88,1536]{1,0:T(8,128)(2,1)}, bf16[88,1536]{1,0:T(8,128)(2,1)S(1)}, u32[]{:S(2)}, u32[]{:S(2)}) collective-permute-start(bf16[88,1536]{1,0:T(8,128)(2,1)} %get-tuple-element.85), channel_id=1, source_target_pairs={{0,4},{4,0},{8,12},{12,8},{16,20},{20,16},{24,28},{28,24},{1,5},{5... | collective-permute-start | bytes 811016 | tf_op jit(solution)/shard_map/ppermute | solution.py:329
  146.4 15.0 %collective-permute-start.9 = (bf16[88,1536]{1,0:T(8,128)(2,1)}, bf16[88,1536]{1,0:T(8,128)(2,1)S(1)}, u32[]{:S(2)}, u32[]{:S(2)}) collective-permute-start(bf16[88,1536]{1,0:T(8,128)(2,1)} %get-tuple-element.86), channel_id=1, source_target_pairs={{0,8},{4,12},{8,0},{12,4},{16,24},{20,28},{24,16},{28,20},{1,9},{5... | collective-permute-start | bytes 811016 | tf_op jit(solution)/shard_map/ppermute | solution.py:329
  147.9 13.7 %collective-permute-start.10 = (bf16[88,1536]{1,0:T(8,128)(2,1)}, bf16[88,1536]{1,0:T(8,128)(2,1)S(1)}, u32[]{:S(2)}, u32[]{:S(2)}) collective-permute-start(bf16[88,1536]{1,0:T(8,128)(2,1)} %get-tuple-element.87), channel_id=1, source_target_pairs={{0,12},{4,8},{8,4},{12,0},{16,28},{20,24},{24,20},{28,16},{1,13},{... | collective-permute-start | bytes 811016 | tf_op jit(solution)/shard_map/ppermute | solution.py:329
  148.2 13.8 %collective-permute-start.11 = (bf16[88,1536]{1,0:T(8,128)(2,1)}, bf16[88,1536]{1,0:T(8,128)(2,1)S(1)}, u32[]{:S(2)}, u32[]{:S(2)}) collective-permute-start(bf16[88,1536]{1,0:T(8,128)(2,1)} %get-tuple-element.88), channel_id=1, source_target_pairs={{0,16},{4,20},{8,24},{12,28},{16,0},{20,4},{24,8},{28,12},{1,17},{... | collective-permute-start | bytes 811016 | tf_op jit(solution)/shard_map/ppermute | solution.py:329
  149.7 12.7 %collective-permute-start.12 = (bf16[88,1536]{1,0:T(8,128)(2,1)}, bf16[88,1536]{1,0:T(8,128)(2,1)S(1)}, u32[]{:S(2)}, u32[]{:S(2)}) collective-permute-start(bf16[88,1536]{1,0:T(8,128)(2,1)} %get-tuple-element.89), channel_id=1, source_target_pairs={{0,20},{4,16},{8,28},{12,24},{16,4},{20,0},{24,12},{28,8},{1,21},{... | collective-permute-start | bytes 811016 | tf_op jit(solution)/shard_map/ppermute | solution.py:329
  158.8 28.6 %copy-start.17 = (bf16[88,1536]{1,0:T(8,128)(2,1)S(1)}, bf16[88,1536]{1,0:T(8,128)(2,1)}, u32[]{:S(2)}) copy-start(bf16[88,1536]{1,0:T(8,128)(2,1)} %get-tuple-element.107) | copy-start | bytes 811012
  158.8 33.4 %copy-start.16 = (bf16[88,1536]{1,0:T(8,128)(2,1)S(1)}, bf16[88,1536]{1,0:T(8,128)(2,1)}, u32[]{:S(2)}) copy-start(bf16[88,1536]{1,0:T(8,128)(2,1)} %get-tuple-element.108) | copy-start | bytes 811012
  158.8 49.8 %copy-start = (f32[12,224,128]{2,1,0:T(8,128)S(1)}, f32[12,224,128]{2,1,0:T(8,128)}, u32[]{:S(2)}) copy-start(f32[12,224,128]{2,1,0:T(8,128)} %get-tuple-element.71.second_ref) | copy-start | bytes 4128772
  158.8 49.8 %copy-start.1 = (bf16[88,1536]{1,0:T(8,128)(2,1)S(1)}, bf16[88,1536]{1,0:T(8,128)(2,1)}, u32[]{:S(2)}) copy-start(bf16[88,1536]{1,0:T(8,128)(2,1)} %get-tuple-element.102.refs_0_) | copy-start | bytes 811012
  158.8 49.8 %copy-start.2 = (f32[224,128]{1,0:T(8,128)S(1)}, f32[224,128]{1,0:T(8,128)}, u32[]{:S(2)}) copy-start(f32[224,128]{1,0:T(8,128)} %get-tuple-element.70.info_ref) | copy-start | bytes 344068
  158.9 10.4 %collective-permute-start.13 = (bf16[88,1536]{1,0:T(8,128)(2,1)S(1)}, bf16[88,1536]{1,0:T(8,128)(2,1)S(1)}, u32[]{:S(2)}, u32[]{:S(2)}) collective-permute-start(bf16[88,1536]{1,0:T(8,128)(2,1)S(1)} %copy-done.23), channel_id=1, source_target_pairs={{0,24},{4,28},{8,16},{12,20},{16,8},{20,12},{24,0},{28,4},{1,25},{... | collective-permute-start | bytes 811016 | tf_op jit(solution)/shard_map/ppermute | solution.py:329
  161.4 12.7 %collective-permute-start.14 = (bf16[88,1536]{1,0:T(8,128)(2,1)S(1)}, bf16[88,1536]{1,0:T(8,128)(2,1)S(1)}, u32[]{:S(2)}, u32[]{:S(2)}) collective-permute-start(bf16[88,1536]{1,0:T(8,128)(2,1)S(1)} %copy-done.22), channel_id=1, source_target_pairs={{0,28},{4,24},{8,20},{12,16},{16,12},{20,8},{24,4},{28,0},{1,29},{... | collective-permute-start | bytes 811016 | tf_op jit(solution)/shard_map/ppermute | solution.py:329
  161.6 12.5 %collective-permute-start.15 = (bf16[88,1536]{1,0:T(8,128)(2,1)}, bf16[88,1536]{1,0:T(8,128)(2,1)S(1)}, u32[]{:S(2)}, u32[]{:S(2)}) collective-permute-start(bf16[88,1536]{1,0:T(8,128)(2,1)} %get-tuple-element.93), channel_id=1, source_target_pairs={{0,4},{4,0},{8,12},{12,8},{16,20},{20,16},{24,28},{28,24},{1,5},{5... | collective-permute-start | bytes 811016 | tf_op jit(solution)/shard_map/ppermute | solution.py:329
  174.9 33.7 %collective-permute-start.16 = (bf16[224,1536]{1,0:T(8,128)(2,1)S(1)}, bf16[224,1536]{1,0:T(8,128)(2,1)S(1)}, u32[]{:S(2)}, u32[]{:S(2)}) collective-permute-start(bf16[224,1536]{1,0:T(8,128)(2,1)S(1)} %theirs.1), channel_id=1, source_target_pairs={{0,2},{1,3},{2,0},{3,1},{4,6},{5,7},{6,4},{7,5},{8,10},{9,11},{10,... | collective-permute-start | bytes 2064392 | tf_op jit(solution)/shard_map/ppermute | solution.py:476
  178.0 9.3 %collective-permute-start.17 = (bf16[88,1536]{1,0:T(8,128)(2,1)S(1)}, bf16[88,1536]{1,0:T(8,128)(2,1)S(1)}, u32[]{:S(2)}, u32[]{:S(2)}) collective-permute-start(bf16[88,1536]{1,0:T(8,128)(2,1)S(1)} %copy-done.21), channel_id=1, source_target_pairs={{0,8},{4,12},{8,0},{12,4},{16,24},{20,28},{24,16},{28,20},{1,9},{5... | collective-permute-start | bytes 811016 | tf_op jit(solution)/shard_map/ppermute | solution.py:329
  179.5 12.7 %collective-permute-start.18 = (bf16[88,1536]{1,0:T(8,128)(2,1)S(1)}, bf16[88,1536]{1,0:T(8,128)(2,1)S(1)}, u32[]{:S(2)}, u32[]{:S(2)}) collective-permute-start(bf16[88,1536]{1,0:T(8,128)(2,1)S(1)} %copy-done.20), channel_id=1, source_target_pairs={{0,12},{4,8},{8,4},{12,0},{16,28},{20,24},{24,20},{28,16},{1,13},{... | collective-permute-start | bytes 811016 | tf_op jit(solution)/shard_map/ppermute | solution.py:329
  179.5 15.8 %collective-permute-start.19 = (bf16[88,1536]{1,0:T(8,128)(2,1)S(1)}, bf16[88,1536]{1,0:T(8,128)(2,1)S(1)}, u32[]{:S(2)}, u32[]{:S(2)}) collective-permute-start(bf16[88,1536]{1,0:T(8,128)(2,1)S(1)} %copy-done.19), channel_id=1, source_target_pairs={{0,16},{4,20},{8,24},{12,28},{16,0},{20,4},{24,8},{28,12},{1,17},{... | collective-permute-start | bytes 811016 | tf_op jit(solution)/shard_map/ppermute | solution.py:329
  181.1 24.5 %collective-permute-start.20 = (bf16[88,1536]{1,0:T(8,128)(2,1)S(1)}, bf16[88,1536]{1,0:T(8,128)(2,1)S(1)}, u32[]{:S(2)}, u32[]{:S(2)}) collective-permute-start(bf16[88,1536]{1,0:T(8,128)(2,1)S(1)} %copy-done.18), channel_id=1, source_target_pairs={{0,20},{4,16},{8,28},{12,24},{16,4},{20,0},{24,12},{28,8},{1,21},{... | collective-permute-start | bytes 811016 | tf_op jit(solution)/shard_map/ppermute | solution.py:329
  187.4 18.3 %collective-permute-start.21 = (bf16[88,1536]{1,0:T(8,128)(2,1)S(1)}, bf16[88,1536]{1,0:T(8,128)(2,1)S(1)}, u32[]{:S(2)}, u32[]{:S(2)}) collective-permute-start(bf16[88,1536]{1,0:T(8,128)(2,1)S(1)} %copy-done.17), channel_id=1, source_target_pairs={{0,24},{4,28},{8,16},{12,20},{16,8},{20,12},{24,0},{28,4},{1,25},{... | collective-permute-start | bytes 811016 | tf_op jit(solution)/shard_map/ppermute | solution.py:329
  192.2 13.5 %collective-permute-start.22 = (bf16[88,1536]{1,0:T(8,128)(2,1)S(1)}, bf16[88,1536]{1,0:T(8,128)(2,1)S(1)}, u32[]{:S(2)}, u32[]{:S(2)}) collective-permute-start(bf16[88,1536]{1,0:T(8,128)(2,1)S(1)} %copy-done.16), channel_id=1, source_target_pairs={{0,28},{4,24},{8,20},{12,16},{16,12},{20,8},{24,4},{28,0},{1,29},{... | collective-permute-start | bytes 811016 | tf_op jit(solution)/shard_map/ppermute | solution.py:329
  (21 other events, 240.7 us)

commit v11 on v10

--- a/solution.py
+++ b/solution.py
@@ -252,15 +252,16 @@
 
 
 def joined(refs):
-    if len(refs) == 1:
-        return refs[0][...]
-    return jnp.concatenate([ref[...].astype(F32) for ref in refs], axis=0).astype(BF16)
-
-
-def expert_kernel(experts, units, spans, expert_ref, *refs):
-    count = (len(refs) - experts - 2) // 2
-    sources, o_refs = refs[:count], refs[count : count + experts]
-    held, (sum_ref, sem_ref) = refs[count + experts : -2], refs[-2:]
+    order = far_first(len(refs))
+    parts = [refs[order.index(r)][...].astype(F32) for r in range(len(refs))]
+    return jnp.concatenate(parts, axis=0).astype(BF16)
+
+
+def expert_kernel(experts, units, spans, begun, expert_ref, *refs):
+    results = max(1, experts)
+    count = (len(refs) - results - 2) // 2
+    sources, o_refs = refs[:count], refs[count : count + results]
+    held, (sum_ref, sem_ref) = refs[count + results : -2], refs[-2:]
     copies = [
         pltpu.make_async_copy(sources[k], held[k], sem_ref.at[k]) for k in range(count)
     ]
@@ -275,7 +276,7 @@
         return held[k]
 
     tokens = ready(0)[...]
-    total = None
+    products = []
     for (into, first), (out, second) in spans:
         raw = lax.dot_general(
             tokens,
@@ -284,10 +285,15 @@
             preferred_element_type=F32,
         )
         hidden = (raw / (1.0 + jnp.exp(-raw))).astype(BF16)
-        product = jnp.dot(
-            hidden, ready(1 + out)[second : second + units, :], preferred_element_type=F32
+        products.append(
+            jnp.dot(hidden, ready(1 + out)[second : second + units, :], preferred_element_type=F32)
         )
-        total = product if total is None else total + product
+    if begun:
+        products.append(ready(count - 1)[...])
+    total = functools.reduce(jnp.add, products)
+    if experts == 0:
+        o_refs[0][...] = total
+        return
     sum_ref[...] = total
     tall = o_refs[0].shape[0]
     for r, o_ref in enumerate(o_refs):
@@ -330,6 +336,10 @@
         for r in range(count - 1, 0, -1)
     }
     return [arrays[0]] + [moved[r] for r in range(1, count)]
+
+
+def far_first(count):
+    return sorted(range(count), key=lambda r: (r == 0, -bin(r >> 1).count("1"), r))
 
 
 def after(arrays, markers):
@@ -439,17 +449,27 @@
         )(me, expert, lengths, out_proj, taps, router, block_routes, block_routes.T, *windows)
         return made
 
-    def run_expert(tokens):
-        operands = (*tokens, *weights)
+    def run_expert(tokens, matrices, parts, partial=(), last=True):
+        operands = (*tokens, *matrices, *partial)
+        if last:
+            made = (jax.ShapeDtypeStruct((capacity, D), BF16),) * experts
+        else:
+            made = (jax.ShapeDtypeStruct((slots, D), F32),)
+        kernel = functools.partial(
+            expert_kernel, experts if last else 0, units, parts, len(partial) > 0
+        )
         return pl.pallas_call(
-            functools.partial(expert_kernel, experts, units, spans),
-            out_shape=(jax.ShapeDtypeStruct((capacity, D), BF16),) * experts,
+            kernel,
+            out_shape=made,
             in_specs=[SMEM] + [pl.BlockSpec(memory_space=pl.ANY)] * len(operands),
-            out_specs=(VMEM,) * experts,
-            scratch_shapes=[pltpu.VMEM(one.shape, BF16) for one in operands]
-            + [pltpu.VMEM((slots, D), F32), pltpu.SemaphoreType.DMA((len(operands),))],
+            out_specs=(VMEM,) * len(made),
+            scratch_shapes=[pltpu.VMEM(one.shape, one.dtype) for one in operands]
+            + [
+                pltpu.VMEM((slots, D) if last else (8, LANES), F32),
+                pltpu.SemaphoreType.DMA((len(operands),)),
+            ],
             compiler_params=params(56),
-            cost_estimate=cost(8),
+            cost_estimate=cost(8 if len(parts) > 1 else 5),
             name="experts",
         )(expert, *operands)
 
@@ -458,11 +478,18 @@
     windows = after(windows, (outgoing_a,))
     outgoing_b, info_b, second = send_frames(windows, 0, routes[0])
     tokens_b = route(after((outgoing_b,), tokens_a)[0])
-    produced_a = run_expert(tokens_a)
+    if half == 2:
+        begun = run_expert(tokens_a, weights[:2], spans[:1], last=False)
+        rest = (((0, 0), (0, units)),)
+        produced_a = run_expert(tokens_a, weights[2:], rest, begun)
+    else:
+        produced_a = run_expert(tokens_a, weights, spans)
     back_a = trade(after(produced_a, tokens_b), "dp")
-    produced_b = run_expert(after(tokens_b, produced_a))
+    produced_b = run_expert(after(tokens_b, produced_a), weights, spans)
     back_b = trade(produced_b, "dp")
-    back_a = after(back_a, back_b[1:2])
+    order = far_first(experts)
+    back_a = after([back_a[r] for r in order], back_b[1:2])
+    back_b = [back_b[r] for r in order]
 
     theirs = pl.pallas_call(
         theirs_kernel,

time: 211 us -> 230 us (1.090)
  waiting for transfers between devices: 103 us -> 120 us
  Pallas kernels: 51.8 us -> 57.5 us
  starting transfers between devices: 47.2 us -> 44.4 us
    ppermute x1, waiting for transfers between devices: 0.01 us -> 18.3 us  [body(): partner_routes = lax.ppermute(routes[0], 'tm', partner)]
    ppermute x1, waiting for transfers between devices: 18.5 us -> 34.3 us  [body(): moved = lax.ppermute(shard, 'tm', [(i, i ^ 1) for i in range(count)])]
    ppermute x20, waiting for transfers between devices: 67.4 us -> 53.8 us  [trade(): lax.ppermute(arrays[r], axis, [(i, i ^ r) for i in range(count)])]
    pallas_call x2 -> x3, Pallas kernels: 17.6 us -> 22.6 us  [run_expert(): pl.pallas_call(kernel, out_shape=made, in_specs=[SMEM] + [pl.BlockSpec(me...]
    all_to_all x2, waiting for transfers between devices: 13.9 us -> 9.09 us  [route(): moved = lax.all_to_all(whole, 'dp', split_axis=0, concat_axis=0, tiled=True)]
  transfers between devices with their start and end apart: 25 -> 25, of which waited for: 14 -> 15; matrix products, arithmetic and copies ran while one was open for 2% -> 2% of each run, Pallas kernels for 22% -> 16%
where the time goes in v11:
time: 230 us
  waiting for transfers between devices  120 us (52%)
  Pallas kernels  57.5 us (25%)
  starting transfers between devices  44.4 us (19%)
  local copies, waits for them, and re-layouts  5.93 us (3%)
    ppermute x20, waiting for transfers between devices, trade(): lax.ppermute(arrays[r], axis, [(i, i ^ r) for i in range(count)])  53.8 us
    ppermute x1, waiting for transfers between devices, body(): moved = lax.ppermute(shard, 'tm', [(i, i ^ 1) for i in range(count)])  34.3 us
    ppermute x20, starting transfers between devices, trade(): lax.ppermute(arrays[r], axis, [(i, i ^ r) for i in range(count)])  29.3 us
    pallas_call x2, Pallas kernels, send_frames(): pl.pallas_call(functools.partial(frame_kernel, count, rows, experts, capa...  24.2 us
    pallas_call x3, Pallas kernels, run_expert(): pl.pallas_call(kernel, out_shape=made, in_specs=[SMEM] + [pl.BlockSpec(me...  22.6 us
    ppermute x1, waiting for transfers between devices, body(): partner_routes = lax.ppermute(routes[0], 'tm', partner)  18.3 us
    all_to_all x2, waiting for transfers between devices, route(): moved = lax.all_to_all(whole, 'dp', split_axis=0, concat_axis=0, tiled=True)  9.09 us
    all_to_all x2, starting transfers between devices, route(): moved = lax.all_to_all(whole, 'dp', split_axis=0, concat_axis=0, tiled=True)  8.84 us
  transfers between devices with their start and end apart: 25, of which 15 were waited for; matrix products, arithmetic and copies ran while one was open for 2% of the time, Pallas kernels for 16%

profile of v11, /device:TPU:0, one launch (start us, length us, event | category | flops | bytes accessed | tf_op | source)
XLA Modules:
  0.0 230.3 jit_solution(9083858145769273536)
XLA Ops:
  0.0 2.6 %pack.1 = (bf16[3,224,256]{2,1,0:T(8,128)(2,1)}, bf16[3,224,256]{2,1,0:T(8,128)(2,1)}, bf16[3,224,256]{2,1,0:T(8,128)(2,1)}, bf16[3,224,256]{2,1,0:T(8,128)(2,1)}) custom-call(s32[1]{0:T(128)} %bitcast.me_ref, bf16[224,1024]{1,0:T(8,128)(2,1)} %bitcast.33, bf16[224,1024]{1,0:T(8,128)(2,1)} %bitcast.34, bf16[224,1024]{1,0:T(8,128)(2,1)} %bitcast.35), custom_call_target="tpu_custom_call" | custom-call | flops 1100000000 | tf_op jit(solution)/shard_map/pack/pallas_call | solution.py:376
  2.6 3.1 %collective-permute-start = (bf16[3,224,256]{2,1,0:T(8,128)(2,1)}, bf16[3,224,256]{2,1,0:T(8,128)(2,1)S(1)}, u32[]{:S(2)}, u32[]{:S(2)}) collective-permute-start(bf16[3,224,256]{2,1,0:T(8,128)(2,1)} %get-tuple-element.58), channel_id=1, source_target_pairs={{0,1},{1,0},{2,3},{3,2},{4,5},{5,4},{6,7},{7,6},{8,9},{9,8},{10,11... | collective-permute-start | bytes 1032200 | tf_op jit(solution)/shard_map/ppermute | solution.py:335
  5.7 2.6 %collective-permute-start.1 = (bf16[3,224,256]{2,1,0:T(8,128)(2,1)}, bf16[3,224,256]{2,1,0:T(8,128)(2,1)S(1)}, u32[]{:S(2)}, u32[]{:S(2)}) collective-permute-start(bf16[3,224,256]{2,1,0:T(8,128)(2,1)} %get-tuple-element.59), channel_id=1, source_target_pairs={{0,2},{1,3},{2,0},{3,1},{4,6},{5,7},{6,4},{7,5},{8,10},{9,11},{10,... | collective-permute-start | bytes 1032200 | tf_op jit(solution)/shard_map/ppermute | solution.py:335
  8.4 12.2 %collective-permute-done.refs_1_ = bf16[3,224,256]{2,1,0:T(8,128)(2,1)S(1)} collective-permute-done((bf16[3,224,256]{2,1,0:T(8,128)(2,1)}, bf16[3,224,256]{2,1,0:T(8,128)(2,1)S(1)}, u32[]{:S(2)}, u32[]{:S(2)}) %collective-permute-start) | collective-permute-done | bytes 344096 | tf_op jit(solution)/shard_map/ppermute | solution.py:335
  20.6 12.0 %collective-permute-done.1.refs_2_ = bf16[3,224,256]{2,1,0:T(8,128)(2,1)S(1)} collective-permute-done((bf16[3,224,256]{2,1,0:T(8,128)(2,1)}, bf16[3,224,256]{2,1,0:T(8,128)(2,1)S(1)}, u32[]{:S(2)}, u32[]{:S(2)}) %collective-permute-start.1) | collective-permute-done | bytes 344096 | tf_op jit(solution)/shard_map/ppermute | solution.py:335
  33.5 5.5 %attend.1 = (bf16[2,256,256]{2,1,0:T(8,128)(2,1)S(1)}, bf16[2,256,256]{2,1,0:T(8,128)(2,1)S(1)}, bf16[2,256,256]{2,1,0:T(8,128)(2,1)S(1)}, bf16[2,256,256]{2,1,0:T(8,128)(2,1)S(1)}) custom-call(s32[1]{0:T(128)} %bitcast.me_ref, f32[4]{0:T(128)S(1)} %dynamic_slice.3.scale_ref, s32[1,4]{1,0:T(1,128)S(1)} %copy-done.3, bf16[3,224,256]{2,1,0:T(8,128)(2,1)S(1)} %copy-done.6, ...), custom_call_target="tpu_custom_call" | custom-call | flops 6600000000 | tf_op jit(solution)/shard_map/attend/pallas_call | solution.py:392
  39.8 6.5 %collective-permute-start.3 = (bf16[2,256,256]{2,1,0:T(8,128)(2,1)S(1)}, bf16[2,256,256]{2,1,0:T(8,128)(2,1)S(1)}, u32[]{:S(2)}, u32[]{:S(2)}) collective-permute-start(bf16[2,256,256]{2,1,0:T(8,128)(2,1)S(1)} %get-tuple-element.62), channel_id=1, source_target_pairs={{0,1},{1,0},{2,3},{3,2},{4,5},{5,4},{6,7},{7,6},{8,9},{9,8},{10,11... | collective-permute-start | bytes 786440 | tf_op jit(solution)/shard_map/ppermute | solution.py:335
  48.8 2.0 collective-permute-start.6
  52.5 18.3 %collective-permute-done.6 = s32[224,2]{0,1:T(2,128)S(1)} collective-permute-done((s32[224,2]{0,1:T(2,128)S(1)}, s32[224,2]{0,1:T(2,128)S(1)}, u32[]{:S(2)}, u32[]{:S(2)}) %collective-permute-start.6) | collective-permute-done | bytes 1824 | tf_op jit(solution)/shard_map/ppermute | solution.py:388
  72.5 10.8 %frames.2 = (bf16[704,1536]{1,0:T(8,128)(2,1)}, f32[224,128]{1,0:T(8,128)}, f32[12,224,128]{2,1,0:T(8,128)}) custom-call(s32[1]{0:T(128)} %bitcast.me_ref, s32[1]{0:T(128)} %bitcast.1.expert_ref, s32[1,4]{1,0:T(1,128)} %len_ref.5, bf16[1024,1536]{1,0:T(8,128)(2,1)} %proj_ref.3, f32[12,31,128]{2,1,0:T(8,128)} %bitcast.27, bf16[1536,8]{1,0:T(8,128)(2,1)} %copy.19.router_ref, ...), custom_call_target="tpu_custom_call" | custom-call | flops 11000000512 | tf_op jit(solution)/shard_map/frames/pallas_call | solution.py:432
  83.3 4.5 %all-to-all-start = ((bf16[8,88,1536]{2,1,0:T(8,128)(2,1)}), bf16[8,88,1536]{2,1,0:T(8,128)(2,1)}, u32[]{:S(2)}, u32[]{:S(2)}) async-start(bf16[8,88,1536]{2,1,0:T(8,128)(2,1)} %bitcast.20), calls=%async_computation | async-start | bytes 4325376 | tf_op jit(solution)/shard_map/all_to_all | solution.py:428
  87.8 2.1 pad_maximum_fusion
  89.9 2.1 collective-permute-start.7
  92.7 13.4 %frames.3 = (bf16[704,1536]{1,0:T(8,128)(2,1)}, f32[224,128]{1,0:T(8,128)}, f32[12,224,128]{2,1,0:T(8,128)}) custom-call(s32[1]{0:T(128)} %bitcast.me_ref, s32[1]{0:T(128)} %bitcast.1.expert_ref, s32[1,4]{1,0:T(1,128)} %len_ref.5, bf16[1024,1536]{1,0:T(8,128)(2,1)} %proj_ref.3, f32[12,31,128]{2,1,0:T(8,128)} %bitcast.28, bf16[1536,8]{1,0:T(8,128)(2,1)} %copy.19.router_ref, ...), custom_call_target="tpu_custom_call" | custom-call | flops 11000000512 | tf_op jit(solution)/shard_map/frames/pallas_call | solution.py:432
  106.1 9.1 %all-to-all-done = bf16[8,88,1536]{2,1,0:T(8,128)(2,1)} async-done(((bf16[8,88,1536]{2,1,0:T(8,128)(2,1)}), bf16[8,88,1536]{2,1,0:T(8,128)(2,1)}, u32[]{:S(2)}, u32[]{:S(2)}) %all-to-all-start) | async-done | bytes 2162720 | tf_op jit(solution)/shard_map/all_to_all | solution.py:428
  115.2 4.3 %all-to-all-start.1 = ((bf16[8,88,1536]{2,1,0:T(8,128)(2,1)}), bf16[8,88,1536]{2,1,0:T(8,128)(2,1)}, u32[]{:S(2)}, u32[]{:S(2)}) async-start(bf16[8,88,1536]{2,1,0:T(8,128)(2,1)} %bitcast.19), calls=%async_computation.1 | async-start | bytes 4325376 | tf_op jit(solution)/shard_map/all_to_all | solution.py:428
  119.6 6.9 %experts.3.refs_2_ = f32[704,1536]{1,0:T(8,128)} custom-call(s32[1]{0:T(128)} %bitcast.1.expert_ref, bf16[704,1536]{1,0:T(8,128)(2,1)} %bitcast.10.refs_0_, bf16[512,1536]{1,0:T(8,128)(2,1)} %bitcast.25, bf16[512,1536]{1,0:T(8,128)(2,1)} %bitcast.22), custom_call_target="tpu_custom_call" | custom-call | flops 5500000256 | tf_op jit(solution)/shard_map/experts/pallas_call | solution.py:461
  126.5 34.3 %collective-permute-done.7.refs_1_.refs_3_ = bf16[1024,1536]{1,0:T(8,128)(2,1)} collective-permute-done((bf16[1024,1536]{1,0:T(8,128)(2,1)S(1)}, bf16[1024,1536]{1,0:T(8,128)(2,1)}, u32[]{:S(2)}, u32[]{:S(2)}) %collective-permute-start.7) | collective-permute-done | bytes 3145760 | tf_op jit(solution)/shard_map/ppermute | solution.py:411
  160.8 6.8 %experts.4 = (bf16[88,1536]{1,0:T(8,128)(2,1)}, bf16[88,1536]{1,0:T(8,128)(2,1)}, bf16[88,1536]{1,0:T(8,128)(2,1)}, bf16[88,1536]{1,0:T(8,128)(2,1)}, bf16[88,15...) custom-call(s32[1]{0:T(128)} %bitcast.1.expert_ref, ...), custom_call_target="tpu_custom_call" | custom-call | flops 5500000256 | tf_op jit(solution)/shard_map/experts/pallas_call | solution.py:461
  167.7 2.6 %collective-permute-start.8 = (bf16[88,1536]{1,0:T(8,128)(2,1)}, bf16[88,1536]{1,0:T(8,128)(2,1)S(1)}, u32[]{:S(2)}, u32[]{:S(2)}) collective-permute-start(bf16[88,1536]{1,0:T(8,128)(2,1)} %get-tuple-element.84), channel_id=1, source_target_pairs={{0,24},{4,28},{8,16},{12,20},{16,8},{20,12},{24,0},{28,4},{1,25},{... | collective-permute-start | bytes 811016 | tf_op jit(solution)/shard_map/ppermute | solution.py:335
  173.8 8.9 %experts.5 = (bf16[88,1536]{1,0:T(8,128)(2,1)}, bf16[88,1536]{1,0:T(8,128)(2,1)}, bf16[88,1536]{1,0:T(8,128)(2,1)}, bf16[88,1536]{1,0:T(8,128)(2,1)}, bf16[88,15...) custom-call(s32[1]{0:T(128)} %bitcast.1.expert_ref, ...), custom_call_target="tpu_custom_call" | custom-call | flops 8800000000 | tf_op jit(solution)/shard_map/experts/pallas_call | solution.py:461
  183.9 6.2 %collective-permute-done.10.refs_2_ = bf16[88,1536]{1,0:T(8,128)(2,1)S(1)} collective-permute-done((bf16[88,1536]{1,0:T(8,128)(2,1)}, bf16[88,1536]{1,0:T(8,128)(2,1)S(1)}, u32[]{:S(2)}, u32[]{:S(2)}) %collective-permute-start.10) | collective-permute-done | bytes 270368 | tf_op jit(solution)/shard_map/ppermute | solution.py:335
  190.1 3.4 %collective-permute-done.11.refs_3_ = bf16[88,1536]{1,0:T(8,128)(2,1)S(1)} collective-permute-done((bf16[88,1536]{1,0:T(8,128)(2,1)}, bf16[88,1536]{1,0:T(8,128)(2,1)S(1)}, u32[]{:S(2)}, u32[]{:S(2)}) %collective-permute-start.11) | collective-permute-done | bytes 270368 | tf_op jit(solution)/shard_map/ppermute | solution.py:335
  195.4 2.2 collective-permute-start.16
  197.5 2.3 %collective-permute-start.17 = (bf16[88,1536]{1,0:T(8,128)(2,1)S(1)}, bf16[88,1536]{1,0:T(8,128)(2,1)S(1)}, u32[]{:S(2)}, u32[]{:S(2)}) collective-permute-start(bf16[88,1536]{1,0:T(8,128)(2,1)S(1)} %copy-done.17), channel_id=1, source_target_pairs={{0,24},{4,28},{8,16},{12,20},{16,8},{20,12},{24,0},{28,4},{1,25},{... | collective-permute-start | bytes 811016 | tf_op jit(solution)/shard_map/ppermute | solution.py:335
  201.9 5.9 %collective-permute-done.17.refs_0_ = bf16[88,1536]{1,0:T(8,128)(2,1)S(1)} collective-permute-done((bf16[88,1536]{1,0:T(8,128)(2,1)S(1)}, bf16[88,1536]{1,0:T(8,128)(2,1)S(1)}, u32[]{:S(2)}, u32[]{:S(2)}) %collective-permute-start.17) | collective-permute-done | bytes 270368 | tf_op jit(solution)/shard_map/ppermute | solution.py:335
  209.2 3.4 %collective-permute-done.18.refs_1_ = bf16[88,1536]{1,0:T(8,128)(2,1)S(1)} collective-permute-done((bf16[88,1536]{1,0:T(8,128)(2,1)S(1)}, bf16[88,1536]{1,0:T(8,128)(2,1)S(1)}, u32[]{:S(2)}, u32[]{:S(2)}) %collective-permute-start.18) | collective-permute-done | bytes 270368 | tf_op jit(solution)/shard_map/ppermute | solution.py:335
  212.6 2.2 collective-permute-start.22
  214.8 4.6 %collective-permute-done.19.refs_2_ = bf16[88,1536]{1,0:T(8,128)(2,1)S(1)} collective-permute-done((bf16[88,1536]{1,0:T(8,128)(2,1)S(1)}, bf16[88,1536]{1,0:T(8,128)(2,1)S(1)}, u32[]{:S(2)}, u32[]{:S(2)}) %collective-permute-start.19) | collective-permute-done | bytes 270368 | tf_op jit(solution)/shard_map/ppermute | solution.py:335
  219.4 3.6 %collective-permute-done.20.refs_3_ = bf16[88,1536]{1,0:T(8,128)(2,1)S(1)} collective-permute-done((bf16[88,1536]{1,0:T(8,128)(2,1)S(1)}, bf16[88,1536]{1,0:T(8,128)(2,1)S(1)}, u32[]{:S(2)}, u32[]{:S(2)}) %collective-permute-start.20) | collective-permute-done | bytes 270368 | tf_op jit(solution)/shard_map/ppermute | solution.py:335
  224.0 4.6 %collective-permute-done.16.part_ref = bf16[224,1536]{1,0:T(8,128)(2,1)S(1)} collective-permute-done((bf16[224,1536]{1,0:T(8,128)(2,1)S(1)}, bf16[224,1536]{1,0:T(8,128)(2,1)S(1)}, u32[]{:S(2)}, u32[]{:S(2)}) %collective-permute-start.16) | collective-permute-done | bytes 688160 | tf_op jit(solution)/shard_map/ppermute | solution.py:503
  228.5 1.7 mine.1
  (82 shorter events, 19.3 us)
Async XLA Ops:
  0.0 32.6 %copy-start.3 = (s32[1,4]{1,0:T(1,128)S(1)}, s32[1,4]{1,0:T(1,128)}, u32[]{:S(2)}) copy-start(s32[1,4]{1,0:T(1,128)} %len_ref.5) | copy-start | bytes 52
  2.6 18.0 %collective-permute-start = (bf16[3,224,256]{2,1,0:T(8,128)(2,1)}, bf16[3,224,256]{2,1,0:T(8,128)(2,1)S(1)}, u32[]{:S(2)}, u32[]{:S(2)}) collective-permute-start(bf16[3,224,256]{2,1,0:T(8,128)(2,1)} %get-tuple-element.58), channel_id=1, source_target_pairs={{0,1},{1,0},{2,3},{3,2},{4,5},{5,4},{6,7},{7,6},{8,9},{9,8},{10,11... | collective-permute-start | bytes 1032200 | tf_op jit(solution)/shard_map/ppermute | solution.py:335
  5.7 26.8 %collective-permute-start.1 = (bf16[3,224,256]{2,1,0:T(8,128)(2,1)}, bf16[3,224,256]{2,1,0:T(8,128)(2,1)S(1)}, u32[]{:S(2)}, u32[]{:S(2)}) collective-permute-start(bf16[3,224,256]{2,1,0:T(8,128)(2,1)} %get-tuple-element.59), channel_id=1, source_target_pairs={{0,2},{1,3},{2,0},{3,1},{4,6},{5,7},{6,4},{7,5},{8,10},{9,11},{10,... | collective-permute-start | bytes 1032200 | tf_op jit(solution)/shard_map/ppermute | solution.py:335
  8.3 24.3 %collective-permute-start.2 = (bf16[3,224,256]{2,1,0:T(8,128)(2,1)}, bf16[3,224,256]{2,1,0:T(8,128)(2,1)S(1)}, u32[]{:S(2)}, u32[]{:S(2)}) collective-permute-start(bf16[3,224,256]{2,1,0:T(8,128)(2,1)} %get-tuple-element.60), channel_id=1, source_target_pairs={{0,3},{1,2},{2,1},{3,0},{4,7},{5,6},{6,5},{7,4},{8,11},{9,10},{10,... | collective-permute-start | bytes 1032200 | tf_op jit(solution)/shard_map/ppermute | solution.py:335
  39.8 31.8 %collective-permute-start.3 = (bf16[2,256,256]{2,1,0:T(8,128)(2,1)S(1)}, bf16[2,256,256]{2,1,0:T(8,128)(2,1)S(1)}, u32[]{:S(2)}, u32[]{:S(2)}) collective-permute-start(bf16[2,256,256]{2,1,0:T(8,128)(2,1)S(1)} %get-tuple-element.62), channel_id=1, source_target_pairs={{0,1},{1,0},{2,3},{3,2},{4,5},{5,4},{6,7},{7,6},{8,9},{9,8},{10,11... | collective-permute-start | bytes 786440 | tf_op jit(solution)/shard_map/ppermute | solution.py:335
  46.3 25.3 %collective-permute-start.4 = (bf16[2,256,256]{2,1,0:T(8,128)(2,1)S(1)}, bf16[2,256,256]{2,1,0:T(8,128)(2,1)S(1)}, u32[]{:S(2)}, u32[]{:S(2)}) collective-permute-start(bf16[2,256,256]{2,1,0:T(8,128)(2,1)S(1)} %get-tuple-element.63), channel_id=1, source_target_pairs={{0,2},{1,3},{2,0},{3,1},{4,6},{5,7},{6,4},{7,5},{8,10},{9,11},{10,... | collective-permute-start | bytes 786440 | tf_op jit(solution)/shard_map/ppermute | solution.py:335
  47.3 24.3 %collective-permute-start.5 = (bf16[2,256,256]{2,1,0:T(8,128)(2,1)S(1)}, bf16[2,256,256]{2,1,0:T(8,128)(2,1)S(1)}, u32[]{:S(2)}, u32[]{:S(2)}) collective-permute-start(bf16[2,256,256]{2,1,0:T(8,128)(2,1)S(1)} %get-tuple-element.64), channel_id=1, source_target_pairs={{0,3},{1,2},{2,1},{3,0},{4,7},{5,6},{6,5},{7,4},{8,11},{9,10},{10,... | collective-permute-start | bytes 786440 | tf_op jit(solution)/shard_map/ppermute | solution.py:335
  48.8 22.0 %collective-permute-start.6 = (s32[224,2]{0,1:T(2,128)S(1)}, s32[224,2]{0,1:T(2,128)S(1)}, u32[]{:S(2)}, u32[]{:S(2)}) collective-permute-start(s32[224,2]{0,1:T(2,128)S(1)} %bitcast.30), channel_id=1, source_target_pairs={{0,2},{1,3},{2,0},{3,1},{4,6},{5,7},{6,4},{7,5},{8,10},{9,11},{10,... | collective-permute-start | bytes 5384 | tf_op jit(solution)/shard_map/ppermute | solution.py:388
  83.3 31.9 %all-to-all-start = ((bf16[8,88,1536]{2,1,0:T(8,128)(2,1)}), bf16[8,88,1536]{2,1,0:T(8,128)(2,1)}, u32[]{:S(2)}, u32[]{:S(2)}) async-start(bf16[8,88,1536]{2,1,0:T(8,128)(2,1)} %bitcast.20), calls=%async_computation | async-start | bytes 4325376 | tf_op jit(solution)/shard_map/all_to_all | solution.py:428
  89.9 71.0 %collective-permute-start.7 = (bf16[1024,1536]{1,0:T(8,128)(2,1)S(1)}, bf16[1024,1536]{1,0:T(8,128)(2,1)}, u32[]{:S(2)}, u32[]{:S(2)}) collective-permute-start(bf16[1024,1536]{1,0:T(8,128)(2,1)S(1)} %pad_maximum_fusion), channel_id=1, source_target_pairs={{0,1},{1,0},{2,3},{3,2},{4,5},{5,4},{6,7},{7,6},{8,9},{9,8},{10,11... | collective-permute-start | bytes 9437192 | tf_op jit(solution)/shard_map/ppermute | solution.py:411
  115.2 52.4 %all-to-all-start.1 = ((bf16[8,88,1536]{2,1,0:T(8,128)(2,1)}), bf16[8,88,1536]{2,1,0:T(8,128)(2,1)}, u32[]{:S(2)}, u32[]{:S(2)}) async-start(bf16[8,88,1536]{2,1,0:T(8,128)(2,1)} %bitcast.19), calls=%async_computation.1 | async-start | bytes 4325376 | tf_op jit(solution)/shard_map/all_to_all | solution.py:428
  167.7 26.8 %copy-start.4 = (bf16[88,1536]{1,0:T(8,128)(2,1)S(1)}, bf16[88,1536]{1,0:T(8,128)(2,1)}, u32[]{:S(2)}) copy-start(bf16[88,1536]{1,0:T(8,128)(2,1)} %get-tuple-element.101.refs_7_) | copy-start | bytes 811012
  167.7 26.8 %copy-start.5 = (f32[224,128]{1,0:T(8,128)S(1)}, f32[224,128]{1,0:T(8,128)}, u32[]{:S(2)}) copy-start(f32[224,128]{1,0:T(8,128)} %get-tuple-element.72.info_ref) | copy-start | bytes 344068
  167.7 15.1 %collective-permute-start.8 = (bf16[88,1536]{1,0:T(8,128)(2,1)}, bf16[88,1536]{1,0:T(8,128)(2,1)S(1)}, u32[]{:S(2)}, u32[]{:S(2)}) collective-permute-start(bf16[88,1536]{1,0:T(8,128)(2,1)} %get-tuple-element.84), channel_id=1, source_target_pairs={{0,24},{4,28},{8,16},{12,20},{16,8},{20,12},{24,0},{28,4},{1,25},{... | collective-permute-start | bytes 811016 | tf_op jit(solution)/shard_map/ppermute | solution.py:335
  170.3 13.1 %collective-permute-start.9 = (bf16[88,1536]{1,0:T(8,128)(2,1)}, bf16[88,1536]{1,0:T(8,128)(2,1)S(1)}, u32[]{:S(2)}, u32[]{:S(2)}) collective-permute-start(bf16[88,1536]{1,0:T(8,128)(2,1)} %get-tuple-element.85), channel_id=1, source_target_pairs={{0,28},{4,24},{8,20},{12,16},{16,12},{20,8},{24,4},{28,0},{1,29},{... | collective-permute-start | bytes 811016 | tf_op jit(solution)/shard_map/ppermute | solution.py:335
  170.3 19.8 %collective-permute-start.10 = (bf16[88,1536]{1,0:T(8,128)(2,1)}, bf16[88,1536]{1,0:T(8,128)(2,1)S(1)}, u32[]{:S(2)}, u32[]{:S(2)}) collective-permute-start(bf16[88,1536]{1,0:T(8,128)(2,1)} %get-tuple-element.86), channel_id=1, source_target_pairs={{0,8},{4,12},{8,0},{12,4},{16,24},{20,28},{24,16},{28,20},{1,9},{5... | collective-permute-start | bytes 811016 | tf_op jit(solution)/shard_map/ppermute | solution.py:335
  171.3 22.2 %collective-permute-start.11 = (bf16[88,1536]{1,0:T(8,128)(2,1)}, bf16[88,1536]{1,0:T(8,128)(2,1)S(1)}, u32[]{:S(2)}, u32[]{:S(2)}) collective-permute-start(bf16[88,1536]{1,0:T(8,128)(2,1)} %get-tuple-element.87), channel_id=1, source_target_pairs={{0,12},{4,8},{8,4},{12,0},{16,28},{20,24},{24,20},{28,16},{1,13},{... | collective-permute-start | bytes 811016 | tf_op jit(solution)/shard_map/ppermute | solution.py:335
  172.2 21.3 %collective-permute-start.12 = (bf16[88,1536]{1,0:T(8,128)(2,1)}, bf16[88,1536]{1,0:T(8,128)(2,1)S(1)}, u32[]{:S(2)}, u32[]{:S(2)}) collective-permute-start(bf16[88,1536]{1,0:T(8,128)(2,1)} %get-tuple-element.88), channel_id=1, source_target_pairs={{0,16},{4,20},{8,24},{12,28},{16,0},{20,4},{24,8},{28,12},{1,17},{... | collective-permute-start | bytes 811016 | tf_op jit(solution)/shard_map/ppermute | solution.py:335
  182.7 29.8 %copy-start.12 = (bf16[88,1536]{1,0:T(8,128)(2,1)S(1)}, bf16[88,1536]{1,0:T(8,128)(2,1)}, u32[]{:S(2)}) copy-start(bf16[88,1536]{1,0:T(8,128)(2,1)} %get-tuple-element.107) | copy-start | bytes 811012
  182.7 45.8 %copy-start = (f32[12,224,128]{2,1,0:T(8,128)S(1)}, f32[12,224,128]{2,1,0:T(8,128)}, u32[]{:S(2)}) copy-start(f32[12,224,128]{2,1,0:T(8,128)} %get-tuple-element.71.second_ref) | copy-start | bytes 4128772
  182.8 45.8 %copy-start.1 = (bf16[88,1536]{1,0:T(8,128)(2,1)S(1)}, bf16[88,1536]{1,0:T(8,128)(2,1)}, u32[]{:S(2)}) copy-start(bf16[88,1536]{1,0:T(8,128)(2,1)} %get-tuple-element.108.refs_7_) | copy-start | bytes 811012
  182.8 45.8 %copy-start.2 = (f32[224,128]{1,0:T(8,128)S(1)}, f32[224,128]{1,0:T(8,128)}, u32[]{:S(2)}) copy-start(f32[224,128]{1,0:T(8,128)} %get-tuple-element.70.info_ref) | copy-start | bytes 344068
  182.8 11.7 %collective-permute-start.13 = (bf16[88,1536]{1,0:T(8,128)(2,1)S(1)}, bf16[88,1536]{1,0:T(8,128)(2,1)S(1)}, u32[]{:S(2)}, u32[]{:S(2)}) collective-permute-start(bf16[88,1536]{1,0:T(8,128)(2,1)S(1)} %copy-done.19), channel_id=1, source_target_pairs={{0,20},{4,16},{8,28},{12,24},{16,4},{20,0},{24,12},{28,8},{1,21},{... | collective-permute-start | bytes 811016 | tf_op jit(solution)/shard_map/ppermute | solution.py:335
  183.4 11.1 %collective-permute-start.14 = (bf16[88,1536]{1,0:T(8,128)(2,1)S(1)}, bf16[88,1536]{1,0:T(8,128)(2,1)S(1)}, u32[]{:S(2)}, u32[]{:S(2)}) collective-permute-start(bf16[88,1536]{1,0:T(8,128)(2,1)S(1)} %copy-done.18), channel_id=1, source_target_pairs={{0,4},{4,0},{8,12},{12,8},{16,20},{20,16},{24,28},{28,24},{1,5},{5... | collective-permute-start | bytes 811016 | tf_op jit(solution)/shard_map/ppermute | solution.py:335
  190.1 4.4 %collective-permute-start.15 = (bf16[88,1536]{1,0:T(8,128)(2,1)}, bf16[88,1536]{1,0:T(8,128)(2,1)S(1)}, u32[]{:S(2)}, u32[]{:S(2)}) collective-permute-start(bf16[88,1536]{1,0:T(8,128)(2,1)} %get-tuple-element.93), channel_id=1, source_target_pairs={{0,4},{4,0},{8,12},{12,8},{16,20},{20,16},{24,28},{28,24},{1,5},{5... | collective-permute-start | bytes 811016 | tf_op jit(solution)/shard_map/ppermute | solution.py:335
  195.4 33.2 %collective-permute-start.16 = (bf16[224,1536]{1,0:T(8,128)(2,1)S(1)}, bf16[224,1536]{1,0:T(8,128)(2,1)S(1)}, u32[]{:S(2)}, u32[]{:S(2)}) collective-permute-start(bf16[224,1536]{1,0:T(8,128)(2,1)S(1)} %theirs.1), channel_id=1, source_target_pairs={{0,2},{1,3},{2,0},{3,1},{4,6},{5,7},{6,4},{7,5},{8,10},{9,11},{10,... | collective-permute-start | bytes 2064392 | tf_op jit(solution)/shard_map/ppermute | solution.py:503
  197.5 10.3 %collective-permute-start.17 = (bf16[88,1536]{1,0:T(8,128)(2,1)S(1)}, bf16[88,1536]{1,0:T(8,128)(2,1)S(1)}, u32[]{:S(2)}, u32[]{:S(2)}) collective-permute-start(bf16[88,1536]{1,0:T(8,128)(2,1)S(1)} %copy-done.17), channel_id=1, source_target_pairs={{0,24},{4,28},{8,16},{12,20},{16,8},{20,12},{24,0},{28,4},{1,25},{... | collective-permute-start | bytes 811016 | tf_op jit(solution)/shard_map/ppermute | solution.py:335
  199.8 12.7 %collective-permute-start.18 = (bf16[88,1536]{1,0:T(8,128)(2,1)S(1)}, bf16[88,1536]{1,0:T(8,128)(2,1)S(1)}, u32[]{:S(2)}, u32[]{:S(2)}) collective-permute-start(bf16[88,1536]{1,0:T(8,128)(2,1)S(1)} %copy-done.16), channel_id=1, source_target_pairs={{0,28},{4,24},{8,20},{12,16},{16,12},{20,8},{24,4},{28,0},{1,29},{... | collective-permute-start | bytes 811016 | tf_op jit(solution)/shard_map/ppermute | solution.py:335
  199.9 19.5 %collective-permute-start.19 = (bf16[88,1536]{1,0:T(8,128)(2,1)S(1)}, bf16[88,1536]{1,0:T(8,128)(2,1)S(1)}, u32[]{:S(2)}, u32[]{:S(2)}) collective-permute-start(bf16[88,1536]{1,0:T(8,128)(2,1)S(1)} %copy-done.15), channel_id=1, source_target_pairs={{0,8},{4,12},{8,0},{12,4},{16,24},{20,28},{24,16},{28,20},{1,9},{5... | collective-permute-start | bytes 811016 | tf_op jit(solution)/shard_map/ppermute | solution.py:335
  201.0 22.0 %collective-permute-start.20 = (bf16[88,1536]{1,0:T(8,128)(2,1)S(1)}, bf16[88,1536]{1,0:T(8,128)(2,1)S(1)}, u32[]{:S(2)}, u32[]{:S(2)}) collective-permute-start(bf16[88,1536]{1,0:T(8,128)(2,1)S(1)} %copy-done.14), channel_id=1, source_target_pairs={{0,12},{4,8},{8,4},{12,0},{16,28},{20,24},{24,20},{28,16},{1,13},{... | collective-permute-start | bytes 811016 | tf_op jit(solution)/shard_map/ppermute | solution.py:335
  207.8 15.2 %collective-permute-start.21 = (bf16[88,1536]{1,0:T(8,128)(2,1)S(1)}, bf16[88,1536]{1,0:T(8,128)(2,1)S(1)}, u32[]{:S(2)}, u32[]{:S(2)}) collective-permute-start(bf16[88,1536]{1,0:T(8,128)(2,1)S(1)} %copy-done.13), channel_id=1, source_target_pairs={{0,16},{4,20},{8,24},{12,28},{16,0},{20,4},{24,8},{28,12},{1,17},{... | collective-permute-start | bytes 811016 | tf_op jit(solution)/shard_map/ppermute | solution.py:335
  212.6 11.4 %collective-permute-start.22 = (bf16[88,1536]{1,0:T(8,128)(2,1)S(1)}, bf16[88,1536]{1,0:T(8,128)(2,1)S(1)}, u32[]{:S(2)}, u32[]{:S(2)}) collective-permute-start(bf16[88,1536]{1,0:T(8,128)(2,1)S(1)} %copy-done.12), channel_id=1, source_target_pairs={{0,20},{4,16},{8,28},{12,24},{16,4},{20,0},{24,12},{28,8},{1,21},{... | collective-permute-start | bytes 811016 | tf_op jit(solution)/shard_map/ppermute | solution.py:335
  (17 other events, 187.1 us)

commit v12 on v11

--- a/solution.py
+++ b/solution.py
@@ -444,7 +444,7 @@
                 pltpu.VMEM((window, LANES), F32),
             ],
             compiler_params=params(56),
-            cost_estimate=cost(10),
+            cost_estimate=cost(7),
             name="frames",
         )(me, expert, lengths, out_proj, taps, router, block_routes, block_routes.T, *windows)
         return made
@@ -469,7 +469,7 @@
                 pltpu.SemaphoreType.DMA((len(operands),)),
             ],
             compiler_params=params(56),
-            cost_estimate=cost(8 if len(parts) > 1 else 5),
+            cost_estimate=cost(8 if last else 0),
             name="experts",
         )(expert, *operands)
 

time: 230 us -> 207 us (0.900)
  waiting for transfers between devices: 120 us -> 95.1 us
  starting transfers between devices: 44.4 us -> 47.1 us
    ppermute x1, waiting for transfers between devices: 34.3 us -> 12.9 us  [body(): moved = lax.ppermute(shard, 'tm', [(i, i ^ 1) for i in range(count)])]
    ppermute x1, waiting for transfers between devices: 18.3 us -> 0.01 us  [body(): partner_routes = lax.ppermute(routes[0], 'tm', partner)]
    ppermute x20, waiting for transfers between devices: 53.8 us -> 64.4 us  [trade(): lax.ppermute(arrays[r], axis, [(i, i ^ r) for i in range(count)])]
    all_to_all x2, waiting for transfers between devices: 9.09 us -> 13.8 us  [route(): moved = lax.all_to_all(whole, 'dp', split_axis=0, concat_axis=0, tiled=True)]
  transfers between devices with their start and end apart: 25 -> 25, of which waited for: 15 -> 17; matrix products, arithmetic and copies ran while one was open for 2% -> 3% of each run, Pallas kernels for 16% -> 25%
where the time goes in v12:
time: 207 us
  waiting for transfers between devices  95.1 us (46%)
  Pallas kernels  57.6 us (28%)
  starting transfers between devices  47.1 us (23%)
  local copies, waits for them, and re-layouts  5.1 us (2%)
    ppermute x20, waiting for transfers between devices, trade(): lax.ppermute(arrays[r], axis, [(i, i ^ r) for i in range(count)])  64.4 us
    ppermute x20, starting transfers between devices, trade(): lax.ppermute(arrays[r], axis, [(i, i ^ r) for i in range(count)])  29.5 us
    pallas_call x2, Pallas kernels, send_frames(): pl.pallas_call(functools.partial(frame_kernel, count, rows, experts, capa...  24.3 us
    pallas_call x3, Pallas kernels, run_expert(): pl.pallas_call(kernel, out_shape=made, in_specs=[SMEM] + [pl.BlockSpec(me...  22.5 us
    all_to_all x2, waiting for transfers between devices, route(): moved = lax.all_to_all(whole, 'dp', split_axis=0, concat_axis=0, tiled=True)  13.8 us
    ppermute x1, waiting for transfers between devices, body(): moved = lax.ppermute(shard, 'tm', [(i, i ^ 1) for i in range(count)])  12.9 us
    all_to_all x2, starting transfers between devices, route(): moved = lax.all_to_all(whole, 'dp', split_axis=0, concat_axis=0, tiled=True)  8.08 us
    pallas_call x1, Pallas kernels, body(): pl.pallas_call(functools.partial(attend_kernel, count, rows, heads, place...  5.53 us
  transfers between devices with their start and end apart: 25, of which 17 were waited for; matrix products, arithmetic and copies ran while one was open for 3% of the time, Pallas kernels for 25%

profile of v12, /device:TPU:0, one launch (start us, length us, event | category | flops | bytes accessed | tf_op | source)
XLA Modules:
  0.0 207.1 jit_solution(1456895698787582029)
XLA Ops:
  0.0 2.6 %pack.1 = (bf16[3,224,256]{2,1,0:T(8,128)(2,1)}, bf16[3,224,256]{2,1,0:T(8,128)(2,1)}, bf16[3,224,256]{2,1,0:T(8,128)(2,1)}, bf16[3,224,256]{2,1,0:T(8,128)(2,1)}) custom-call(s32[1]{0:T(128)} %bitcast.me_ref, bf16[224,1024]{1,0:T(8,128)(2,1)} %bitcast.35, bf16[224,1024]{1,0:T(8,128)(2,1)} %bitcast.36, bf16[224,1024]{1,0:T(8,128)(2,1)} %bitcast.37), custom_call_target="tpu_custom_call" | custom-call | flops 1100000000 | tf_op jit(solution)/shard_map/pack/pallas_call | solution.py:376
  2.6 3.1 %collective-permute-start = (bf16[3,224,256]{2,1,0:T(8,128)(2,1)}, bf16[3,224,256]{2,1,0:T(8,128)(2,1)S(1)}, u32[]{:S(2)}, u32[]{:S(2)}) collective-permute-start(bf16[3,224,256]{2,1,0:T(8,128)(2,1)} %get-tuple-element.58), channel_id=1, source_target_pairs={{0,1},{1,0},{2,3},{3,2},{4,5},{5,4},{6,7},{7,6},{8,9},{9,8},{10,11... | collective-permute-start | bytes 1032200 | tf_op jit(solution)/shard_map/ppermute | solution.py:335
  5.7 2.6 %collective-permute-start.1 = (bf16[3,224,256]{2,1,0:T(8,128)(2,1)}, bf16[3,224,256]{2,1,0:T(8,128)(2,1)S(1)}, u32[]{:S(2)}, u32[]{:S(2)}) collective-permute-start(bf16[3,224,256]{2,1,0:T(8,128)(2,1)} %get-tuple-element.59), channel_id=1, source_target_pairs={{0,2},{1,3},{2,0},{3,1},{4,6},{5,7},{6,4},{7,5},{8,10},{9,11},{10,... | collective-permute-start | bytes 1032200 | tf_op jit(solution)/shard_map/ppermute | solution.py:335
  8.3 1.9 collective-permute-start.6
  10.3 10.3 %collective-permute-done.refs_1_ = bf16[3,224,256]{2,1,0:T(8,128)(2,1)S(1)} collective-permute-done((bf16[3,224,256]{2,1,0:T(8,128)(2,1)}, bf16[3,224,256]{2,1,0:T(8,128)(2,1)S(1)}, u32[]{:S(2)}, u32[]{:S(2)}) %collective-permute-start) | collective-permute-done | bytes 344096 | tf_op jit(solution)/shard_map/ppermute | solution.py:335
  20.6 12.0 %collective-permute-done.1.refs_2_ = bf16[3,224,256]{2,1,0:T(8,128)(2,1)S(1)} collective-permute-done((bf16[3,224,256]{2,1,0:T(8,128)(2,1)}, bf16[3,224,256]{2,1,0:T(8,128)(2,1)S(1)}, u32[]{:S(2)}, u32[]{:S(2)}) %collective-permute-start.1) | collective-permute-done | bytes 344096 | tf_op jit(solution)/shard_map/ppermute | solution.py:335
  33.6 5.5 %attend.1 = (bf16[2,256,256]{2,1,0:T(8,128)(2,1)S(1)}, bf16[2,256,256]{2,1,0:T(8,128)(2,1)S(1)}, bf16[2,256,256]{2,1,0:T(8,128)(2,1)S(1)}, bf16[2,256,256]{2,1,0:T(8,128)(2,1)S(1)}) custom-call(s32[1]{0:T(128)} %bitcast.me_ref, f32[4]{0:T(128)S(1)} %dynamic_slice.3.scale_ref, s32[1,4]{1,0:T(1,128)S(1)} %copy-done.3, bf16[3,224,256]{2,1,0:T(8,128)(2,1)S(1)} %copy-done.6, ...), custom_call_target="tpu_custom_call" | custom-call | flops 6600000000 | tf_op jit(solution)/shard_map/attend/pallas_call | solution.py:392
  39.9 6.5 %collective-permute-start.3 = (bf16[2,256,256]{2,1,0:T(8,128)(2,1)S(1)}, bf16[2,256,256]{2,1,0:T(8,128)(2,1)S(1)}, u32[]{:S(2)}, u32[]{:S(2)}) collective-permute-start(bf16[2,256,256]{2,1,0:T(8,128)(2,1)S(1)} %get-tuple-element.62), channel_id=1, source_target_pairs={{0,1},{1,0},{2,3},{3,2},{4,5},{5,4},{6,7},{7,6},{8,9},{9,8},{10,11... | collective-permute-start | bytes 786440 | tf_op jit(solution)/shard_map/ppermute | solution.py:335
  48.9 1.9 pad_maximum_fusion
  53.3 2.3 %collective-permute-done.3.refs_1_ = bf16[2,256,256]{2,1,0:T(8,128)(2,1)S(1)} collective-permute-done((bf16[2,256,256]{2,1,0:T(8,128)(2,1)S(1)}, bf16[2,256,256]{2,1,0:T(8,128)(2,1)S(1)}, u32[]{:S(2)}, u32[]{:S(2)}) %collective-permute-start.3) | collective-permute-done | bytes 262176 | tf_op jit(solution)/shard_map/ppermute | solution.py:335
  55.6 12.2 %collective-permute-done.4.refs_2_ = bf16[2,256,256]{2,1,0:T(8,128)(2,1)S(1)} collective-permute-done((bf16[2,256,256]{2,1,0:T(8,128)(2,1)S(1)}, bf16[2,256,256]{2,1,0:T(8,128)(2,1)S(1)}, u32[]{:S(2)}, u32[]{:S(2)}) %collective-permute-start.4) | collective-permute-done | bytes 262176 | tf_op jit(solution)/shard_map/ppermute | solution.py:335
  67.8 3.6 %collective-permute-start.7 = (bf16[1024,1536]{1,0:T(8,128)(2,1)}, bf16[1024,1536]{1,0:T(8,128)(2,1)}, u32[]{:S(2)}, u32[]{:S(2)}) collective-permute-start(bf16[1024,1536]{1,0:T(8,128)(2,1)} %pad_maximum_fusion), channel_id=1, source_target_pairs={{0,1},{1,0},{2,3},{3,2},{4,5},{5,4},{6,7},{7,6},{8,9},{9,8},{10,11... | collective-permute-start | bytes 9437192 | tf_op jit(solution)/shard_map/ppermute | solution.py:411
  71.4 10.8 %frames.2 = (bf16[704,1536]{1,0:T(8,128)(2,1)}, f32[224,128]{1,0:T(8,128)}, f32[12,224,128]{2,1,0:T(8,128)}) custom-call(s32[1]{0:T(128)} %bitcast.me_ref, s32[1]{0:T(128)} %bitcast.1.expert_ref, s32[1,4]{1,0:T(1,128)} %len_ref.5, bf16[1024,1536]{1,0:T(8,128)(2,1)} %proj_ref.3, f32[12,31,128]{2,1,0:T(8,128)} %bitcast.29, bf16[1536,8]{1,0:T(8,128)(2,1)} %copy.19.router_ref, ...), custom_call_target="tpu_custom_call" | custom-call | flops 7699999744 | tf_op jit(solution)/shard_map/frames/pallas_call | solution.py:432
  82.2 3.7 %all-to-all-start = ((bf16[8,88,1536]{2,1,0:T(8,128)(2,1)}), bf16[8,88,1536]{2,1,0:T(8,128)(2,1)S(1)}, u32[]{:S(2)}, u32[]{:S(2)}) async-start(bf16[8,88,1536]{2,1,0:T(8,128)(2,1)} %bitcast.28), calls=%async_computation | async-start | bytes 4325376 | tf_op jit(solution)/shard_map/all_to_all | solution.py:428
  86.7 13.5 %frames.3 = (bf16[704,1536]{1,0:T(8,128)(2,1)}, f32[224,128]{1,0:T(8,128)}, f32[12,224,128]{2,1,0:T(8,128)}) custom-call(s32[1]{0:T(128)} %bitcast.me_ref, s32[1]{0:T(128)} %bitcast.1.expert_ref, s32[1,4]{1,0:T(1,128)} %len_ref.5, bf16[1024,1536]{1,0:T(8,128)(2,1)} %proj_ref.3, f32[12,31,128]{2,1,0:T(8,128)} %bitcast.30, bf16[1536,8]{1,0:T(8,128)(2,1)} %copy.19.router_ref, ...), custom_call_target="tpu_custom_call" | custom-call | flops 7699999744 | tf_op jit(solution)/shard_map/frames/pallas_call | solution.py:432
  100.2 13.1 %all-to-all-done = bf16[8,88,1536]{2,1,0:T(8,128)(2,1)S(1)} async-done(((bf16[8,88,1536]{2,1,0:T(8,128)(2,1)}), bf16[8,88,1536]{2,1,0:T(8,128)(2,1)S(1)}, u32[]{:S(2)}, u32[]{:S(2)}) %all-to-all-start) | async-done | bytes 2162720 | tf_op jit(solution)/shard_map/all_to_all | solution.py:428
  113.3 4.3 %all-to-all-start.1 = ((bf16[8,88,1536]{2,1,0:T(8,128)(2,1)}), bf16[8,88,1536]{2,1,0:T(8,128)(2,1)}, u32[]{:S(2)}, u32[]{:S(2)}) async-start(bf16[8,88,1536]{2,1,0:T(8,128)(2,1)} %bitcast.27), calls=%async_computation.1 | async-start | bytes 4325376 | tf_op jit(solution)/shard_map/all_to_all | solution.py:428
  117.7 6.9 %experts.3.refs_2_ = f32[704,1536]{1,0:T(8,128)} custom-call(s32[1]{0:T(128)} %bitcast.1.expert_ref, bf16[704,1536]{1,0:T(8,128)(2,1)} %bitcast.19, bf16[512,1536]{1,0:T(8,128)(2,1)} %bitcast.24, bf16[512,1536]{1,0:T(8,128)(2,1)} %bitcast.21), custom_call_target="tpu_custom_call" | custom-call | tf_op jit(solution)/shard_map/experts/pallas_call | solution.py:461
  124.6 12.9 %collective-permute-done.7.refs_1_.refs_3_ = bf16[1024,1536]{1,0:T(8,128)(2,1)} collective-permute-done((bf16[1024,1536]{1,0:T(8,128)(2,1)}, bf16[1024,1536]{1,0:T(8,128)(2,1)}, u32[]{:S(2)}, u32[]{:S(2)}) %collective-permute-start.7) | collective-permute-done | bytes 3145760 | tf_op jit(solution)/shard_map/ppermute | solution.py:411
  137.4 6.8 %experts.4 = (bf16[88,1536]{1,0:T(8,128)(2,1)}, bf16[88,1536]{1,0:T(8,128)(2,1)}, bf16[88,1536]{1,0:T(8,128)(2,1)}, bf16[88,1536]{1,0:T(8,128)(2,1)}, bf16[88,15...) custom-call(s32[1]{0:T(128)} %bitcast.1.expert_ref, ...), custom_call_target="tpu_custom_call" | custom-call | flops 8800000000 | tf_op jit(solution)/shard_map/experts/pallas_call | solution.py:461
  150.3 8.8 %experts.5 = (bf16[88,1536]{1,0:T(8,128)(2,1)}, bf16[88,1536]{1,0:T(8,128)(2,1)}, bf16[88,1536]{1,0:T(8,128)(2,1)}, bf16[88,1536]{1,0:T(8,128)(2,1)}, bf16[88,15...) custom-call(s32[1]{0:T(128)} %bitcast.1.expert_ref, ...), custom_call_target="tpu_custom_call" | custom-call | flops 8800000000 | tf_op jit(solution)/shard_map/experts/pallas_call | solution.py:461
  160.6 6.0 %collective-permute-done.10.refs_2_ = bf16[88,1536]{1,0:T(8,128)(2,1)S(1)} collective-permute-done((bf16[88,1536]{1,0:T(8,128)(2,1)}, bf16[88,1536]{1,0:T(8,128)(2,1)S(1)}, u32[]{:S(2)}, u32[]{:S(2)}) %collective-permute-start.10) | collective-permute-done | bytes 270368 | tf_op jit(solution)/shard_map/ppermute | solution.py:335
  166.6 2.5 %collective-permute-done.11.refs_3_ = bf16[88,1536]{1,0:T(8,128)(2,1)S(1)} collective-permute-done((bf16[88,1536]{1,0:T(8,128)(2,1)}, bf16[88,1536]{1,0:T(8,128)(2,1)S(1)}, u32[]{:S(2)}, u32[]{:S(2)}) %collective-permute-start.11) | collective-permute-done | bytes 270368 | tf_op jit(solution)/shard_map/ppermute | solution.py:335
  170.8 4.1 %collective-permute-start.16 = (bf16[224,1536]{1,0:T(8,128)(2,1)S(1)}, bf16[224,1536]{1,0:T(8,128)(2,1)S(1)}, u32[]{:S(2)}, u32[]{:S(2)}) collective-permute-start(bf16[224,1536]{1,0:T(8,128)(2,1)S(1)} %theirs.1), channel_id=1, source_target_pairs={{0,2},{1,3},{2,0},{3,1},{4,6},{5,7},{6,4},{7,5},{8,10},{9,11},{10,... | collective-permute-start | bytes 2064392 | tf_op jit(solution)/shard_map/ppermute | solution.py:503
  174.9 2.3 %collective-permute-start.17 = (bf16[88,1536]{1,0:T(8,128)(2,1)S(1)}, bf16[88,1536]{1,0:T(8,128)(2,1)S(1)}, u32[]{:S(2)}, u32[]{:S(2)}) collective-permute-start(bf16[88,1536]{1,0:T(8,128)(2,1)S(1)} %copy-done.20), channel_id=1, source_target_pairs={{0,24},{4,28},{8,16},{12,20},{16,8},{20,12},{24,0},{28,4},{1,25},{... | collective-permute-start | bytes 811016 | tf_op jit(solution)/shard_map/ppermute | solution.py:335
  177.2 2.3 %collective-permute-start.19 = (bf16[88,1536]{1,0:T(8,128)(2,1)S(1)}, bf16[88,1536]{1,0:T(8,128)(2,1)S(1)}, u32[]{:S(2)}, u32[]{:S(2)}) collective-permute-start(bf16[88,1536]{1,0:T(8,128)(2,1)S(1)} %copy-done.18), channel_id=1, source_target_pairs={{0,8},{4,12},{8,0},{12,4},{16,24},{20,28},{24,16},{28,20},{1,9},{5... | collective-permute-start | bytes 811016 | tf_op jit(solution)/shard_map/ppermute | solution.py:335
  180.1 5.0 %collective-permute-done.17.refs_0_ = bf16[88,1536]{1,0:T(8,128)(2,1)S(1)} collective-permute-done((bf16[88,1536]{1,0:T(8,128)(2,1)S(1)}, bf16[88,1536]{1,0:T(8,128)(2,1)S(1)}, u32[]{:S(2)}, u32[]{:S(2)}) %collective-permute-start.17) | collective-permute-done | bytes 270368 | tf_op jit(solution)/shard_map/ppermute | solution.py:335
  186.5 3.4 %collective-permute-done.18.refs_1_ = bf16[88,1536]{1,0:T(8,128)(2,1)S(1)} collective-permute-done((bf16[88,1536]{1,0:T(8,128)(2,1)S(1)}, bf16[88,1536]{1,0:T(8,128)(2,1)S(1)}, u32[]{:S(2)}, u32[]{:S(2)}) %collective-permute-start.18) | collective-permute-done | bytes 270368 | tf_op jit(solution)/shard_map/ppermute | solution.py:335
  189.9 2.2 %collective-permute-start.22 = (bf16[88,1536]{1,0:T(8,128)(2,1)S(1)}, bf16[88,1536]{1,0:T(8,128)(2,1)S(1)}, u32[]{:S(2)}, u32[]{:S(2)}) collective-permute-start(bf16[88,1536]{1,0:T(8,128)(2,1)S(1)} %copy-done.15), channel_id=1, source_target_pairs={{0,20},{4,16},{8,28},{12,24},{16,4},{20,0},{24,12},{28,8},{1,21},{... | collective-permute-start | bytes 811016 | tf_op jit(solution)/shard_map/ppermute | solution.py:335
  192.0 4.6 %collective-permute-done.19.refs_2_ = bf16[88,1536]{1,0:T(8,128)(2,1)S(1)} collective-permute-done((bf16[88,1536]{1,0:T(8,128)(2,1)S(1)}, bf16[88,1536]{1,0:T(8,128)(2,1)S(1)}, u32[]{:S(2)}, u32[]{:S(2)}) %collective-permute-start.19) | collective-permute-done | bytes 270368 | tf_op jit(solution)/shard_map/ppermute | solution.py:335
  196.6 3.8 %collective-permute-done.20.refs_3_ = bf16[88,1536]{1,0:T(8,128)(2,1)S(1)} collective-permute-done((bf16[88,1536]{1,0:T(8,128)(2,1)S(1)}, bf16[88,1536]{1,0:T(8,128)(2,1)S(1)}, u32[]{:S(2)}, u32[]{:S(2)}) %collective-permute-start.20) | collective-permute-done | bytes 270368 | tf_op jit(solution)/shard_map/ppermute | solution.py:335
  201.3 4.1 %collective-permute-done.16.part_ref = bf16[224,1536]{1,0:T(8,128)(2,1)S(1)} collective-permute-done((bf16[224,1536]{1,0:T(8,128)(2,1)S(1)}, bf16[224,1536]{1,0:T(8,128)(2,1)S(1)}, u32[]{:S(2)}, u32[]{:S(2)}) %collective-permute-start.16) | collective-permute-done | bytes 688160 | tf_op jit(solution)/shard_map/ppermute | solution.py:503
  (88 shorter events, 21.2 us)
Async XLA Ops:
  0.0 32.6 %copy-start.3 = (s32[1,4]{1,0:T(1,128)S(1)}, s32[1,4]{1,0:T(1,128)}, u32[]{:S(2)}) copy-start(s32[1,4]{1,0:T(1,128)} %len_ref.5) | copy-start | bytes 52
  2.6 18.0 %collective-permute-start = (bf16[3,224,256]{2,1,0:T(8,128)(2,1)}, bf16[3,224,256]{2,1,0:T(8,128)(2,1)S(1)}, u32[]{:S(2)}, u32[]{:S(2)}) collective-permute-start(bf16[3,224,256]{2,1,0:T(8,128)(2,1)} %get-tuple-element.58), channel_id=1, source_target_pairs={{0,1},{1,0},{2,3},{3,2},{4,5},{5,4},{6,7},{7,6},{8,9},{9,8},{10,11... | collective-permute-start | bytes 1032200 | tf_op jit(solution)/shard_map/ppermute | solution.py:335
  5.7 26.9 %collective-permute-start.1 = (bf16[3,224,256]{2,1,0:T(8,128)(2,1)}, bf16[3,224,256]{2,1,0:T(8,128)(2,1)S(1)}, u32[]{:S(2)}, u32[]{:S(2)}) collective-permute-start(bf16[3,224,256]{2,1,0:T(8,128)(2,1)} %get-tuple-element.59), channel_id=1, source_target_pairs={{0,2},{1,3},{2,0},{3,1},{4,6},{5,7},{6,4},{7,5},{8,10},{9,11},{10,... | collective-permute-start | bytes 1032200 | tf_op jit(solution)/shard_map/ppermute | solution.py:335
  8.3 24.3 %collective-permute-start.2 = (bf16[3,224,256]{2,1,0:T(8,128)(2,1)}, bf16[3,224,256]{2,1,0:T(8,128)(2,1)S(1)}, u32[]{:S(2)}, u32[]{:S(2)}) collective-permute-start(bf16[3,224,256]{2,1,0:T(8,128)(2,1)} %get-tuple-element.60), channel_id=1, source_target_pairs={{0,3},{1,2},{2,1},{3,0},{4,7},{5,6},{6,5},{7,4},{8,11},{9,10},{10,... | collective-permute-start | bytes 1032200 | tf_op jit(solution)/shard_map/ppermute | solution.py:335
  8.3 44.2 %collective-permute-start.6 = (s32[224,2]{0,1:T(2,128)S(1)}, s32[224,2]{0,1:T(2,128)S(1)}, u32[]{:S(2)}, u32[]{:S(2)}) collective-permute-start(s32[224,2]{0,1:T(2,128)S(1)} %bitcast.32), channel_id=1, source_target_pairs={{0,2},{1,3},{2,0},{3,1},{4,6},{5,7},{6,4},{7,5},{8,10},{9,11},{10,... | collective-permute-start | bytes 5384 | tf_op jit(solution)/shard_map/ppermute | solution.py:388
  39.9 15.8 %collective-permute-start.3 = (bf16[2,256,256]{2,1,0:T(8,128)(2,1)S(1)}, bf16[2,256,256]{2,1,0:T(8,128)(2,1)S(1)}, u32[]{:S(2)}, u32[]{:S(2)}) collective-permute-start(bf16[2,256,256]{2,1,0:T(8,128)(2,1)S(1)} %get-tuple-element.62), channel_id=1, source_target_pairs={{0,1},{1,0},{2,3},{3,2},{4,5},{5,4},{6,7},{7,6},{8,9},{9,8},{10,11... | collective-permute-start | bytes 786440 | tf_op jit(solution)/shard_map/ppermute | solution.py:335
  46.4 21.4 %collective-permute-start.4 = (bf16[2,256,256]{2,1,0:T(8,128)(2,1)S(1)}, bf16[2,256,256]{2,1,0:T(8,128)(2,1)S(1)}, u32[]{:S(2)}, u32[]{:S(2)}) collective-permute-start(bf16[2,256,256]{2,1,0:T(8,128)(2,1)S(1)} %get-tuple-element.63), channel_id=1, source_target_pairs={{0,2},{1,3},{2,0},{3,1},{4,6},{5,7},{6,4},{7,5},{8,10},{9,11},{10,... | collective-permute-start | bytes 786440 | tf_op jit(solution)/shard_map/ppermute | solution.py:335
  47.4 20.4 %collective-permute-start.5 = (bf16[2,256,256]{2,1,0:T(8,128)(2,1)S(1)}, bf16[2,256,256]{2,1,0:T(8,128)(2,1)S(1)}, u32[]{:S(2)}, u32[]{:S(2)}) collective-permute-start(bf16[2,256,256]{2,1,0:T(8,128)(2,1)S(1)} %get-tuple-element.64), channel_id=1, source_target_pairs={{0,3},{1,2},{2,1},{3,0},{4,7},{5,6},{6,5},{7,4},{8,11},{9,10},{10,... | collective-permute-start | bytes 786440 | tf_op jit(solution)/shard_map/ppermute | solution.py:335
  67.8 69.7 %collective-permute-start.7 = (bf16[1024,1536]{1,0:T(8,128)(2,1)}, bf16[1024,1536]{1,0:T(8,128)(2,1)}, u32[]{:S(2)}, u32[]{:S(2)}) collective-permute-start(bf16[1024,1536]{1,0:T(8,128)(2,1)} %pad_maximum_fusion), channel_id=1, source_target_pairs={{0,1},{1,0},{2,3},{3,2},{4,5},{5,4},{6,7},{7,6},{8,9},{9,8},{10,11... | collective-permute-start | bytes 9437192 | tf_op jit(solution)/shard_map/ppermute | solution.py:411
  82.2 31.1 %all-to-all-start = ((bf16[8,88,1536]{2,1,0:T(8,128)(2,1)}), bf16[8,88,1536]{2,1,0:T(8,128)(2,1)S(1)}, u32[]{:S(2)}, u32[]{:S(2)}) async-start(bf16[8,88,1536]{2,1,0:T(8,128)(2,1)} %bitcast.28), calls=%async_computation | async-start | bytes 4325376 | tf_op jit(solution)/shard_map/all_to_all | solution.py:428
  113.3 31.7 %all-to-all-start.1 = ((bf16[8,88,1536]{2,1,0:T(8,128)(2,1)}), bf16[8,88,1536]{2,1,0:T(8,128)(2,1)}, u32[]{:S(2)}, u32[]{:S(2)}) async-start(bf16[8,88,1536]{2,1,0:T(8,128)(2,1)} %bitcast.27), calls=%async_computation.1 | async-start | bytes 4325376 | tf_op jit(solution)/shard_map/all_to_all | solution.py:428
  145.0 24.9 %copy-start.5 = (f32[224,128]{1,0:T(8,128)S(1)}, f32[224,128]{1,0:T(8,128)}, u32[]{:S(2)}) copy-start(f32[224,128]{1,0:T(8,128)} %get-tuple-element.72.info_ref) | copy-start | bytes 344068
  145.0 14.2 %collective-permute-start.8 = (bf16[88,1536]{1,0:T(8,128)(2,1)}, bf16[88,1536]{1,0:T(8,128)(2,1)S(1)}, u32[]{:S(2)}, u32[]{:S(2)}) collective-permute-start(bf16[88,1536]{1,0:T(8,128)(2,1)} %get-tuple-element.84), channel_id=1, source_target_pairs={{0,24},{4,28},{8,16},{12,20},{16,8},{20,12},{24,0},{28,4},{1,25},{... | collective-permute-start | bytes 811016 | tf_op jit(solution)/shard_map/ppermute | solution.py:335
  146.8 13.1 %collective-permute-start.9 = (bf16[88,1536]{1,0:T(8,128)(2,1)}, bf16[88,1536]{1,0:T(8,128)(2,1)S(1)}, u32[]{:S(2)}, u32[]{:S(2)}) collective-permute-start(bf16[88,1536]{1,0:T(8,128)(2,1)} %get-tuple-element.85), channel_id=1, source_target_pairs={{0,28},{4,24},{8,20},{12,16},{16,12},{20,8},{24,4},{28,0},{1,29},{... | collective-permute-start | bytes 811016 | tf_op jit(solution)/shard_map/ppermute | solution.py:335
  146.8 19.8 %collective-permute-start.10 = (bf16[88,1536]{1,0:T(8,128)(2,1)}, bf16[88,1536]{1,0:T(8,128)(2,1)S(1)}, u32[]{:S(2)}, u32[]{:S(2)}) collective-permute-start(bf16[88,1536]{1,0:T(8,128)(2,1)} %get-tuple-element.86), channel_id=1, source_target_pairs={{0,8},{4,12},{8,0},{12,4},{16,24},{20,28},{24,16},{28,20},{1,9},{5... | collective-permute-start | bytes 811016 | tf_op jit(solution)/shard_map/ppermute | solution.py:335
  147.9 21.2 %collective-permute-start.11 = (bf16[88,1536]{1,0:T(8,128)(2,1)}, bf16[88,1536]{1,0:T(8,128)(2,1)S(1)}, u32[]{:S(2)}, u32[]{:S(2)}) collective-permute-start(bf16[88,1536]{1,0:T(8,128)(2,1)} %get-tuple-element.87), channel_id=1, source_target_pairs={{0,12},{4,8},{8,4},{12,0},{16,28},{20,24},{24,20},{28,16},{1,13},{... | collective-permute-start | bytes 811016 | tf_op jit(solution)/shard_map/ppermute | solution.py:335
  149.5 19.6 %collective-permute-start.12 = (bf16[88,1536]{1,0:T(8,128)(2,1)}, bf16[88,1536]{1,0:T(8,128)(2,1)S(1)}, u32[]{:S(2)}, u32[]{:S(2)}) collective-permute-start(bf16[88,1536]{1,0:T(8,128)(2,1)} %get-tuple-element.88), channel_id=1, source_target_pairs={{0,16},{4,20},{8,24},{12,28},{16,0},{20,4},{24,8},{28,12},{1,17},{... | collective-permute-start | bytes 811016 | tf_op jit(solution)/shard_map/ppermute | solution.py:335
  159.2 26.0 %copy-start.16 = (bf16[88,1536]{1,0:T(8,128)(2,1)S(1)}, bf16[88,1536]{1,0:T(8,128)(2,1)}, u32[]{:S(2)}) copy-start(bf16[88,1536]{1,0:T(8,128)(2,1)} %get-tuple-element.106) | copy-start | bytes 811012
  159.2 30.7 %copy-start.15 = (bf16[88,1536]{1,0:T(8,128)(2,1)S(1)}, bf16[88,1536]{1,0:T(8,128)(2,1)}, u32[]{:S(2)}) copy-start(bf16[88,1536]{1,0:T(8,128)(2,1)} %get-tuple-element.107) | copy-start | bytes 811012
  159.2 46.2 %copy-start = (f32[12,224,128]{2,1,0:T(8,128)S(1)}, f32[12,224,128]{2,1,0:T(8,128)}, u32[]{:S(2)}) copy-start(f32[12,224,128]{2,1,0:T(8,128)} %get-tuple-element.71.second_ref) | copy-start | bytes 4128772
  159.2 46.2 %copy-start.1 = (bf16[88,1536]{1,0:T(8,128)(2,1)S(1)}, bf16[88,1536]{1,0:T(8,128)(2,1)}, u32[]{:S(2)}) copy-start(bf16[88,1536]{1,0:T(8,128)(2,1)} %get-tuple-element.108.refs_7_) | copy-start | bytes 811012
  159.2 46.2 %copy-start.2 = (f32[224,128]{1,0:T(8,128)S(1)}, f32[224,128]{1,0:T(8,128)}, u32[]{:S(2)}) copy-start(f32[224,128]{1,0:T(8,128)} %get-tuple-element.70.info_ref) | copy-start | bytes 344068
  159.2 10.7 %collective-permute-start.13 = (bf16[88,1536]{1,0:T(8,128)(2,1)S(1)}, bf16[88,1536]{1,0:T(8,128)(2,1)S(1)}, u32[]{:S(2)}, u32[]{:S(2)}) collective-permute-start(bf16[88,1536]{1,0:T(8,128)(2,1)S(1)} %copy-done.22), channel_id=1, source_target_pairs={{0,20},{4,16},{8,28},{12,24},{16,4},{20,0},{24,12},{28,8},{1,21},{... | collective-permute-start | bytes 811016 | tf_op jit(solution)/shard_map/ppermute | solution.py:335
  159.9 10.0 %collective-permute-start.14 = (bf16[88,1536]{1,0:T(8,128)(2,1)S(1)}, bf16[88,1536]{1,0:T(8,128)(2,1)S(1)}, u32[]{:S(2)}, u32[]{:S(2)}) collective-permute-start(bf16[88,1536]{1,0:T(8,128)(2,1)S(1)} %copy-done.21), channel_id=1, source_target_pairs={{0,4},{4,0},{8,12},{12,8},{16,20},{20,16},{24,28},{28,24},{1,5},{5... | collective-permute-start | bytes 811016 | tf_op jit(solution)/shard_map/ppermute | solution.py:335
  166.6 3.3 %collective-permute-start.15 = (bf16[88,1536]{1,0:T(8,128)(2,1)}, bf16[88,1536]{1,0:T(8,128)(2,1)S(1)}, u32[]{:S(2)}, u32[]{:S(2)}) collective-permute-start(bf16[88,1536]{1,0:T(8,128)(2,1)} %get-tuple-element.93), channel_id=1, source_target_pairs={{0,4},{4,0},{8,12},{12,8},{16,20},{20,16},{24,28},{28,24},{1,5},{5... | collective-permute-start | bytes 811016 | tf_op jit(solution)/shard_map/ppermute | solution.py:335
  170.8 34.6 %collective-permute-start.16 = (bf16[224,1536]{1,0:T(8,128)(2,1)S(1)}, bf16[224,1536]{1,0:T(8,128)(2,1)S(1)}, u32[]{:S(2)}, u32[]{:S(2)}) collective-permute-start(bf16[224,1536]{1,0:T(8,128)(2,1)S(1)} %theirs.1), channel_id=1, source_target_pairs={{0,2},{1,3},{2,0},{3,1},{4,6},{5,7},{6,4},{7,5},{8,10},{9,11},{10,... | collective-permute-start | bytes 2064392 | tf_op jit(solution)/shard_map/ppermute | solution.py:503
  174.9 10.3 %collective-permute-start.17 = (bf16[88,1536]{1,0:T(8,128)(2,1)S(1)}, bf16[88,1536]{1,0:T(8,128)(2,1)S(1)}, u32[]{:S(2)}, u32[]{:S(2)}) collective-permute-start(bf16[88,1536]{1,0:T(8,128)(2,1)S(1)} %copy-done.20), channel_id=1, source_target_pairs={{0,24},{4,28},{8,16},{12,20},{16,8},{20,12},{24,0},{28,4},{1,25},{... | collective-permute-start | bytes 811016 | tf_op jit(solution)/shard_map/ppermute | solution.py:335
  177.2 12.7 %collective-permute-start.18 = (bf16[88,1536]{1,0:T(8,128)(2,1)S(1)}, bf16[88,1536]{1,0:T(8,128)(2,1)S(1)}, u32[]{:S(2)}, u32[]{:S(2)}) collective-permute-start(bf16[88,1536]{1,0:T(8,128)(2,1)S(1)} %copy-done.19), channel_id=1, source_target_pairs={{0,28},{4,24},{8,20},{12,16},{16,12},{20,8},{24,4},{28,0},{1,29},{... | collective-permute-start | bytes 811016 | tf_op jit(solution)/shard_map/ppermute | solution.py:335
  177.2 19.5 %collective-permute-start.19 = (bf16[88,1536]{1,0:T(8,128)(2,1)S(1)}, bf16[88,1536]{1,0:T(8,128)(2,1)S(1)}, u32[]{:S(2)}, u32[]{:S(2)}) collective-permute-start(bf16[88,1536]{1,0:T(8,128)(2,1)S(1)} %copy-done.18), channel_id=1, source_target_pairs={{0,8},{4,12},{8,0},{12,4},{16,24},{20,28},{24,16},{28,20},{1,9},{5... | collective-permute-start | bytes 811016 | tf_op jit(solution)/shard_map/ppermute | solution.py:335
  179.5 20.9 %collective-permute-start.20 = (bf16[88,1536]{1,0:T(8,128)(2,1)S(1)}, bf16[88,1536]{1,0:T(8,128)(2,1)S(1)}, u32[]{:S(2)}, u32[]{:S(2)}) collective-permute-start(bf16[88,1536]{1,0:T(8,128)(2,1)S(1)} %copy-done.17), channel_id=1, source_target_pairs={{0,12},{4,8},{8,4},{12,0},{16,28},{20,24},{24,20},{28,16},{1,13},{... | collective-permute-start | bytes 811016 | tf_op jit(solution)/shard_map/ppermute | solution.py:335
  185.2 15.3 %collective-permute-start.21 = (bf16[88,1536]{1,0:T(8,128)(2,1)S(1)}, bf16[88,1536]{1,0:T(8,128)(2,1)S(1)}, u32[]{:S(2)}, u32[]{:S(2)}) collective-permute-start(bf16[88,1536]{1,0:T(8,128)(2,1)S(1)} %copy-done.16), channel_id=1, source_target_pairs={{0,16},{4,20},{8,24},{12,28},{16,0},{20,4},{24,8},{28,12},{1,17},{... | collective-permute-start | bytes 811016 | tf_op jit(solution)/shard_map/ppermute | solution.py:335
  189.9 11.4 %collective-permute-start.22 = (bf16[88,1536]{1,0:T(8,128)(2,1)S(1)}, bf16[88,1536]{1,0:T(8,128)(2,1)S(1)}, u32[]{:S(2)}, u32[]{:S(2)}) collective-permute-start(bf16[88,1536]{1,0:T(8,128)(2,1)S(1)} %copy-done.15), channel_id=1, source_target_pairs={{0,20},{4,16},{8,28},{12,24},{16,4},{20,0},{24,12},{28,8},{1,21},{... | collective-permute-start | bytes 811016 | tf_op jit(solution)/shard_map/ppermute | solution.py:335
  (20 other events, 227.8 us)

commit v13 on v12

--- a/solution.py
+++ b/solution.py
@@ -72,7 +72,7 @@
 
 
 def attend_kernel(count, rows, heads, place, me_ref, scale_ref, len_ref, *refs):
-    x_refs, o_refs = refs[:count], refs[count : 2 * count]
+    x_refs, o_refs = refs[:count][::-1], refs[count : 2 * count]
     k_ref, v_ref, a_ref = refs[2 * count :]
     me = me_ref[0]
     width = heads * HEAD_DIM
@@ -157,7 +157,7 @@
     turned_ref,
     *refs,
 ):
-    att_refs, out_ref = refs[:count], refs[count]
+    att_refs, out_ref = refs[:count][::-1], refs[count]
     info_ref, second_ref, x_ref, first_ref, lab_ref = refs[-5:]
     me = me_ref[0]
     turn = expert_ref[0]
@@ -402,11 +402,11 @@
         compiler_params=params(16),
         cost_estimate=cost(6),
         name="attend",
-    )(me, scales, lengths, *arrived)
+    )(me, scales, lengths, *arrived[::-1])
     windows = trade(attended, "tm", direct)
 
     units = expert_in.shape[1]
-    (shard,) = after((jnp.concatenate([expert_in[0], expert_out[0]]),), windows)
+    (shard,) = after((jnp.concatenate([expert_in[0], expert_out[0]]),), windows[::-1])
     if half == 2:
         moved = lax.ppermute(shard, "tm", [(i, i ^ 1) for i in range(count)])
         weights = [expert_in[0], expert_out[0], moved]
@@ -446,7 +446,7 @@
             compiler_params=params(56),
             cost_estimate=cost(7),
             name="frames",
-        )(me, expert, lengths, out_proj, taps, router, block_routes, block_routes.T, *windows)
+        )(me, expert, lengths, out_proj, taps, router, block_routes, block_routes.T, *windows[::-1])
         return made
 
     def run_expert(tokens, matrices, parts, partial=(), last=True):
@@ -475,7 +475,7 @@
 
     outgoing_a, info_a, _ = send_frames(windows, half, partner_routes)
     tokens_a = route(outgoing_a)
-    windows = after(windows, (outgoing_a,))
+    windows = after(windows[::-1], (outgoing_a,))[::-1]
     outgoing_b, info_b, second = send_frames(windows, 0, routes[0])
     tokens_b = route(after((outgoing_b,), tokens_a)[0])
     if half == 2:

time: 207 us -> 204 us (0.986)
  starting transfers between devices: 47.1 us -> 38.1 us
  waiting for transfers between devices: 95.1 us -> 100 us
    ppermute x20, starting transfers between devices: 29.5 us -> 25 us  [trade(): lax.ppermute(arrays[r], axis, [(i, i ^ r) for i in range(count)])]
    ppermute x20, waiting for transfers between devices: 64.4 us -> 68.6 us  [trade(): lax.ppermute(arrays[r], axis, [(i, i ^ r) for i in range(count)])]
    ppermute x1, starting transfers between devices: 3.58 us -> 0.07 us  [body(): moved = lax.ppermute(shard, 'tm', [(i, i ^ 1) for i in range(count)])]
  transfers between devices with their start and end apart: 25 -> 25, of which waited for: 17 -> 16; matrix products, arithmetic and copies ran while one was open for 3% -> 3% of each run, Pallas kernels for 25% -> 26%
where the time goes in v13:
time: 204 us
  waiting for transfers between devices  100 us (49%)
  Pallas kernels  57.5 us (28%)
  starting transfers between devices  38.1 us (19%)
  local copies, waits for them, and re-layouts  5.78 us (3%)
    ppermute x20, waiting for transfers between devices, trade(): lax.ppermute(arrays[r], axis, [(i, i ^ r) for i in range(count)])  68.6 us
    ppermute x20, starting transfers between devices, trade(): lax.ppermute(arrays[r], axis, [(i, i ^ r) for i in range(count)])  25 us
    pallas_call x2, Pallas kernels, send_frames(): pl.pallas_call(functools.partial(frame_kernel, count, rows, experts, capa...  24.3 us
    pallas_call x3, Pallas kernels, run_expert(): pl.pallas_call(kernel, out_shape=made, in_specs=[SMEM] + [pl.BlockSpec(me...  22.5 us
    ppermute x1, waiting for transfers between devices, body(): moved = lax.ppermute(shard, 'tm', [(i, i ^ 1) for i in range(count)])  14.4 us
    all_to_all x2, waiting for transfers between devices, route(): moved = lax.all_to_all(whole, 'dp', split_axis=0, concat_axis=0, tiled=True)  13.1 us
    all_to_all x2, starting transfers between devices, route(): moved = lax.all_to_all(whole, 'dp', split_axis=0, concat_axis=0, tiled=True)  8.08 us
    pallas_call x1, Pallas kernels, body(): pl.pallas_call(functools.partial(attend_kernel, count, rows, heads, place...  5.53 us
  transfers between devices with their start and end apart: 25, of which 16 were waited for; matrix products, arithmetic and copies ran while one was open for 3% of the time, Pallas kernels for 26%

profile of v13, /device:TPU:0, one launch (start us, length us, event | category | flops | bytes accessed | tf_op | source)
XLA Modules:
  0.0 203.8 jit_solution(12421693121416679830)
XLA Ops:
  0.0 2.6 %pack.1 = (bf16[3,224,256]{2,1,0:T(8,128)(2,1)}, bf16[3,224,256]{2,1,0:T(8,128)(2,1)}, bf16[3,224,256]{2,1,0:T(8,128)(2,1)}, bf16[3,224,256]{2,1,0:T(8,128)(2,1)}) custom-call(s32[1]{0:T(128)} %bitcast.me_ref, bf16[224,1024]{1,0:T(8,128)(2,1)} %bitcast.35, bf16[224,1024]{1,0:T(8,128)(2,1)} %bitcast.36, bf16[224,1024]{1,0:T(8,128)(2,1)} %bitcast.37), custom_call_target="tpu_custom_call" | custom-call | flops 1100000000 | tf_op jit(solution)/shard_map/pack/pallas_call | solution.py:376
  2.6 5.1 %collective-permute-start = (bf16[3,224,256]{2,1,0:T(8,128)(2,1)}, bf16[3,224,256]{2,1,0:T(8,128)(2,1)S(1)}, u32[]{:S(2)}, u32[]{:S(2)}) collective-permute-start(bf16[3,224,256]{2,1,0:T(8,128)(2,1)} %get-tuple-element.57), channel_id=1, source_target_pairs={{0,3},{1,2},{2,1},{3,0},{4,7},{5,6},{6,5},{7,4},{8,11},{9,10},{10,... | collective-permute-start | bytes 1032200 | tf_op jit(solution)/shard_map/ppermute | solution.py:335
  8.4 2.3 %collective-permute-start.6 = (s32[224,2]{0,1:T(2,128)S(1)}, s32[224,2]{0,1:T(2,128)S(1)}, u32[]{:S(2)}, u32[]{:S(2)}) collective-permute-start(s32[224,2]{0,1:T(2,128)S(1)} %bitcast.32), channel_id=1, source_target_pairs={{0,2},{1,3},{2,0},{3,1},{4,6},{5,7},{6,4},{7,5},{8,10},{9,11},{10,... | collective-permute-start | bytes 5384 | tf_op jit(solution)/shard_map/ppermute | solution.py:388
  10.8 6.2 %collective-permute-done.refs_0_ = bf16[3,224,256]{2,1,0:T(8,128)(2,1)S(1)} collective-permute-done((bf16[3,224,256]{2,1,0:T(8,128)(2,1)}, bf16[3,224,256]{2,1,0:T(8,128)(2,1)S(1)}, u32[]{:S(2)}, u32[]{:S(2)}) %collective-permute-start) | collective-permute-done | bytes 344096 | tf_op jit(solution)/shard_map/ppermute | solution.py:335
  17.0 20.4 %collective-permute-done.1.refs_1_ = bf16[3,224,256]{2,1,0:T(8,128)(2,1)S(1)} collective-permute-done((bf16[3,224,256]{2,1,0:T(8,128)(2,1)}, bf16[3,224,256]{2,1,0:T(8,128)(2,1)S(1)}, u32[]{:S(2)}, u32[]{:S(2)}) %collective-permute-start.1) | collective-permute-done | bytes 344096 | tf_op jit(solution)/shard_map/ppermute | solution.py:335
  38.3 5.5 %attend.1 = (bf16[2,256,256]{2,1,0:T(8,128)(2,1)S(1)}, bf16[2,256,256]{2,1,0:T(8,128)(2,1)S(1)}, bf16[2,256,256]{2,1,0:T(8,128)(2,1)S(1)}, bf16[2,256,256]{2,1,0:T(8,128)(2,1)S(1)}) custom-call(s32[1]{0:T(128)} %bitcast.me_ref, f32[4]{0:T(128)S(1)} %dynamic_slice.3.scale_ref, s32[1,4]{1,0:T(1,128)S(1)} %copy-done.3, ...), custom_call_target="tpu_custom_call" | custom-call | flops 6600000000 | tf_op jit(solution)/shard_map/attend/pallas_call | solution.py:392
  44.6 2.5 %collective-permute-start.3 = (bf16[2,256,256]{2,1,0:T(8,128)(2,1)S(1)}, bf16[2,256,256]{2,1,0:T(8,128)(2,1)S(1)}, u32[]{:S(2)}, u32[]{:S(2)}) collective-permute-start(bf16[2,256,256]{2,1,0:T(8,128)(2,1)S(1)} %get-tuple-element.61), channel_id=1, source_target_pairs={{0,3},{1,2},{2,1},{3,0},{4,7},{5,6},{6,5},{7,4},{8,11},{9,10},{10,... | collective-permute-start | bytes 786440 | tf_op jit(solution)/shard_map/ppermute | solution.py:335
  47.1 1.9 collective-permute-start.5
  49.0 1.9 pad_maximum_fusion
  53.4 2.3 %collective-permute-done.3.refs_0_ = bf16[2,256,256]{2,1,0:T(8,128)(2,1)S(1)} collective-permute-done((bf16[2,256,256]{2,1,0:T(8,128)(2,1)S(1)}, bf16[2,256,256]{2,1,0:T(8,128)(2,1)S(1)}, u32[]{:S(2)}, u32[]{:S(2)}) %collective-permute-start.3) | collective-permute-done | bytes 262176 | tf_op jit(solution)/shard_map/ppermute | solution.py:335
  55.7 12.1 %collective-permute-done.4.refs_1_ = bf16[2,256,256]{2,1,0:T(8,128)(2,1)S(1)} collective-permute-done((bf16[2,256,256]{2,1,0:T(8,128)(2,1)S(1)}, bf16[2,256,256]{2,1,0:T(8,128)(2,1)S(1)}, u32[]{:S(2)}, u32[]{:S(2)}) %collective-permute-start.4) | collective-permute-done | bytes 262176 | tf_op jit(solution)/shard_map/ppermute | solution.py:335
  68.6 10.8 %frames.2 = (bf16[704,1536]{1,0:T(8,128)(2,1)}, f32[224,128]{1,0:T(8,128)}, f32[12,224,128]{2,1,0:T(8,128)}) custom-call(s32[1]{0:T(128)} %bitcast.me_ref, s32[1]{0:T(128)} %bitcast.1.expert_ref, s32[1,4]{1,0:T(1,128)} %len_ref.5, bf16[1024,1536]{1,0:T(8,128)(2,1)} %proj_ref.3, f32[12,31,128]{2,1,0:T(8,128)} %bitcast.29, bf16[1536,8]{1,0:T(8,128)(2,1)} %copy.19.router_ref, ...), custom_call_target="tpu_custom_call" | custom-call | flops 7699999744 | tf_op jit(solution)/shard_map/frames/pallas_call | solution.py:432
  79.4 3.7 %all-to-all-start = ((bf16[8,88,1536]{2,1,0:T(8,128)(2,1)}), bf16[8,88,1536]{2,1,0:T(8,128)(2,1)S(1)}, u32[]{:S(2)}, u32[]{:S(2)}) async-start(bf16[8,88,1536]{2,1,0:T(8,128)(2,1)} %bitcast.28), calls=%async_computation | async-start | bytes 4325376 | tf_op jit(solution)/shard_map/all_to_all | solution.py:428
  83.9 13.5 %frames.3 = (bf16[704,1536]{1,0:T(8,128)(2,1)}, f32[224,128]{1,0:T(8,128)}, f32[12,224,128]{2,1,0:T(8,128)}) custom-call(s32[1]{0:T(128)} %bitcast.me_ref, s32[1]{0:T(128)} %bitcast.1.expert_ref, s32[1,4]{1,0:T(1,128)} %len_ref.5, bf16[1024,1536]{1,0:T(8,128)(2,1)} %proj_ref.3, f32[12,31,128]{2,1,0:T(8,128)} %bitcast.30, bf16[1536,8]{1,0:T(8,128)(2,1)} %copy.19.router_ref, ...), custom_call_target="tpu_custom_call" | custom-call | flops 7699999744 | tf_op jit(solution)/shard_map/frames/pallas_call | solution.py:432
  97.5 13.1 %all-to-all-done = bf16[8,88,1536]{2,1,0:T(8,128)(2,1)S(1)} async-done(((bf16[8,88,1536]{2,1,0:T(8,128)(2,1)}), bf16[8,88,1536]{2,1,0:T(8,128)(2,1)S(1)}, u32[]{:S(2)}, u32[]{:S(2)}) %all-to-all-start) | async-done | bytes 2162720 | tf_op jit(solution)/shard_map/all_to_all | solution.py:428
  110.5 4.3 %all-to-all-start.1 = ((bf16[8,88,1536]{2,1,0:T(8,128)(2,1)}), bf16[8,88,1536]{2,1,0:T(8,128)(2,1)}, u32[]{:S(2)}, u32[]{:S(2)}) async-start(bf16[8,88,1536]{2,1,0:T(8,128)(2,1)} %bitcast.27), calls=%async_computation.1 | async-start | bytes 4325376 | tf_op jit(solution)/shard_map/all_to_all | solution.py:428
  114.9 6.9 %experts.3.refs_2_ = f32[704,1536]{1,0:T(8,128)} custom-call(s32[1]{0:T(128)} %bitcast.1.expert_ref, bf16[704,1536]{1,0:T(8,128)(2,1)} %bitcast.19, bf16[512,1536]{1,0:T(8,128)(2,1)} %bitcast.24, bf16[512,1536]{1,0:T(8,128)(2,1)} %bitcast.21), custom_call_target="tpu_custom_call" | custom-call | tf_op jit(solution)/shard_map/experts/pallas_call | solution.py:461
  121.8 14.4 %collective-permute-done.7.refs_1_.refs_3_ = bf16[1024,1536]{1,0:T(8,128)(2,1)} collective-permute-done((bf16[1024,1536]{1,0:T(8,128)(2,1)}, bf16[1024,1536]{1,0:T(8,128)(2,1)}, u32[]{:S(2)}, u32[]{:S(2)}) %collective-permute-start.7) | collective-permute-done | bytes 3145760 | tf_op jit(solution)/shard_map/ppermute | solution.py:411
  136.2 6.8 %experts.4 = (bf16[88,1536]{1,0:T(8,128)(2,1)}, bf16[88,1536]{1,0:T(8,128)(2,1)}, bf16[88,1536]{1,0:T(8,128)(2,1)}, bf16[88,1536]{1,0:T(8,128)(2,1)}, bf16[88,15...) custom-call(s32[1]{0:T(128)} %bitcast.1.expert_ref, ...), custom_call_target="tpu_custom_call" | custom-call | flops 8800000000 | tf_op jit(solution)/shard_map/experts/pallas_call | solution.py:461
  143.1 2.5 %collective-permute-start.8 = (bf16[88,1536]{1,0:T(8,128)(2,1)}, bf16[88,1536]{1,0:T(8,128)(2,1)S(1)}, u32[]{:S(2)}, u32[]{:S(2)}) collective-permute-start(bf16[88,1536]{1,0:T(8,128)(2,1)} %get-tuple-element.84), channel_id=1, source_target_pairs={{0,24},{4,28},{8,16},{12,20},{16,8},{20,12},{24,0},{28,4},{1,25},{... | collective-permute-start | bytes 811016 | tf_op jit(solution)/shard_map/ppermute | solution.py:335
  149.1 8.8 %experts.5 = (bf16[88,1536]{1,0:T(8,128)(2,1)}, bf16[88,1536]{1,0:T(8,128)(2,1)}, bf16[88,1536]{1,0:T(8,128)(2,1)}, bf16[88,1536]{1,0:T(8,128)(2,1)}, bf16[88,15...) custom-call(s32[1]{0:T(128)} %bitcast.1.expert_ref, ...), custom_call_target="tpu_custom_call" | custom-call | flops 8800000000 | tf_op jit(solution)/shard_map/experts/pallas_call | solution.py:461
  158.7 5.8 %collective-permute-done.10.refs_2_ = bf16[88,1536]{1,0:T(8,128)(2,1)S(1)} collective-permute-done((bf16[88,1536]{1,0:T(8,128)(2,1)}, bf16[88,1536]{1,0:T(8,128)(2,1)S(1)}, u32[]{:S(2)}, u32[]{:S(2)}) %collective-permute-start.10) | collective-permute-done | bytes 270368 | tf_op jit(solution)/shard_map/ppermute | solution.py:335
  164.5 2.8 %collective-permute-done.11.refs_3_ = bf16[88,1536]{1,0:T(8,128)(2,1)S(1)} collective-permute-done((bf16[88,1536]{1,0:T(8,128)(2,1)}, bf16[88,1536]{1,0:T(8,128)(2,1)S(1)}, u32[]{:S(2)}, u32[]{:S(2)}) %collective-permute-start.11) | collective-permute-done | bytes 270368 | tf_op jit(solution)/shard_map/ppermute | solution.py:335
  168.9 2.7 %collective-permute-start.16 = (bf16[224,1536]{1,0:T(8,128)(2,1)S(1)}, bf16[224,1536]{1,0:T(8,128)(2,1)S(1)}, u32[]{:S(2)}, u32[]{:S(2)}) collective-permute-start(bf16[224,1536]{1,0:T(8,128)(2,1)S(1)} %theirs.1), channel_id=1, source_target_pairs={{0,2},{1,3},{2,0},{3,1},{4,6},{5,7},{6,4},{7,5},{8,10},{9,11},{10,... | collective-permute-start | bytes 2064392 | tf_op jit(solution)/shard_map/ppermute | solution.py:503
  171.6 2.3 %collective-permute-start.17 = (bf16[88,1536]{1,0:T(8,128)(2,1)S(1)}, bf16[88,1536]{1,0:T(8,128)(2,1)S(1)}, u32[]{:S(2)}, u32[]{:S(2)}) collective-permute-start(bf16[88,1536]{1,0:T(8,128)(2,1)S(1)} %copy-done.20), channel_id=1, source_target_pairs={{0,24},{4,28},{8,16},{12,20},{16,8},{20,12},{24,0},{28,4},{1,25},{... | collective-permute-start | bytes 811016 | tf_op jit(solution)/shard_map/ppermute | solution.py:335
  173.9 2.3 %collective-permute-start.19 = (bf16[88,1536]{1,0:T(8,128)(2,1)S(1)}, bf16[88,1536]{1,0:T(8,128)(2,1)S(1)}, u32[]{:S(2)}, u32[]{:S(2)}) collective-permute-start(bf16[88,1536]{1,0:T(8,128)(2,1)S(1)} %copy-done.18), channel_id=1, source_target_pairs={{0,8},{4,12},{8,0},{12,4},{16,24},{20,28},{24,16},{28,20},{1,9},{5... | collective-permute-start | bytes 811016 | tf_op jit(solution)/shard_map/ppermute | solution.py:335
  176.9 5.0 %collective-permute-done.17.refs_0_ = bf16[88,1536]{1,0:T(8,128)(2,1)S(1)} collective-permute-done((bf16[88,1536]{1,0:T(8,128)(2,1)S(1)}, bf16[88,1536]{1,0:T(8,128)(2,1)S(1)}, u32[]{:S(2)}, u32[]{:S(2)}) %collective-permute-start.17) | collective-permute-done | bytes 270368 | tf_op jit(solution)/shard_map/ppermute | solution.py:335
  183.2 3.4 %collective-permute-done.18.refs_1_ = bf16[88,1536]{1,0:T(8,128)(2,1)S(1)} collective-permute-done((bf16[88,1536]{1,0:T(8,128)(2,1)S(1)}, bf16[88,1536]{1,0:T(8,128)(2,1)S(1)}, u32[]{:S(2)}, u32[]{:S(2)}) %collective-permute-start.18) | collective-permute-done | bytes 270368 | tf_op jit(solution)/shard_map/ppermute | solution.py:335
  186.6 2.1 %collective-permute-start.22 = (bf16[88,1536]{1,0:T(8,128)(2,1)S(1)}, bf16[88,1536]{1,0:T(8,128)(2,1)S(1)}, u32[]{:S(2)}, u32[]{:S(2)}) collective-permute-start(bf16[88,1536]{1,0:T(8,128)(2,1)S(1)} %copy-done.15), channel_id=1, source_target_pairs={{0,20},{4,16},{8,28},{12,24},{16,4},{20,0},{24,12},{28,8},{1,21},{... | collective-permute-start | bytes 811016 | tf_op jit(solution)/shard_map/ppermute | solution.py:335
  188.8 4.6 %collective-permute-done.19.refs_2_ = bf16[88,1536]{1,0:T(8,128)(2,1)S(1)} collective-permute-done((bf16[88,1536]{1,0:T(8,128)(2,1)S(1)}, bf16[88,1536]{1,0:T(8,128)(2,1)S(1)}, u32[]{:S(2)}, u32[]{:S(2)}) %collective-permute-start.19) | collective-permute-done | bytes 270368 | tf_op jit(solution)/shard_map/ppermute | solution.py:335
  193.4 3.8 %collective-permute-done.20.refs_3_ = bf16[88,1536]{1,0:T(8,128)(2,1)S(1)} collective-permute-done((bf16[88,1536]{1,0:T(8,128)(2,1)S(1)}, bf16[88,1536]{1,0:T(8,128)(2,1)S(1)}, u32[]{:S(2)}, u32[]{:S(2)}) %collective-permute-start.20) | collective-permute-done | bytes 270368 | tf_op jit(solution)/shard_map/ppermute | solution.py:335
  198.1 4.1 %collective-permute-done.16.part_ref = bf16[224,1536]{1,0:T(8,128)(2,1)S(1)} collective-permute-done((bf16[224,1536]{1,0:T(8,128)(2,1)S(1)}, bf16[224,1536]{1,0:T(8,128)(2,1)S(1)}, u32[]{:S(2)}, u32[]{:S(2)}) %collective-permute-start.16) | collective-permute-done | bytes 688160 | tf_op jit(solution)/shard_map/ppermute | solution.py:503
  (88 shorter events, 16.9 us)
Async XLA Ops:
  0.0 37.4 %copy-start.3 = (s32[1,4]{1,0:T(1,128)S(1)}, s32[1,4]{1,0:T(1,128)}, u32[]{:S(2)}) copy-start(s32[1,4]{1,0:T(1,128)} %len_ref.5) | copy-start | bytes 52
  2.6 14.4 %collective-permute-start = (bf16[3,224,256]{2,1,0:T(8,128)(2,1)}, bf16[3,224,256]{2,1,0:T(8,128)(2,1)S(1)}, u32[]{:S(2)}, u32[]{:S(2)}) collective-permute-start(bf16[3,224,256]{2,1,0:T(8,128)(2,1)} %get-tuple-element.57), channel_id=1, source_target_pairs={{0,3},{1,2},{2,1},{3,0},{4,7},{5,6},{6,5},{7,4},{8,11},{9,10},{10,... | collective-permute-start | bytes 1032200 | tf_op jit(solution)/shard_map/ppermute | solution.py:335
  7.7 29.6 %collective-permute-start.1 = (bf16[3,224,256]{2,1,0:T(8,128)(2,1)}, bf16[3,224,256]{2,1,0:T(8,128)(2,1)S(1)}, u32[]{:S(2)}, u32[]{:S(2)}) collective-permute-start(bf16[3,224,256]{2,1,0:T(8,128)(2,1)} %get-tuple-element.58), channel_id=1, source_target_pairs={{0,2},{1,3},{2,0},{3,1},{4,6},{5,7},{6,4},{7,5},{8,10},{9,11},{10,... | collective-permute-start | bytes 1032200 | tf_op jit(solution)/shard_map/ppermute | solution.py:335
  7.8 29.6 %collective-permute-start.2 = (bf16[3,224,256]{2,1,0:T(8,128)(2,1)}, bf16[3,224,256]{2,1,0:T(8,128)(2,1)S(1)}, u32[]{:S(2)}, u32[]{:S(2)}) collective-permute-start(bf16[3,224,256]{2,1,0:T(8,128)(2,1)} %get-tuple-element.59), channel_id=1, source_target_pairs={{0,1},{1,0},{2,3},{3,2},{4,5},{5,4},{6,7},{7,6},{8,9},{9,8},{10,11... | collective-permute-start | bytes 1032200 | tf_op jit(solution)/shard_map/ppermute | solution.py:335
  8.4 44.3 %collective-permute-start.6 = (s32[224,2]{0,1:T(2,128)S(1)}, s32[224,2]{0,1:T(2,128)S(1)}, u32[]{:S(2)}, u32[]{:S(2)}) collective-permute-start(s32[224,2]{0,1:T(2,128)S(1)} %bitcast.32), channel_id=1, source_target_pairs={{0,2},{1,3},{2,0},{3,1},{4,6},{5,7},{6,4},{7,5},{8,10},{9,11},{10,... | collective-permute-start | bytes 5384 | tf_op jit(solution)/shard_map/ppermute | solution.py:388
  44.6 11.1 %collective-permute-start.3 = (bf16[2,256,256]{2,1,0:T(8,128)(2,1)S(1)}, bf16[2,256,256]{2,1,0:T(8,128)(2,1)S(1)}, u32[]{:S(2)}, u32[]{:S(2)}) collective-permute-start(bf16[2,256,256]{2,1,0:T(8,128)(2,1)S(1)} %get-tuple-element.61), channel_id=1, source_target_pairs={{0,3},{1,2},{2,1},{3,0},{4,7},{5,6},{6,5},{7,4},{8,11},{9,10},{10,... | collective-permute-start | bytes 786440 | tf_op jit(solution)/shard_map/ppermute | solution.py:335
  47.1 20.7 %collective-permute-start.4 = (bf16[2,256,256]{2,1,0:T(8,128)(2,1)S(1)}, bf16[2,256,256]{2,1,0:T(8,128)(2,1)S(1)}, u32[]{:S(2)}, u32[]{:S(2)}) collective-permute-start(bf16[2,256,256]{2,1,0:T(8,128)(2,1)S(1)} %get-tuple-element.62), channel_id=1, source_target_pairs={{0,2},{1,3},{2,0},{3,1},{4,6},{5,7},{6,4},{7,5},{8,10},{9,11},{10,... | collective-permute-start | bytes 786440 | tf_op jit(solution)/shard_map/ppermute | solution.py:335
  47.1 20.7 %collective-permute-start.5 = (bf16[2,256,256]{2,1,0:T(8,128)(2,1)S(1)}, bf16[2,256,256]{2,1,0:T(8,128)(2,1)S(1)}, u32[]{:S(2)}, u32[]{:S(2)}) collective-permute-start(bf16[2,256,256]{2,1,0:T(8,128)(2,1)S(1)} %get-tuple-element.63), channel_id=1, source_target_pairs={{0,1},{1,0},{2,3},{3,2},{4,5},{5,4},{6,7},{7,6},{8,9},{9,8},{10,11... | collective-permute-start | bytes 786440 | tf_op jit(solution)/shard_map/ppermute | solution.py:335
  67.8 68.4 %collective-permute-start.7 = (bf16[1024,1536]{1,0:T(8,128)(2,1)}, bf16[1024,1536]{1,0:T(8,128)(2,1)}, u32[]{:S(2)}, u32[]{:S(2)}) collective-permute-start(bf16[1024,1536]{1,0:T(8,128)(2,1)} %pad_maximum_fusion), channel_id=1, source_target_pairs={{0,1},{1,0},{2,3},{3,2},{4,5},{5,4},{6,7},{7,6},{8,9},{9,8},{10,11... | collective-permute-start | bytes 9437192 | tf_op jit(solution)/shard_map/ppermute | solution.py:411
  79.4 31.1 %all-to-all-start = ((bf16[8,88,1536]{2,1,0:T(8,128)(2,1)}), bf16[8,88,1536]{2,1,0:T(8,128)(2,1)S(1)}, u32[]{:S(2)}, u32[]{:S(2)}) async-start(bf16[8,88,1536]{2,1,0:T(8,128)(2,1)} %bitcast.28), calls=%async_computation | async-start | bytes 4325376 | tf_op jit(solution)/shard_map/all_to_all | solution.py:428
  110.5 32.5 %all-to-all-start.1 = ((bf16[8,88,1536]{2,1,0:T(8,128)(2,1)}), bf16[8,88,1536]{2,1,0:T(8,128)(2,1)}, u32[]{:S(2)}, u32[]{:S(2)}) async-start(bf16[8,88,1536]{2,1,0:T(8,128)(2,1)} %bitcast.27), calls=%async_computation.1 | async-start | bytes 4325376 | tf_op jit(solution)/shard_map/all_to_all | solution.py:428
  143.1 25.0 %copy-start.4 = (bf16[88,1536]{1,0:T(8,128)(2,1)S(1)}, bf16[88,1536]{1,0:T(8,128)(2,1)}, u32[]{:S(2)}) copy-start(bf16[88,1536]{1,0:T(8,128)(2,1)} %get-tuple-element.101.refs_7_) | copy-start | bytes 811012
  143.1 25.0 %copy-start.5 = (f32[224,128]{1,0:T(8,128)S(1)}, f32[224,128]{1,0:T(8,128)}, u32[]{:S(2)}) copy-start(f32[224,128]{1,0:T(8,128)} %get-tuple-element.72.info_ref) | copy-start | bytes 344068
  143.1 14.9 %collective-permute-start.8 = (bf16[88,1536]{1,0:T(8,128)(2,1)}, bf16[88,1536]{1,0:T(8,128)(2,1)S(1)}, u32[]{:S(2)}, u32[]{:S(2)}) collective-permute-start(bf16[88,1536]{1,0:T(8,128)(2,1)} %get-tuple-element.84), channel_id=1, source_target_pairs={{0,24},{4,28},{8,16},{12,20},{16,8},{20,12},{24,0},{28,4},{1,25},{... | collective-permute-start | bytes 811016 | tf_op jit(solution)/shard_map/ppermute | solution.py:335
  145.6 13.0 %collective-permute-start.9 = (bf16[88,1536]{1,0:T(8,128)(2,1)}, bf16[88,1536]{1,0:T(8,128)(2,1)S(1)}, u32[]{:S(2)}, u32[]{:S(2)}) collective-permute-start(bf16[88,1536]{1,0:T(8,128)(2,1)} %get-tuple-element.85), channel_id=1, source_target_pairs={{0,28},{4,24},{8,20},{12,16},{16,12},{20,8},{24,4},{28,0},{1,29},{... | collective-permute-start | bytes 811016 | tf_op jit(solution)/shard_map/ppermute | solution.py:335
  145.6 18.9 %collective-permute-start.10 = (bf16[88,1536]{1,0:T(8,128)(2,1)}, bf16[88,1536]{1,0:T(8,128)(2,1)S(1)}, u32[]{:S(2)}, u32[]{:S(2)}) collective-permute-start(bf16[88,1536]{1,0:T(8,128)(2,1)} %get-tuple-element.86), channel_id=1, source_target_pairs={{0,8},{4,12},{8,0},{12,4},{16,24},{20,28},{24,16},{28,20},{1,9},{5... | collective-permute-start | bytes 811016 | tf_op jit(solution)/shard_map/ppermute | solution.py:335
  146.2 21.1 %collective-permute-start.11 = (bf16[88,1536]{1,0:T(8,128)(2,1)}, bf16[88,1536]{1,0:T(8,128)(2,1)S(1)}, u32[]{:S(2)}, u32[]{:S(2)}) collective-permute-start(bf16[88,1536]{1,0:T(8,128)(2,1)} %get-tuple-element.87), channel_id=1, source_target_pairs={{0,12},{4,8},{8,4},{12,0},{16,28},{20,24},{24,20},{28,16},{1,13},{... | collective-permute-start | bytes 811016 | tf_op jit(solution)/shard_map/ppermute | solution.py:335
  147.6 19.7 %collective-permute-start.12 = (bf16[88,1536]{1,0:T(8,128)(2,1)}, bf16[88,1536]{1,0:T(8,128)(2,1)S(1)}, u32[]{:S(2)}, u32[]{:S(2)}) collective-permute-start(bf16[88,1536]{1,0:T(8,128)(2,1)} %get-tuple-element.88), channel_id=1, source_target_pairs={{0,16},{4,20},{8,24},{12,28},{16,0},{20,4},{24,8},{28,12},{1,17},{... | collective-permute-start | bytes 811016 | tf_op jit(solution)/shard_map/ppermute | solution.py:335
  157.9 28.7 %copy-start.15 = (bf16[88,1536]{1,0:T(8,128)(2,1)S(1)}, bf16[88,1536]{1,0:T(8,128)(2,1)}, u32[]{:S(2)}) copy-start(bf16[88,1536]{1,0:T(8,128)(2,1)} %get-tuple-element.107) | copy-start | bytes 811012
  157.9 44.2 %copy-start = (f32[12,224,128]{2,1,0:T(8,128)S(1)}, f32[12,224,128]{2,1,0:T(8,128)}, u32[]{:S(2)}) copy-start(f32[12,224,128]{2,1,0:T(8,128)} %get-tuple-element.71.second_ref) | copy-start | bytes 4128772
  158.0 44.2 %copy-start.1 = (bf16[88,1536]{1,0:T(8,128)(2,1)S(1)}, bf16[88,1536]{1,0:T(8,128)(2,1)}, u32[]{:S(2)}) copy-start(bf16[88,1536]{1,0:T(8,128)(2,1)} %get-tuple-element.108.refs_7_) | copy-start | bytes 811012
  158.0 44.2 %copy-start.2 = (f32[224,128]{1,0:T(8,128)S(1)}, f32[224,128]{1,0:T(8,128)}, u32[]{:S(2)}) copy-start(f32[224,128]{1,0:T(8,128)} %get-tuple-element.70.info_ref) | copy-start | bytes 344068
  158.0 10.0 %collective-permute-start.13 = (bf16[88,1536]{1,0:T(8,128)(2,1)S(1)}, bf16[88,1536]{1,0:T(8,128)(2,1)S(1)}, u32[]{:S(2)}, u32[]{:S(2)}) collective-permute-start(bf16[88,1536]{1,0:T(8,128)(2,1)S(1)} %copy-done.22), channel_id=1, source_target_pairs={{0,20},{4,16},{8,28},{12,24},{16,4},{20,0},{24,12},{28,8},{1,21},{... | collective-permute-start | bytes 811016 | tf_op jit(solution)/shard_map/ppermute | solution.py:335
  158.6 9.4 %collective-permute-start.14 = (bf16[88,1536]{1,0:T(8,128)(2,1)S(1)}, bf16[88,1536]{1,0:T(8,128)(2,1)S(1)}, u32[]{:S(2)}, u32[]{:S(2)}) collective-permute-start(bf16[88,1536]{1,0:T(8,128)(2,1)S(1)} %copy-done.21), channel_id=1, source_target_pairs={{0,4},{4,0},{8,12},{12,8},{16,20},{20,16},{24,28},{28,24},{1,5},{5... | collective-permute-start | bytes 811016 | tf_op jit(solution)/shard_map/ppermute | solution.py:335
  164.5 3.6 %collective-permute-start.15 = (bf16[88,1536]{1,0:T(8,128)(2,1)}, bf16[88,1536]{1,0:T(8,128)(2,1)S(1)}, u32[]{:S(2)}, u32[]{:S(2)}) collective-permute-start(bf16[88,1536]{1,0:T(8,128)(2,1)} %get-tuple-element.93), channel_id=1, source_target_pairs={{0,4},{4,0},{8,12},{12,8},{16,20},{20,16},{24,28},{28,24},{1,5},{5... | collective-permute-start | bytes 811016 | tf_op jit(solution)/shard_map/ppermute | solution.py:335
  168.9 33.2 %collective-permute-start.16 = (bf16[224,1536]{1,0:T(8,128)(2,1)S(1)}, bf16[224,1536]{1,0:T(8,128)(2,1)S(1)}, u32[]{:S(2)}, u32[]{:S(2)}) collective-permute-start(bf16[224,1536]{1,0:T(8,128)(2,1)S(1)} %theirs.1), channel_id=1, source_target_pairs={{0,2},{1,3},{2,0},{3,1},{4,6},{5,7},{6,4},{7,5},{8,10},{9,11},{10,... | collective-permute-start | bytes 2064392 | tf_op jit(solution)/shard_map/ppermute | solution.py:503
  171.6 10.3 %collective-permute-start.17 = (bf16[88,1536]{1,0:T(8,128)(2,1)S(1)}, bf16[88,1536]{1,0:T(8,128)(2,1)S(1)}, u32[]{:S(2)}, u32[]{:S(2)}) collective-permute-start(bf16[88,1536]{1,0:T(8,128)(2,1)S(1)} %copy-done.20), channel_id=1, source_target_pairs={{0,24},{4,28},{8,16},{12,20},{16,8},{20,12},{24,0},{28,4},{1,25},{... | collective-permute-start | bytes 811016 | tf_op jit(solution)/shard_map/ppermute | solution.py:335
  173.9 12.7 %collective-permute-start.18 = (bf16[88,1536]{1,0:T(8,128)(2,1)S(1)}, bf16[88,1536]{1,0:T(8,128)(2,1)S(1)}, u32[]{:S(2)}, u32[]{:S(2)}) collective-permute-start(bf16[88,1536]{1,0:T(8,128)(2,1)S(1)} %copy-done.19), channel_id=1, source_target_pairs={{0,28},{4,24},{8,20},{12,16},{16,12},{20,8},{24,4},{28,0},{1,29},{... | collective-permute-start | bytes 811016 | tf_op jit(solution)/shard_map/ppermute | solution.py:335
  173.9 19.5 %collective-permute-start.19 = (bf16[88,1536]{1,0:T(8,128)(2,1)S(1)}, bf16[88,1536]{1,0:T(8,128)(2,1)S(1)}, u32[]{:S(2)}, u32[]{:S(2)}) collective-permute-start(bf16[88,1536]{1,0:T(8,128)(2,1)S(1)} %copy-done.18), channel_id=1, source_target_pairs={{0,8},{4,12},{8,0},{12,4},{16,24},{20,28},{24,16},{28,20},{1,9},{5... | collective-permute-start | bytes 811016 | tf_op jit(solution)/shard_map/ppermute | solution.py:335
  176.2 20.9 %collective-permute-start.20 = (bf16[88,1536]{1,0:T(8,128)(2,1)S(1)}, bf16[88,1536]{1,0:T(8,128)(2,1)S(1)}, u32[]{:S(2)}, u32[]{:S(2)}) collective-permute-start(bf16[88,1536]{1,0:T(8,128)(2,1)S(1)} %copy-done.17), channel_id=1, source_target_pairs={{0,12},{4,8},{8,4},{12,0},{16,28},{20,24},{24,20},{28,16},{1,13},{... | collective-permute-start | bytes 811016 | tf_op jit(solution)/shard_map/ppermute | solution.py:335
  181.9 15.3 %collective-permute-start.21 = (bf16[88,1536]{1,0:T(8,128)(2,1)S(1)}, bf16[88,1536]{1,0:T(8,128)(2,1)S(1)}, u32[]{:S(2)}, u32[]{:S(2)}) collective-permute-start(bf16[88,1536]{1,0:T(8,128)(2,1)S(1)} %copy-done.16), channel_id=1, source_target_pairs={{0,16},{4,20},{8,24},{12,28},{16,0},{20,4},{24,8},{28,12},{1,17},{... | collective-permute-start | bytes 811016 | tf_op jit(solution)/shard_map/ppermute | solution.py:335
  186.6 11.4 %collective-permute-start.22 = (bf16[88,1536]{1,0:T(8,128)(2,1)S(1)}, bf16[88,1536]{1,0:T(8,128)(2,1)S(1)}, u32[]{:S(2)}, u32[]{:S(2)}) collective-permute-start(bf16[88,1536]{1,0:T(8,128)(2,1)S(1)} %copy-done.15), channel_id=1, source_target_pairs={{0,20},{4,16},{8,28},{12,24},{16,4},{20,0},{24,12},{28,8},{1,21},{... | collective-permute-start | bytes 811016 | tf_op jit(solution)/shard_map/ppermute | solution.py:335
  (20 other events, 198.6 us)

commit v14 on v13

--- a/solution.py
+++ b/solution.py
@@ -377,7 +377,7 @@
         functools.partial(pack_kernel, place),
         out_shape=(jax.ShapeDtypeStruct((3, rows, width), BF16),) * count,
         in_specs=[SMEM] + [pl.BlockSpec(memory_space=pltpu.HBM) if direct else VMEM] * 3,
-        out_specs=(VMEM,) * count,
+        out_specs=(pl.BlockSpec(memory_space=pltpu.HBM) if direct else VMEM,) * count,
         scratch_shapes=[pltpu.SemaphoreType.DMA((3 * count,))],
         compiler_params=params(60),
         cost_estimate=cost(1),

time: 204 us -> 244 us (1.20)
  Pallas kernels: 57.5 us -> 96.3 us
    pallas_call x1, Pallas kernels: 2.62 us -> 42.9 us  [body(): pl.pallas_call(functools.partial(pack_kernel, place), out_shape=(jax.Shap...]
  transfers between devices with their start and end apart: 25 -> 25, of which waited for: 16 -> 16; matrix products, arithmetic and copies ran while one was open for 3% -> 2% of each run, Pallas kernels for 26% -> 21%
where the time goes in v14:
time: 244 us
  waiting for transfers between devices  102 us (42%)
  Pallas kernels  96.3 us (39%)
  starting transfers between devices  37.4 us (15%)
  local copies, waits for them, and re-layouts  5.78 us (2%)
    ppermute x20, waiting for transfers between devices, trade(): lax.ppermute(arrays[r], axis, [(i, i ^ r) for i in range(count)])  68.6 us
    pallas_call x1, Pallas kernels, body(): pl.pallas_call(functools.partial(pack_kernel, place), out_shape=(jax.Shap...  42.9 us
    ppermute x20, starting transfers between devices, trade(): lax.ppermute(arrays[r], axis, [(i, i ^ r) for i in range(count)])  25 us
    pallas_call x2, Pallas kernels, send_frames(): pl.pallas_call(functools.partial(frame_kernel, count, rows, experts, capa...  22.8 us
    pallas_call x3, Pallas kernels, run_expert(): pl.pallas_call(kernel, out_shape=made, in_specs=[SMEM] + [pl.BlockSpec(me...  22.5 us
    all_to_all x2, waiting for transfers between devices, route(): moved = lax.all_to_all(whole, 'dp', split_axis=0, concat_axis=0, tiled=True)  15.3 us
    ppermute x1, waiting for transfers between devices, body(): moved = lax.ppermute(shard, 'tm', [(i, i ^ 1) for i in range(count)])  13.8 us
    all_to_all x2, starting transfers between devices, route(): moved = lax.all_to_all(whole, 'dp', split_axis=0, concat_axis=0, tiled=True)  7.96 us
  transfers between devices with their start and end apart: 25, of which 16 were waited for; matrix products, arithmetic and copies ran while one was open for 2% of the time, Pallas kernels for 21%

profile of v14, /device:TPU:0, one launch (start us, length us, event | category | flops | bytes accessed | tf_op | source)
XLA Modules:
  0.0 244.1 jit_solution(83195465810500881)
XLA Ops:
  0.0 42.9 %pack.1 = (bf16[3,224,256]{2,1,0:T(8,128)(2,1)}, bf16[3,224,256]{2,1,0:T(8,128)(2,1)}, bf16[3,224,256]{2,1,0:T(8,128)(2,1)}, bf16[3,224,256]{2,1,0:T(8,128)(2,1)}) custom-call(s32[1]{0:T(128)} %bitcast.me_ref, bf16[224,1024]{1,0:T(8,128)(2,1)} %bitcast.35, bf16[224,1024]{1,0:T(8,128)(2,1)} %bitcast.36, bf16[224,1024]{1,0:T(8,128)(2,1)} %bitcast.37), custom_call_target="tpu_custom_call" | custom-call | flops 1100000000 | tf_op jit(solution)/shard_map/pack/pallas_call | solution.py:376
  42.9 5.1 %collective-permute-start = (bf16[3,224,256]{2,1,0:T(8,128)(2,1)}, bf16[3,224,256]{2,1,0:T(8,128)(2,1)S(1)}, u32[]{:S(2)}, u32[]{:S(2)}) collective-permute-start(bf16[3,224,256]{2,1,0:T(8,128)(2,1)} %get-tuple-element.57), channel_id=1, source_target_pairs={{0,3},{1,2},{2,1},{3,0},{4,7},{5,6},{6,5},{7,4},{8,11},{9,10},{10,... | collective-permute-start | bytes 1032200 | tf_op jit(solution)/shard_map/ppermute | solution.py:335
  48.7 2.3 collective-permute-start.6
  51.0 6.2 %collective-permute-done.refs_0_ = bf16[3,224,256]{2,1,0:T(8,128)(2,1)S(1)} collective-permute-done((bf16[3,224,256]{2,1,0:T(8,128)(2,1)}, bf16[3,224,256]{2,1,0:T(8,128)(2,1)S(1)}, u32[]{:S(2)}, u32[]{:S(2)}) %collective-permute-start) | collective-permute-done | bytes 344096 | tf_op jit(solution)/shard_map/ppermute | solution.py:335
  57.3 20.4 %collective-permute-done.1.refs_1_ = bf16[3,224,256]{2,1,0:T(8,128)(2,1)S(1)} collective-permute-done((bf16[3,224,256]{2,1,0:T(8,128)(2,1)}, bf16[3,224,256]{2,1,0:T(8,128)(2,1)S(1)}, u32[]{:S(2)}, u32[]{:S(2)}) %collective-permute-start.1) | collective-permute-done | bytes 344096 | tf_op jit(solution)/shard_map/ppermute | solution.py:335
  78.6 5.5 %attend.1 = (bf16[2,256,256]{2,1,0:T(8,128)(2,1)S(1)}, bf16[2,256,256]{2,1,0:T(8,128)(2,1)S(1)}, bf16[2,256,256]{2,1,0:T(8,128)(2,1)S(1)}, bf16[2,256,256]{2,1,0:T(8,128)(2,1)S(1)}) custom-call(s32[1]{0:T(128)} %bitcast.me_ref, f32[4]{0:T(128)S(1)} %dynamic_slice.3.scale_ref, s32[1,4]{1,0:T(1,128)S(1)} %copy-done.3, ...), custom_call_target="tpu_custom_call" | custom-call | flops 6600000000 | tf_op jit(solution)/shard_map/attend/pallas_call | solution.py:392
  84.9 2.5 %collective-permute-start.3 = (bf16[2,256,256]{2,1,0:T(8,128)(2,1)S(1)}, bf16[2,256,256]{2,1,0:T(8,128)(2,1)S(1)}, u32[]{:S(2)}, u32[]{:S(2)}) collective-permute-start(bf16[2,256,256]{2,1,0:T(8,128)(2,1)S(1)} %get-tuple-element.61), channel_id=1, source_target_pairs={{0,3},{1,2},{2,1},{3,0},{4,7},{5,6},{6,5},{7,4},{8,11},{9,10},{10,... | collective-permute-start | bytes 786440 | tf_op jit(solution)/shard_map/ppermute | solution.py:335
  87.4 1.9 collective-permute-start.5
  89.3 1.9 pad_maximum_fusion
  93.7 2.3 collective-permute-done.3.refs_0_
  96.0 12.1 %collective-permute-done.4.refs_1_ = bf16[2,256,256]{2,1,0:T(8,128)(2,1)S(1)} collective-permute-done((bf16[2,256,256]{2,1,0:T(8,128)(2,1)S(1)}, bf16[2,256,256]{2,1,0:T(8,128)(2,1)S(1)}, u32[]{:S(2)}, u32[]{:S(2)}) %collective-permute-start.4) | collective-permute-done | bytes 262176 | tf_op jit(solution)/shard_map/ppermute | solution.py:335
  108.9 11.6 %frames.2 = (bf16[704,1536]{1,0:T(8,128)(2,1)}, f32[224,128]{1,0:T(8,128)}, f32[12,224,128]{2,1,0:T(8,128)}) custom-call(s32[1]{0:T(128)} %bitcast.me_ref, s32[1]{0:T(128)} %bitcast.1.expert_ref, s32[1,4]{1,0:T(1,128)} %len_ref.5, bf16[1024,1536]{1,0:T(8,128)(2,1)} %proj_ref.3, f32[12,31,128]{2,1,0:T(8,128)} %bitcast.29, bf16[1536,8]{1,0:T(8,128)(2,1)} %copy.19.router_ref, ...), custom_call_target="tpu_custom_call" | custom-call | flops 7699999744 | tf_op jit(solution)/shard_map/frames/pallas_call | solution.py:432
  120.5 3.6 %all-to-all-start = ((bf16[8,88,1536]{2,1,0:T(8,128)(2,1)}), bf16[8,88,1536]{2,1,0:T(8,128)(2,1)S(1)}, u32[]{:S(2)}, u32[]{:S(2)}) async-start(bf16[8,88,1536]{2,1,0:T(8,128)(2,1)} %bitcast.28), calls=%async_computation | async-start | bytes 4325376 | tf_op jit(solution)/shard_map/all_to_all | solution.py:428
  124.9 11.1 %frames.3 = (bf16[704,1536]{1,0:T(8,128)(2,1)}, f32[224,128]{1,0:T(8,128)}, f32[12,224,128]{2,1,0:T(8,128)}) custom-call(s32[1]{0:T(128)} %bitcast.me_ref, s32[1]{0:T(128)} %bitcast.1.expert_ref, s32[1,4]{1,0:T(1,128)} %len_ref.5, bf16[1024,1536]{1,0:T(8,128)(2,1)} %proj_ref.3, f32[12,31,128]{2,1,0:T(8,128)} %bitcast.30, bf16[1536,8]{1,0:T(8,128)(2,1)} %copy.19.router_ref, ...), custom_call_target="tpu_custom_call" | custom-call | flops 7699999744 | tf_op jit(solution)/shard_map/frames/pallas_call | solution.py:432
  136.0 15.3 %all-to-all-done = bf16[8,88,1536]{2,1,0:T(8,128)(2,1)S(1)} async-done(((bf16[8,88,1536]{2,1,0:T(8,128)(2,1)}), bf16[8,88,1536]{2,1,0:T(8,128)(2,1)S(1)}, u32[]{:S(2)}, u32[]{:S(2)}) %all-to-all-start) | async-done | bytes 2162720 | tf_op jit(solution)/shard_map/all_to_all | solution.py:428
  151.4 4.3 %all-to-all-start.1 = ((bf16[8,88,1536]{2,1,0:T(8,128)(2,1)}), bf16[8,88,1536]{2,1,0:T(8,128)(2,1)}, u32[]{:S(2)}, u32[]{:S(2)}) async-start(bf16[8,88,1536]{2,1,0:T(8,128)(2,1)} %bitcast.27), calls=%async_computation.1 | async-start | bytes 4325376 | tf_op jit(solution)/shard_map/all_to_all | solution.py:428
  155.8 6.9 %experts.3.refs_2_ = f32[704,1536]{1,0:T(8,128)} custom-call(s32[1]{0:T(128)} %bitcast.1.expert_ref, bf16[704,1536]{1,0:T(8,128)(2,1)} %bitcast.19, bf16[512,1536]{1,0:T(8,128)(2,1)} %bitcast.24, bf16[512,1536]{1,0:T(8,128)(2,1)} %bitcast.21), custom_call_target="tpu_custom_call" | custom-call | tf_op jit(solution)/shard_map/experts/pallas_call | solution.py:461
  162.7 13.8 %collective-permute-done.7.refs_1_.refs_3_ = bf16[1024,1536]{1,0:T(8,128)(2,1)} collective-permute-done((bf16[1024,1536]{1,0:T(8,128)(2,1)}, bf16[1024,1536]{1,0:T(8,128)(2,1)}, u32[]{:S(2)}, u32[]{:S(2)}) %collective-permute-start.7) | collective-permute-done | bytes 3145760 | tf_op jit(solution)/shard_map/ppermute | solution.py:411
  176.5 6.8 %experts.4 = (bf16[88,1536]{1,0:T(8,128)(2,1)}, bf16[88,1536]{1,0:T(8,128)(2,1)}, bf16[88,1536]{1,0:T(8,128)(2,1)}, bf16[88,1536]{1,0:T(8,128)(2,1)}, bf16[88,15...) custom-call(s32[1]{0:T(128)} %bitcast.1.expert_ref, ...), custom_call_target="tpu_custom_call" | custom-call | flops 8800000000 | tf_op jit(solution)/shard_map/experts/pallas_call | solution.py:461
  183.4 2.5 %collective-permute-start.8 = (bf16[88,1536]{1,0:T(8,128)(2,1)}, bf16[88,1536]{1,0:T(8,128)(2,1)S(1)}, u32[]{:S(2)}, u32[]{:S(2)}) collective-permute-start(bf16[88,1536]{1,0:T(8,128)(2,1)} %get-tuple-element.84), channel_id=1, source_target_pairs={{0,24},{4,28},{8,16},{12,20},{16,8},{20,12},{24,0},{28,4},{1,25},{... | collective-permute-start | bytes 811016 | tf_op jit(solution)/shard_map/ppermute | solution.py:335
  189.4 8.8 %experts.5 = (bf16[88,1536]{1,0:T(8,128)(2,1)}, bf16[88,1536]{1,0:T(8,128)(2,1)}, bf16[88,1536]{1,0:T(8,128)(2,1)}, bf16[88,1536]{1,0:T(8,128)(2,1)}, bf16[88,15...) custom-call(s32[1]{0:T(128)} %bitcast.1.expert_ref, ...), custom_call_target="tpu_custom_call" | custom-call | flops 8800000000 | tf_op jit(solution)/shard_map/experts/pallas_call | solution.py:461
  199.0 5.8 %collective-permute-done.10.refs_2_ = bf16[88,1536]{1,0:T(8,128)(2,1)S(1)} collective-permute-done((bf16[88,1536]{1,0:T(8,128)(2,1)}, bf16[88,1536]{1,0:T(8,128)(2,1)S(1)}, u32[]{:S(2)}, u32[]{:S(2)}) %collective-permute-start.10) | collective-permute-done | bytes 270368 | tf_op jit(solution)/shard_map/ppermute | solution.py:335
  204.8 2.7 %collective-permute-done.11.refs_3_ = bf16[88,1536]{1,0:T(8,128)(2,1)S(1)} collective-permute-done((bf16[88,1536]{1,0:T(8,128)(2,1)}, bf16[88,1536]{1,0:T(8,128)(2,1)S(1)}, u32[]{:S(2)}, u32[]{:S(2)}) %collective-permute-start.11) | collective-permute-done | bytes 270368 | tf_op jit(solution)/shard_map/ppermute | solution.py:335
  209.2 2.1 collective-permute-start.16
  211.3 2.3 collective-permute-start.17
  213.6 2.3 collective-permute-start.19
  216.6 5.0 %collective-permute-done.17.refs_0_ = bf16[88,1536]{1,0:T(8,128)(2,1)S(1)} collective-permute-done((bf16[88,1536]{1,0:T(8,128)(2,1)S(1)}, bf16[88,1536]{1,0:T(8,128)(2,1)S(1)}, u32[]{:S(2)}, u32[]{:S(2)}) %collective-permute-start.17) | collective-permute-done | bytes 270368 | tf_op jit(solution)/shard_map/ppermute | solution.py:335
  222.9 3.4 %collective-permute-done.18.refs_1_ = bf16[88,1536]{1,0:T(8,128)(2,1)S(1)} collective-permute-done((bf16[88,1536]{1,0:T(8,128)(2,1)S(1)}, bf16[88,1536]{1,0:T(8,128)(2,1)S(1)}, u32[]{:S(2)}, u32[]{:S(2)}) %collective-permute-start.18) | collective-permute-done | bytes 270368 | tf_op jit(solution)/shard_map/ppermute | solution.py:335
  226.3 2.2 collective-permute-start.22
  228.5 4.6 %collective-permute-done.19.refs_2_ = bf16[88,1536]{1,0:T(8,128)(2,1)S(1)} collective-permute-done((bf16[88,1536]{1,0:T(8,128)(2,1)S(1)}, bf16[88,1536]{1,0:T(8,128)(2,1)S(1)}, u32[]{:S(2)}, u32[]{:S(2)}) %collective-permute-start.19) | collective-permute-done | bytes 270368 | tf_op jit(solution)/shard_map/ppermute | solution.py:335
  233.1 3.8 %collective-permute-done.20.refs_3_ = bf16[88,1536]{1,0:T(8,128)(2,1)S(1)} collective-permute-done((bf16[88,1536]{1,0:T(8,128)(2,1)S(1)}, bf16[88,1536]{1,0:T(8,128)(2,1)S(1)}, u32[]{:S(2)}, u32[]{:S(2)}) %collective-permute-start.20) | collective-permute-done | bytes 270368 | tf_op jit(solution)/shard_map/ppermute | solution.py:335
  237.8 4.6 %collective-permute-done.16.part_ref = bf16[224,1536]{1,0:T(8,128)(2,1)S(1)} collective-permute-done((bf16[224,1536]{1,0:T(8,128)(2,1)S(1)}, bf16[224,1536]{1,0:T(8,128)(2,1)S(1)}, u32[]{:S(2)}, u32[]{:S(2)}) %collective-permute-start.16) | collective-permute-done | bytes 688160 | tf_op jit(solution)/shard_map/ppermute | solution.py:503
  (88 shorter events, 16.9 us)
Async XLA Ops:
  0.0 48.7 %copy-start.13 = (s32[1,224,2]{1,2,0:T(2,128)S(1)}, s32[1,224,2]{1,2,0:T(2,128)}, u32[]{:S(2)}) copy-start(s32[1,224,2]{1,2,0:T(2,128)} %param.21) | copy-start | bytes 5380
  0.0 51.0 %copy-start.26 = (f32[16]{0:T(128)S(1)}, f32[16]{0:T(128)}, u32[]{:S(2)}) copy-start(f32[16]{0:T(128)} %param.14) | copy-start | bytes 196
  0.0 77.6 %copy-start.3 = (s32[1,4]{1,0:T(1,128)S(1)}, s32[1,4]{1,0:T(1,128)}, u32[]{:S(2)}) copy-start(s32[1,4]{1,0:T(1,128)} %len_ref.5) | copy-start | bytes 52
  42.9 14.4 %collective-permute-start = (bf16[3,224,256]{2,1,0:T(8,128)(2,1)}, bf16[3,224,256]{2,1,0:T(8,128)(2,1)S(1)}, u32[]{:S(2)}, u32[]{:S(2)}) collective-permute-start(bf16[3,224,256]{2,1,0:T(8,128)(2,1)} %get-tuple-element.57), channel_id=1, source_target_pairs={{0,3},{1,2},{2,1},{3,0},{4,7},{5,6},{6,5},{7,4},{8,11},{9,10},{10,... | collective-permute-start | bytes 1032200 | tf_op jit(solution)/shard_map/ppermute | solution.py:335
  48.0 29.6 %collective-permute-start.1 = (bf16[3,224,256]{2,1,0:T(8,128)(2,1)}, bf16[3,224,256]{2,1,0:T(8,128)(2,1)S(1)}, u32[]{:S(2)}, u32[]{:S(2)}) collective-permute-start(bf16[3,224,256]{2,1,0:T(8,128)(2,1)} %get-tuple-element.58), channel_id=1, source_target_pairs={{0,2},{1,3},{2,0},{3,1},{4,6},{5,7},{6,4},{7,5},{8,10},{9,11},{10,... | collective-permute-start | bytes 1032200 | tf_op jit(solution)/shard_map/ppermute | solution.py:335
  48.0 29.6 %collective-permute-start.2 = (bf16[3,224,256]{2,1,0:T(8,128)(2,1)}, bf16[3,224,256]{2,1,0:T(8,128)(2,1)S(1)}, u32[]{:S(2)}, u32[]{:S(2)}) collective-permute-start(bf16[3,224,256]{2,1,0:T(8,128)(2,1)} %get-tuple-element.59), channel_id=1, source_target_pairs={{0,1},{1,0},{2,3},{3,2},{4,5},{5,4},{6,7},{7,6},{8,9},{9,8},{10,11... | collective-permute-start | bytes 1032200 | tf_op jit(solution)/shard_map/ppermute | solution.py:335
  48.7 44.3 %collective-permute-start.6 = (s32[224,2]{0,1:T(2,128)S(1)}, s32[224,2]{0,1:T(2,128)S(1)}, u32[]{:S(2)}, u32[]{:S(2)}) collective-permute-start(s32[224,2]{0,1:T(2,128)S(1)} %bitcast.32), channel_id=1, source_target_pairs={{0,2},{1,3},{2,0},{3,1},{4,6},{5,7},{6,4},{7,5},{8,10},{9,11},{10,... | collective-permute-start | bytes 5384 | tf_op jit(solution)/shard_map/ppermute | solution.py:388
  84.9 11.1 %collective-permute-start.3 = (bf16[2,256,256]{2,1,0:T(8,128)(2,1)S(1)}, bf16[2,256,256]{2,1,0:T(8,128)(2,1)S(1)}, u32[]{:S(2)}, u32[]{:S(2)}) collective-permute-start(bf16[2,256,256]{2,1,0:T(8,128)(2,1)S(1)} %get-tuple-element.61), channel_id=1, source_target_pairs={{0,3},{1,2},{2,1},{3,0},{4,7},{5,6},{6,5},{7,4},{8,11},{9,10},{10,... | collective-permute-start | bytes 786440 | tf_op jit(solution)/shard_map/ppermute | solution.py:335
  87.4 20.7 %collective-permute-start.4 = (bf16[2,256,256]{2,1,0:T(8,128)(2,1)S(1)}, bf16[2,256,256]{2,1,0:T(8,128)(2,1)S(1)}, u32[]{:S(2)}, u32[]{:S(2)}) collective-permute-start(bf16[2,256,256]{2,1,0:T(8,128)(2,1)S(1)} %get-tuple-element.62), channel_id=1, source_target_pairs={{0,2},{1,3},{2,0},{3,1},{4,6},{5,7},{6,4},{7,5},{8,10},{9,11},{10,... | collective-permute-start | bytes 786440 | tf_op jit(solution)/shard_map/ppermute | solution.py:335
  87.4 20.7 %collective-permute-start.5 = (bf16[2,256,256]{2,1,0:T(8,128)(2,1)S(1)}, bf16[2,256,256]{2,1,0:T(8,128)(2,1)S(1)}, u32[]{:S(2)}, u32[]{:S(2)}) collective-permute-start(bf16[2,256,256]{2,1,0:T(8,128)(2,1)S(1)} %get-tuple-element.63), channel_id=1, source_target_pairs={{0,1},{1,0},{2,3},{3,2},{4,5},{5,4},{6,7},{7,6},{8,9},{9,8},{10,11... | collective-permute-start | bytes 786440 | tf_op jit(solution)/shard_map/ppermute | solution.py:335
  108.1 68.4 %collective-permute-start.7 = (bf16[1024,1536]{1,0:T(8,128)(2,1)}, bf16[1024,1536]{1,0:T(8,128)(2,1)}, u32[]{:S(2)}, u32[]{:S(2)}) collective-permute-start(bf16[1024,1536]{1,0:T(8,128)(2,1)} %pad_maximum_fusion), channel_id=1, source_target_pairs={{0,1},{1,0},{2,3},{3,2},{4,5},{5,4},{6,7},{7,6},{8,9},{9,8},{10,11... | collective-permute-start | bytes 9437192 | tf_op jit(solution)/shard_map/ppermute | solution.py:411
  120.5 30.9 %all-to-all-start = ((bf16[8,88,1536]{2,1,0:T(8,128)(2,1)}), bf16[8,88,1536]{2,1,0:T(8,128)(2,1)S(1)}, u32[]{:S(2)}, u32[]{:S(2)}) async-start(bf16[8,88,1536]{2,1,0:T(8,128)(2,1)} %bitcast.28), calls=%async_computation | async-start | bytes 4325376 | tf_op jit(solution)/shard_map/all_to_all | solution.py:428
  151.4 31.9 %all-to-all-start.1 = ((bf16[8,88,1536]{2,1,0:T(8,128)(2,1)}), bf16[8,88,1536]{2,1,0:T(8,128)(2,1)}, u32[]{:S(2)}, u32[]{:S(2)}) async-start(bf16[8,88,1536]{2,1,0:T(8,128)(2,1)} %bitcast.27), calls=%async_computation.1 | async-start | bytes 4325376 | tf_op jit(solution)/shard_map/all_to_all | solution.py:428
  183.4 14.9 %collective-permute-start.8 = (bf16[88,1536]{1,0:T(8,128)(2,1)}, bf16[88,1536]{1,0:T(8,128)(2,1)S(1)}, u32[]{:S(2)}, u32[]{:S(2)}) collective-permute-start(bf16[88,1536]{1,0:T(8,128)(2,1)} %get-tuple-element.84), channel_id=1, source_target_pairs={{0,24},{4,28},{8,16},{12,20},{16,8},{20,12},{24,0},{28,4},{1,25},{... | collective-permute-start | bytes 811016 | tf_op jit(solution)/shard_map/ppermute | solution.py:335
  185.9 13.0 %collective-permute-start.9 = (bf16[88,1536]{1,0:T(8,128)(2,1)}, bf16[88,1536]{1,0:T(8,128)(2,1)S(1)}, u32[]{:S(2)}, u32[]{:S(2)}) collective-permute-start(bf16[88,1536]{1,0:T(8,128)(2,1)} %get-tuple-element.85), channel_id=1, source_target_pairs={{0,28},{4,24},{8,20},{12,16},{16,12},{20,8},{24,4},{28,0},{1,29},{... | collective-permute-start | bytes 811016 | tf_op jit(solution)/shard_map/ppermute | solution.py:335
  185.9 18.9 %collective-permute-start.10 = (bf16[88,1536]{1,0:T(8,128)(2,1)}, bf16[88,1536]{1,0:T(8,128)(2,1)S(1)}, u32[]{:S(2)}, u32[]{:S(2)}) collective-permute-start(bf16[88,1536]{1,0:T(8,128)(2,1)} %get-tuple-element.86), channel_id=1, source_target_pairs={{0,8},{4,12},{8,0},{12,4},{16,24},{20,28},{24,16},{28,20},{1,9},{5... | collective-permute-start | bytes 811016 | tf_op jit(solution)/shard_map/ppermute | solution.py:335
  186.4 21.1 %collective-permute-start.11 = (bf16[88,1536]{1,0:T(8,128)(2,1)}, bf16[88,1536]{1,0:T(8,128)(2,1)S(1)}, u32[]{:S(2)}, u32[]{:S(2)}) collective-permute-start(bf16[88,1536]{1,0:T(8,128)(2,1)} %get-tuple-element.87), channel_id=1, source_target_pairs={{0,12},{4,8},{8,4},{12,0},{16,28},{20,24},{24,20},{28,16},{1,13},{... | collective-permute-start | bytes 811016 | tf_op jit(solution)/shard_map/ppermute | solution.py:335
  187.8 19.7 %collective-permute-start.12 = (bf16[88,1536]{1,0:T(8,128)(2,1)}, bf16[88,1536]{1,0:T(8,128)(2,1)S(1)}, u32[]{:S(2)}, u32[]{:S(2)}) collective-permute-start(bf16[88,1536]{1,0:T(8,128)(2,1)} %get-tuple-element.88), channel_id=1, source_target_pairs={{0,16},{4,20},{8,24},{12,28},{16,0},{20,4},{24,8},{28,12},{1,17},{... | collective-permute-start | bytes 811016 | tf_op jit(solution)/shard_map/ppermute | solution.py:335
  198.2 28.1 %copy-start.15 = (bf16[88,1536]{1,0:T(8,128)(2,1)S(1)}, bf16[88,1536]{1,0:T(8,128)(2,1)}, u32[]{:S(2)}) copy-start(bf16[88,1536]{1,0:T(8,128)(2,1)} %get-tuple-element.107) | copy-start | bytes 811012
  198.2 44.1 %copy-start = (f32[12,224,128]{2,1,0:T(8,128)S(1)}, f32[12,224,128]{2,1,0:T(8,128)}, u32[]{:S(2)}) copy-start(f32[12,224,128]{2,1,0:T(8,128)} %get-tuple-element.71.second_ref) | copy-start | bytes 4128772
  198.3 44.1 %copy-start.1 = (bf16[88,1536]{1,0:T(8,128)(2,1)S(1)}, bf16[88,1536]{1,0:T(8,128)(2,1)}, u32[]{:S(2)}) copy-start(bf16[88,1536]{1,0:T(8,128)(2,1)} %get-tuple-element.108.refs_7_) | copy-start | bytes 811012
  198.3 44.1 %copy-start.2 = (f32[224,128]{1,0:T(8,128)S(1)}, f32[224,128]{1,0:T(8,128)}, u32[]{:S(2)}) copy-start(f32[224,128]{1,0:T(8,128)} %get-tuple-element.70.info_ref) | copy-start | bytes 344068
  198.3 10.0 %collective-permute-start.13 = (bf16[88,1536]{1,0:T(8,128)(2,1)S(1)}, bf16[88,1536]{1,0:T(8,128)(2,1)S(1)}, u32[]{:S(2)}, u32[]{:S(2)}) collective-permute-start(bf16[88,1536]{1,0:T(8,128)(2,1)S(1)} %copy-done.22), channel_id=1, source_target_pairs={{0,20},{4,16},{8,28},{12,24},{16,4},{20,0},{24,12},{28,8},{1,21},{... | collective-permute-start | bytes 811016 | tf_op jit(solution)/shard_map/ppermute | solution.py:335
  198.9 9.4 %collective-permute-start.14 = (bf16[88,1536]{1,0:T(8,128)(2,1)S(1)}, bf16[88,1536]{1,0:T(8,128)(2,1)S(1)}, u32[]{:S(2)}, u32[]{:S(2)}) collective-permute-start(bf16[88,1536]{1,0:T(8,128)(2,1)S(1)} %copy-done.21), channel_id=1, source_target_pairs={{0,4},{4,0},{8,12},{12,8},{16,20},{20,16},{24,28},{28,24},{1,5},{5... | collective-permute-start | bytes 811016 | tf_op jit(solution)/shard_map/ppermute | solution.py:335
  204.8 3.6 %collective-permute-start.15 = (bf16[88,1536]{1,0:T(8,128)(2,1)}, bf16[88,1536]{1,0:T(8,128)(2,1)S(1)}, u32[]{:S(2)}, u32[]{:S(2)}) collective-permute-start(bf16[88,1536]{1,0:T(8,128)(2,1)} %get-tuple-element.93), channel_id=1, source_target_pairs={{0,4},{4,0},{8,12},{12,8},{16,20},{20,16},{24,28},{28,24},{1,5},{5... | collective-permute-start | bytes 811016 | tf_op jit(solution)/shard_map/ppermute | solution.py:335
  209.2 33.2 %collective-permute-start.16 = (bf16[224,1536]{1,0:T(8,128)(2,1)S(1)}, bf16[224,1536]{1,0:T(8,128)(2,1)S(1)}, u32[]{:S(2)}, u32[]{:S(2)}) collective-permute-start(bf16[224,1536]{1,0:T(8,128)(2,1)S(1)} %theirs.1), channel_id=1, source_target_pairs={{0,2},{1,3},{2,0},{3,1},{4,6},{5,7},{6,4},{7,5},{8,10},{9,11},{10,... | collective-permute-start | bytes 2064392 | tf_op jit(solution)/shard_map/ppermute | solution.py:503
  211.3 10.3 %collective-permute-start.17 = (bf16[88,1536]{1,0:T(8,128)(2,1)S(1)}, bf16[88,1536]{1,0:T(8,128)(2,1)S(1)}, u32[]{:S(2)}, u32[]{:S(2)}) collective-permute-start(bf16[88,1536]{1,0:T(8,128)(2,1)S(1)} %copy-done.20), channel_id=1, source_target_pairs={{0,24},{4,28},{8,16},{12,20},{16,8},{20,12},{24,0},{28,4},{1,25},{... | collective-permute-start | bytes 811016 | tf_op jit(solution)/shard_map/ppermute | solution.py:335
  213.6 12.7 %collective-permute-start.18 = (bf16[88,1536]{1,0:T(8,128)(2,1)S(1)}, bf16[88,1536]{1,0:T(8,128)(2,1)S(1)}, u32[]{:S(2)}, u32[]{:S(2)}) collective-permute-start(bf16[88,1536]{1,0:T(8,128)(2,1)S(1)} %copy-done.19), channel_id=1, source_target_pairs={{0,28},{4,24},{8,20},{12,16},{16,12},{20,8},{24,4},{28,0},{1,29},{... | collective-permute-start | bytes 811016 | tf_op jit(solution)/shard_map/ppermute | solution.py:335
  213.6 19.5 %collective-permute-start.19 = (bf16[88,1536]{1,0:T(8,128)(2,1)S(1)}, bf16[88,1536]{1,0:T(8,128)(2,1)S(1)}, u32[]{:S(2)}, u32[]{:S(2)}) collective-permute-start(bf16[88,1536]{1,0:T(8,128)(2,1)S(1)} %copy-done.18), channel_id=1, source_target_pairs={{0,8},{4,12},{8,0},{12,4},{16,24},{20,28},{24,16},{28,20},{1,9},{5... | collective-permute-start | bytes 811016 | tf_op jit(solution)/shard_map/ppermute | solution.py:335
  215.9 20.9 %collective-permute-start.20 = (bf16[88,1536]{1,0:T(8,128)(2,1)S(1)}, bf16[88,1536]{1,0:T(8,128)(2,1)S(1)}, u32[]{:S(2)}, u32[]{:S(2)}) collective-permute-start(bf16[88,1536]{1,0:T(8,128)(2,1)S(1)} %copy-done.17), channel_id=1, source_target_pairs={{0,12},{4,8},{8,4},{12,0},{16,28},{20,24},{24,20},{28,16},{1,13},{... | collective-permute-start | bytes 811016 | tf_op jit(solution)/shard_map/ppermute | solution.py:335
  221.6 15.3 %collective-permute-start.21 = (bf16[88,1536]{1,0:T(8,128)(2,1)S(1)}, bf16[88,1536]{1,0:T(8,128)(2,1)S(1)}, u32[]{:S(2)}, u32[]{:S(2)}) collective-permute-start(bf16[88,1536]{1,0:T(8,128)(2,1)S(1)} %copy-done.16), channel_id=1, source_target_pairs={{0,16},{4,20},{8,24},{12,28},{16,0},{20,4},{24,8},{28,12},{1,17},{... | collective-permute-start | bytes 811016 | tf_op jit(solution)/shard_map/ppermute | solution.py:335
  226.3 11.4 %collective-permute-start.22 = (bf16[88,1536]{1,0:T(8,128)(2,1)S(1)}, bf16[88,1536]{1,0:T(8,128)(2,1)S(1)}, u32[]{:S(2)}, u32[]{:S(2)}) collective-permute-start(bf16[88,1536]{1,0:T(8,128)(2,1)S(1)} %copy-done.15), channel_id=1, source_target_pairs={{0,20},{4,16},{8,28},{12,24},{16,4},{20,0},{24,12},{28,8},{1,21},{... | collective-permute-start | bytes 811016 | tf_op jit(solution)/shard_map/ppermute | solution.py:335
  (20 other events, 226.4 us)
